TPU v7x, 32 devices: a whole 2x2x4 slice. The times are simulated.
32 devices in a mesh: blk: 8 (over y, x, core), ch: 4 (over z).
Axes of the slice: x: 2, y: 2, z: 4, core: 2. Of those that a mesh axis runs over, the one named last changes fastest.
Arguments:
- features_in: bfloat16 [32, 128, 2048], P('blk', None, 'ch'), may hold values from -6 to 6
- w_reduce: bfloat16 [2, 512, 2048], P(None, 'ch'), may hold values from -0.125 to 0.125
- w_dilated: bfloat16 [2, 512, 9, 512], P(None, 'ch'), may hold values from -0.09375 to 0.09375
- w_expand: bfloat16 [2, 512, 2048], P(None, None, 'ch'), may hold values from -0.25 to 0.25
- w_heads: bfloat16 [2, 4, 512, 9, 2048], P(None, None, 'ch'), may hold values from -0.046875 to 0.046875
- w_messages: bfloat16 [2, 6, 512, 9, 512], P(None, None, 'ch'), may hold values from -0.09375 to 0.09375
- norm_gain: float32 [2, 2, 512], P(None, None, 'ch'), may hold values from 0.5 to 1.5
- norm_bias: float32 [2, 2, 512], P(None, None, 'ch'), may hold values from -3 to 3
- wide_gain: float32 [2, 2048], P(None, 'ch'), may hold values from 0.5 to 1.5
- wide_bias: float32 [2, 2048], P(None, 'ch'), may hold values from -3 to 3
- gate_gain: float32 [2, 6, 512], P(None, None, 'ch'), may hold values from -4 to 4
- gate_bias: float32 [2, 6, 512], P(None, None, 'ch'), may hold values from -4 to 4
- canvas_ids: int32 [32, 128], replicated, may hold values from 0 to 8, as said below
- output_cotangent: bfloat16 [32, 128, 2048], P('blk', None, 'ch'), may hold values from -6 to 6
- task_cotangents: bfloat16 [2, 2, 32, 128, 512], P(None, None, 'blk', None, 'ch'), may hold values from -6 to 6
Outputs:
- output: bfloat16 [32, 128, 2048], P('blk', None, 'ch')
- task_maps: bfloat16 [2, 2, 32, 128, 512], P(None, None, 'blk', None, 'ch')
- input_grad: float32 [32, 128, 2048], P('blk', None, 'ch')
- w_reduce_grad: float32 [2, 2048, 512], P(None, 'blk', 'ch')
- w_dilated_grad: float32 [2, 9, 512, 512], P(None, None, 'blk', 'ch')
- w_expand_grad: float32 [2, 512, 2048], P(None, 'blk', 'ch')
- w_heads_grad: float32 [2, 4, 9, 2048, 512], P(None, None, None, 'blk', 'ch')
- w_messages_grad: float32 [2, 6, 9, 512, 512], P(None, None, None, 'blk', 'ch')
- norm_gain_grad: float32 [2, 2, 512], P(None, None, 'ch')
- norm_bias_grad: float32 [2, 2, 512], P(None, None, 'ch')
- wide_gain_grad: float32 [2, 2048], P(None, 'ch')
- wide_bias_grad: float32 [2, 2048], P(None, 'ch')
- gate_gain_grad: float32 [2, 6, 512], P(None, None, 'ch')
- gate_bias_grad: float32 [2, 6, 512], P(None, None, 'ch')
Inputs may be any that keep to these rules, and one draw needn't show every extreme that they name: `canvas_ids`: each image id marks one rectangle of the canvas; images lie in four vertical strips, and one image covers every canvas row.
All inputs are finite; a program needn't handle non-finite values.
Results may differ from a plain program's by a relative error of at most 0.03.
Values may be sent and summed in bfloat16 or wider, within the bound.
A program may use at most 384 MiB of HBM per device.

v0:
```python
import jax
import jax.numpy as jnp
from jax import lax
from jax.sharding import PartitionSpec as P

epsilon = 1e-05
tap_offsets = tuple(((row_step, col_step) for row_step in (-1, 0, 1) for col_step in (-1, 0, 1)))
message_pairs = ((1, 0), (2, 0), (3, 0), (0, 3), (1, 3), (2, 3))


def extended_2(block, sides, width):
    for axis, dim in sides:
        count = lax.axis_size(axis)
        forward = [(i, i + 1) for i in range(count - 1)]
        backward = [(target, source) for source, target in forward]
        low = lax.ppermute(
            lax.slice_in_dim(block, block.shape[dim] - width, None, axis=dim), axis, forward
        )
        high = lax.ppermute(lax.slice_in_dim(block, 0, width, axis=dim), axis, backward)
        block = jnp.concatenate([low, block, high], axis=dim)
    return block


def silu_slope(values):
    sigmoid_value = jax.nn.sigmoid(values)
    return sigmoid_value * (1.0 + values * (1.0 - sigmoid_value))


def gather_channels(values):
    return lax.all_gather(values, "ch", axis=3, tiled=True)


def reduce_channels(values):
    return lax.psum_scatter(
        values.astype(jnp.bfloat16), "ch", scatter_dimension=3, tiled=True
    ).astype(jnp.float32)


def extend_rows(values, halo_width):
    return extended_2(values, (("blk", 0),), halo_width)


def pixel_totals(first_sum, second_sum):
    return lax.psum((first_sum, second_sum), "blk")


def weight_totals(reduce_grad, dilated_grad, expand_grad, heads_grad, messages_grad):
    return (
        lax.psum_scatter(
            reduce_grad.astype(jnp.bfloat16), "blk", scatter_dimension=1, tiled=True
        ).astype(jnp.float32),
        lax.psum_scatter(
            dilated_grad.astype(jnp.bfloat16), "blk", scatter_dimension=2, tiled=True
        ).astype(jnp.float32),
        lax.psum_scatter(
            expand_grad.astype(jnp.bfloat16), "blk", scatter_dimension=1, tiled=True
        ).astype(jnp.float32),
        lax.psum_scatter(
            heads_grad.astype(jnp.bfloat16), "blk", scatter_dimension=3, tiled=True
        ).astype(jnp.float32),
        lax.psum_scatter(
            messages_grad.astype(jnp.bfloat16), "blk", scatter_dimension=3, tiled=True
        ).astype(jnp.float32),
    )


def widen(values, halo_width):
    return extend_rows(gather_channels(values), halo_width)


def local_masks(canvas_ids, row_count, dilation):
    col_count = canvas_ids.shape[1]
    padded = jnp.pad(canvas_ids, 2, constant_values=-1)
    start = lax.axis_index("blk") * row_count
    window = lax.dynamic_slice(padded, (start, jnp.int32(0)), (row_count + 4, col_count + 4))
    centre = window[2 : 2 + row_count, 2 : 2 + col_count]
    result = []
    for row_step, col_step in tap_offsets:
        top = 2 + row_step * dilation
        left = 2 + col_step * dilation
        result.append(window[top : top + row_count, left : left + col_count] == centre)
    return jnp.stack(result)


def shifted(padded, halo_width, dilation, row_step, col_step, row_count, col_count):
    top = halo_width + row_step * dilation
    left = dilation + col_step * dilation
    return padded[top : top + row_count, left : left + col_count]


def conv_forward(extended, halo_width, dilation, weights, tap_masks):
    row_count = extended.shape[0] - 2 * halo_width
    col_count = extended.shape[1]
    padded = jnp.pad(extended, ((0, 0), (dilation, dilation), (0, 0)))
    running = jnp.zeros((row_count, col_count, weights.shape[0], weights.shape[1]), jnp.float32)
    for tap_index, (row_step, col_step) in enumerate(tap_offsets):
        window = shifted(padded, halo_width, dilation, row_step, col_step, row_count, col_count)
        product = jnp.einsum(
            "rwc,koc->rwko", window, weights[:, :, tap_index], preferred_element_type=jnp.float32
        )
        running = running + jnp.where(tap_masks[tap_index][:, :, None, None], product, 0.0)
    return running


def conv_weight_grad(extended, halo_width, dilation, gradient, tap_masks):
    row_count = extended.shape[0] - 2 * halo_width
    col_count = extended.shape[1]
    padded = jnp.pad(extended, ((0, 0), (dilation, dilation), (0, 0)))
    result = []
    for tap_index, (row_step, col_step) in enumerate(tap_offsets):
        window = shifted(padded, halo_width, dilation, row_step, col_step, row_count, col_count)
        masked = jnp.where(
            tap_masks[tap_index][:, :, None, None], gradient, jnp.zeros((), gradient.dtype)
        )
        result.append(
            jnp.einsum("rwc,rwko->kco", window, masked, preferred_element_type=jnp.float32)
        )
    return jnp.stack(result, axis=1)


def conv_input_grad(grad_extended, halo_width, dilation, weights, tap_masks):
    row_count = grad_extended.shape[0] - 2 * halo_width
    col_count = grad_extended.shape[1]
    padded = jnp.pad(grad_extended, ((0, 0), (dilation, dilation), (0, 0), (0, 0)))
    running = jnp.zeros((row_count, col_count, weights.shape[3]), jnp.float32)
    for tap_index, (row_step, col_step) in enumerate(tap_offsets):
        window = shifted(padded, halo_width, dilation, -row_step, -col_step, row_count, col_count)
        product = jnp.einsum(
            "rwko,koc->rwc", window, weights[:, :, tap_index], preferred_element_type=jnp.float32
        )
        running = running + jnp.where(tap_masks[8 - tap_index][:, :, None], product, 0.0)
    return running


def norm_forward(hidden, gain, bias, pixel_count):
    total_sum, square_sum = pixel_totals(
        jnp.sum(hidden, axis=(0, 1)), jnp.sum(hidden * hidden, axis=(0, 1))
    )
    mean_value = total_sum / pixel_count
    variance = square_sum / pixel_count - mean_value * mean_value
    inverse = lax.rsqrt(variance + epsilon)
    normed = (hidden - mean_value) * inverse
    return (gain * normed + bias, normed, inverse)


def norm_backward(upstream, normed, inverse, gain, pixel_count):
    bias_grad, gain_grad = pixel_totals(
        jnp.sum(upstream, axis=(0, 1)), jnp.sum(upstream * normed, axis=(0, 1))
    )
    hidden_grad = (
        gain * inverse * (upstream - bias_grad / pixel_count - normed * gain_grad / pixel_count)
    )
    return (hidden_grad, gain_grad, bias_grad)


def layer_forward(inputs, params, masks_one, masks_two, pixel_count):
    (
        reduce_w,
        dilated_w,
        expand_w,
        heads_w,
        messages_w,
        narrow_gain,
        narrow_bias,
        wide_g,
        wide_b,
        gate_g,
        gate_b,
    ) = params
    stored = {}
    inputs_full = gather_channels(inputs[:, :, None, :])[:, :, 0, :]
    first_pre = jnp.einsum("rwc,oc->rwo", inputs_full, reduce_w, preferred_element_type=jnp.float32)
    first_norm, first_normed, first_inverse = norm_forward(
        first_pre, narrow_gain[0], narrow_bias[0], pixel_count
    )
    first_act = jax.nn.silu(first_norm).astype(jnp.bfloat16)
    first_ext = widen(first_act[:, :, None, :], 2)[:, :, 0, :]
    second_pre = conv_forward(first_ext, 2, 2, dilated_w[None], masks_two)[:, :, 0, :]
    second_norm, second_normed, second_inverse = norm_forward(
        second_pre, narrow_gain[1], narrow_bias[1], pixel_count
    )
    second_act = jax.nn.silu(second_norm).astype(jnp.bfloat16)
    second_full = gather_channels(second_act[:, :, None, :])[:, :, 0, :]
    third_pre = jnp.einsum("rwc,co->rwo", second_full, expand_w, preferred_element_type=jnp.float32)
    third_norm, third_normed, third_inverse = norm_forward(third_pre, wide_g, wide_b, pixel_count)
    summed = third_norm + inputs.astype(jnp.float32)
    output = jax.nn.silu(summed).astype(jnp.bfloat16)
    output_ext = widen(output[:, :, None, :], 1)[:, :, 0, :]
    heads_pre = conv_forward(output_ext, 1, 1, heads_w, masks_one)
    features = jax.nn.silu(heads_pre).astype(jnp.bfloat16)
    features_ext = widen(features, 1)
    feature_values = features.astype(jnp.float32)
    depth_map = feature_values[:, :, 0]
    segment_map = feature_values[:, :, 3]
    message_list = []
    for pair_index, (source, target) in enumerate(message_pairs):
        message = conv_forward(
            features_ext[:, :, source], 1, 1, messages_w[pair_index][None], masks_one
        )[:, :, 0]
        gate_value = jax.nn.sigmoid(
            gate_g[pair_index] * feature_values[:, :, target] + gate_b[pair_index]
        )
        message_list.append(message)
        if target == 0:
            depth_map = depth_map + gate_value * message
        else:
            segment_map = segment_map + gate_value * message
    stored["inputs_full"] = inputs_full
    stored["first_norm"] = first_norm
    stored["first_normed"] = first_normed
    stored["first_inverse"] = first_inverse
    stored["first_ext"] = first_ext
    stored["second_norm"] = second_norm
    stored["second_normed"] = second_normed
    stored["second_inverse"] = second_inverse
    stored["second_full"] = second_full
    stored["third_normed"] = third_normed
    stored["third_inverse"] = third_inverse
    stored["summed"] = summed
    stored["output_ext"] = output_ext
    stored["heads_pre"] = heads_pre
    stored["features"] = feature_values
    stored["features_ext"] = features_ext
    stored["messages"] = message_list
    return (output, depth_map, segment_map, stored)


def layer_backward(
    stored, upstream, depth_grad, segment_grad, params, masks_one, masks_two, pixel_count
):
    (
        reduce_w,
        dilated_w,
        expand_w,
        heads_w,
        messages_w,
        narrow_gain,
        narrow_bias,
        wide_g,
        wide_b,
        gate_g,
        gate_b,
    ) = params
    feature_values = stored["features"]
    zero_map = jnp.zeros_like(depth_grad)
    feature_grads = [depth_grad, zero_map, zero_map, segment_grad]
    message_grads = []
    gain_terms = []
    bias_terms = []
    for pair_index, (source, target) in enumerate(message_pairs):
        target_grad = depth_grad if target == 0 else segment_grad
        gate_value = jax.nn.sigmoid(
            gate_g[pair_index] * feature_values[:, :, target] + gate_b[pair_index]
        )
        message_grads.append(target_grad * gate_value)
        slope = target_grad * stored["messages"][pair_index] * gate_value * (1.0 - gate_value)
        gain_terms.append(jnp.sum(slope * feature_values[:, :, target], axis=(0, 1)))
        bias_terms.append(jnp.sum(slope, axis=(0, 1)))
        feature_grads[target] = feature_grads[target] + slope * gate_g[pair_index]
    gate_gain_grad, gate_bias_grad = pixel_totals(jnp.stack(gain_terms), jnp.stack(bias_terms))
    message_stack = jnp.stack(message_grads, axis=2).astype(jnp.bfloat16)
    message_ext = extend_rows(message_stack, 1)
    weight_parts = []
    source_partials = [None, None, None, None]
    for pair_index, (source, target) in enumerate(message_pairs):
        weight_parts.append(
            conv_weight_grad(
                stored["features_ext"][:, :, source],
                1,
                1,
                message_stack[:, :, pair_index : pair_index + 1],
                masks_one,
            )
        )
        partial_grad = conv_input_grad(
            message_ext[:, :, pair_index : pair_index + 1],
            1,
            1,
            messages_w[pair_index][None],
            masks_one,
        )
        if source_partials[source] is None:
            source_partials[source] = partial_grad
        else:
            source_partials[source] = source_partials[source] + partial_grad
    messages_w_grad = jnp.concatenate(weight_parts, axis=0)
    source_sums = reduce_channels(jnp.stack(source_partials, axis=2))
    features_total = jnp.stack(feature_grads, axis=2) + source_sums
    heads_grad = (features_total * silu_slope(stored["heads_pre"])).astype(jnp.bfloat16)
    heads_w_grad = conv_weight_grad(stored["output_ext"], 1, 1, heads_grad, masks_one)
    heads_ext = extend_rows(heads_grad, 1)
    output_partial = conv_input_grad(heads_ext, 1, 1, heads_w, masks_one)
    output_total = upstream + reduce_channels(output_partial[:, :, None, :])[:, :, 0, :]
    summed_grad = output_total * silu_slope(stored["summed"])
    third_grad, wide_gain_grad, wide_bias_grad = norm_backward(
        summed_grad, stored["third_normed"], stored["third_inverse"], wide_g, pixel_count
    )
    third_low = third_grad.astype(jnp.bfloat16)
    expand_w_grad = jnp.einsum(
        "rwc,rwo->co", stored["second_full"], third_low, preferred_element_type=jnp.float32
    )
    second_partial = jnp.einsum(
        "rwo,co->rwc", third_low, expand_w, preferred_element_type=jnp.float32
    )
    second_act_grad = reduce_channels(second_partial[:, :, None, :])[:, :, 0, :]
    second_grad, second_gain_grad, second_bias_grad = norm_backward(
        second_act_grad * silu_slope(stored["second_norm"]),
        stored["second_normed"],
        stored["second_inverse"],
        narrow_gain[1],
        pixel_count,
    )
    second_low = second_grad.astype(jnp.bfloat16)[:, :, None, :]
    dilated_w_grad = conv_weight_grad(stored["first_ext"], 2, 2, second_low, masks_two)[0]
    second_ext = extend_rows(second_low, 2)
    first_partial = conv_input_grad(second_ext, 2, 2, dilated_w[None], masks_two)
    first_act_grad = reduce_channels(first_partial[:, :, None, :])[:, :, 0, :]
    first_grad, first_gain_grad, first_bias_grad = norm_backward(
        first_act_grad * silu_slope(stored["first_norm"]),
        stored["first_normed"],
        stored["first_inverse"],
        narrow_gain[0],
        pixel_count,
    )
    first_low = first_grad.astype(jnp.bfloat16)
    reduce_w_grad = jnp.einsum(
        "rwc,rwo->co", stored["inputs_full"], first_low, preferred_element_type=jnp.float32
    )
    inputs_partial = jnp.einsum(
        "rwo,oc->rwc", first_low, reduce_w, preferred_element_type=jnp.float32
    )
    inputs_grad = reduce_channels(inputs_partial[:, :, None, :])[:, :, 0, :] + summed_grad
    weight_grads = (reduce_w_grad, dilated_w_grad, expand_w_grad, heads_w_grad, messages_w_grad)
    small_grads = (
        jnp.stack([first_gain_grad, second_gain_grad]),
        jnp.stack([first_bias_grad, second_bias_grad]),
        wide_gain_grad,
        wide_bias_grad,
        gate_gain_grad,
        gate_bias_grad,
    )
    return (inputs_grad, weight_grads, small_grads)


def shards(
    features_in,
    w_reduce,
    w_dilated,
    w_expand,
    w_heads,
    w_messages,
    norm_gain,
    norm_bias,
    wide_gain,
    wide_bias,
    gate_gain,
    gate_bias,
    canvas_ids,
    output_cotangent,
    task_cotangents,
):
    row_count = features_in.shape[0]
    col_count = features_in.shape[1]
    pixel_count = float(row_count * col_count * lax.axis_size("blk"))
    masks_one = local_masks(canvas_ids, row_count, 1)
    masks_two = local_masks(canvas_ids, row_count, 2)
    layer_count = w_reduce.shape[0]
    layer_params = []
    for layer_index in range(layer_count):
        layer_params.append(
            (
                w_reduce[layer_index],
                w_dilated[layer_index],
                w_expand[layer_index],
                w_heads[layer_index],
                w_messages[layer_index],
                norm_gain[layer_index],
                norm_bias[layer_index],
                wide_gain[layer_index],
                wide_bias[layer_index],
                gate_gain[layer_index],
                gate_bias[layer_index],
            )
        )
    current = features_in
    stored_list = []
    task_list = []
    for layer_index in range(layer_count):
        current, depth_map, segment_map, stored = layer_forward(
            current, layer_params[layer_index], masks_one, masks_two, pixel_count
        )
        stored_list.append(stored)
        task_list.append(jnp.stack([depth_map, segment_map]).astype(jnp.bfloat16))
    upstream = output_cotangent.astype(jnp.float32)
    weight_list = [None] * layer_count
    small_list = [None] * layer_count
    for layer_index in reversed(range(layer_count)):
        upstream, weight_grads, small_grads = layer_backward(
            stored_list[layer_index],
            upstream,
            task_cotangents[layer_index, 0].astype(jnp.float32),
            task_cotangents[layer_index, 1].astype(jnp.float32),
            layer_params[layer_index],
            masks_one,
            masks_two,
            pixel_count,
        )
        weight_list[layer_index] = weight_grads
        small_list[layer_index] = small_grads
    stacked = [
        jnp.stack([weight_list[layer_index][member] for layer_index in range(layer_count)])
        for member in range(5)
    ]
    weight_sums = weight_totals(stacked[0], stacked[1], stacked[2], stacked[3], stacked[4])
    small_sums = [
        jnp.stack([small_list[layer_index][member] for layer_index in range(layer_count)])
        for member in range(6)
    ]
    return (
        current,
        jnp.stack(task_list),
        upstream,
        weight_sums[0],
        weight_sums[1],
        weight_sums[2],
        weight_sums[3],
        weight_sums[4],
        small_sums[0],
        small_sums[1],
        small_sums[2],
        small_sums[3],
        small_sums[4],
        small_sums[5],
    )


def solution(mesh):
    placed = (
        P("blk", None, "ch"),
        P(None, "ch", None),
        P(None, "ch", None, None),
        P(None, None, "ch"),
        P(None, None, "ch", None, None),
        P(None, None, "ch", None, None),
        P(None, None, "ch"),
        P(None, None, "ch"),
        P(None, "ch"),
        P(None, "ch"),
        P(None, None, "ch"),
        P(None, None, "ch"),
        P(),
        P("blk", None, "ch"),
        P(None, None, "blk", None, "ch"),
    )
    return jax.shard_map(
        shards,
        mesh=mesh,
        in_specs=placed,
        out_specs=(
            P("blk", None, "ch"),
            P(None, None, "blk", None, "ch"),
            P("blk", None, "ch"),
            P(None, "blk", "ch"),
            P(None, None, "blk", "ch"),
            P(None, "blk", "ch"),
            P(None, None, None, "blk", "ch"),
            P(None, None, None, "blk", "ch"),
            P(None, None, "ch"),
            P(None, None, "ch"),
            P(None, "ch"),
            P(None, "ch"),
            P(None, None, "ch"),
            P(None, None, "ch"),
        ),
        check_vma=False,
    )
```

profile of v0, /device:TPU:0, one launch (start us, length us, event | category | flops | bytes accessed | tf_op | source)
XLA Modules:
  0.0 1623.3 jit_solution(6068746726230079054)
XLA Ops:
  13.6 44.6 %all-gather.17.cloned.1.call-done = bf16[4,128,2048]{2,1,0:T(8,128)(2,1)} async-done(((bf16[4,128,512]{2,1,0:T(8,128)(2,1)}), bf16[4,128,2048]{2,1,0:T(8,128)(2,1)}) %all-gather.17.cloned.1.call-update) | async-done | bytes 2097168 | tf_op jit(solution)/shard_map/all_gather | solution.py:30
  60.7 13.8 all-reduce.42
  74.6 13.8 all-gather.1
  97.2 17.4 %all-reduce.41 = (f32[128]{0:T(128)S(1)}, f32[128]{0:T(128)S(1)}) all-reduce(f32[128]{0:T(128)S(1)} %get-tuple-element.87, f32[128]{0:T(128)S(1)} %get-tuple-element.86), channel_id=1, replica_groups=mesh['blk'=8,'ch'=4] {'blk'}, use_global_device_ids=true, to_apply=%region_7.8 | all-reduce | flops 256 | bytes 2048 | tf_op jit(solution)/shard_map/psum | solution.py:44
  114.8 14.4 all-gather.2
  130.8 11.8 all-reduce.40
  144.5 25.3 %fusion.2336 = (bf16[1,4,128,9,2048]{4,2,3,1,0:T(8,128)(2,1)}, bf16[1,4,128,9,2048]{4,2,3,1,0:T(8,128)(2,1)}) fusion(bf16[2,4,128,9,2048]{4,2,3,1,0:T(8,128)(2,1)} %param.19), kind=kLoop, calls=%fused_computation.3235 | loop fusion | bytes 75497472 | tf_op jit(solution)/shard_map/slice | solution.py:375
  169.9 16.9 %copy.680 = bf16[1,4,128,9,2048]{4,2,1,3,0:T(8,128)(2,1)} copy(bf16[1,4,128,9,2048]{4,2,3,1,0:T(8,128)(2,1)} %get-tuple-element.152) | data formatting | bytes 37748736
  192.0 13.7 all-reduce.39
  206.5 13.8 all-gather.4
  237.1 14.0 all-reduce.38
  251.8 15.3 all-gather.5
  269.4 11.8 all-reduce.37
  307.3 19.2 %copy.679 = bf16[1,4,128,9,2048]{4,2,1,3,0:T(8,128)(2,1)} copy(bf16[1,4,128,9,2048]{4,2,3,1,0:T(8,128)(2,1)} %get-tuple-element.153) | data formatting | bytes 37748736
  344.5 32.9 %all-gather.13.cloned.1.call-done = bf16[4,128,4,512]{3,1,0,2:T(8,128)(2,1)} async-done(((bf16[4,128,4,128]{3,1,0,2:T(8,128)(2,1)}), bf16[4,128,4,512]{3,1,0,2:T(8,128)(2,1)}) %all-gather.13.cloned.1.call-update) | async-done | bytes 2097168 | tf_op jit(solution)/shard_map/all_gather | solution.py:30
  636.3 12.4 collective-permute-start.14
  685.0 12.2 fusion.18
  744.3 13.4 all-reduce.36
  790.1 12.6 all-reduce.35
  825.2 14.8 fusion.19
  863.5 15.6 all-reduce.34
  905.1 33.9 %reduce-scatter.28.cloned.1.call-done = bf16[4,128,1,512]{3,1,0,2:T(8,128)(2,1)} async-done(((bf16[4,128,1,2048]{3,1,0,2:T(8,128)(2,1)}), bf16[4,128,1,512]{3,1,0,2:T(8,128)(2,1)}) %reduce-scatter.28.cloned.1.call-update) | async-done | bytes 524304 | tf_op jit(solution)/shard_map/reduce_scatter | solution.py:34
  942.8 13.0 all-reduce.33
  969.5 11.6 reduce-scatter.48.cloned.1.call-done
  982.3 11.9 all-reduce.32
  1026.4 11.5 reduce-scatter.50.cloned.1.call-done
  1039.3 22.4 %all-reduce.31 = (f32[128]{0:T(128)S(1)}, f32[128]{0:T(128)S(1)}, f32[1,6,128]{2,1,0:T(8,128)S(1)}, f32[1,6,128]{2,1,0:T(8,128)S(1)}, f32[1,6,128]{2,1,0:T(8,128)S(1)}, /*index=5*/f32[1,6,128]{2,1,0:T(8,128)S(1)}) all-reduce(f32[128]{0:T(128)S(1)} %get-tuple-element.63, ...), channel_id=1, replica_groups=mesh['blk'=8,'ch'=4] {'blk'}, use_global_device_ids=true, to_apply=%region_56.57 | all-reduce | flops 3328 | bytes 26624 | tf_op jit(solution)/shard_map/psum | solution.py:44
  1068.1 10.6 pad_maximum_fusion.1
  1078.7 35.4 %copy.426 = bf16[2,6,9,512,128]{4,0,2,1,3:T(2,128)(2,1)} copy(bf16[2,6,9,512,128]{3,4,2,1,0:T(8,128)(2,1)} %pad_maximum_fusion.1) | data formatting | bytes 28311552 | tf_op jit(solution)/shard_map/stack | solution.py:411
  1177.1 27.2 %pad_maximum_fusion = bf16[2,4,9,2048,128]{3,4,1,2,0:T(8,128)(2,1)} fusion(bf16[1,4,9,2048,128]{3,4,1,2,0:T(8,128)(2,1)} %bitcast.5428, bf16[1,4,9,2048,128]{3,4,1,2,0:T(8,128)(2,1)} %bitcast.5429), kind=kLoop, calls=%fused_computation | loop fusion | flops 18874368 | bytes 75497472 | tf_op jit(solution)/shard_map/stack | solution.py:411
  1215.7 163.7 %all-reduce.46.cloned.1.call-done = (bf16[2,9,512,128]{3,0,1,2:T(2,128)(2,1)}, bf16[2,6,9,512,128]{4,0,2,1,3:T(2,128)(2,1)}) async-done(((bf16[2,9,512,128]{3,0,1,2:T(2,128)(2,1)}, bf16[2,6,9,512,128]{4,0,2,1,3:T(2,128)(2,1)}), (bf16[2,9,512,128]{3,0,1,2:T(2,128)(2,1)}, bf16[2,6,9,512,128]{4,0,2,1,3:T(2,128)(2,1)})) %all-reduce.46.cloned.1.call-update) | async-done | bytes 16515088
  1386.4 222.5 %reduce-scatter.38.cloned.1.call-done = bf16[2,4,9,256,128]{3,4,1,2,0:T(8,128)(2,1)} async-done(((bf16[2,4,9,2048,128]{3,4,1,2,0:T(8,128)(2,1)}), bf16[2,4,9,256,128]{3,4,1,2,0:T(8,128)(2,1)}) %reduce-scatter.38.cloned.1.call-update) | async-done | bytes 4718608 | tf_op jit(solution)/shard_map/reduce_scatter | solution.py:58
  (1504 shorter events, 677.1 us)
Async XLA Ops:
  7.2 51.1 %all-gather.17.cloned.1.call-start = ((), (), s32[]{:S(2)}) async-start(), calls=%async_computation.22 | async-start | bytes 2621440 | tf_op jit(solution)/shard_map/all_gather | solution.py:30
  7.9 181.6 %all-gather.19.cloned.1.call-start = ((), (), s32[]{:S(2)}) async-start(), calls=%async_computation.23 | async-start | bytes 2621440 | tf_op jit(solution)/shard_map/all_gather | solution.py:30
  144.5 190.0 %all-gather.21.cloned.1.call-start = ((), (), s32[]{:S(2)}) async-start(), calls=%async_computation.24 | async-start | bytes 2621440 | tf_op jit(solution)/shard_map/all_gather | solution.py:30
  220.4 13.5 collective-permute-start.2
  221.7 12.2 collective-permute-start.3
  224.0 60.1 %collective-permute-start.4 = (bf16[1,128,1,2048]{3,1,2,0:T(8,128)(2,1)}, bf16[1,128,1,2048]{3,1,2,0:T(8,128)(2,1)}, u32[]{:S(2)}, u32[]{:S(2)}) collective-permute-start(bf16[1,128,1,2048]{3,1,2,0:T(8,128)(2,1)} %get-tuple-element.179), channel_id=1, source_target_pairs={{0,4},{4,8},{8,12},{12,16},{16,20},{20,24},{24,28},{1,5},{5,9},{9,... | collective-permute-start | bytes 1572872 | tf_op jit(solution)/shard_map/ppermute | solution.py:16
  228.6 55.6 %collective-permute-start.5 = (bf16[1,128,1,2048]{3,1,2,0:T(8,128)(2,1)}, bf16[1,128,1,2048]{3,1,2,0:T(8,128)(2,1)}, u32[]{:S(2)}, u32[]{:S(2)}) collective-permute-start(bf16[1,128,1,2048]{3,1,2,0:T(8,128)(2,1)} %get-tuple-element.180), channel_id=1, source_target_pairs={{4,0},{8,4},{12,8},{16,12},{20,16},{24,20},{28,24},{5,1},{9,5},{13... | collective-permute-start | bytes 1572872 | tf_op jit(solution)/shard_map/ppermute | solution.py:19
  284.1 93.3 %all-gather.13.cloned.1.call-start = ((), (), s32[]{:S(2)}) async-start(), calls=%async_computation.13 | async-start | bytes 2621440 | tf_op jit(solution)/shard_map/all_gather | solution.py:30
  307.2 276.9 %all-gather.15.cloned.1.call-start = ((), (), s32[]{:S(2)}) async-start(), calls=%async_computation.14 | async-start | bytes 2621440 | tf_op jit(solution)/shard_map/all_gather | solution.py:30
  336.8 55.3 %collective-permute-start.8 = (bf16[1,128,1,2048]{3,1,2,0:T(8,128)(2,1)}, bf16[1,128,1,2048]{3,1,2,0:T(8,128)(2,1)S(1)}, u32[]{:S(2)}, u32[]{:S(2)}) collective-permute-start(bf16[1,128,1,2048]{3,1,2,0:T(8,128)(2,1)} %get-tuple-element.186), channel_id=1, source_target_pairs={{0,4},{4,8},{8,12},{12,16},{16,20},{20,24},{24,28},{1,5},{5,9},{9,... | collective-permute-start | bytes 1572872 | tf_op jit(solution)/shard_map/ppermute | solution.py:16
  338.6 53.5 %collective-permute-start.9 = (bf16[1,128,1,2048]{3,1,2,0:T(8,128)(2,1)}, bf16[1,128,1,2048]{3,1,2,0:T(8,128)(2,1)S(1)}, u32[]{:S(2)}, u32[]{:S(2)}) collective-permute-start(bf16[1,128,1,2048]{3,1,2,0:T(8,128)(2,1)} %get-tuple-element.187), channel_id=1, source_target_pairs={{4,0},{8,4},{12,8},{16,12},{20,16},{24,20},{28,24},{5,1},{9,5},{13... | collective-permute-start | bytes 1572872 | tf_op jit(solution)/shard_map/ppermute | solution.py:19
  379.7 158.6 %collective-permute-start.6 = (bf16[1,128,4,512]{3,1,0,2:T(8,128)(2,1)}, bf16[1,128,4,512]{3,1,0,2:T(8,128)(2,1)}, u32[]{:S(2)}, u32[]{:S(2)}) collective-permute-start(bf16[1,128,4,512]{3,1,0,2:T(8,128)(2,1)} %get-tuple-element.178), channel_id=1, source_target_pairs={{0,4},{4,8},{8,12},{12,16},{16,20},{20,24},{24,28},{1,5},{5,9},{9,... | collective-permute-start | bytes 1572872 | tf_op jit(solution)/shard_map/ppermute | solution.py:16
  381.8 158.6 %collective-permute-start.7 = (bf16[1,128,4,512]{3,1,0,2:T(8,128)(2,1)}, bf16[1,128,4,512]{3,1,0,2:T(8,128)(2,1)}, u32[]{:S(2)}, u32[]{:S(2)}) collective-permute-start(bf16[1,128,4,512]{3,1,0,2:T(8,128)(2,1)} %get-tuple-element.177), channel_id=1, source_target_pairs={{4,0},{8,4},{12,8},{16,12},{20,16},{24,20},{28,24},{5,1},{9,5},{13... | collective-permute-start | bytes 1572872 | tf_op jit(solution)/shard_map/ppermute | solution.py:19
  420.6 9.7 collective-permute-start.18
  425.9 13.2 collective-permute-start.12
  430.2 193.4 %reduce-scatter.46.cloned.1.call-start = ((), (), s32[]{:S(2)}) async-start(), calls=%async_computation.28 | async-start | bytes 2621440
  511.1 117.0 %reduce-scatter.40.cloned.1.call-start = ((), (), s32[]{:S(2)}) async-start(), calls=%async_computation.25 | async-start | bytes 2621440
  537.8 203.0 %reduce-scatter.26.cloned.1.call-start = ((), (), s32[]{:S(2)}) async-start(), calls=%async_computation.15 | async-start | bytes 2621440 | tf_op jit(solution)/shard_map/reduce_scatter | solution.py:34
  585.4 9.0 collective-permute-start.10
  636.3 18.5 %collective-permute-start.14 = (bf16[1,128,4,128]{3,1,0,2:T(8,128)(2,1)S(1)}, bf16[1,128,4,128]{3,1,0,2:T(8,128)(2,1)S(1)}, u32[]{:S(2)}, u32[]{:S(2)}) collective-permute-start(bf16[1,128,4,128]{3,1,0,2:T(8,128)(2,1)S(1)} %get-tuple-element.221), channel_id=1, source_target_pairs={{0,4},{4,8},{8,12},{12,16},{16,20},{20,24},{24,28},{1,5},{5,9},{9,... | collective-permute-start | bytes 393224 | tf_op jit(solution)/shard_map/ppermute | solution.py:16
  697.3 88.0 %reduce-scatter.42.cloned.1.call-start = ((), (), s32[]{:S(2)}) async-start(), calls=%async_computation.26 | async-start | bytes 655360
  708.5 9.7 collective-permute-start.20
  765.7 95.5 %reduce-scatter.44.cloned.1.call-start = ((), (), s32[]{:S(2)}) async-start(), calls=%async_computation.27 | async-start | bytes 655360
  825.1 80.1 %reduce-scatter.30.cloned.1.call-start = ((), (), s32[]{:S(2)}) async-start(), calls=%async_computation.17 | async-start | bytes 2621440 | tf_op jit(solution)/shard_map/reduce_scatter | solution.py:34
  840.0 99.0 %reduce-scatter.28.cloned.1.call-start = ((), (), s32[]{:S(2)}) async-start(), calls=%async_computation.16 | async-start | bytes 2621440 | tf_op jit(solution)/shard_map/reduce_scatter | solution.py:34
  882.5 98.5 %reduce-scatter.48.cloned.1.call-start = ((), (), s32[]{:S(2)}) async-start(), calls=%async_computation.29 | async-start | bytes 655360
  961.0 77.0 %reduce-scatter.50.cloned.1.call-start = ((), (), s32[]{:S(2)}) async-start(), calls=%async_computation.30 | async-start | bytes 655360
  1014.2 193.5 %reduce-scatter.36.cloned.1.call-start = ((), (), s32[]{:S(2)}) async-start(), calls=%async_computation.20 | async-start | bytes 1179648 | tf_op jit(solution)/shard_map/reduce_scatter | solution.py:55
  1022.1 189.7 %reduce-scatter.34.cloned.1.call-start = ((), (), s32[]{:S(2)}) async-start(), calls=%async_computation.19 | async-start | bytes 1179648 | tf_op jit(solution)/shard_map/reduce_scatter | solution.py:49
  1065.0 148.5 %reduce-scatter.32.cloned.1.call-start = ((), (), s32[]{:S(2)}) async-start(), calls=%async_computation.18 | async-start | bytes 2621440 | tf_op jit(solution)/shard_map/reduce_scatter | solution.py:34
  1116.2 263.1 %all-reduce.46.cloned.1.call-start = ((), (), s32[]{:S(2)}) async-start(), calls=%async_computation.31 | async-start | bytes 33030144
  1128.0 480.9 %reduce-scatter.38.cloned.1.call-start = ((), (), s32[]{:S(2)}) async-start(), calls=%async_computation.21 | async-start | bytes 42467328 | tf_op jit(solution)/shard_map/reduce_scatter | solution.py:58
  (420 other events, 8535.8 us)
Sparse Core Ops, SparseCore 0:
  9.6 48.6 all-gather.16
  144.6 44.8 all-gather.18
  284.2 46.1 all-gather.20
  332.4 44.9 all-gather.12
  430.4 46.6 all-gather.14
  511.2 46.3 reduce-scatter.45
  560.0 43.2 reduce-scatter.39
  697.4 43.4 reduce-scatter.25
  765.9 19.3 reduce-scatter.41
  825.2 23.7 reduce-scatter.43
  851.4 42.2 reduce-scatter.29
  895.8 43.2 reduce-scatter.27
  961.1 19.8 reduce-scatter.47
  1014.3 23.6 reduce-scatter.49
  1041.3 34.3 reduce-scatter.35
  1079.0 36.0 reduce-scatter.33
  1117.4 43.8 reduce-scatter.31
  1165.7 213.6 all-reduce.45
  1383.4 225.4 reduce-scatter.37
where the time goes:
time: 1640 us; the launch traced here: 1620 us
  waiting for transfers between devices  538 us (33%)
  matrix products  448 us (27%)
  blocking collectives  229 us (14%)
  local copies, waits for them, and re-layouts  214 us (13%)
  other arithmetic  102 us (6%)
  starting transfers between devices  70.2 us (4%)
  between operations  22.6 us (1%)
    reduce_scatter x1, waiting for transfers between devices, weight_totals(): lax.psum_scatter(heads_grad.astype(jnp.bfloat16), 'blk', scatter_dimensio...  223 us
    dot_general x144, matrix products, conv_input_grad(): jnp.einsum('rwko,koc->rwc', window, weights[:, :, tap_index], preferred_e...  198 us
    unnamed x26, waiting for transfers between devices  192 us
    psum x12, blocking collectives, pixel_totals(): return lax.psum((first_sum, second_sum), 'blk')  171 us
    dot_general x144, matrix products, conv_weight_grad(): jnp.einsum('rwc,rwko->kco', window, masked, preferred_element_type=jnp.fl...  135 us
    unnamed x855, local copies, waits for them, and re-layouts  128 us
    dot_general x144, matrix products, conv_forward(): jnp.einsum('rwc,koc->rwko', window, weights[:, :, tap_index], preferred_e...  92.3 us
    all_gather x5, waiting for transfers between devices, gather_channels(): return lax.all_gather(values, 'ch', axis=3, tiled=True)  80.2 us
  transfers between devices with their start and end apart: 43, of which 14 were waited for; matrix products, arithmetic and copies ran while one was open for 37% of the time, Pallas kernels for 0%

commit v1 on v0

--- a/solution.py
+++ b/solution.py
@@ -1,9 +1,16 @@
+import functools
+import types
+
 import jax
 import jax.numpy as jnp
 from jax import lax
+from jax.experimental import pallas as pl
+from jax.experimental.pallas import tpu as pltpu
 from jax.sharding import PartitionSpec as P
 
 epsilon = 1e-05
+BLK = "blk"
+CH = "ch"
 tap_offsets = tuple(((row_step, col_step) for row_step in (-1, 0, 1) for col_step in (-1, 0, 1)))
 message_pairs = ((1, 0), (2, 0), (3, 0), (0, 3), (1, 3), (2, 3))
 
@@ -27,39 +34,39 @@
 
 
 def gather_channels(values):
-    return lax.all_gather(values, "ch", axis=3, tiled=True)
+    return lax.all_gather(values, CH, axis=3, tiled=True)
 
 
 def reduce_channels(values):
     return lax.psum_scatter(
-        values.astype(jnp.bfloat16), "ch", scatter_dimension=3, tiled=True
+        values.astype(jnp.bfloat16), CH, scatter_dimension=3, tiled=True
     ).astype(jnp.float32)
 
 
 def extend_rows(values, halo_width):
-    return extended_2(values, (("blk", 0),), halo_width)
+    return extended_2(values, ((BLK, 0),), halo_width)
 
 
 def pixel_totals(first_sum, second_sum):
-    return lax.psum((first_sum, second_sum), "blk")
+    return lax.psum((first_sum, second_sum), BLK)
 
 
 def weight_totals(reduce_grad, dilated_grad, expand_grad, heads_grad, messages_grad):
     return (
         lax.psum_scatter(
-            reduce_grad.astype(jnp.bfloat16), "blk", scatter_dimension=1, tiled=True
+            reduce_grad.astype(jnp.bfloat16), BLK, scatter_dimension=1, tiled=True
         ).astype(jnp.float32),
         lax.psum_scatter(
-            dilated_grad.astype(jnp.bfloat16), "blk", scatter_dimension=2, tiled=True
+            dilated_grad.astype(jnp.bfloat16), BLK, scatter_dimension=2, tiled=True
         ).astype(jnp.float32),
         lax.psum_scatter(
-            expand_grad.astype(jnp.bfloat16), "blk", scatter_dimension=1, tiled=True
+            expand_grad.astype(jnp.bfloat16), BLK, scatter_dimension=1, tiled=True
         ).astype(jnp.float32),
         lax.psum_scatter(
-            heads_grad.astype(jnp.bfloat16), "blk", scatter_dimension=3, tiled=True
+            heads_grad.astype(jnp.bfloat16), BLK, scatter_dimension=3, tiled=True
         ).astype(jnp.float32),
         lax.psum_scatter(
-            messages_grad.astype(jnp.bfloat16), "blk", scatter_dimension=3, tiled=True
+            messages_grad.astype(jnp.bfloat16), BLK, scatter_dimension=3, tiled=True
         ).astype(jnp.float32),
     )
 
@@ -71,7 +78,7 @@
 def local_masks(canvas_ids, row_count, dilation):
     col_count = canvas_ids.shape[1]
     padded = jnp.pad(canvas_ids, 2, constant_values=-1)
-    start = lax.axis_index("blk") * row_count
+    start = lax.axis_index(BLK) * row_count
     window = lax.dynamic_slice(padded, (start, jnp.int32(0)), (row_count + 4, col_count + 4))
     centre = window[2 : 2 + row_count, 2 : 2 + col_count]
     result = []
@@ -167,7 +174,7 @@
         gate_g,
         gate_b,
     ) = params
-    stored = {}
+    stored = types.SimpleNamespace()
     inputs_full = gather_channels(inputs[:, :, None, :])[:, :, 0, :]
     first_pre = jnp.einsum("rwc,oc->rwo", inputs_full, reduce_w, preferred_element_type=jnp.float32)
     first_norm, first_normed, first_inverse = norm_forward(
@@ -205,23 +212,23 @@
             depth_map = depth_map + gate_value * message
         else:
             segment_map = segment_map + gate_value * message
-    stored["inputs_full"] = inputs_full
-    stored["first_norm"] = first_norm
-    stored["first_normed"] = first_normed
-    stored["first_inverse"] = first_inverse
-    stored["first_ext"] = first_ext
-    stored["second_norm"] = second_norm
-    stored["second_normed"] = second_normed
-    stored["second_inverse"] = second_inverse
-    stored["second_full"] = second_full
-    stored["third_normed"] = third_normed
-    stored["third_inverse"] = third_inverse
-    stored["summed"] = summed
-    stored["output_ext"] = output_ext
-    stored["heads_pre"] = heads_pre
-    stored["features"] = feature_values
-    stored["features_ext"] = features_ext
-    stored["messages"] = message_list
+    stored.inputs_full = inputs_full
+    stored.first_norm = first_norm
+    stored.first_normed = first_normed
+    stored.first_inverse = first_inverse
+    stored.first_ext = first_ext
+    stored.second_norm = second_norm
+    stored.second_normed = second_normed
+    stored.second_inverse = second_inverse
+    stored.second_full = second_full
+    stored.third_normed = third_normed
+    stored.third_inverse = third_inverse
+    stored.summed = summed
+    stored.output_ext = output_ext
+    stored.heads_pre = heads_pre
+    stored.features = feature_values
+    stored.features_ext = features_ext
+    stored.messages = message_list
     return (output, depth_map, segment_map, stored)
 
 
@@ -241,7 +248,7 @@
         gate_g,
         gate_b,
     ) = params
-    feature_values = stored["features"]
+    feature_values = stored.features
     zero_map = jnp.zeros_like(depth_grad)
     feature_grads = [depth_grad, zero_map, zero_map, segment_grad]
     message_grads = []
@@ -253,7 +260,7 @@
             gate_g[pair_index] * feature_values[:, :, target] + gate_b[pair_index]
         )
         message_grads.append(target_grad * gate_value)
-        slope = target_grad * stored["messages"][pair_index] * gate_value * (1.0 - gate_value)
+        slope = target_grad * stored.messages[pair_index] * gate_value * (1.0 - gate_value)
         gain_terms.append(jnp.sum(slope * feature_values[:, :, target], axis=(0, 1)))
         bias_terms.append(jnp.sum(slope, axis=(0, 1)))
         feature_grads[target] = feature_grads[target] + slope * gate_g[pair_index]
@@ -265,7 +272,7 @@
     for pair_index, (source, target) in enumerate(message_pairs):
         weight_parts.append(
             conv_weight_grad(
-                stored["features_ext"][:, :, source],
+                stored.features_ext[:, :, source],
                 1,
                 1,
                 message_stack[:, :, pair_index : pair_index + 1],
@@ -286,45 +293,45 @@
     messages_w_grad = jnp.concatenate(weight_parts, axis=0)
     source_sums = reduce_channels(jnp.stack(source_partials, axis=2))
     features_total = jnp.stack(feature_grads, axis=2) + source_sums
-    heads_grad = (features_total * silu_slope(stored["heads_pre"])).astype(jnp.bfloat16)
-    heads_w_grad = conv_weight_grad(stored["output_ext"], 1, 1, heads_grad, masks_one)
+    heads_grad = (features_total * silu_slope(stored.heads_pre)).astype(jnp.bfloat16)
+    heads_w_grad = conv_weight_grad(stored.output_ext, 1, 1, heads_grad, masks_one)
     heads_ext = extend_rows(heads_grad, 1)
     output_partial = conv_input_grad(heads_ext, 1, 1, heads_w, masks_one)
     output_total = upstream + reduce_channels(output_partial[:, :, None, :])[:, :, 0, :]
-    summed_grad = output_total * silu_slope(stored["summed"])
+    summed_grad = output_total * silu_slope(stored.summed)
     third_grad, wide_gain_grad, wide_bias_grad = norm_backward(
-        summed_grad, stored["third_normed"], stored["third_inverse"], wide_g, pixel_count
+        summed_grad, stored.third_normed, stored.third_inverse, wide_g, pixel_count
     )
     third_low = third_grad.astype(jnp.bfloat16)
     expand_w_grad = jnp.einsum(
-        "rwc,rwo->co", stored["second_full"], third_low, preferred_element_type=jnp.float32
+        "rwc,rwo->co", stored.second_full, third_low, preferred_element_type=jnp.float32
     )
     second_partial = jnp.einsum(
         "rwo,co->rwc", third_low, expand_w, preferred_element_type=jnp.float32
     )
     second_act_grad = reduce_channels(second_partial[:, :, None, :])[:, :, 0, :]
     second_grad, second_gain_grad, second_bias_grad = norm_backward(
-        second_act_grad * silu_slope(stored["second_norm"]),
-        stored["second_normed"],
-        stored["second_inverse"],
+        second_act_grad * silu_slope(stored.second_norm),
+        stored.second_normed,
+        stored.second_inverse,
         narrow_gain[1],
         pixel_count,
     )
     second_low = second_grad.astype(jnp.bfloat16)[:, :, None, :]
-    dilated_w_grad = conv_weight_grad(stored["first_ext"], 2, 2, second_low, masks_two)[0]
+    dilated_w_grad = conv_weight_grad(stored.first_ext, 2, 2, second_low, masks_two)[0]
     second_ext = extend_rows(second_low, 2)
     first_partial = conv_input_grad(second_ext, 2, 2, dilated_w[None], masks_two)
     first_act_grad = reduce_channels(first_partial[:, :, None, :])[:, :, 0, :]
     first_grad, first_gain_grad, first_bias_grad = norm_backward(
-        first_act_grad * silu_slope(stored["first_norm"]),
-        stored["first_normed"],
-        stored["first_inverse"],
+        first_act_grad * silu_slope(stored.first_norm),
+        stored.first_normed,
+        stored.first_inverse,
         narrow_gain[0],
         pixel_count,
     )
     first_low = first_grad.astype(jnp.bfloat16)
     reduce_w_grad = jnp.einsum(
-        "rwc,rwo->co", stored["inputs_full"], first_low, preferred_element_type=jnp.float32
+        "rwc,rwo->co", stored.inputs_full, first_low, preferred_element_type=jnp.float32
     )
     inputs_partial = jnp.einsum(
         "rwo,oc->rwc", first_low, reduce_w, preferred_element_type=jnp.float32
@@ -342,7 +349,7 @@
     return (inputs_grad, weight_grads, small_grads)
 
 
-def shards(
+def plain_shards(
     features_in,
     w_reduce,
     w_dilated,
@@ -361,7 +368,7 @@
 ):
     row_count = features_in.shape[0]
     col_count = features_in.shape[1]
-    pixel_count = float(row_count * col_count * lax.axis_size("blk"))
+    pixel_count = float(row_count * col_count * lax.axis_size(BLK))
     masks_one = local_masks(canvas_ids, row_count, 1)
     masks_two = local_masks(canvas_ids, row_count, 2)
     layer_count = w_reduce.shape[0]
@@ -434,43 +441,1373 @@
     )
 
 
+lanes = 128
+source_order = ((1, 0, 4), (2, 1, 5), (0, 3), (3, 2))
+
+
+def kernel_params():
+    return pltpu.CompilerParams(vmem_limit_bytes=56 * 2**20)
+
+
+def whole(shape):
+    return pl.BlockSpec(shape, lambda *_: (0,) * len(shape))
+
+
+def contract_last(left, right):
+    return lax.dot_general(
+        left, right, (((1,), (1,)), ((), ())), preferred_element_type=jnp.float32
+    )
+
+
+def sigmoid(values):
+    return 1.0 / (1.0 + jnp.exp(-values))
+
+
+def heads_forward_kernel(v_ref, w_ref, mask_ref, pre_ref, act_ref, z_ref):
+    tap = pl.program_id(0)
+    head_count, pixels, mid = pre_ref.shape
+    cols = (v_ref.shape[0] - pixels) // 2
+    row_step = tap // 3
+    col_step = lax.rem(tap, 3)
+    window = v_ref[pl.ds(pl.multiple_of(row_step * cols, cols), pixels), :]
+    weights = w_ref[...].reshape(head_count * mid, v_ref.shape[1])
+    product = contract_last(window, weights)
+    mask = mask_ref[0]
+
+    @pl.when(tap < 3)
+    def _():
+        for head in range(head_count):
+            part = slice(head * mid, (head + 1) * mid)
+            z_ref[col_step, :, part] = mask * product[:, part]
+
+    @pl.when(tap >= 3)
+    def _():
+        for head in range(head_count):
+            part = slice(head * mid, (head + 1) * mid)
+            z_ref[col_step, :, part] += mask * product[:, part]
+
+    @pl.when(tap == 8)
+    def _():
+        for head in range(head_count):
+            part = slice(head * mid, (head + 1) * mid)
+            total = (
+                z_ref[1, :, part]
+                + pltpu.roll(z_ref[0, :, part], 1, 0)
+                + pltpu.roll(z_ref[2, :, part], pixels - 1, 0)
+            )
+            pre_ref[head] = total
+            act_ref[head] = (total * sigmoid(total)).astype(jnp.bfloat16)
+
+
+def heads_forward(extended, weights, mask):
+    head_count, _, mid, feat = weights.shape
+    pixels = mask.shape[1]
+    return pl.pallas_call(
+        heads_forward_kernel,
+        grid=(9,),
+        in_specs=[
+            whole(extended.shape),
+            pl.BlockSpec((head_count, 1, mid, feat), lambda t: (0, t, 0, 0)),
+            pl.BlockSpec((1, pixels, lanes), lambda t: (t, 0, 0)),
+        ],
+        out_specs=[whole((head_count, pixels, mid))] * 2,
+        out_shape=[
+            jax.ShapeDtypeStruct((head_count, pixels, mid), jnp.float32),
+            jax.ShapeDtypeStruct((head_count, pixels, mid), jnp.bfloat16),
+        ],
+        scratch_shapes=[pltpu.VMEM((3, pixels, head_count * mid), jnp.float32)],
+        compiler_params=kernel_params(),
+        cost_estimate=pl.CostEstimate(
+            flops=2 * pixels * weights.size, bytes_accessed=2 * weights.size, transcendentals=0
+        ),
+    )(extended, weights, mask)
+
+
+def tapped_conv(window_of, weights_of, mask_ref, pixels, mid, dilation):
+    totals = [None, None, None]
+    for row_step in range(3):
+        product = contract_last(window_of(row_step), weights_of(row_step))
+        for col_step in range(3):
+            part = mask_ref[row_step * 3 + col_step] * product[:, col_step * mid : (col_step + 1) * mid]
+            totals[col_step] = part if totals[col_step] is None else totals[col_step] + part
+    return (
+        totals[1]
+        + pltpu.roll(totals[0], dilation, 0)
+        + pltpu.roll(totals[2], pixels - dilation, 0)
+    )
+
+
+def messages_forward_kernel(low_ref, main_ref, high_ref, wa_ref, wb_ref, mask_ref, out_ref, lhs_ref):
+    step = pl.program_id(0)
+    parts, _, pixels, mid = main_ref.shape
+    cols = low_ref.shape[2]
+
+    def load(slot, source):
+        for part in range(parts):
+            chan = slice(part * mid, (part + 1) * mid)
+            lhs_ref[slot, 0:cols, chan] = low_ref[part, source]
+            lhs_ref[slot, cols : cols + pixels, chan] = main_ref[part, source]
+            lhs_ref[slot, cols + pixels :, chan] = high_ref[part, source]
+
+    def run(slot, w_ref, place):
+        out_ref[place] = tapped_conv(
+            lambda r: lhs_ref[slot, r * cols : r * cols + pixels, :],
+            lambda r: w_ref[0, 3 * r : 3 * r + 3].reshape(3 * mid, parts * mid),
+            mask_ref,
+            pixels,
+            mid,
+            1,
+        )
+
+    for index, places in enumerate(((0, 4), (1, 5), (3, 2))):
+
+        @pl.when(step == index)
+        def _(index=index, places=places):
+            if index < 2:
+                load(0, index + 1)
+                run(0, wa_ref, places[0])
+                run(0, wb_ref, places[1])
+            else:
+                load(0, 0)
+                load(1, 3)
+                run(0, wa_ref, places[0])
+                run(1, wb_ref, places[1])
+
+
+def messages_forward(low, main, high, weights, mask):
+    pixels = mask.shape[1]
+    pairs, taps, mid, width = weights.shape
+    cols = low.shape[2]
+    return pl.pallas_call(
+        messages_forward_kernel,
+        grid=(3,),
+        in_specs=[
+            whole(low.shape),
+            whole(main.shape),
+            whole(high.shape),
+            pl.BlockSpec((1, taps, mid, width), lambda i: (i + i // 2, 0, 0, 0)),
+            pl.BlockSpec((1, taps, mid, width), lambda i: (4 + i - 4 * (i // 2), 0, 0, 0)),
+            whole(mask.shape),
+        ],
+        out_specs=whole((pairs, pixels, mid)),
+        out_shape=jax.ShapeDtypeStruct((pairs, pixels, mid), jnp.float32),
+        scratch_shapes=[pltpu.VMEM((2, pixels + 2 * cols, width), jnp.bfloat16)],
+        compiler_params=kernel_params(),
+        cost_estimate=pl.CostEstimate(
+            flops=2 * pixels * weights.size, bytes_accessed=2 * weights.size, transcendentals=0
+        ),
+    )(low, main, high, weights, weights, mask)
+
+
+def dilated_forward_kernel(v_ref, w_ref, mask_ref, out_ref):
+    pixels, mid = out_ref.shape
+    cols = (v_ref.shape[0] - pixels) // 4
+    out_ref[...] = tapped_conv(
+        lambda r: v_ref[2 * r * cols : 2 * r * cols + pixels, :],
+        lambda r: w_ref[3 * r : 3 * r + 3].reshape(3 * mid, v_ref.shape[1]),
+        mask_ref,
+        pixels,
+        mid,
+        2,
+    )
+
+
+def dilated_forward(extended, weights, mask):
+    pixels, mid = mask.shape[1], weights.shape[1]
+    return pl.pallas_call(
+        dilated_forward_kernel,
+        out_shape=jax.ShapeDtypeStruct((pixels, mid), jnp.float32),
+        compiler_params=kernel_params(),
+    )(extended, weights, mask)
+
+
+def fill_taps(im_ref, slot, grad, mask_ref, pixels, cols, dilation):
+    rows, mid = grad.shape
+    wide = grad.astype(jnp.float32)
+    shifted_by = (pltpu.roll(wide, rows - dilation, 0), wide, pltpu.roll(wide, dilation, 0))
+    for tap, (row_step, col_step) in enumerate(tap_offsets):
+        start = (1 - row_step) * dilation * cols
+        part = shifted_by[col_step + 1][start : start + pixels]
+        im_ref[slot, :, tap * mid : (tap + 1) * mid] = (part * mask_ref[tap]).astype(jnp.bfloat16)
+
+
+def heads_backward_kernel(low_ref, main_ref, high_ref, w_ref, mask_ref, out_ref, im_ref):
+    step = pl.program_id(0)
+    head_count, pixels, mid = main_ref.shape
+    cols = low_ref.shape[1]
+
+    @pl.when(step == 0)
+    def _():
+        for head in range(head_count):
+            grad = jnp.concatenate([low_ref[head], main_ref[head], high_ref[head]], axis=0)
+            fill_taps(im_ref, head, grad, mask_ref, pixels, cols, 1)
+
+    total = None
+    for head in range(head_count):
+        product = jnp.dot(
+            im_ref[head],
+            w_ref[head].reshape(9 * mid, w_ref.shape[3]),
+            preferred_element_type=jnp.float32,
+        )
+        total = product if total is None else total + product
+    out_ref[0] = total.astype(jnp.bfloat16)
+
+
+def heads_backward(low, main, high, weights, mask, parts):
+    head_count, taps, mid, feat = weights.shape
+    pixels = mask.shape[1]
+    width = feat // parts
+    return pl.pallas_call(
+        heads_backward_kernel,
+        grid=(parts,),
+        in_specs=[
+            whole(low.shape),
+            whole(main.shape),
+            whole(high.shape),
+            pl.BlockSpec((head_count, taps, mid, width), lambda j: (0, 0, 0, j)),
+            whole(mask.shape),
+        ],
+        out_specs=pl.BlockSpec((1, pixels, width), lambda j: (j, 0, 0)),
+        out_shape=jax.ShapeDtypeStruct((parts, pixels, width), jnp.bfloat16),
+        scratch_shapes=[pltpu.VMEM((head_count, pixels, taps * mid), jnp.bfloat16)],
+        compiler_params=kernel_params(),
+        cost_estimate=pl.CostEstimate(
+            flops=2 * pixels * weights.size, bytes_accessed=2 * weights.size, transcendentals=0
+        ),
+    )(low, main, high, weights, mask)
+
+
+def messages_backward_kernel(low_ref, main_ref, high_ref, wa_ref, wb_ref, mask_ref, out_ref, im_ref):
+    step = pl.program_id(0)
+    parts, _, pixels, mid = out_ref.shape
+    cols = low_ref.shape[1]
+
+    def product(slot, pair, w_ref):
+        grad = jnp.concatenate([low_ref[pair], main_ref[pair], high_ref[pair]], axis=0)
+        fill_taps(im_ref, slot, grad, mask_ref, pixels, cols, 1)
+        return jnp.dot(
+            im_ref[slot],
+            w_ref[0].reshape(9 * mid, parts * mid),
+            preferred_element_type=jnp.float32,
+        )
+
+    def store(source, total):
+        for part in range(parts):
+            out_ref[part, source] = total[:, part * mid : (part + 1) * mid].astype(jnp.bfloat16)
+
+    for index, pairs in enumerate(((0, 4), (1, 5), (3, 2))):
+
+        @pl.when(step == index)
+        def _(index=index, pairs=pairs):
+            first = product(0, pairs[0], wa_ref)
+            second = product(1, pairs[1], wb_ref)
+            if index < 2:
+                store(index + 1, first + second)
+            else:
+                store(0, first)
+                store(3, second)
+
+
+def messages_backward(low, main, high, weights, mask, parts):
+    pixels = mask.shape[1]
+    pairs, taps, mid, width = weights.shape
+    return pl.pallas_call(
+        messages_backward_kernel,
+        grid=(3,),
+        in_specs=[
+            whole(low.shape),
+            whole(main.shape),
+            whole(high.shape),
+            pl.BlockSpec((1, taps, mid, width), lambda i: (i + i // 2, 0, 0, 0)),
+            pl.BlockSpec((1, taps, mid, width), lambda i: (4 + i - 4 * (i // 2), 0, 0, 0)),
+            whole(mask.shape),
+        ],
+        out_specs=whole((parts, 4, pixels, mid)),
+        out_shape=jax.ShapeDtypeStruct((parts, 4, pixels, mid), jnp.bfloat16),
+        scratch_shapes=[pltpu.VMEM((2, pixels, taps * mid), jnp.bfloat16)],
+        compiler_params=kernel_params(),
+        cost_estimate=pl.CostEstimate(
+            flops=2 * pixels * weights.size, bytes_accessed=2 * weights.size, transcendentals=0
+        ),
+    )(low, main, high, weights, weights, mask)
+
+
+def dilated_backward_kernel(g_ref, w_ref, mask_ref, out_ref, im_ref):
+    parts, pixels, mid = out_ref.shape
+    cols = (g_ref.shape[0] - pixels) // 4
+    fill_taps(im_ref, 0, g_ref[...], mask_ref, pixels, cols, 2)
+    total = jnp.dot(
+        im_ref[0], w_ref[...].reshape(9 * mid, parts * mid), preferred_element_type=jnp.float32
+    )
+    for part in range(parts):
+        out_ref[part] = total[:, part * mid : (part + 1) * mid].astype(jnp.bfloat16)
+
+
+def dilated_backward(extended, weights, mask, parts):
+    pixels, mid = mask.shape[1], weights.shape[1]
+    return pl.pallas_call(
+        dilated_backward_kernel,
+        out_shape=jax.ShapeDtypeStruct((parts, pixels, mid), jnp.bfloat16),
+        scratch_shapes=[pltpu.VMEM((1, pixels, 9 * mid), jnp.bfloat16)],
+        compiler_params=kernel_params(),
+    )(extended, weights, mask)
+
+
+def tap_rows(lhs_ref, start, window, mask_ref, pixels, cols):
+    count = window.shape[0]
+    size = window.shape[1]
+    wide = window.astype(jnp.float32)
+    shifted_by = (pltpu.roll(wide, 1, 1), wide, pltpu.roll(wide, size - 1, 1))
+    for tap, (row_step, col_step) in enumerate(tap_offsets):
+        left = (1 + row_step) * cols
+        part = shifted_by[col_step + 1][:, left : left + pixels]
+        lhs_ref[start + tap * count : start + (tap + 1) * count, :] = (
+            part * mask_ref[0, tap : tap + 1, :]
+        ).astype(jnp.bfloat16)
+
+
+def heads_weight_kernel(before_ref, v_ref, after_ref, g_ref, mask_ref, out_ref, lhs_ref, acc_ref):
+    step = pl.program_id(0)
+    head_count, taps, chans, mid = out_ref.shape
+    pixels = v_ref.shape[2]
+    cols = before_ref.shape[2]
+    window = jnp.concatenate([before_ref[0], v_ref[0], after_ref[0]], axis=1)
+    tap_rows(lhs_ref, 0, window, mask_ref, pixels, cols)
+    grads = jnp.concatenate([g_ref[0, head] for head in range(head_count)], axis=1)
+    product = jnp.dot(lhs_ref[...], grads, preferred_element_type=jnp.float32)
+
+    @pl.when(step == 0)
+    def _():
+        acc_ref[...] = product
+
+    @pl.when(step > 0)
+    def _():
+        acc_ref[...] += product
+
+    @pl.when(step == pl.num_programs(0) - 1)
+    def _():
+        for head in range(head_count):
+            for tap in range(taps):
+                out_ref[head, tap] = acc_ref[
+                    tap * chans : (tap + 1) * chans, head * mid : (head + 1) * mid
+                ]
+
+
+def heads_weight(values, grads, mask, cols):
+    count, chans, pixels = values.shape
+    _, head_count, _, mid = grads.shape
+    last = count - 1
+    tail = pixels // cols - 1
+    return pl.pallas_call(
+        heads_weight_kernel,
+        grid=(count,),
+        in_specs=[
+            pl.BlockSpec((1, chans, cols), lambda i: (jnp.maximum(i - 1, 0), 0, tail)),
+            pl.BlockSpec((1, chans, pixels), lambda i: (i, 0, 0)),
+            pl.BlockSpec((1, chans, cols), lambda i: (jnp.minimum(i + 1, last), 0, 0)),
+            pl.BlockSpec((1, head_count, pixels, mid), lambda i: (i, 0, 0, 0)),
+            pl.BlockSpec((1, 9, pixels), lambda i: (i, 0, 0)),
+        ],
+        out_specs=whole((head_count, 9, chans, mid)),
+        out_shape=jax.ShapeDtypeStruct((head_count, 9, chans, mid), jnp.float32),
+        scratch_shapes=[
+            pltpu.VMEM((9 * chans, pixels), jnp.bfloat16),
+            pltpu.VMEM((9 * chans, head_count * mid), jnp.float32),
+        ],
+        compiler_params=kernel_params(),
+        cost_estimate=pl.CostEstimate(
+            flops=18 * chans * count * pixels * head_count * mid,
+            bytes_accessed=4 * 9 * chans * head_count * mid,
+            transcendentals=0,
+        ),
+    )(values, values, values, grads, mask)
+
+
+def messages_weight_kernel(before_ref, v_ref, after_ref, g_ref, mask_ref, out_ref, lhs_ref, *acc_refs):
+    step = pl.program_id(0)
+    pairs, taps, chans, mid = out_ref.shape
+    pixels = v_ref.shape[3]
+    cols = before_ref.shape[3]
+    for index, (source, *members) in enumerate(source_order):
+        window = jnp.concatenate(
+            [before_ref[0, source], v_ref[0, source], after_ref[0, source]], axis=1
+        )
+        tap_rows(lhs_ref, index * taps * chans, window, mask_ref, pixels, cols)
+        grads = jnp.concatenate([g_ref[0, pair] for pair in members], axis=1)
+        product = jnp.dot(
+            lhs_ref[index * taps * chans : (index + 1) * taps * chans, :],
+            grads,
+            preferred_element_type=jnp.float32,
+        )
+        acc_ref = acc_refs[index]
+
+        @pl.when(step == 0)
+        def _(acc_ref=acc_ref, product=product):
+            acc_ref[...] = product
+
+        @pl.when(step > 0)
+        def _(acc_ref=acc_ref, product=product):
+            acc_ref[...] += product
+
+    @pl.when(step == pl.num_programs(0) - 1)
+    def _():
+        for index, (source, *members) in enumerate(source_order):
+            for place, pair in enumerate(members):
+                for tap in range(taps):
+                    out_ref[pair, tap] = acc_refs[index][
+                        tap * chans : (tap + 1) * chans, place * mid : (place + 1) * mid
+                    ]
+
+
+def messages_weight(values, grads, mask, cols):
+    count, sources, chans, pixels = values.shape
+    _, pairs, _, mid = grads.shape
+    last = count - 1
+    tail = pixels // cols - 1
+    return pl.pallas_call(
+        messages_weight_kernel,
+        grid=(count,),
+        in_specs=[
+            pl.BlockSpec((1, sources, chans, cols), lambda i: (jnp.maximum(i - 1, 0), 0, 0, tail)),
+            pl.BlockSpec((1, sources, chans, pixels), lambda i: (i, 0, 0, 0)),
+            pl.BlockSpec((1, sources, chans, cols), lambda i: (jnp.minimum(i + 1, last), 0, 0, 0)),
+            pl.BlockSpec((1, pairs, pixels, mid), lambda i: (i, 0, 0, 0)),
+            pl.BlockSpec((1, 9, pixels), lambda i: (i, 0, 0)),
+        ],
+        out_specs=whole((pairs, 9, chans, mid)),
+        out_shape=jax.ShapeDtypeStruct((pairs, 9, chans, mid), jnp.float32),
+        scratch_shapes=[pltpu.VMEM((sources * 9 * chans, pixels), jnp.bfloat16)]
+        + [
+            pltpu.VMEM((9 * chans, (len(entry) - 1) * mid), jnp.float32) for entry in source_order
+        ],
+        compiler_params=kernel_params(),
+        cost_estimate=pl.CostEstimate(
+            flops=18 * chans * count * pixels * pairs * mid,
+            bytes_accessed=4 * 9 * chans * pairs * mid,
+            transcendentals=0,
+        ),
+    )(values, values, values, grads, mask)
+
+
+MESH = pl.DeviceIdType.MESH
+
+
+def greet(blocks, parts):
+    barrier = pltpu.get_barrier_semaphore()
+    blk, ch = lax.axis_index(BLK), lax.axis_index(CH)
+    for step in range(1, blocks):
+        pl.semaphore_signal(
+            barrier, inc=1, device_id={BLK: lax.rem(blk + step, blocks)}, device_id_type=MESH
+        )
+    for step in range(1, parts):
+        pl.semaphore_signal(
+            barrier, inc=1, device_id={CH: lax.rem(ch + step, parts)}, device_id_type=MESH
+        )
+    pl.semaphore_wait(barrier, blocks + parts - 2)
+
+
+def send_slots(source_of, target_ref, send_sem, recv_sem, axis, count):
+    me = lax.axis_index(axis)
+    copies = []
+    for step in range(1, count):
+        peer = lax.rem(me + step, count)
+        copy = pltpu.make_async_remote_copy(
+            src_ref=source_of(peer),
+            dst_ref=target_ref.at[me],
+            send_sem=send_sem.at[step],
+            recv_sem=recv_sem.at[me],
+            device_id={axis: peer},
+            device_id_type=MESH,
+        )
+        copy.start()
+        copies.append(copy)
+
+    def finish():
+        for step in range(1, count):
+            peer = lax.rem(me + step, count)
+            pltpu.make_async_remote_copy(
+                src_ref=target_ref.at[peer],
+                dst_ref=target_ref.at[peer],
+                send_sem=send_sem.at[step],
+                recv_sem=recv_sem.at[peer],
+                device_id={axis: peer},
+                device_id_type=MESH,
+            ).wait_recv()
+        for copy in copies:
+            copy.wait_send()
+
+    return finish
+
+
+def block_totals(first, second, stat_ref, send_sem, recv_sem, blocks):
+    me = lax.axis_index(BLK)
+    stat_ref[me, 0:1] = first
+    stat_ref[me, 1:2] = second
+    send_slots(lambda _: stat_ref.at[me], stat_ref, send_sem, recv_sem, BLK, blocks)()
+    total = stat_ref[0]
+    for block in range(1, blocks):
+        total = total + stat_ref[block]
+    return total[0:1], total[1:2]
+
+
+def fold(values):
+    rows, width = values.shape
+    return values.reshape(rows // 8, 8, width).sum(axis=0)
+
+
+def row_loop(rows, block, body, carry):
+    def step(index, state):
+        return body(pl.ds(pl.multiple_of(index * block, block), block), state)
+
+    return lax.fori_loop(0, rows // block, step, carry)
+
+
+def moments(ref, block):
+    rows, width = ref.shape
+
+    def body(part, state):
+        values = ref[part, :]
+        return state[0] + fold(values), state[1] + fold(values * values)
+
+    zero = jnp.zeros((8, width), jnp.float32)
+    total, square = row_loop(rows, block, body, (zero, zero))
+    return total.sum(axis=0, keepdims=True), square.sum(axis=0, keepdims=True)
+
+
+def halo_copies(ref, edge, pixels, send_sem, recv_sem, blocks):
+    me = lax.axis_index(BLK)
+
+    def copy(source, target, side, peer):
+        return pltpu.make_async_remote_copy(
+            src_ref=ref.at[pl.ds(source, edge)],
+            dst_ref=ref.at[pl.ds(target, edge)],
+            send_sem=send_sem.at[side],
+            recv_sem=recv_sem.at[side],
+            device_id={BLK: peer},
+            device_id_type=MESH,
+        )
+
+    up = copy(pixels, 0, 0, lax.rem(me + 1, blocks))
+    down = copy(edge, edge + pixels, 1, lax.rem(me + blocks - 1, blocks))
+
+    @pl.when(me < blocks - 1)
+    def _():
+        up.start()
+
+    @pl.when(me > 0)
+    def _():
+        down.start()
+
+    @pl.when(me == 0)
+    def _():
+        ref[0:edge, :] = jnp.zeros((edge, ref.shape[1]), ref.dtype)
+
+    @pl.when(me == blocks - 1)
+    def _():
+        ref[edge + pixels :, :] = jnp.zeros((edge, ref.shape[1]), ref.dtype)
+
+    def finish():
+        @pl.when(me > 0)
+        def _():
+            up.wait_recv()
+            down.wait_send()
+
+        @pl.when(me < blocks - 1)
+        def _():
+            down.wait_recv()
+            up.wait_send()
+
+    return finish
+
+
+def trunk_forward_kernel(
+    blocks,
+    parts,
+    cur_ref,
+    wr_ref,
+    wd_ref,
+    we_ref,
+    mask_ref,
+    gain1_ref,
+    bias1_ref,
+    gain2_ref,
+    bias2_ref,
+    gain3_ref,
+    bias3_ref,
+    out_ref,
+    ext_out_ref,
+    full_ref,
+    normed1_ref,
+    inverse1_ref,
+    normed2_ref,
+    inverse2_ref,
+    normed3_ref,
+    inverse3_ref,
+    pre1_ref,
+    pre3_ref,
+    ext_ref,
+    z_ref,
+    gath_ref,
+    stat1_ref,
+    stat2_ref,
+    stat3_ref,
+    term1_ref,
+    term3_ref,
+    stat_send,
+    stat_recv,
+    halo_send,
+    halo_recv,
+    part_send,
+    part_recv,
+):
+    pixels, feat = cur_ref.shape
+    mid = normed1_ref.shape[1]
+    wide = normed3_ref.shape[1]
+    edge = (ext_ref.shape[0] - pixels) // 2
+    ch = lax.axis_index(CH)
+    pixel_count = float(pixels * blocks)
+    greet(blocks, parts)
+
+    def terms(total, square):
+        mean_value = total / pixel_count
+        variance = square / pixel_count - mean_value * mean_value
+        return mean_value, lax.rsqrt(variance + epsilon)
+
+    pre1_ref[...] = contract_last(cur_ref[...], wr_ref[...])
+    total, square = moments(pre1_ref, 64)
+    mean_value, inverse = terms(
+        *block_totals(total, square, stat1_ref, stat_send.at[0], stat_recv.at[0], blocks)
+    )
+    term1_ref[0:1] = mean_value
+    term1_ref[1:2] = inverse
+
+    def first(part, state):
+        value = gain1_ref[...] * ((pre1_ref[part, :] - mean_value) * inverse) + bias1_ref[...]
+        pre1_ref[part, :] = value * sigmoid(value)
+        return state
+
+    own_mid = pl.ds(pl.multiple_of(ch * mid, mid), mid)
+    normed1_ref[...] = (pre1_ref[:, own_mid] - term1_ref[0:1, own_mid]) * term1_ref[1:2, own_mid]
+    inverse1_ref[...] = term1_ref[1:2, own_mid]
+    row_loop(pixels, 64, first, 0)
+    ext_ref[edge : edge + pixels, :] = pre1_ref[...].astype(jnp.bfloat16)
+    wait_halo = halo_copies(ext_ref, edge, pixels, halo_send, halo_recv, blocks)
+
+    half = edge // 2
+    for row_step in (1, 0, 2):
+        if row_step == 0:
+            wait_halo()
+        top = 2 * row_step * half
+        product = contract_last(
+            ext_ref[top : top + pixels, :],
+            wd_ref[3 * row_step : 3 * row_step + 3].reshape(3 * mid, parts * mid),
+        )
+        for col_step in range(3):
+            part = mask_ref[row_step * 3 + col_step] * product[:, col_step * mid : (col_step + 1) * mid]
+            if row_step == 1:
+                z_ref[col_step] = part
+            else:
+                z_ref[col_step] += part
+    second_pre = (
+        z_ref[1] + pltpu.roll(z_ref[0], 2, 0) + pltpu.roll(z_ref[2], pixels - 2, 0)
+    )
+    mean_value, inverse = terms(
+        *block_totals(
+            jnp.sum(second_pre, axis=0, keepdims=True),
+            jnp.sum(second_pre * second_pre, axis=0, keepdims=True),
+            stat2_ref,
+            stat_send.at[1],
+            stat_recv.at[1],
+            blocks,
+        )
+    )
+    normed = (second_pre - mean_value) * inverse
+    normed2_ref[...] = normed
+    inverse2_ref[...] = inverse
+    value = gain2_ref[...] * normed + bias2_ref[...]
+    gath_ref[ch] = (value * sigmoid(value)).astype(jnp.bfloat16)
+    wait_parts = send_slots(
+        lambda _: gath_ref.at[ch], gath_ref, part_send, part_recv, CH, parts
+    )
+    ext_out_ref[...] = ext_ref[...]
+    wait_parts()
+    for part in range(parts):
+        full_ref[:, part * mid : (part + 1) * mid] = gath_ref[part]
+    for part in range(parts):
+        lane = slice(part * wide, (part + 1) * wide)
+        pre3_ref[:, lane] = jnp.dot(
+            full_ref[...], we_ref[:, lane], preferred_element_type=jnp.float32
+        )
+    total, square = moments(pre3_ref, 16)
+    mean_value, inverse = terms(
+        *block_totals(total, square, stat3_ref, stat_send.at[2], stat_recv.at[2], blocks)
+    )
+    term3_ref[0:1] = mean_value
+    term3_ref[1:2] = inverse
+
+    def last(part, state):
+        value = (
+            gain3_ref[...] * ((pre3_ref[part, :] - mean_value) * inverse)
+            + bias3_ref[...]
+            + cur_ref[part, :].astype(jnp.float32)
+        )
+        out_ref[part, :] = (value * sigmoid(value)).astype(jnp.bfloat16)
+        return state
+
+    row_loop(pixels, 16, last, 0)
+    own_wide = pl.ds(pl.multiple_of(ch * wide, wide), wide)
+    normed3_ref[...] = (pre3_ref[:, own_wide] - term3_ref[0:1, own_wide]) * term3_ref[1:2, own_wide]
+    inverse3_ref[...] = term3_ref[1:2, own_wide]
+
+
+def trunk_params(key):
+    return pltpu.CompilerParams(
+        vmem_limit_bytes=60 * 2**20, collective_id=key, has_side_effects=True
+    )
+
+
+def trunk_forward(blocks, parts, cols, current, reduce_w, dilated_w, expand_w, mask, norms):
+    pixels, feat = current.shape
+    narrow = reduce_w.shape[0]
+    mid, wide = narrow // parts, feat // parts
+    edge = 2 * cols
+    f32, low = jnp.float32, jnp.bfloat16
+    shape = jax.ShapeDtypeStruct
+    rows = edge * 2 + pixels
+    return pl.pallas_call(
+        functools.partial(trunk_forward_kernel, blocks, parts),
+        out_shape=[
+            shape((pixels, feat), low),
+            shape((rows, narrow), low),
+            shape((pixels, narrow), low),
+            shape((pixels, mid), f32),
+            shape((1, mid), f32),
+            shape((pixels, mid), f32),
+            shape((1, mid), f32),
+            shape((pixels, wide), f32),
+            shape((1, wide), f32),
+        ],
+        scratch_shapes=[
+            pltpu.VMEM((pixels, narrow), f32),
+            pltpu.VMEM((pixels, feat), f32),
+            pltpu.VMEM((rows, narrow), low),
+            pltpu.VMEM((3, pixels, mid), f32),
+            pltpu.VMEM((parts, pixels, mid), low),
+            pltpu.VMEM((blocks, 2, narrow), f32),
+            pltpu.VMEM((blocks, 2, mid), f32),
+            pltpu.VMEM((blocks, 2, feat), f32),
+            pltpu.VMEM((2, narrow), f32),
+            pltpu.VMEM((2, feat), f32),
+            pltpu.SemaphoreType.DMA((3, blocks)),
+            pltpu.SemaphoreType.DMA((3, blocks)),
+            pltpu.SemaphoreType.DMA((2,)),
+            pltpu.SemaphoreType.DMA((2,)),
+            pltpu.SemaphoreType.DMA((parts,)),
+            pltpu.SemaphoreType.DMA((parts,)),
+        ],
+        compiler_params=trunk_params(1),
+        cost_estimate=pl.CostEstimate(
+            flops=2 * pixels * (2 * narrow * feat + 9 * mid * narrow),
+            bytes_accessed=20 * 2**20,
+            transcendentals=0,
+        ),
+    )(current, reduce_w, dilated_w, expand_w, mask, *norms)
+
+
+def slope_of(values):
+    gate = sigmoid(values)
+    return gate * (1.0 + values * (1.0 - gate))
+
+
+def sum_slots(ref, count):
+    total = ref[0].astype(jnp.float32)
+    for slot in range(1, count):
+        total = total + ref[slot].astype(jnp.float32)
+    return total
+
+
+def trunk_backward_kernel(
+    blocks,
+    parts,
+    up_ref,
+    heads_ref,
+    cur_ref,
+    normed3_ref,
+    inverse3_ref,
+    gain3_ref,
+    bias3_ref,
+    we_ref,
+    full_ref,
+    normed2_ref,
+    inverse2_ref,
+    gain2_ref,
+    bias2_ref,
+    wd_ref,
+    mask_f_ref,
+    mask_b_ref,
+    ext_ref,
+    normed1_ref,
+    inverse1_ref,
+    gain1_ref,
+    bias1_ref,
+    wr_ref,
+    out_ref,
+    expand_ref,
+    dilated_ref,
+    reduce_ref,
+    wide_ref,
+    second_ref,
+    first_ref,
+    third_ref,
+    grad_ref,
+    im_ref,
+    send2_ref,
+    recv2_ref,
+    send1_ref,
+    recv1_ref,
+    gath_ref,
+    low_ref,
+    ex_send_ref,
+    ex_recv_ref,
+    di_send_ref,
+    di_recv_ref,
+    re_send_ref,
+    re_recv_ref,
+    stat3_ref,
+    stat2_ref,
+    stat1_ref,
+    stat_send,
+    stat_recv,
+    halo_send,
+    halo_recv,
+    part_send,
+    part_recv,
+    sum_send,
+    sum_recv,
+):
+    pixels, wide = up_ref.shape
+    mid = normed1_ref.shape[1]
+    narrow = mid * parts
+    feat = cur_ref.shape[1]
+    edge = (grad_ref.shape[0] - pixels) // 2
+    half = edge // 2
+    blk = lax.axis_index(BLK)
+    ch = lax.axis_index(CH)
+    pixel_count = float(pixels * blocks)
+    low = jnp.bfloat16
+    greet(blocks, parts)
+    own_wide = pl.ds(pl.multiple_of(ch * wide, wide), wide)
+
+    def start(part, state):
+        normed = normed3_ref[part, :]
+        summed = (
+            gain3_ref[...] * normed + bias3_ref[...] + cur_ref[part, own_wide].astype(jnp.float32)
+        )
+        value = (up_ref[part, :] + heads_ref[part, :].astype(jnp.float32)) * slope_of(summed)
+        out_ref[part, :] = value
+        return state[0] + fold(value), state[1] + fold(value * normed)
+
+    zero = jnp.zeros((8, wide), jnp.float32)
+    bias_sum, gain_sum = row_loop(pixels, 32, start, (zero, zero))
+    bias_grad, gain_grad = block_totals(
+        bias_sum.sum(axis=0, keepdims=True),
+        gain_sum.sum(axis=0, keepdims=True),
+        stat3_ref,
+        stat_send.at[0],
+        stat_recv.at[0],
+        blocks,
+    )
+    wide_ref[0:1] = gain_grad
+    wide_ref[1:2] = bias_grad
+    scale = gain3_ref[...] * inverse3_ref[...]
+    bias_part = bias_grad / pixel_count
+    gain_part = gain_grad / pixel_count
+
+    def third(part, state):
+        third_ref[part, :] = (
+            scale * (out_ref[part, :] - bias_part - normed3_ref[part, :] * gain_part)
+        ).astype(low)
+        return state
+
+    row_loop(pixels, 32, third, 0)
+    product = contract_last(third_ref[...], we_ref[...])
+    for part in range(parts):
+        send2_ref[part] = product[:, part * mid : (part + 1) * mid].astype(low)
+    recv2_ref[ch] = send2_ref[ch]
+    wait_parts = send_slots(
+        lambda peer: send2_ref.at[peer], recv2_ref, part_send.at[0], part_recv.at[0], CH, parts
+    )
+    size = narrow // blocks
+    product = lax.dot_general(
+        full_ref[...], third_ref[...], (((0,), (0,)), ((), ())), preferred_element_type=jnp.float32
+    )
+    for block in range(blocks):
+        ex_send_ref[block] = product[block * size : (block + 1) * size].astype(low)
+    ex_recv_ref[blk] = ex_send_ref[blk]
+    wait_expand = send_slots(
+        lambda peer: ex_send_ref.at[peer], ex_recv_ref, sum_send.at[0], sum_recv.at[0], BLK, blocks
+    )
+    wait_parts()
+
+    def narrow_norm(recv_ref, normed_ref, inverse_ref, gain_ref, bias_ref, stat_ref, phase, sums_ref):
+        normed = normed_ref[...]
+        value = sum_slots(recv_ref, parts) * slope_of(gain_ref[...] * normed + bias_ref[...])
+        bias_grad, gain_grad = block_totals(
+            jnp.sum(value, axis=0, keepdims=True),
+            jnp.sum(value * normed, axis=0, keepdims=True),
+            stat_ref,
+            stat_send.at[phase],
+            stat_recv.at[phase],
+            blocks,
+        )
+        sums_ref[0:1] = gain_grad
+        sums_ref[1:2] = bias_grad
+        return (
+            gain_ref[...]
+            * inverse_ref[...]
+            * (value - bias_grad / pixel_count - normed * (gain_grad / pixel_count))
+        )
+
+    grad = narrow_norm(
+        recv2_ref, normed2_ref, inverse2_ref, gain2_ref, bias2_ref, stat2_ref, 1, second_ref
+    )
+    grad_ref[edge : edge + pixels, :] = grad.astype(low)
+    wait_halo = halo_copies(grad_ref, edge, pixels, halo_send, halo_recv, blocks)
+    own = grad_ref[edge : edge + pixels, :].astype(jnp.float32)
+    turned = (pltpu.roll(own, pixels - 2, 0), own, pltpu.roll(own, 2, 0))
+    for row_step in range(3):
+        side = jnp.concatenate(
+            [
+                (mask_f_ref[row_step * 3 + col_step] * turned[col_step]).astype(low)
+                for col_step in range(3)
+            ],
+            axis=1,
+        )
+        top = 2 * row_step * half
+        product = lax.dot_general(
+            ext_ref[top : top + pixels, :],
+            side,
+            (((0,), (0,)), ((), ())),
+            preferred_element_type=jnp.float32,
+        )
+        for block in range(blocks):
+            for col_step in range(3):
+                di_send_ref[block, row_step * 3 + col_step] = product[
+                    block * size : (block + 1) * size, col_step * mid : (col_step + 1) * mid
+                ].astype(low)
+    di_recv_ref[blk] = di_send_ref[blk]
+    wait_halo()
+    fill_taps(im_ref, 0, grad_ref[...], mask_b_ref, pixels, half, 2)
+    product = jnp.dot(
+        im_ref[0], wd_ref[...].reshape(9 * mid, narrow), preferred_element_type=jnp.float32
+    )
+    for part in range(parts):
+        send1_ref[part] = product[:, part * mid : (part + 1) * mid].astype(low)
+    recv1_ref[ch] = send1_ref[ch]
+    wait_parts = send_slots(
+        lambda peer: send1_ref.at[peer], recv1_ref, part_send.at[1], part_recv.at[1], CH, parts
+    )
+    wait_dilated = send_slots(
+        lambda peer: di_send_ref.at[peer], di_recv_ref, sum_send.at[1], sum_recv.at[1], BLK, blocks
+    )
+    wait_parts()
+    grad = narrow_norm(
+        recv1_ref, normed1_ref, inverse1_ref, gain1_ref, bias1_ref, stat1_ref, 2, first_ref
+    )
+    gath_ref[ch] = grad.astype(low)
+    wait_parts = send_slots(
+        lambda _: gath_ref.at[ch], gath_ref, part_send.at[2], part_recv.at[2], CH, parts
+    )
+    product = lax.dot_general(
+        cur_ref[...], gath_ref[ch], (((0,), (0,)), ((), ())), preferred_element_type=jnp.float32
+    )
+    size = feat // blocks
+    for block in range(blocks):
+        re_send_ref[block] = product[block * size : (block + 1) * size].astype(low)
+    re_recv_ref[blk] = re_send_ref[blk]
+    wait_reduce = send_slots(
+        lambda peer: re_send_ref.at[peer], re_recv_ref, sum_send.at[2], sum_recv.at[2], BLK, blocks
+    )
+    wait_parts()
+    for part in range(parts):
+        low_ref[:, part * mid : (part + 1) * mid] = gath_ref[part]
+    out_ref[...] += jnp.dot(low_ref[...], wr_ref[:, own_wide], preferred_element_type=jnp.float32)
+    wait_expand()
+    expand_ref[...] = sum_slots(ex_recv_ref, blocks)
+    wait_dilated()
+    dilated_ref[...] = sum_slots(di_recv_ref, blocks)
+    wait_reduce()
+    reduce_ref[...] = sum_slots(re_recv_ref, blocks)
+
+
+def trunk_backward(blocks, parts, operands):
+    pixels, wide = operands[0].shape
+    feat = wide * parts
+    mid = operands[9].shape[1]
+    narrow = mid * parts
+    rows = operands[16].shape[0]
+    f32, low = jnp.float32, jnp.bfloat16
+    shape = jax.ShapeDtypeStruct
+    small, large = narrow // blocks, feat // blocks
+    return pl.pallas_call(
+        functools.partial(trunk_backward_kernel, blocks, parts),
+        out_shape=[
+            shape((pixels, wide), f32),
+            shape((small, wide), f32),
+            shape((9, small, mid), f32),
+            shape((large, mid), f32),
+            shape((2, wide), f32),
+            shape((2, mid), f32),
+            shape((2, mid), f32),
+        ],
+        scratch_shapes=[
+            pltpu.VMEM((pixels, wide), low),
+            pltpu.VMEM((rows, mid), low),
+            pltpu.VMEM((1, pixels, 9 * mid), low),
+            pltpu.VMEM((parts, pixels, mid), low),
+            pltpu.VMEM((parts, pixels, mid), low),
+            pltpu.VMEM((parts, pixels, mid), low),
+            pltpu.VMEM((parts, pixels, mid), low),
+            pltpu.VMEM((parts, pixels, mid), low),
+            pltpu.VMEM((pixels, narrow), low),
+            pltpu.VMEM((blocks, small, wide), low),
+            pltpu.VMEM((blocks, small, wide), low),
+            pltpu.VMEM((blocks, 9, small, mid), low),
+            pltpu.VMEM((blocks, 9, small, mid), low),
+            pltpu.VMEM((blocks, large, mid), low),
+            pltpu.VMEM((blocks, large, mid), low),
+            pltpu.VMEM((blocks, 2, wide), f32),
+            pltpu.VMEM((blocks, 2, mid), f32),
+            pltpu.VMEM((blocks, 2, mid), f32),
+            pltpu.SemaphoreType.DMA((3, blocks)),
+            pltpu.SemaphoreType.DMA((3, blocks)),
+            pltpu.SemaphoreType.DMA((2,)),
+            pltpu.SemaphoreType.DMA((2,)),
+            pltpu.SemaphoreType.DMA((3, parts)),
+            pltpu.SemaphoreType.DMA((3, parts)),
+            pltpu.SemaphoreType.DMA((3, blocks)),
+            pltpu.SemaphoreType.DMA((3, blocks)),
+        ],
+        compiler_params=trunk_params(2),
+        cost_estimate=pl.CostEstimate(
+            flops=4 * pixels * (2 * narrow * wide + 9 * mid * narrow),
+            bytes_accessed=20 * 2**20,
+            transcendentals=0,
+        ),
+    )(*operands)
+
+
+def neighbour_rows(low_part, high_part):
+    count = lax.axis_size(BLK)
+    forward = [(i, i + 1) for i in range(count - 1)]
+    backward = [(target, source) for source, target in forward]
+    return lax.ppermute(low_part, BLK, forward), lax.ppermute(high_part, BLK, backward)
+
+
+def gather_parts(values):
+    return lax.all_gather(values, CH, axis=0, tiled=False)
+
+
+def reduce_parts(values):
+    return lax.psum_scatter(values, CH, scatter_dimension=0, tiled=False)
+
+
+def own_slice(values, size, axis):
+    return lax.dynamic_slice_in_dim(values, lax.axis_index(CH) * size, size, axis)
+
+
+def gather_weights(weights, axis):
+    blocks = lax.axis_size(BLK)
+    parts = lax.axis_size(CH)
+    other = 3 - axis
+    size = weights.shape[other] // blocks
+    mine = lax.dynamic_slice_in_dim(weights, lax.axis_index(BLK) * size, size, other)
+    everything = lax.all_gather(mine, (BLK, CH), axis=0, tiled=False)
+    everything = everything.reshape((blocks, parts) + mine.shape)
+    layers = weights.shape[0]
+    if axis == 1:
+        return everything.transpose(2, 1, 3, 0, 4).reshape(
+            layers, parts * weights.shape[1], weights.shape[2]
+        )
+    return everything.transpose(2, 0, 3, 1, 4).reshape(
+        layers, weights.shape[1], parts * weights.shape[2]
+    )
+
+
+def canvas_masks(canvas_ids, dilation):
+    rows, cols = canvas_ids.shape
+    padded = jnp.pad(canvas_ids, 2, constant_values=-1)
+    result = []
+    for row_step, col_step in tap_offsets:
+        top = 2 + row_step * dilation
+        left = 2 + col_step * dilation
+        result.append(padded[top : top + rows, left : left + cols] == canvas_ids)
+    return jnp.stack(result).astype(jnp.float32)
+
+
+def spread(mask):
+    taps, rows, cols = mask.shape
+    return jnp.broadcast_to(mask.reshape(taps, rows * cols, 1), (taps, rows * cols, lanes))
+
+
+def mask_set(canvas_ids, row_count, dilation):
+    everything = canvas_masks(canvas_ids, dilation)
+    own = lax.dynamic_slice_in_dim(everything, lax.axis_index(BLK) * row_count, row_count, 1)
+    turned = jnp.stack(
+        [jnp.roll(own[tap], step[1] * dilation, axis=1) for tap, step in enumerate(tap_offsets)]
+    )
+    return everything, own, spread(turned), spread(own[::-1])
+
+
+def shards(
+    features_in,
+    w_reduce,
+    w_dilated,
+    w_expand,
+    w_heads,
+    w_messages,
+    norm_gain,
+    norm_bias,
+    wide_gain,
+    wide_bias,
+    gate_gain,
+    gate_bias,
+    canvas_ids,
+    output_cotangent,
+    task_cotangents,
+):
+    rows, cols, wide = features_in.shape
+    pixels = rows * cols
+    blocks = lax.axis_size(BLK)
+    parts = lax.axis_size(CH)
+    pixel_count = float(pixels * blocks)
+    layers = w_reduce.shape[0]
+    mid = w_reduce.shape[1]
+    feat = wide * parts
+    narrow = mid * parts
+    low = jnp.bfloat16
+    all_masks, _, forward_one, backward_one = mask_set(canvas_ids, rows, 1)
+    _, _, forward_two, backward_two = mask_set(canvas_ids, rows, 2)
+    chunk_masks = all_masks.reshape(9, blocks, pixels).transpose(1, 0, 2)
+
+    reduce_full = gather_weights(w_reduce, 1)
+    expand_full = gather_weights(w_expand, 2)
+    small = jnp.concatenate(
+        [norm_gain[:, 0], norm_bias[:, 0]], axis=0
+    )
+    small_full = gather_parts(small).transpose(1, 0, 2).reshape(2, layers, narrow)
+    wide_full = (
+        gather_parts(jnp.concatenate([wide_gain, wide_bias], axis=0))
+        .transpose(1, 0, 2)
+        .reshape(2, layers, feat)
+    )
+    current = gather_parts(features_in.reshape(pixels, wide)).transpose(1, 0, 2).reshape(pixels, feat)
+    dilated_t = w_dilated.transpose(0, 2, 1, 3)
+    heads_t = w_heads.transpose(0, 1, 3, 2, 4)
+    messages_t = w_messages.transpose(0, 1, 3, 2, 4)
+
+    kept = []
+    task_list = []
+    for layer in range(layers):
+        keep = types.SimpleNamespace(input=current)
+        (
+            current,
+            keep.first_ext,
+            keep.second_full,
+            keep.normed1,
+            keep.inverse1,
+            keep.normed2,
+            keep.inverse2,
+            keep.normed3,
+            keep.inverse3,
+        ) = trunk_forward(
+            blocks,
+            parts,
+            cols,
+            current,
+            reduce_full[layer],
+            dilated_t[layer],
+            expand_full[layer],
+            forward_two,
+            (
+                small_full[0, layer][None],
+                small_full[1, layer][None],
+                norm_gain[layer, 1][None],
+                norm_bias[layer, 1][None],
+                wide_full[0, layer][None],
+                wide_full[1, layer][None],
+            ),
+        )
+        keep.output = current
+        kept.append(keep)
+    output = own_slice(current, wide, 1).reshape(rows, cols, wide)
+
+    partial_heads = []
+    gate_grads = []
+    for layer in range(layers):
+        keep = kept[layer]
+        out_full = keep.output
+        before, after = neighbour_rows(out_full[-cols:], out_full[:cols])
+        extended = jnp.concatenate([before, out_full, after], axis=0)
+        heads_pre, features = heads_forward(extended, heads_t[layer], forward_one)
+        keep.heads_pre = heads_pre
+        features_all = gather_parts(features)
+        before, after = neighbour_rows(features_all[:, :, -cols:], features_all[:, :, :cols])
+        messages = messages_forward(before, features_all, after, messages_t[layer], forward_one)
+        values = features.astype(jnp.float32)
+        maps = [values[0], None, None, values[3]]
+        cotangents = [
+            task_cotangents[layer, 0].reshape(pixels, mid).astype(jnp.float32),
+            None,
+            None,
+            task_cotangents[layer, 1].reshape(pixels, mid).astype(jnp.float32),
+        ]
+        head_grads = [cotangents[0], jnp.zeros_like(cotangents[0]), jnp.zeros_like(cotangents[0]), cotangents[3]]
+        message_grads, gain_terms, bias_terms = [], [], []
+        for pair, (source, target) in enumerate(message_pairs):
+            gate = jax.nn.sigmoid(gate_gain[layer, pair] * values[target] + gate_bias[layer, pair])
+            maps[target] = maps[target] + gate * messages[pair]
+            message_grads.append((cotangents[target] * gate).astype(low))
+            slope = cotangents[target] * messages[pair] * gate * (1.0 - gate)
+            gain_terms.append(jnp.sum(slope * values[target], axis=0))
+            bias_terms.append(jnp.sum(slope, axis=0))
+            head_grads[target] = head_grads[target] + slope * gate_gain[layer, pair]
+        task_list.append(jnp.stack([maps[0], maps[3]]).astype(low).reshape(2, rows, cols, mid))
+        gate_grads.append(jnp.stack([jnp.stack(gain_terms), jnp.stack(bias_terms)]))
+        message_low = jnp.stack(message_grads)
+        before, after = neighbour_rows(message_low[:, -cols:], message_low[:, :cols])
+        source_sums = reduce_parts(
+            messages_backward(before, message_low, after, messages_t[layer], backward_one, parts)
+        )
+        chans = narrow // blocks
+        feature_cols = features_all.transpose(1, 0, 3, 2).reshape(4, blocks, chans, pixels)
+        feature_cols = feature_cols.transpose(1, 0, 2, 3)
+        feature_cols = lax.all_to_all(feature_cols, BLK, 0, 0)
+        grads_all = lax.all_gather(message_low, BLK, axis=0, tiled=False)
+        keep.messages_grad = messages_weight(feature_cols, grads_all, chunk_masks, cols)
+        head_total = jnp.stack(head_grads) + source_sums.astype(jnp.float32)
+        heads_low = (head_total * silu_slope(heads_pre)).astype(low)
+        before, after = neighbour_rows(heads_low[:, -cols:], heads_low[:, :cols])
+        partial_heads.append(
+            reduce_parts(
+                heads_backward(before, heads_low, after, heads_t[layer], backward_one, parts)
+            )
+        )
+        chans = feat // blocks
+        value_cols = out_full.T.reshape(blocks, chans, pixels)
+        value_cols = lax.all_to_all(value_cols, BLK, 0, 0)
+        grads_all = lax.all_gather(heads_low, BLK, axis=0, tiled=False)
+        keep.heads_grad = heads_weight(value_cols, grads_all, chunk_masks, cols)
+
+    gate_sums = lax.psum(jnp.stack(gate_grads), BLK)
+
+    upstream = output_cotangent.reshape(pixels, wide).astype(jnp.float32)
+    for layer in reversed(range(layers)):
+        keep = kept[layer]
+        (
+            upstream,
+            keep.expand_grad,
+            keep.dilated_grad,
+            keep.reduce_grad,
+            keep.wide_sums,
+            keep.second_sums,
+            keep.first_sums,
+        ) = trunk_backward(
+            blocks,
+            parts,
+            (
+                upstream,
+                partial_heads[layer],
+                keep.input,
+                keep.normed3,
+                keep.inverse3,
+                wide_gain[layer][None],
+                wide_bias[layer][None],
+                w_expand[layer],
+                keep.second_full,
+                keep.normed2,
+                keep.inverse2,
+                norm_gain[layer, 1][None],
+                norm_bias[layer, 1][None],
+                dilated_t[layer],
+                forward_two,
+                backward_two,
+                keep.first_ext,
+                keep.normed1,
+                keep.inverse1,
+                norm_gain[layer, 0][None],
+                norm_bias[layer, 0][None],
+                reduce_full[layer],
+            ),
+        )
+
+    def stacked(of):
+        return jnp.stack([of(keep) for keep in kept])
+
+    narrow_sums = stacked(lambda keep: jnp.stack([keep.first_sums, keep.second_sums]))
+    wide_sums = stacked(lambda keep: keep.wide_sums)
+    return (
+        output,
+        jnp.stack(task_list),
+        upstream.reshape(rows, cols, wide),
+        stacked(lambda keep: keep.reduce_grad),
+        stacked(lambda keep: keep.dilated_grad),
+        stacked(lambda keep: keep.expand_grad),
+        stacked(lambda keep: keep.heads_grad),
+        stacked(lambda keep: keep.messages_grad),
+        narrow_sums[:, :, 0],
+        narrow_sums[:, :, 1],
+        wide_sums[:, 0],
+        wide_sums[:, 1],
+        gate_sums[:, 0],
+        gate_sums[:, 1],
+    )
+
+
+def route(*args):
+    mid = args[1].shape[1]
+    if mid % lanes == 0 and args[0].shape[1] % lanes == 0:
+        return shards(*args)
+    return plain_shards(*args)
+
+
 def solution(mesh):
     placed = (
-        P("blk", None, "ch"),
-        P(None, "ch", None),
-        P(None, "ch", None, None),
-        P(None, None, "ch"),
-        P(None, None, "ch", None, None),
-        P(None, None, "ch", None, None),
-        P(None, None, "ch"),
-        P(None, None, "ch"),
-        P(None, "ch"),
-        P(None, "ch"),
-        P(None, None, "ch"),
-        P(None, None, "ch"),
+        P(BLK, None, CH),
+        P(None, CH, None),
+        P(None, CH, None, None),
+        P(None, None, CH),
+        P(None, None, CH, None, None),
+        P(None, None, CH, None, None),
+        P(None, None, CH),
+        P(None, None, CH),
+        P(None, CH),
+        P(None, CH),
+        P(None, None, CH),
+        P(None, None, CH),
         P(),
-        P("blk", None, "ch"),
-        P(None, None, "blk", None, "ch"),
+        P(BLK, None, CH),
+        P(None, None, BLK, None, CH),
     )
     return jax.shard_map(
-        shards,
+        route,
         mesh=mesh,
         in_specs=placed,
         out_specs=(
-            P("blk", None, "ch"),
-            P(None, None, "blk", None, "ch"),
-            P("blk", None, "ch"),
-            P(None, "blk", "ch"),
-            P(None, None, "blk", "ch"),
-            P(None, "blk", "ch"),
-            P(None, None, None, "blk", "ch"),
-            P(None, None, None, "blk", "ch"),
-            P(None, None, "ch"),
-            P(None, None, "ch"),
-            P(None, "ch"),
-            P(None, "ch"),
-            P(None, None, "ch"),
-            P(None, None, "ch"),
+            P(BLK, None, CH),
+            P(None, None, BLK, None, CH),
+            P(BLK, None, CH),
+            P(None, BLK, CH),
+            P(None, None, BLK, CH),
+            P(None, BLK, CH),
+            P(None, None, None, BLK, CH),
+            P(None, None, None, BLK, CH),
+            P(None, None, CH),
+            P(None, None, CH),
+            P(None, CH),
+            P(None, CH),
+            P(None, None, CH),
+            P(None, None, CH),
         ),
         check_vma=False,
     )

time: 1640 us -> 996 us (0.61)
  matrix products: 448 us -> 0 us
  Pallas kernels: 0 us -> 422 us
  waiting for transfers between devices: 538 us -> 190 us
  blocking collectives: 229 us -> 74.6 us
  local copies, waits for them, and re-layouts: 214 us -> 137 us
  other arithmetic: 102 us -> 57 us
    dot_general x444 -> x0, matrix products: 448 us -> none  [the longest x144 198 us: conv_input_grad(): jnp.einsum('rwko,koc->rwc', window, weights[:, :, tap_index], preferred_e...]
    pallas_call x0 -> x16, Pallas kernels: none -> 422 us  [the longest x2 141 us: trunk_backward(): pl.pallas_call(functools.partial(trunk_backward_kernel, blocks, parts), o...]
    reduce_scatter x7 -> x4, waiting for transfers between devices: 259 us -> 44.8 us  [reduce_parts(): return lax.psum_scatter(values, CH, scatter_dimension=0, tiled=False)]
    unnamed x26 -> x13, waiting for transfers between devices: 192 us -> 3.25 us
    psum x12 -> x1, blocking collectives: 171 us -> 47.6 us  [shards(): gate_sums = lax.psum(jnp.stack(gate_grads), BLK)]
    unnamed x855 -> x230, local copies, waits for them, and re-layouts: 128 us -> 25.3 us
    squeeze x2 -> x7, local copies, waits for them, and re-layouts: 0.46 us -> 42.4 us  [the longest x1 26.3 us: shards(): heads_pre, features = heads_forward(extended, heads_t[layer], forward_one)]
    another operation x8 -> x23, local copies, waits for them, and re-layouts: 40.7 us -> 7.34 us  [the longest x4 2.83 us: shards(): gate_grads.append(jnp.stack([jnp.stack(gain_terms), jnp.stack(bias_terms)]))]
  transfers between devices with their start and end apart: 43 -> 33, of which waited for: 14 -> 12; matrix products, arithmetic and copies ran while one was open for 37% -> 16% of each run, Pallas kernels for 0% -> 28%
where the time goes in v1:
time: 996 us; the launch traced here: 980 us
  Pallas kernels  422 us (42%)
  waiting for transfers between devices  190 us (19%)
  local copies, waits for them, and re-layouts  137 us (14%)
  starting transfers between devices  84 us (8%)
  blocking collectives  74.6 us (7%)
  other arithmetic  57 us (6%)
  between operations  15.7 us (2%)
    pallas_call x2, Pallas kernels, trunk_backward(): pl.pallas_call(functools.partial(trunk_backward_kernel, blocks, parts), o...  141 us
    all_gather x2, waiting for transfers between devices, gather_weights(): everything = lax.all_gather(mine, (BLK, CH), axis=0, tiled=False)  94 us
    pallas_call x2, Pallas kernels, trunk_forward(): pl.pallas_call(functools.partial(trunk_forward_kernel, blocks, parts), ou...  91.5 us
    ppermute x8, starting transfers between devices, neighbour_rows(): lax.ppermute(low_part, BLK, forward)  53 us
    psum x1, blocking collectives, shards(): gate_sums = lax.psum(jnp.stack(gate_grads), BLK)  47.6 us
    reduce_scatter x4, waiting for transfers between devices, reduce_parts(): return lax.psum_scatter(values, CH, scatter_dimension=0, tiled=False)  44.8 us
    pallas_call x2, Pallas kernels, messages_weight(): pl.pallas_call(messages_weight_kernel, grid=(count,), in_specs=[pl.BlockS...  41.7 us
    pallas_call x2, Pallas kernels, heads_weight(): pl.pallas_call(heads_weight_kernel, grid=(count,), in_specs=[pl.BlockSpec...  39.8 us
  transfers between devices with their start and end apart: 33, of which 12 were waited for; matrix products, arithmetic and copies ran while one was open for 16% of the time, Pallas kernels for 28%

profile of v1, /device:TPU:0, one launch (start us, length us, event | category | flops | bytes accessed | tf_op | source)
XLA Modules:
  0.0 980.4 jit_solution(1883233560778025085)
XLA Ops:
  21.6 14.9 %all-gather.11 = f32[4,4,512]{2,1,0:T(4,128)S(1)} all-gather(f32[1,4,512]{2,1,0:T(4,128)S(1)} %maximum_bitcast_fusion), channel_id=5, replica_groups=mesh['blk'=8,'ch'=4] {'ch'}, dimensions={0}, use_global_device_ids=true | all-gather | bytes 40960 | tf_op jit(solution)/shard_map/all_gather | solution.py:1508
  37.9 12.1 %all-gather.10 = f32[4,4,128]{2,1,0:T(4,128)S(1)} all-gather(f32[1,4,128]{2,1,0:T(4,128)S(1)} %maximum_bitcast_fusion.3), channel_id=4, replica_groups=mesh['blk'=8,'ch'=4] {'ch'}, dimensions={0}, use_global_device_ids=true | all-gather | bytes 10240 | tf_op jit(solution)/shard_map/all_gather | solution.py:1508
  57.0 26.3 %slice_bitcast_fusion.1 = (bf16[4,9,128,2048]{3,2,1,0:T(8,128)(2,1)}, bf16[4,9,128,2048]{3,2,1,0:T(8,128)(2,1)}) fusion(bf16[2,4,9,128,2048]{4,3,2,1,0:T(8,128)(2,1)} %bitcast.822), kind=kLoop, calls=%fused_computation.1 | loop fusion | bytes 75497472 | tf_op jit(solution)/shard_map/squeeze | solution.py:1652
  86.5 36.8 %all-gather.24.cloned.1.call-done = bf16[64,128,256]{2,1,0:T(8,128)(2,1)} async-done(((bf16[2,128,256]{2,1,0:T(8,128)(2,1)}), bf16[64,128,256]{2,1,0:T(8,128)(2,1)}) %all-gather.24.cloned.1.call-update) | async-done | bytes 4194320 | tf_op jit(solution)/shard_map/all_gather | solution.py:1525
  130.4 57.2 %all-gather.26.cloned.1.call-done = bf16[64,64,512]{2,1,0:T(8,128)(2,1)} async-done(((bf16[2,64,512]{2,1,0:T(8,128)(2,1)}), bf16[64,64,512]{2,1,0:T(8,128)(2,1)}) %all-gather.26.cloned.1.call-update) | async-done | bytes 4194320 | tf_op jit(solution)/shard_map/all_gather | solution.py:1525
  202.4 45.1 %shard_map.254 = (bf16[512,2048]{1,0:T(8,128)(2,1)}, bf16[1024,512]{1,0:T(8,128)(2,1)}, bf16[512,512]{1,0:T(8,128)(2,1)}, f32[512,128]{1,0:T(8,128)}, f32[1,128]...) custom-call(bf16[512,2048]{1,0:T(8,128)(2,1)} %bitcast.834, ...), custom_call_target="tpu_custom_call" | custom-call | flops 2751463424 | bytes 20971520 | tf_op jit(solution)/shard_map/pallas_call | solution.py:1177
  247.6 46.4 %shard_map.255 = (bf16[512,2048]{1,0:T(8,128)(2,1)}, bf16[1024,512]{1,0:T(8,128)(2,1)}, bf16[512,512]{1,0:T(8,128)(2,1)}, f32[512,128]{1,0:T(8,128)}, f32[1,128]...) custom-call(bf16[512,2048]{1,0:T(8,128)(2,1)} %get-tuple-element.50.cur_ref, ...), custom_call_target="tpu_custom_call" | custom-call | flops 2751463424 | bytes 20971520 | tf_op jit(solution)/shard_map/pallas_call | solution.py:1177
  306.6 18.1 %shard_map.258 = (f32[4,512,128]{2,1,0:T(8,128)}, bf16[4,512,128]{2,1,0:T(8,128)(2,1)}) custom-call(bf16[768,2048]{1,0:T(8,128)(2,1)} %pad_maximum_fusion.3.v_ref, bf16[4,9,128,2048]{3,2,1,0:T(8,128)(2,1)} %get-tuple-element.169.w_ref, f32[9,512,128]{2,1,0:T(8,128)} %broadcast_in_dim.31.mask_ref), custom_call_target="tpu_custom_call" | custom-call | flops 9663676416 | bytes 18874368 | tf_op jit(solution)/shard_map/pallas_call | solution.py:505
  324.9 12.0 %collective-permute-start = (bf16[128,2048]{1,0:T(8,128)(2,1)S(1)}, bf16[128,2048]{1,0:T(8,128)(2,1)S(1)}, u32[]{:S(2)}, u32[]{:S(2)}) collective-permute-start(bf16[128,2048]{1,0:T(8,128)(2,1)S(1)} %get-tuple-element.200), channel_id=1, source_target_pairs={{0,4},{4,8},{8,12},{12,16},{16,20},{20,24},{24,28},{1,5},{5,9},{9,... | collective-permute-start | bytes 1572872 | tf_op jit(solution)/shard_map/ppermute | solution.py:1504
  338.2 10.6 %slice_bitcast_fusion.3 = (bf16[6,9,128,512]{3,2,1,0:T(8,128)(2,1)}, bf16[6,9,128,512]{3,2,1,0:T(8,128)(2,1)}) fusion(bf16[2,6,9,128,512]{4,3,2,1,0:T(8,128)(2,1)} %bitcast.827), kind=kLoop, calls=%fused_computation.4 | loop fusion | bytes 28311552 | tf_op jit(solution)/shard_map/squeeze | solution.py:1656
  350.7 18.1 %shard_map.256 = (f32[4,512,128]{2,1,0:T(8,128)}, bf16[4,512,128]{2,1,0:T(8,128)(2,1)}) custom-call(bf16[768,2048]{1,0:T(8,128)(2,1)} %pad_maximum_fusion.2.v_ref, bf16[4,9,128,2048]{3,2,1,0:T(8,128)(2,1)} %get-tuple-element.168.w_ref, f32[9,512,128]{2,1,0:T(8,128)} %broadcast_in_dim.31.mask_ref), custom_call_target="tpu_custom_call" | custom-call | flops 9663676416 | bytes 18874368 | tf_op jit(solution)/shard_map/pallas_call | solution.py:505
  368.8 12.5 %all-gather.30.cloned.1.call-done = bf16[16,512,128]{2,1,0:T(8,128)(2,1)} async-done(((bf16[4,512,128]{2,1,0:T(8,128)(2,1)}), bf16[16,512,128]{2,1,0:T(8,128)(2,1)}) %all-gather.30.cloned.1.call-update) | async-done | bytes 2097168 | tf_op jit(solution)/shard_map/all_gather | solution.py:1508
  390.9 10.2 %shard_map.259 = f32[6,512,128]{2,1,0:T(8,128)} custom-call(bf16[4,4,128,128]{3,2,1,0:T(8,128)(2,1)} %copy-done.22, bf16[4,4,512,128]{3,2,1,0:T(8,128)(2,1)} %bitcast.829, bf16[4,4,128,128]{3,2,1,0:T(8,128)(2,1)} %copy-done.23, bf16[6,9,128,512]{3,2,1,0:T(8,128)(2,1)} %get-tuple-element.171.wa_ref.wb_ref, ...), custom_call_target="tpu_custom_call" | custom-call | flops 3623878656 | bytes 7077888 | tf_op jit(solution)/shard_map/pallas_call | solution.py:581
  410.3 12.5 %collective-permute-start.8 = (bf16[6,128,128]{2,1,0:T(8,128)(2,1)}, bf16[6,128,128]{2,1,0:T(8,128)(2,1)}, u32[]{:S(2)}, u32[]{:S(2)}) collective-permute-start(bf16[6,128,128]{2,1,0:T(8,128)(2,1)} %get-tuple-element.223), channel_id=1, source_target_pairs={{0,4},{4,8},{8,12},{12,16},{16,20},{20,24},{24,28},{1,5},{5,9},{9,... | collective-permute-start | bytes 589832 | tf_op jit(solution)/shard_map/ppermute | solution.py:1504
  428.3 8.8 shard_map.260
  448.1 10.3 %shard_map.257 = f32[6,512,128]{2,1,0:T(8,128)} custom-call(bf16[4,4,128,128]{3,2,1,0:T(8,128)(2,1)} %copy-done.24, bf16[4,4,512,128]{3,2,1,0:T(8,128)(2,1)} %bitcast.832, bf16[4,4,128,128]{3,2,1,0:T(8,128)(2,1)} %copy-done.25, bf16[6,9,128,512]{3,2,1,0:T(8,128)(2,1)} %get-tuple-element.170.wa_ref.wb_ref, ...), custom_call_target="tpu_custom_call" | custom-call | flops 3623878656 | bytes 7077888 | tf_op jit(solution)/shard_map/pallas_call | solution.py:581
  467.1 12.8 %collective-permute-start.12 = (bf16[6,128,128]{2,1,0:T(8,128)(2,1)S(1)}, bf16[6,128,128]{2,1,0:T(8,128)(2,1)S(1)}, u32[]{:S(2)}, u32[]{:S(2)}) collective-permute-start(bf16[6,128,128]{2,1,0:T(8,128)(2,1)S(1)} %get-tuple-element.221), channel_id=1, source_target_pairs={{0,4},{4,8},{8,12},{12,16},{16,20},{20,24},{24,28},{1,5},{5,9},{9,... | collective-permute-start | bytes 589832 | tf_op jit(solution)/shard_map/ppermute | solution.py:1504
  483.9 8.8 shard_map.263
  492.9 44.8 %reduce-scatter.9.cloned.1.call-done = bf16[1,4,512,128]{3,2,1,0:T(8,128)(2,1)} async-done(((bf16[4,4,512,128]{3,2,1,0:T(8,128)(2,1)}), bf16[1,4,512,128]{3,2,1,0:T(8,128)(2,1)}) %reduce-scatter.9.cloned.1.call-update) | async-done | bytes 524304 | tf_op jit(solution)/shard_map/reduce_scatter | solution.py:1512
  549.5 16.7 %shard_map.261 = bf16[4,512,512]{2,1,0:T(8,128)(2,1)} custom-call(bf16[4,128,128]{2,1,0:T(8,128)(2,1)} %copy-done.98, bf16[4,512,128]{2,1,0:T(8,128)(2,1)} %get-tuple-element.307.main_ref, bf16[4,128,128]{2,1,0:T(8,128)(2,1)} %copy-done.100, bf16[4,9,128,2048]{3,2,1,0:T(8,128)(2,1)} %get-tuple-element.169.w_ref, f32[9,512,128]{2,1,0:T(8,128)} %broadcast_in_dim.33.mask_ref), custom_call_target="tpu_custom_call" | custom-call | flops 9663676416 | bytes 18874368 | tf_op jit(solution)/shard_map/pallas_call | solution.py:660
  576.6 16.7 %shard_map.264 = bf16[4,512,512]{2,1,0:T(8,128)(2,1)} custom-call(bf16[4,128,128]{2,1,0:T(8,128)(2,1)} %copy-done.97, bf16[4,512,128]{2,1,0:T(8,128)(2,1)} %get-tuple-element.306.main_ref, bf16[4,128,128]{2,1,0:T(8,128)(2,1)} %copy-done.99, bf16[4,9,128,2048]{3,2,1,0:T(8,128)(2,1)} %get-tuple-element.168.w_ref, f32[9,512,128]{2,1,0:T(8,128)} %broadcast_in_dim.33.mask_ref), custom_call_target="tpu_custom_call" | custom-call | flops 9663676416 | bytes 18874368 | tf_op jit(solution)/shard_map/pallas_call | solution.py:660
  597.8 7.4 all-to-all-start
  615.7 16.4 %all-to-all-done.before_ref.v_ref.after_ref = bf16[8,256,512]{2,1,0:T(8,128)(2,1)} async-done(((bf16[8,256,512]{2,1,0:T(8,128)(2,1)}), bf16[8,256,512]{2,1,0:T(8,128)(2,1)}, u32[]{:S(2)}, u32[]{:S(2)}) %all-to-all-start) | async-done | bytes 2097184 | tf_op jit(solution)/shard_map/all_to_all | solution.py:1698
  655.9 6.3 all-to-all-done.2.before_ref.v_ref.after_ref
  671.7 47.6 %psum.7 = f32[2,2,6,128]{3,2,1,0:T(8,128)S(1)} all-reduce(f32[2,2,6,128]{3,2,1,0:T(8,128)S(1)} %pad_maximum_fusion.7), channel_id=1, replica_groups=mesh['blk'=8,'ch'=4] {'blk'}, use_global_device_ids=true, to_apply=%region_28.29 | all-reduce | flops 3072 | bytes 24576 | tf_op jit(solution)/shard_map/psum | solution.py:1702
  724.9 73.6 %shard_map.262 = (f32[512,512]{1,0:T(8,128)}, f32[64,512]{1,0:T(8,128)}, f32[9,64,128]{2,1,0:T(8,128)}, f32[256,128]{1,0:T(8,128)}, f32[2,512]{1,0:T(2,128)}, /*index=5*/f32[2,128]{1,0:T(2,128)}, f32[2,128]{1,0:T(2,128)}) custom-call(f32[512,512]{1,0:T(8,128)} %bitcast_convert_fusion.up_ref, bf16[512,512]{1,0:T(8,128)(2,1)} %bitcast.864, ...), custom_call_target="tpu_custom_call" | custom-call | flops 2281701376 | bytes 20971520 | tf_op jit(solution)/shard_map/pallas_call | solution.py:1452
  798.6 67.8 %shard_map.265 = (f32[512,512]{1,0:T(8,128)}, f32[64,512]{1,0:T(8,128)}, f32[9,64,128]{2,1,0:T(8,128)}, f32[256,128]{1,0:T(8,128)}, f32[2,512]{1,0:T(2,128)}, /*index=5*/f32[2,128]{1,0:T(2,128)}, f32[2,128]{1,0:T(2,128)}) custom-call(f32[512,512]{1,0:T(8,128)} %get-tuple-element.63.up_ref, bf16[512,512]{1,0:T(8,128)(2,1)} %bitcast.865, ...), custom_call_target="tpu_custom_call" | custom-call | flops 2281701376 | bytes 20971520 | tf_op jit(solution)/shard_map/pallas_call | solution.py:1452
  878.6 20.8 %shard_map.268 = f32[6,9,64,128]{3,2,1,0:T(8,128)} custom-call(bf16[8,4,64,512]{3,2,1,0:T(8,128)(2,1)} %copy-done.2, bf16[8,4,64,512]{3,2,1,0:T(8,128)(2,1)} %copy-done.2, bf16[8,4,64,512]{3,2,1,0:T(8,128)(2,1)} %copy-done.2, bf16[8,6,512,128]{3,2,1,0:T(8,128)(2,1)} %bitcast.851, f32[8,9,512]{2,1,0:T(8,128)} %convert_bitcast_fusion.mask_ref), custom_call_target="tpu_custom_call" | custom-call | flops 3623878656 | bytes 1769472 | tf_op jit(solution)/shard_map/pallas_call | solution.py:867
  899.4 20.9 %shard_map.269 = f32[6,9,64,128]{3,2,1,0:T(8,128)} custom-call(bf16[8,4,64,512]{3,2,1,0:T(8,128)(2,1)} %all-to-all-done.3.before_ref.v_ref.after_ref, bf16[8,4,64,512]{3,2,1,0:T(8,128)(2,1)} %all-to-all-done.3.before_ref.v_ref.after_ref, bf16[8,4,64,512]{3,2,1,0:T(8,128)(2,1)} %all-to-all-done.3.before_ref.v_ref.after_ref, ...), custom_call_target="tpu_custom_call" | custom-call | flops 3623878656 | bytes 1769472 | tf_op jit(solution)/shard_map/pallas_call | solution.py:867
  924.1 19.6 %shard_map.266 = f32[4,9,256,128]{3,2,1,0:T(8,128)} custom-call(bf16[8,256,512]{2,1,0:T(8,128)(2,1)} %all-to-all-done.before_ref.v_ref.after_ref, bf16[8,256,512]{2,1,0:T(8,128)(2,1)} %all-to-all-done.before_ref.v_ref.after_ref, bf16[8,256,512]{2,1,0:T(8,128)(2,1)} %all-to-all-done.before_ref.v_ref.after_ref, bf16[8,4,512,128]{3,2,1,0:T(8,128)(2,1)} %bitcast.956, ...), custom_call_target="tpu_custom_call" | custom-call | flops 9663676416 | bytes 4718592 | tf_op jit(solution)/shard_map/pallas_call | solution.py:801
  945.0 20.2 %shard_map.267 = f32[4,9,256,128]{3,2,1,0:T(8,128)} custom-call(bf16[8,256,512]{2,1,0:T(8,128)(2,1)} %copy-done.18, bf16[8,256,512]{2,1,0:T(8,128)(2,1)} %copy-done.18, bf16[8,256,512]{2,1,0:T(8,128)(2,1)} %copy-done.18, bf16[8,4,512,128]{3,2,1,0:T(8,128)(2,1)} %bitcast.957, f32[8,9,512]{2,1,0:T(8,128)} %convert_bitcast_fusion.mask_ref), custom_call_target="tpu_custom_call" | custom-call | flops 9663676416 | bytes 4718592 | tf_op jit(solution)/shard_map/pallas_call | solution.py:801
  965.3 7.4 pad_maximum_fusion
  (431 shorter events, 205.0 us)
Async XLA Ops:
  7.2 76.1 %all-gather.22.cloned.1.call-start = ((), (), s32[]{:S(2)}) async-start(), calls=%async_computation.8 | async-start | bytes 2621440 | tf_op jit(solution)/shard_map/all_gather | solution.py:1508
  7.9 115.4 %all-gather.24.cloned.1.call-start = ((), (), s32[]{:S(2)}) async-start(), calls=%async_computation.13 | async-start | bytes 4325376 | tf_op jit(solution)/shard_map/all_gather | solution.py:1525
  9.1 178.5 %all-gather.26.cloned.1.call-start = ((), (), s32[]{:S(2)}) async-start(), calls=%async_computation.14 | async-start | bytes 4325376 | tf_op jit(solution)/shard_map/all_gather | solution.py:1525
  10.8 370.6 %all-gather.30.cloned.1.call-start = ((), (), s32[]{:S(2)}) async-start(), calls=%async_computation.16 | async-start | bytes 2621440 | tf_op jit(solution)/shard_map/all_gather | solution.py:1508
  296.4 3.8 collective-permute-start.4
  298.5 4.6 collective-permute-start.5
  324.8 112.4 %all-gather.28.cloned.1.call-start = ((), (), s32[]{:S(2)}) async-start(), calls=%async_computation.15 | async-start | bytes 2621440 | tf_op jit(solution)/shard_map/all_gather | solution.py:1508
  324.9 23.9 %collective-permute-start = (bf16[128,2048]{1,0:T(8,128)(2,1)S(1)}, bf16[128,2048]{1,0:T(8,128)(2,1)S(1)}, u32[]{:S(2)}, u32[]{:S(2)}) collective-permute-start(bf16[128,2048]{1,0:T(8,128)(2,1)S(1)} %get-tuple-element.200), channel_id=1, source_target_pairs={{0,4},{4,8},{8,12},{12,16},{16,20},{20,24},{24,28},{1,5},{5,9},{9,... | collective-permute-start | bytes 1572872 | tf_op jit(solution)/shard_map/ppermute | solution.py:1504
  336.9 11.9 %collective-permute-start.1 = (bf16[128,2048]{1,0:T(8,128)(2,1)S(1)}, bf16[128,2048]{1,0:T(8,128)(2,1)S(1)}, u32[]{:S(2)}, u32[]{:S(2)}) collective-permute-start(bf16[128,2048]{1,0:T(8,128)(2,1)S(1)} %get-tuple-element.201), channel_id=1, source_target_pairs={{4,0},{8,4},{12,8},{16,12},{20,16},{24,20},{28,24},{5,1},{9,5},{13... | collective-permute-start | bytes 1572872 | tf_op jit(solution)/shard_map/ppermute | solution.py:1504
  368.8 124.1 %reduce-scatter.5.cloned.1.call-start = ((), (), s32[]{:S(2)}) async-start(), calls=%async_computation.9 | async-start | bytes 2621440 | tf_op jit(solution)/shard_map/reduce_scatter | solution.py:1512
  382.7 7.2 collective-permute-start.6
  384.5 5.4 collective-permute-start.7
  410.3 15.9 %collective-permute-start.8 = (bf16[6,128,128]{2,1,0:T(8,128)(2,1)}, bf16[6,128,128]{2,1,0:T(8,128)(2,1)}, u32[]{:S(2)}, u32[]{:S(2)}) collective-permute-start(bf16[6,128,128]{2,1,0:T(8,128)(2,1)} %get-tuple-element.223), channel_id=1, source_target_pairs={{0,4},{4,8},{8,12},{12,16},{16,20},{20,24},{24,28},{1,5},{5,9},{9,... | collective-permute-start | bytes 589832 | tf_op jit(solution)/shard_map/ppermute | solution.py:1504
  422.8 3.7 collective-permute-start.9
  437.1 100.5 %reduce-scatter.9.cloned.1.call-start = ((), (), s32[]{:S(2)}) async-start(), calls=%async_computation.11 | async-start | bytes 2621440 | tf_op jit(solution)/shard_map/reduce_scatter | solution.py:1512
  438.5 6.5 collective-permute-start.2
  443.4 3.8 collective-permute-start.3
  467.1 14.1 %collective-permute-start.12 = (bf16[6,128,128]{2,1,0:T(8,128)(2,1)S(1)}, bf16[6,128,128]{2,1,0:T(8,128)(2,1)S(1)}, u32[]{:S(2)}, u32[]{:S(2)}) collective-permute-start(bf16[6,128,128]{2,1,0:T(8,128)(2,1)S(1)} %get-tuple-element.221), channel_id=1, source_target_pairs={{0,4},{4,8},{8,12},{12,16},{16,20},{20,24},{24,28},{1,5},{5,9},{9,... | collective-permute-start | bytes 589832 | tf_op jit(solution)/shard_map/ppermute | solution.py:1504
  479.9 3.3 collective-permute-start.13
  492.7 229.7 %reduce-scatter.7.cloned.1.call-start = ((), (), s32[]{:S(2)}) async-start(), calls=%async_computation.10 | async-start | bytes 2621440 | tf_op jit(solution)/shard_map/reduce_scatter | solution.py:1512
  542.6 3.3 collective-permute-start.10
  544.1 4.7 collective-permute-start.11
  566.2 232.3 %reduce-scatter.11.cloned.1.call-start = ((), (), s32[]{:S(2)}) async-start(), calls=%async_computation.12 | async-start | bytes 2621440 | tf_op jit(solution)/shard_map/reduce_scatter | solution.py:1512
  567.3 6.8 collective-permute-start.14
  593.4 285.2 %all-gather.36.cloned.1.call-start = ((), (), s32[]{:S(2)}) async-start(), calls=%async_computation.19 | async-start | bytes 7077888 | tf_op jit(solution)/shard_map/all_gather | solution.py:1686
  594.0 305.4 %all-gather.38.cloned.1.call-start = ((), (), s32[]{:S(2)}) async-start(), calls=%async_computation.20 | async-start | bytes 7077888 | tf_op jit(solution)/shard_map/all_gather | solution.py:1686
  594.7 329.3 %all-gather.32.cloned.1.call-start = ((), (), s32[]{:S(2)}) async-start(), calls=%async_computation.17 | async-start | bytes 4718592 | tf_op jit(solution)/shard_map/all_gather | solution.py:1699
  597.8 34.2 %all-to-all-start = ((bf16[8,256,512]{2,1,0:T(8,128)(2,1)}), bf16[8,256,512]{2,1,0:T(8,128)(2,1)}, u32[]{:S(2)}, u32[]{:S(2)}) async-start(bf16[8,256,512]{2,1,0:T(8,128)(2,1)} %bitcast.842), calls=%async_computation.4 | async-start | bytes 4194304 | tf_op jit(solution)/shard_map/all_to_all | solution.py:1698
  605.3 338.4 %all-gather.34.cloned.1.call-start = ((), (), s32[]{:S(2)}) async-start(), calls=%async_computation.18 | async-start | bytes 4718592 | tf_op jit(solution)/shard_map/all_gather | solution.py:1699
  632.0 30.2 %all-to-all-start.2 = ((bf16[8,4,64,512]{3,2,1,0:T(8,128)(2,1)}), bf16[8,4,64,512]{3,2,1,0:T(8,128)(2,1)S(1)}, u32[]{:S(2)}, u32[]{:S(2)}) async-start(bf16[8,4,64,512]{3,2,1,0:T(8,128)(2,1)} %bitcast.841), calls=%async_computation.6 | async-start | bytes 4194304 | tf_op jit(solution)/shard_map/all_to_all | solution.py:1685
  662.2 210.7 %all-to-all-start.3 = ((bf16[8,4,64,512]{3,2,1,0:T(8,128)(2,1)}), bf16[8,4,64,512]{3,2,1,0:T(8,128)(2,1)}, u32[]{:S(2)}, u32[]{:S(2)}) async-start(bf16[8,4,64,512]{3,2,1,0:T(8,128)(2,1)} %bitcast.840), calls=%async_computation.7 | async-start | bytes 4194304 | tf_op jit(solution)/shard_map/all_to_all | solution.py:1685
  873.0 70.7 %all-to-all-start.1 = ((bf16[8,256,512]{2,1,0:T(8,128)(2,1)}), bf16[8,256,512]{2,1,0:T(8,128)(2,1)S(1)}, u32[]{:S(2)}, u32[]{:S(2)}) async-start(bf16[8,256,512]{2,1,0:T(8,128)(2,1)} %bitcast.158), calls=%async_computation.5 | async-start | bytes 4194304 | tf_op jit(solution)/shard_map/all_to_all | solution.py:1698
  (104 other events, 1218.9 us)
Sparse Core Ops, SparseCore 0:
  9.6 49.2 all-gather.21
  62.5 60.7 all-gather.23
  126.9 60.6 all-gather.25
  324.9 56.3 all-gather.29
  383.3 44.6 all-gather.27
  437.2 45.1 reduce-scatter.4
  492.9 44.7 reduce-scatter.8
  566.4 46.3 reduce-scatter.6
  615.1 43.1 reduce-scatter.10
  660.1 62.9 all-gather.35
  725.0 63.5 all-gather.37
  790.3 42.7 all-gather.31
  835.0 40.9 all-gather.33

commit v2 on v1

--- a/solution.py
+++ b/solution.py
@@ -445,10 +445,6 @@
 source_order = ((1, 0, 4), (2, 1, 5), (0, 3), (3, 2))
 
 
-def kernel_params():
-    return pltpu.CompilerParams(vmem_limit_bytes=56 * 2**20)
-
-
 def whole(shape):
     return pl.BlockSpec(shape, lambda *_: (0,) * len(shape))
 
@@ -463,30 +459,582 @@
     return 1.0 / (1.0 + jnp.exp(-values))
 
 
-def heads_forward_kernel(v_ref, w_ref, mask_ref, pre_ref, act_ref, z_ref):
-    tap = pl.program_id(0)
+MESH = pl.DeviceIdType.MESH
+groups = ((1, 2), (0, 3))
+group_pairs = ((0, 4, 1, 5), (3, 2))
+
+
+def remote(source, target, send_sem, recv_sem, axis, peer):
+    return pltpu.make_async_remote_copy(
+        src_ref=source,
+        dst_ref=target,
+        send_sem=send_sem,
+        recv_sem=recv_sem,
+        device_id={axis: peer},
+        device_id_type=MESH,
+    )
+
+
+def comm_params(key):
+    return pltpu.CompilerParams(
+        vmem_limit_bytes=60 * 2**20, collective_id=key, has_side_effects=True
+    )
+
+
+def announce(targets):
+    barrier = pltpu.get_barrier_semaphore()
+    for axis, peer in targets:
+        pl.semaphore_signal(barrier, inc=1, device_id={axis: peer}, device_id_type=MESH)
+    pl.semaphore_wait(barrier, len(targets))
+
+
+def near_blocks(blocks):
+    me = lax.axis_index(BLK)
+    sibling = me + 1 - 2 * lax.rem(me, 2)
+    return sibling, [lax.rem(me + 2 * step, blocks) for step in range(1, blocks // 2)]
+
+
+def others(axis, count):
+    me = lax.axis_index(axis)
+    return [lax.rem(me + step, count) for step in range(1, count)]
+
+
+def gather_job(source, target, sems, blocks):
+    near_send, slot_recv, pass_send, local_sem = sems
+    me = lax.axis_index(BLK)
+    sibling, peers = near_blocks(blocks)
+    own = pltpu.make_async_copy(source, target.at[me], local_sem.at[0])
+
+    def near(step, peer):
+        return remote(
+            source, target.at[me], near_send.at[step], slot_recv.at[me], BLK, peer
+        )
+
+    def passing(step, peer):
+        return remote(
+            target.at[peer], target.at[peer], pass_send.at[step], slot_recv.at[peer], BLK, sibling
+        )
+
+    def start():
+        own.start()
+        for step, peer in enumerate(peers + [sibling]):
+            near(step, peer).start()
+
+    def forward():
+        for step, peer in enumerate(peers):
+            copy = passing(step, peer)
+            copy.wait_recv()
+            copy.start()
+
+    def finish():
+        for step in range(blocks // 2):
+            passing(0, lax.rem(sibling + 2 * step, blocks)).wait_recv()
+        for step, peer in enumerate(peers + [sibling]):
+            near(step, peer).wait_send()
+        for step, peer in enumerate(peers):
+            passing(step, peer).wait_send()
+        own.wait()
+
+    return start, forward, finish
+
+
+def swap_job(source, target, sems, blocks):
+    slot_send, slot_recv, _, local_sem = sems
+    me = lax.axis_index(BLK)
+    width = source.shape[1] // blocks
+
+    def part_of(block):
+        return source.at[:, pl.ds(pl.multiple_of(block * width, width), width)]
+
+    own = pltpu.make_async_copy(part_of(me), target.at[me], local_sem.at[0])
+
+    def copy(step, peer, slot):
+        return remote(
+            part_of(peer), target.at[slot], slot_send.at[step], slot_recv.at[slot], BLK, peer
+        )
+
+    def start():
+        for step, peer in enumerate(others(BLK, blocks)):
+            copy(step, peer, me).start()
+        own.start()
+
+    def finish():
+        for step, peer in enumerate(others(BLK, blocks)):
+            copy(step, peer, peer).wait_recv()
+            copy(step, peer, me).wait_send()
+        own.wait()
+
+    return start, lambda: None, finish
+
+
+job_kinds = (gather_job, swap_job)
+gather_kind, swap_kind = 0, 1
+
+
+def job_target(kind, source, blocks):
+    if kind == gather_kind:
+        return jax.ShapeDtypeStruct((blocks,) + source.shape, source.dtype)
+    return jax.ShapeDtypeStruct(
+        (blocks, source.shape[0], source.shape[1] // blocks), source.dtype
+    )
+
+
+def job_sems(blocks):
+    dma = pltpu.SemaphoreType.DMA
+    return [dma((blocks,)), dma((blocks,)), dma((blocks,)), dma((1,))]
+
+
+def job_call(kernel, jobs, blocks, in_specs, out_specs, out_shape, scratch_shapes, **options):
+    anywhere = pl.BlockSpec(memory_space=pl.ANY)
+    n_in, n_out, n_scratch = len(in_specs), len(out_specs), len(scratch_shapes)
+    count = len(jobs)
+
+    def wrapped(*refs):
+        ins, refs = refs[:n_in], refs[n_in:]
+        sources, refs = refs[:count], refs[count:]
+        outs, refs = refs[:n_out], refs[n_out:]
+        targets, refs = refs[:count], refs[count:]
+        scratch, sems = refs[:n_scratch], refs[n_scratch:]
+        running = [
+            job_kinds[kind](
+                sources[place], targets[place], sems[4 * place : 4 * place + 4], blocks
+            )
+            for place, (kind, _) in enumerate(jobs)
+        ]
+        kernel(running, *ins, *outs, *scratch)
+
+    def call(*operands):
+        result = pl.pallas_call(
+            wrapped,
+            in_specs=list(in_specs) + [anywhere] * count,
+            out_specs=list(out_specs) + [anywhere] * count,
+            out_shape=list(out_shape) + [job_target(kind, source, blocks) for kind, source in jobs],
+            scratch_shapes=list(scratch_shapes) + job_sems(blocks) * count,
+            **options,
+        )(*operands, *[source for _, source in jobs])
+        return result[:n_out], result[n_out:]
+
+    return call
+
+
+def weights_job(wr_ref, we_ref, layer, fulls, sems, blocks, parts):
+    part_send, part_recv, near_send, near_recv, pass_send, local_sem = sems
+    _, mid, feat = wr_ref.shape
+    _, narrow, wide = we_ref.shape
+    cw, rw = feat // blocks, narrow // blocks
+    blk, ch = lax.axis_index(BLK), lax.axis_index(CH)
+    sibling, peers = near_blocks(blocks)
+
+    def cut(index, size):
+        return pl.ds(pl.multiple_of(index * size, size), size)
+
+    def source(array):
+        if array == 0:
+            return wr_ref.at[layer, :, cut(blk, cw)]
+        return we_ref.at[layer, cut(blk, rw), :]
+
+    def share(array, part):
+        if array == 0:
+            return fulls[0].at[cut(part, mid), cut(blk, cw)]
+        return fulls[1].at[cut(blk, rw), cut(part, wide)]
+
+    def stripe(array, block):
+        if array == 0:
+            return fulls[0].at[:, cut(block, cw)]
+        return fulls[1].at[cut(block, rw), :]
+
+    def own(array):
+        return pltpu.make_async_copy(source(array), share(array, ch), local_sem.at[array])
+
+    def part_copy(array, step, peer, slot):
+        return remote(
+            source(array),
+            share(array, slot),
+            part_send.at[array, step],
+            part_recv.at[array, slot],
+            CH,
+            peer,
+        )
+
+    def near_copy(array, step, peer):
+        return remote(
+            stripe(array, blk),
+            stripe(array, blk),
+            near_send.at[array, step],
+            near_recv.at[array, blk],
+            BLK,
+            peer,
+        )
+
+    def passing(array, step, peer):
+        return remote(
+            stripe(array, peer),
+            stripe(array, peer),
+            pass_send.at[array, step],
+            near_recv.at[array, peer],
+            BLK,
+            sibling,
+        )
+
+    def start():
+        for array in range(2):
+            own(array).start()
+            for step, peer in enumerate(others(CH, parts)):
+                part_copy(array, step, peer, ch).start()
+
+    def spread():
+        for array in range(2):
+            for step, peer in enumerate(others(CH, parts)):
+                part_copy(array, step, peer, peer).wait_recv()
+            own(array).wait()
+            for step, peer in enumerate(peers + [sibling]):
+                near_copy(array, step, peer).start()
+
+    def forward(array):
+        for step, peer in enumerate(peers):
+            copy = passing(array, step, peer)
+            copy.wait_recv()
+            copy.start()
+
+    def finish():
+        for array in range(2):
+            for step in range(blocks // 2):
+                passing(array, 0, lax.rem(sibling + 2 * step, blocks)).wait_recv()
+            for step, peer in enumerate(others(CH, parts)):
+                part_copy(array, step, peer, ch).wait_send()
+            for step, peer in enumerate(peers + [sibling]):
+                near_copy(array, step, peer).wait_send()
+            for step, peer in enumerate(peers):
+                passing(array, step, peer).wait_send()
+
+    return start, spread, forward, finish
+
+
+def weights_sems(blocks, parts):
+    dma = pltpu.SemaphoreType.DMA
+    near = blocks // 2
+    return [
+        dma((2, parts)),
+        dma((2, parts)),
+        dma((2, near)),
+        dma((2, blocks)),
+        dma((2, near)),
+        dma((2,)),
+    ]
+
+
+def prologue_kernel(
+    blocks,
+    parts,
+    feat_ref,
+    wr_ref,
+    we_ref,
+    narrow_ref,
+    wide_ref,
+    ids_ref,
+    cur_ref,
+    full_r,
+    full_e,
+    narrow_out,
+    wide_out,
+    f1_ref,
+    b1_ref,
+    f2_ref,
+    b2_ref,
+    cols_ref,
+    line_send,
+    line_recv,
+    small_send,
+    small_recv,
+    local_sem,
+    *sems,
+):
+    pixels, wide = feat_ref.shape
+    blk, ch = lax.axis_index(BLK), lax.axis_index(CH)
+    sibling, peers = near_blocks(blocks)
+    smalls = ((narrow_ref, narrow_out), (wide_ref, wide_out))
+
+    def lane_part(index):
+        return cur_ref.at[:, pl.ds(pl.multiple_of(index * wide, wide), wide)]
+
+    start, spread, forward, finish = weights_job(
+        wr_ref, we_ref, 0, (full_r, full_e), sems, blocks, parts
+    )
+    own = pltpu.make_async_copy(feat_ref, lane_part(ch), local_sem.at[0])
+    own.start()
+    announce(
+        [(CH, peer) for peer in others(CH, parts)]
+        + [(BLK, peer) for peer in [sibling] + peers]
+    )
+    start()
+
+    right, left = lax.rem(ch + 1, parts), lax.rem(ch + parts - 1, parts)
+
+    def sides(hop):
+        return (
+            (0, lax.rem(ch + parts - hop, parts), right, ch - hop >= 0, ch < parts - 1),
+            (1, lax.rem(ch + hop, parts), left, ch + hop < parts, ch > 0),
+        )
+
+    def line_copy(block, side, hop, peer):
+        return remote(
+            feat_ref if hop == 0 else lane_part(block),
+            lane_part(block),
+            line_send.at[side, hop],
+            line_recv.at[block],
+            CH,
+            peer,
+        )
+
+    def line_hop(hop):
+        for side, block, peer, valid, goes in sides(hop):
+            if hop > 0:
+
+                @pl.when(valid)
+                def _():
+                    line_copy(block, side, hop, peer).wait_recv()
+
+            if hop < parts - 1:
+
+                @pl.when(valid & goes)
+                def _():
+                    line_copy(block, side, hop, peer).start()
+
+    def small_copy(place, step, peer, slot):
+        source, target = smalls[place]
+        return remote(
+            source,
+            target.at[slot],
+            small_send.at[place, step],
+            small_recv.at[place, slot],
+            CH,
+            peer,
+        )
+
+    def small_own(place):
+        source, target = smalls[place]
+        return pltpu.make_async_copy(source, target.at[ch], local_sem.at[1 + place])
+
+    line_hop(0)
+    for place in range(2):
+        small_own(place).start()
+        for step, peer in enumerate(others(CH, parts)):
+            small_copy(place, step, peer, ch).start()
+    spread()
+
+    rows = f1_ref.shape[1] // lanes
+    for f_ref, b_ref, reach in ((f1_ref, b1_ref, 1), (f2_ref, b2_ref, 2)):
+        for row in range(rows):
+            place = 2 + blk * rows + row
+            for tap, (row_step, col_step) in enumerate(tap_offsets):
+                a, b = row_step * reach, col_step * reach
+                here = ids_ref[place, 4 - b : 4 - b + lanes, :]
+                there = ids_ref[place + a, 4 : 4 + lanes, :]
+                f_ref[tap, row * lanes : (row + 1) * lanes] = jnp.where(
+                    (here == there) & (here >= 0), 1.0, 0.0
+                )
+                here = ids_ref[place, 4 : 4 + lanes, :]
+                there = ids_ref[place - a, 4 - b : 4 - b + lanes, :]
+                b_ref[tap, row * lanes : (row + 1) * lanes] = jnp.where(here == there, 1.0, 0.0)
+    lane = lax.broadcasted_iota(jnp.int32, (lanes, lanes), 1)
+
+    def all_rows(row, state):
+        here = ids_ref[2 + row, 4 : 4 + lanes, :]
+        value = jnp.zeros((lanes, lanes), jnp.float32)
+        for tap, (row_step, col_step) in enumerate(tap_offsets):
+            there = ids_ref[2 + row + row_step, 4 + col_step : 4 + col_step + lanes, :]
+            value = jnp.where((lane == tap) & (here == there), 1.0, value)
+        cols_ref[pl.ds(pl.multiple_of(row * lanes, lanes), lanes), :] = value
+        return state
+
+    lax.fori_loop(0, ids_ref.shape[0] - 4, all_rows, 0)
+    for hop in range(1, parts):
+        line_hop(hop)
+        if hop <= 2:
+            forward(hop - 1)
+    for array in range(parts - 1, 2):
+        forward(array)
+    finish()
+    for hop in range(parts - 1):
+        for side, block, peer, valid, goes in sides(hop):
+
+            @pl.when(valid & goes)
+            def _():
+                line_copy(block, side, hop, peer).wait_send()
+
+    for place in range(2):
+        for step, peer in enumerate(others(CH, parts)):
+            small_copy(place, step, peer, peer).wait_recv()
+            small_copy(place, step, peer, ch).wait_send()
+        small_own(place).wait()
+    own.wait()
+
+
+def prologue(blocks, parts, features, reduce_w, expand_w, narrow_terms, wide_terms, canvas_ids):
+    layers, mid, feat = reduce_w.shape
+    pixels, wide = features.shape
+    narrow = mid * parts
+    f32, low = jnp.float32, jnp.bfloat16
+    shape = jax.ShapeDtypeStruct
+    padded = jnp.pad(canvas_ids, ((2, 2), (4, 4)), constant_values=-1)
+    ids = jnp.broadcast_to(padded[:, :, None], padded.shape + (lanes,))
+    anywhere = pl.BlockSpec(memory_space=pl.ANY)
+    inside = pl.BlockSpec(memory_space=pltpu.VMEM)
+    dma = pltpu.SemaphoreType.DMA
+    mask = shape((9, pixels, lanes), f32)
+    return pl.pallas_call(
+        functools.partial(prologue_kernel, blocks, parts),
+        in_specs=[anywhere] * 5 + [inside],
+        out_specs=[anywhere] * 5 + [inside] * 5,
+        out_shape=[
+            shape((pixels, feat), low),
+            shape((narrow, feat), low),
+            shape((narrow, feat), low),
+            shape((parts,) + narrow_terms.shape, f32),
+            shape((parts,) + wide_terms.shape, f32),
+            mask,
+            mask,
+            mask,
+            mask,
+            shape((pixels * blocks, lanes), f32),
+        ],
+        scratch_shapes=[
+            dma((2, parts)),
+            dma((parts,)),
+            dma((2, parts)),
+            dma((2, parts)),
+            dma((3,)),
+        ]
+        + weights_sems(blocks, parts),
+        compiler_params=comm_params(5),
+        cost_estimate=pl.CostEstimate(flops=10**6, bytes_accessed=10**8, transcendentals=0),
+    )(features, reduce_w, expand_w, narrow_terms, wide_terms, ids)
+
+
+def greet_line(blocks):
+    barrier = pltpu.get_barrier_semaphore()
+    me = lax.axis_index(BLK)
+    for peer in (lax.rem(me + 1, blocks), lax.rem(me + blocks - 1, blocks)):
+        pl.semaphore_signal(barrier, inc=1, device_id={BLK: peer}, device_id_type=MESH)
+    pl.semaphore_wait(barrier, 2)
+
+
+def greet_blocks(blocks):
+    announce([(BLK, peer) for peer in others(BLK, blocks)])
+
+
+def edge_copies(main_ref, low_ref, high_ref, edge, send_sem, recv_sem, blocks):
+    me = lax.axis_index(BLK)
+    lead = (slice(None),) * (len(main_ref.shape) - 2)
+    pixels = main_ref.shape[-2]
+    up = remote(
+        main_ref.at[lead + (pl.ds(pixels - edge, edge),)],
+        low_ref,
+        send_sem.at[0],
+        recv_sem.at[0],
+        BLK,
+        lax.rem(me + 1, blocks),
+    )
+    down = remote(
+        main_ref.at[lead + (pl.ds(0, edge),)],
+        high_ref,
+        send_sem.at[1],
+        recv_sem.at[1],
+        BLK,
+        lax.rem(me + blocks - 1, blocks),
+    )
+
+    def start():
+        @pl.when(me < blocks - 1)
+        def _():
+            up.start()
+
+        @pl.when(me > 0)
+        def _():
+            down.start()
+
+    def finish(zero=True):
+        @pl.when(me > 0)
+        def _():
+            up.wait_recv()
+            down.wait_send()
+
+        @pl.when(me < blocks - 1)
+        def _():
+            down.wait_recv()
+            up.wait_send()
+
+        if zero:
+
+            @pl.when(me == 0)
+            def _():
+                low_ref[...] = jnp.zeros(low_ref.shape, low_ref.dtype)
+
+            @pl.when(me == blocks - 1)
+            def _():
+                high_ref[...] = jnp.zeros(high_ref.shape, high_ref.dtype)
+
+    return start, finish
+
+
+def heads_forward_kernel(
+    blocks,
+    main_ref,
+    w_ref,
+    mask_ref,
+    pre_ref,
+    act_ref,
+    ext_ref,
+    z_ref,
+    local_sem,
+    halo_send,
+    halo_recv,
+):
+    step = pl.program_id(0)
     head_count, pixels, mid = pre_ref.shape
-    cols = (v_ref.shape[0] - pixels) // 2
-    row_step = tap // 3
-    col_step = lax.rem(tap, 3)
-    window = v_ref[pl.ds(pl.multiple_of(row_step * cols, cols), pixels), :]
-    weights = w_ref[...].reshape(head_count * mid, v_ref.shape[1])
-    product = contract_last(window, weights)
+    cols = (ext_ref.shape[0] - pixels) // 2
+    feat = ext_ref.shape[1]
+    start, finish = edge_copies(
+        main_ref,
+        ext_ref.at[pl.ds(0, cols)],
+        ext_ref.at[pl.ds(cols + pixels, cols)],
+        cols,
+        halo_send,
+        halo_recv,
+        blocks,
+    )
+    own = pltpu.make_async_copy(main_ref, ext_ref.at[pl.ds(cols, pixels)], local_sem.at[0])
+
+    @pl.when(step == 0)
+    def _():
+        own.start()
+        greet_line(blocks)
+        start()
+        own.wait()
+
+    @pl.when(step == 3)
+    def _():
+        finish()
+
+    row_step = jnp.where(step < 3, 1, jnp.where(step < 6, 0, 2))
+    col_step = lax.rem(step, 3)
+    window = ext_ref[pl.ds(pl.multiple_of(row_step * cols, cols), pixels), :]
+    product = contract_last(window, w_ref[0].reshape(head_count * mid, feat))
     mask = mask_ref[0]
 
-    @pl.when(tap < 3)
+    @pl.when(step < 3)
     def _():
         for head in range(head_count):
             part = slice(head * mid, (head + 1) * mid)
             z_ref[col_step, :, part] = mask * product[:, part]
 
-    @pl.when(tap >= 3)
+    @pl.when(step >= 3)
     def _():
         for head in range(head_count):
             part = slice(head * mid, (head + 1) * mid)
             z_ref[col_step, :, part] += mask * product[:, part]
 
-    @pl.when(tap == 8)
+    @pl.when(step == 8)
     def _():
         for head in range(head_count):
             part = slice(head * mid, (head + 1) * mid)
@@ -499,126 +1047,42 @@
             act_ref[head] = (total * sigmoid(total)).astype(jnp.bfloat16)
 
 
-def heads_forward(extended, weights, mask):
-    head_count, _, mid, feat = weights.shape
+def tap_at(step):
+    return jnp.where(step < 3, step + 3, jnp.where(step < 6, step - 3, step))
+
+
+def heads_forward(blocks, layer, cols, main, weights, mask):
+    _, head_count, _, mid, feat = weights.shape
     pixels = mask.shape[1]
+    anywhere = pl.BlockSpec(memory_space=pl.ANY)
+    dma = pltpu.SemaphoreType.DMA
     return pl.pallas_call(
-        heads_forward_kernel,
+        functools.partial(heads_forward_kernel, blocks),
         grid=(9,),
         in_specs=[
-            whole(extended.shape),
-            pl.BlockSpec((head_count, 1, mid, feat), lambda t: (0, t, 0, 0)),
-            pl.BlockSpec((1, pixels, lanes), lambda t: (t, 0, 0)),
+            anywhere,
+            pl.BlockSpec((1, head_count, 1, mid, feat), lambda t: (layer, 0, tap_at(t), 0, 0)),
+            pl.BlockSpec((1, pixels, lanes), lambda t: (tap_at(t), 0, 0)),
         ],
         out_specs=[whole((head_count, pixels, mid))] * 2,
         out_shape=[
             jax.ShapeDtypeStruct((head_count, pixels, mid), jnp.float32),
             jax.ShapeDtypeStruct((head_count, pixels, mid), jnp.bfloat16),
         ],
-        scratch_shapes=[pltpu.VMEM((3, pixels, head_count * mid), jnp.float32)],
-        compiler_params=kernel_params(),
+        scratch_shapes=[
+            pltpu.VMEM((pixels + 2 * cols, feat), jnp.bfloat16),
+            pltpu.VMEM((3, pixels, head_count * mid), jnp.float32),
+            dma((1,)),
+            dma((2,)),
+            dma((2,)),
+        ],
+        compiler_params=comm_params(6 + layer),
         cost_estimate=pl.CostEstimate(
-            flops=2 * pixels * weights.size, bytes_accessed=2 * weights.size, transcendentals=0
+            flops=18 * pixels * head_count * mid * feat,
+            bytes_accessed=18 * head_count * mid * feat,
+            transcendentals=0,
         ),
-    )(extended, weights, mask)
-
-
-def tapped_conv(window_of, weights_of, mask_ref, pixels, mid, dilation):
-    totals = [None, None, None]
-    for row_step in range(3):
-        product = contract_last(window_of(row_step), weights_of(row_step))
-        for col_step in range(3):
-            part = mask_ref[row_step * 3 + col_step] * product[:, col_step * mid : (col_step + 1) * mid]
-            totals[col_step] = part if totals[col_step] is None else totals[col_step] + part
-    return (
-        totals[1]
-        + pltpu.roll(totals[0], dilation, 0)
-        + pltpu.roll(totals[2], pixels - dilation, 0)
-    )
-
-
-def messages_forward_kernel(low_ref, main_ref, high_ref, wa_ref, wb_ref, mask_ref, out_ref, lhs_ref):
-    step = pl.program_id(0)
-    parts, _, pixels, mid = main_ref.shape
-    cols = low_ref.shape[2]
-
-    def load(slot, source):
-        for part in range(parts):
-            chan = slice(part * mid, (part + 1) * mid)
-            lhs_ref[slot, 0:cols, chan] = low_ref[part, source]
-            lhs_ref[slot, cols : cols + pixels, chan] = main_ref[part, source]
-            lhs_ref[slot, cols + pixels :, chan] = high_ref[part, source]
-
-    def run(slot, w_ref, place):
-        out_ref[place] = tapped_conv(
-            lambda r: lhs_ref[slot, r * cols : r * cols + pixels, :],
-            lambda r: w_ref[0, 3 * r : 3 * r + 3].reshape(3 * mid, parts * mid),
-            mask_ref,
-            pixels,
-            mid,
-            1,
-        )
-
-    for index, places in enumerate(((0, 4), (1, 5), (3, 2))):
-
-        @pl.when(step == index)
-        def _(index=index, places=places):
-            if index < 2:
-                load(0, index + 1)
-                run(0, wa_ref, places[0])
-                run(0, wb_ref, places[1])
-            else:
-                load(0, 0)
-                load(1, 3)
-                run(0, wa_ref, places[0])
-                run(1, wb_ref, places[1])
-
-
-def messages_forward(low, main, high, weights, mask):
-    pixels = mask.shape[1]
-    pairs, taps, mid, width = weights.shape
-    cols = low.shape[2]
-    return pl.pallas_call(
-        messages_forward_kernel,
-        grid=(3,),
-        in_specs=[
-            whole(low.shape),
-            whole(main.shape),
-            whole(high.shape),
-            pl.BlockSpec((1, taps, mid, width), lambda i: (i + i // 2, 0, 0, 0)),
-            pl.BlockSpec((1, taps, mid, width), lambda i: (4 + i - 4 * (i // 2), 0, 0, 0)),
-            whole(mask.shape),
-        ],
-        out_specs=whole((pairs, pixels, mid)),
-        out_shape=jax.ShapeDtypeStruct((pairs, pixels, mid), jnp.float32),
-        scratch_shapes=[pltpu.VMEM((2, pixels + 2 * cols, width), jnp.bfloat16)],
-        compiler_params=kernel_params(),
-        cost_estimate=pl.CostEstimate(
-            flops=2 * pixels * weights.size, bytes_accessed=2 * weights.size, transcendentals=0
-        ),
-    )(low, main, high, weights, weights, mask)
-
-
-def dilated_forward_kernel(v_ref, w_ref, mask_ref, out_ref):
-    pixels, mid = out_ref.shape
-    cols = (v_ref.shape[0] - pixels) // 4
-    out_ref[...] = tapped_conv(
-        lambda r: v_ref[2 * r * cols : 2 * r * cols + pixels, :],
-        lambda r: w_ref[3 * r : 3 * r + 3].reshape(3 * mid, v_ref.shape[1]),
-        mask_ref,
-        pixels,
-        mid,
-        2,
-    )
-
-
-def dilated_forward(extended, weights, mask):
-    pixels, mid = mask.shape[1], weights.shape[1]
-    return pl.pallas_call(
-        dilated_forward_kernel,
-        out_shape=jax.ShapeDtypeStruct((pixels, mid), jnp.float32),
-        compiler_params=kernel_params(),
-    )(extended, weights, mask)
+    )(main, weights, mask)
 
 
 def fill_taps(im_ref, slot, grad, mask_ref, pixels, cols, dilation):
@@ -631,13 +1095,259 @@
         im_ref[slot, :, tap * mid : (tap + 1) * mid] = (part * mask_ref[tap]).astype(jnp.bfloat16)
 
 
-def heads_backward_kernel(low_ref, main_ref, high_ref, w_ref, mask_ref, out_ref, im_ref):
+def messages_kernel(
+    blocks,
+    layer,
+    jobs,
+    feat_ref,
+    w_hbm,
+    cot_ref,
+    gain_ref,
+    bias_ref,
+    f_ref,
+    b_ref,
+    maps_ref,
+    local_ref,
+    sums_ref,
+    grad_ref,
+    part_ref,
+    cols_out,
+    main_ref,
+    low_ref,
+    high_ref,
+    cot_low,
+    cot_high,
+    w_ref,
+    lhs_ref,
+    z_ref,
+    im_ref,
+    pack_ref,
+    w_sem,
+    local_sem,
+    halo_send,
+    halo_recv,
+    cot_send,
+    cot_recv,
+    slot_send,
+    slot_recv,
+):
+    parts, heads, pixels, mid = feat_ref.shape
+    cols = low_ref.shape[2]
+    pairs = w_ref.shape[0]
+    me, ch = lax.axis_index(BLK), lax.axis_index(CH)
+    low = jnp.bfloat16
+    loads = [
+        pltpu.make_async_copy(w_hbm.at[layer, pair], w_ref.at[pair], w_sem.at[pair])
+        for pair in range(pairs)
+    ]
+    main_copy = pltpu.make_async_copy(feat_ref, main_ref, local_sem.at[0])
+    main_copy.start()
+    for pair in (0, 4, 1, 5, 3, 2):
+        loads[pair].start()
+    announce([(BLK, peer) for peer in others(BLK, blocks)])
+    start, finish = edge_copies(feat_ref, low_ref, high_ref, cols, halo_send, halo_recv, blocks)
+    start()
+    cot_start, cot_finish = edge_copies(
+        cot_ref, cot_low, cot_high, cols, cot_send, cot_recv, blocks
+    )
+    cot_start()
+    main_copy.wait()
+    size = parts * mid // blocks
+    for block in range(blocks):
+        part, first = block * size // mid, block * size % mid
+        for index, (one, two) in enumerate(groups):
+            pack_ref[block, index] = jnp.concatenate(
+                [main_ref[part, one][:, first : first + size], main_ref[part, two][:, first : first + size]],
+                axis=1,
+            )
+    for index, peer in enumerate(others(BLK, blocks)):
+        remote(
+            pack_ref.at[peer], cols_out.at[me], slot_send.at[index], slot_recv.at[me], BLK, peer
+        ).start()
+    keep = pltpu.make_async_copy(pack_ref.at[me], cols_out.at[me], local_sem.at[1])
+    keep.start()
+    for job in jobs:
+        job[0]()
+
+    for source in range(heads):
+        for part in range(parts):
+            lhs_ref[source, cols : cols + pixels, part * mid : (part + 1) * mid] = main_ref[part, source]
+    order = (0, 4, 1, 5, 3, 2)
+
+    def taps(pair, row_step):
+        source = message_pairs[pair][0]
+        product = contract_last(
+            lhs_ref[source, row_step * cols : row_step * cols + pixels, :],
+            w_ref[pair, 3 * row_step : 3 * row_step + 3].reshape(3 * mid, parts * mid),
+        )
+        for col_step in range(3):
+            value = f_ref[row_step * 3 + col_step] * product[:, col_step * mid : (col_step + 1) * mid]
+            if row_step == 1:
+                z_ref[pair, col_step] = value
+            else:
+                z_ref[pair, col_step] += value
+
+    for pair in order:
+        loads[pair].wait()
+        taps(pair, 1)
+    finish()
+    for source in range(heads):
+        for part in range(parts):
+            chan = slice(part * mid, (part + 1) * mid)
+            lhs_ref[source, 0:cols, chan] = low_ref[part, source]
+            lhs_ref[source, cols + pixels :, chan] = high_ref[part, source]
+    for pair in order:
+        taps(pair, 0)
+        taps(pair, 2)
+    cot_finish()
+    values = {}
+    cots = {}
+    for place, target in enumerate((0, 3)):
+        values[target] = main_ref[ch, target].astype(jnp.float32)
+        cots[target] = cot_ref[place].astype(jnp.float32)
+    for place, target in enumerate((0, 3)):
+        value, cot = values[target], cots[target]
+        total, slopes = value, cot
+        for pair in range(pairs):
+            if message_pairs[pair][1] != target:
+                continue
+            message = (
+                z_ref[pair, 1]
+                + pltpu.roll(z_ref[pair, 0], 1, 0)
+                + pltpu.roll(z_ref[pair, 2], pixels - 1, 0)
+            )
+            gain, bias = gain_ref[layer, pair : pair + 1], bias_ref[layer, pair : pair + 1]
+            gate = sigmoid(gain * value + bias)
+            total = total + gate * message
+            grad_ref[pair] = (cot * gate).astype(low)
+            slope = cot * message * gate * (1.0 - gate)
+            sums_ref[pair : pair + 1] = jnp.sum(slope * value, axis=0, keepdims=True)
+            sums_ref[pairs + pair : pairs + pair + 1] = jnp.sum(slope, axis=0, keepdims=True)
+            slopes = slopes + slope * gain
+        maps_ref[place] = total.astype(low)
+        local_ref[place] = slopes
+
+    def product_of(pair, slot):
+        source, target = message_pairs[pair]
+        place = 0 if target == 0 else 1
+        gain, bias = gain_ref[layer, pair : pair + 1], bias_ref[layer, pair : pair + 1]
+
+        def border(cot, feat):
+            return (
+                cot[place].astype(jnp.float32)
+                * sigmoid(gain * feat[ch, target].astype(jnp.float32) + bias)
+            ).astype(low)
+
+        grad = jnp.concatenate(
+            [border(cot_low, low_ref), grad_ref[pair], border(cot_high, high_ref)], axis=0
+        )
+        fill_taps(im_ref, slot, grad, b_ref, pixels, cols, 1)
+        return jnp.dot(
+            im_ref[slot],
+            w_ref[pair].reshape(9 * mid, parts * mid),
+            preferred_element_type=jnp.float32,
+        )
+
+    for source, *members in source_order:
+        total = product_of(members[0], 0)
+        for pair in members[1:]:
+            total = total + product_of(pair, 1)
+        for part in range(parts):
+            part_ref[part, source] = total[:, part * mid : (part + 1) * mid].astype(low)
+    for job in jobs:
+        job[1]()
+    for index, peer in enumerate(others(BLK, blocks)):
+        copy = remote(
+            pack_ref.at[peer], cols_out.at[peer], slot_send.at[index], slot_recv.at[peer], BLK, peer
+        )
+        copy.wait_recv()
+        copy.wait_send()
+    keep.wait()
+    for job in jobs:
+        job[2]()
+
+
+def messages_both(blocks, layer, jobs, cols, features, weights, cotangents, gains, biases, forward, backward):
+    parts, heads, pixels, mid = features.shape
+    pairs = weights.shape[1]
+    narrow = parts * mid
+    f32, low = jnp.float32, jnp.bfloat16
+    shape = jax.ShapeDtypeStruct
+    anywhere = pl.BlockSpec(memory_space=pl.ANY)
+    inside = pl.BlockSpec(memory_space=pltpu.VMEM)
+    dma = pltpu.SemaphoreType.DMA
+    wide = 2 * narrow // blocks
+    return job_call(
+        functools.partial(messages_kernel, blocks, layer),
+        jobs,
+        blocks,
+        in_specs=[anywhere, anywhere] + [inside] * 5,
+        out_specs=[inside] * 5 + [anywhere],
+        out_shape=[
+            shape((2, pixels, mid), low),
+            shape((2, pixels, mid), f32),
+            shape((2 * pairs, mid), f32),
+            shape((pairs, pixels, mid), low),
+            shape((parts, heads, pixels, mid), low),
+            shape((blocks, 2, pixels, wide), low),
+        ],
+        scratch_shapes=[
+            pltpu.VMEM((parts, heads, pixels, mid), low),
+            pltpu.VMEM((parts, heads, cols, mid), low),
+            pltpu.VMEM((parts, heads, cols, mid), low),
+            pltpu.VMEM((2, cols, mid), low),
+            pltpu.VMEM((2, cols, mid), low),
+            pltpu.VMEM((pairs, 9, mid, narrow), low),
+            pltpu.VMEM((heads, pixels + 2 * cols, narrow), low),
+            pltpu.VMEM((pairs, 3, pixels, mid), f32),
+            pltpu.VMEM((2, pixels, 9 * mid), low),
+            pltpu.VMEM((blocks, 2, pixels, wide), low),
+            dma((pairs,)),
+            dma((2,)),
+            dma((2,)),
+            dma((2,)),
+            dma((2,)),
+            dma((2,)),
+            dma((blocks,)),
+            dma((blocks,)),
+        ],
+        compiler_params=comm_params(10 + layer),
+        cost_estimate=pl.CostEstimate(
+            flops=36 * pixels * pairs * mid * narrow,
+            bytes_accessed=18 * pairs * mid * narrow,
+            transcendentals=0,
+        ),
+    )(features, weights, cotangents, gains, biases, forward, backward)
+
+
+def heads_backward_kernel(
+    blocks,
+    jobs,
+    main_ref,
+    w_ref,
+    mask_ref,
+    out_ref,
+    low_ref,
+    high_ref,
+    im_ref,
+    halo_send,
+    halo_recv,
+):
     step = pl.program_id(0)
     head_count, pixels, mid = main_ref.shape
     cols = low_ref.shape[1]
 
     @pl.when(step == 0)
     def _():
+        start, finish = edge_copies(main_ref, low_ref, high_ref, cols, halo_send, halo_recv, blocks)
+        if jobs:
+            greet_blocks(blocks)
+        else:
+            greet_line(blocks)
+        start()
+        for job in jobs:
+            job[0]()
+        finish()
         for head in range(head_count):
             grad = jnp.concatenate([low_ref[head], main_ref[head], high_ref[head]], axis=0)
             fill_taps(im_ref, head, grad, mask_ref, pixels, cols, 1)
@@ -646,198 +1356,96 @@
     for head in range(head_count):
         product = jnp.dot(
             im_ref[head],
-            w_ref[head].reshape(9 * mid, w_ref.shape[3]),
+            w_ref[0, head].reshape(9 * mid, w_ref.shape[4]),
             preferred_element_type=jnp.float32,
         )
         total = product if total is None else total + product
     out_ref[0] = total.astype(jnp.bfloat16)
 
-
-def heads_backward(low, main, high, weights, mask, parts):
-    head_count, taps, mid, feat = weights.shape
+    if jobs:
+
+        @pl.when(step == pl.num_programs(0) - 1)
+        def _():
+            for job in jobs:
+                job[1]()
+            for job in jobs:
+                job[2]()
+
+
+def heads_backward(blocks, layer, jobs, cols, main, weights, mask, parts):
+    _, head_count, taps, mid, feat = weights.shape
     pixels = mask.shape[1]
     width = feat // parts
-    return pl.pallas_call(
-        heads_backward_kernel,
+    dma = pltpu.SemaphoreType.DMA
+    return job_call(
+        functools.partial(heads_backward_kernel, blocks),
+        jobs,
+        blocks,
         grid=(parts,),
         in_specs=[
-            whole(low.shape),
             whole(main.shape),
-            whole(high.shape),
-            pl.BlockSpec((head_count, taps, mid, width), lambda j: (0, 0, 0, j)),
+            pl.BlockSpec((1, head_count, taps, mid, width), lambda j: (layer, 0, 0, 0, j)),
             whole(mask.shape),
         ],
-        out_specs=pl.BlockSpec((1, pixels, width), lambda j: (j, 0, 0)),
-        out_shape=jax.ShapeDtypeStruct((parts, pixels, width), jnp.bfloat16),
-        scratch_shapes=[pltpu.VMEM((head_count, pixels, taps * mid), jnp.bfloat16)],
-        compiler_params=kernel_params(),
+        out_specs=[pl.BlockSpec((1, pixels, width), lambda j: (j, 0, 0))],
+        out_shape=[jax.ShapeDtypeStruct((parts, pixels, width), jnp.bfloat16)],
+        scratch_shapes=[
+            pltpu.VMEM((head_count, cols, mid), jnp.bfloat16),
+            pltpu.VMEM((head_count, cols, mid), jnp.bfloat16),
+            pltpu.VMEM((head_count, pixels, taps * mid), jnp.bfloat16),
+            dma((2,)),
+            dma((2,)),
+        ],
+        compiler_params=comm_params(20 + layer),
         cost_estimate=pl.CostEstimate(
-            flops=2 * pixels * weights.size, bytes_accessed=2 * weights.size, transcendentals=0
-        ),
-    )(low, main, high, weights, mask)
-
-
-def messages_backward_kernel(low_ref, main_ref, high_ref, wa_ref, wb_ref, mask_ref, out_ref, im_ref):
-    step = pl.program_id(0)
-    parts, _, pixels, mid = out_ref.shape
-    cols = low_ref.shape[1]
-
-    def product(slot, pair, w_ref):
-        grad = jnp.concatenate([low_ref[pair], main_ref[pair], high_ref[pair]], axis=0)
-        fill_taps(im_ref, slot, grad, mask_ref, pixels, cols, 1)
-        return jnp.dot(
-            im_ref[slot],
-            w_ref[0].reshape(9 * mid, parts * mid),
-            preferred_element_type=jnp.float32,
-        )
-
-    def store(source, total):
-        for part in range(parts):
-            out_ref[part, source] = total[:, part * mid : (part + 1) * mid].astype(jnp.bfloat16)
-
-    for index, pairs in enumerate(((0, 4), (1, 5), (3, 2))):
-
-        @pl.when(step == index)
-        def _(index=index, pairs=pairs):
-            first = product(0, pairs[0], wa_ref)
-            second = product(1, pairs[1], wb_ref)
-            if index < 2:
-                store(index + 1, first + second)
-            else:
-                store(0, first)
-                store(3, second)
-
-
-def messages_backward(low, main, high, weights, mask, parts):
-    pixels = mask.shape[1]
-    pairs, taps, mid, width = weights.shape
-    return pl.pallas_call(
-        messages_backward_kernel,
-        grid=(3,),
-        in_specs=[
-            whole(low.shape),
-            whole(main.shape),
-            whole(high.shape),
-            pl.BlockSpec((1, taps, mid, width), lambda i: (i + i // 2, 0, 0, 0)),
-            pl.BlockSpec((1, taps, mid, width), lambda i: (4 + i - 4 * (i // 2), 0, 0, 0)),
-            whole(mask.shape),
-        ],
-        out_specs=whole((parts, 4, pixels, mid)),
-        out_shape=jax.ShapeDtypeStruct((parts, 4, pixels, mid), jnp.bfloat16),
-        scratch_shapes=[pltpu.VMEM((2, pixels, taps * mid), jnp.bfloat16)],
-        compiler_params=kernel_params(),
-        cost_estimate=pl.CostEstimate(
-            flops=2 * pixels * weights.size, bytes_accessed=2 * weights.size, transcendentals=0
-        ),
-    )(low, main, high, weights, weights, mask)
-
-
-def dilated_backward_kernel(g_ref, w_ref, mask_ref, out_ref, im_ref):
-    parts, pixels, mid = out_ref.shape
-    cols = (g_ref.shape[0] - pixels) // 4
-    fill_taps(im_ref, 0, g_ref[...], mask_ref, pixels, cols, 2)
-    total = jnp.dot(
-        im_ref[0], w_ref[...].reshape(9 * mid, parts * mid), preferred_element_type=jnp.float32
-    )
-    for part in range(parts):
-        out_ref[part] = total[:, part * mid : (part + 1) * mid].astype(jnp.bfloat16)
-
-
-def dilated_backward(extended, weights, mask, parts):
-    pixels, mid = mask.shape[1], weights.shape[1]
-    return pl.pallas_call(
-        dilated_backward_kernel,
-        out_shape=jax.ShapeDtypeStruct((parts, pixels, mid), jnp.bfloat16),
-        scratch_shapes=[pltpu.VMEM((1, pixels, 9 * mid), jnp.bfloat16)],
-        compiler_params=kernel_params(),
-    )(extended, weights, mask)
-
-
-def tap_rows(lhs_ref, start, window, mask_ref, pixels, cols):
-    count = window.shape[0]
-    size = window.shape[1]
-    wide = window.astype(jnp.float32)
-    shifted_by = (pltpu.roll(wide, 1, 1), wide, pltpu.roll(wide, size - 1, 1))
-    for tap, (row_step, col_step) in enumerate(tap_offsets):
-        left = (1 + row_step) * cols
-        part = shifted_by[col_step + 1][:, left : left + pixels]
-        lhs_ref[start + tap * count : start + (tap + 1) * count, :] = (
-            part * mask_ref[0, tap : tap + 1, :]
-        ).astype(jnp.bfloat16)
-
-
-def heads_weight_kernel(before_ref, v_ref, after_ref, g_ref, mask_ref, out_ref, lhs_ref, acc_ref):
-    step = pl.program_id(0)
-    head_count, taps, chans, mid = out_ref.shape
-    pixels = v_ref.shape[2]
-    cols = before_ref.shape[2]
-    window = jnp.concatenate([before_ref[0], v_ref[0], after_ref[0]], axis=1)
-    tap_rows(lhs_ref, 0, window, mask_ref, pixels, cols)
-    grads = jnp.concatenate([g_ref[0, head] for head in range(head_count)], axis=1)
-    product = jnp.dot(lhs_ref[...], grads, preferred_element_type=jnp.float32)
-
-    @pl.when(step == 0)
-    def _():
-        acc_ref[...] = product
-
-    @pl.when(step > 0)
-    def _():
-        acc_ref[...] += product
-
-    @pl.when(step == pl.num_programs(0) - 1)
-    def _():
-        for head in range(head_count):
-            for tap in range(taps):
-                out_ref[head, tap] = acc_ref[
-                    tap * chans : (tap + 1) * chans, head * mid : (head + 1) * mid
-                ]
-
-
-def heads_weight(values, grads, mask, cols):
-    count, chans, pixels = values.shape
-    _, head_count, _, mid = grads.shape
-    last = count - 1
-    tail = pixels // cols - 1
-    return pl.pallas_call(
-        heads_weight_kernel,
-        grid=(count,),
-        in_specs=[
-            pl.BlockSpec((1, chans, cols), lambda i: (jnp.maximum(i - 1, 0), 0, tail)),
-            pl.BlockSpec((1, chans, pixels), lambda i: (i, 0, 0)),
-            pl.BlockSpec((1, chans, cols), lambda i: (jnp.minimum(i + 1, last), 0, 0)),
-            pl.BlockSpec((1, head_count, pixels, mid), lambda i: (i, 0, 0, 0)),
-            pl.BlockSpec((1, 9, pixels), lambda i: (i, 0, 0)),
-        ],
-        out_specs=whole((head_count, 9, chans, mid)),
-        out_shape=jax.ShapeDtypeStruct((head_count, 9, chans, mid), jnp.float32),
-        scratch_shapes=[
-            pltpu.VMEM((9 * chans, pixels), jnp.bfloat16),
-            pltpu.VMEM((9 * chans, head_count * mid), jnp.float32),
-        ],
-        compiler_params=kernel_params(),
-        cost_estimate=pl.CostEstimate(
-            flops=18 * chans * count * pixels * head_count * mid,
-            bytes_accessed=4 * 9 * chans * head_count * mid,
+            flops=18 * pixels * head_count * mid * feat,
+            bytes_accessed=18 * head_count * mid * feat,
             transcendentals=0,
         ),
-    )(values, values, values, grads, mask)
-
-
-def messages_weight_kernel(before_ref, v_ref, after_ref, g_ref, mask_ref, out_ref, lhs_ref, *acc_refs):
+    )(main, weights, mask)
+
+
+def weight_kernel(
+    blocks,
+    lists,
+    store,
+    jobs,
+    before_ref,
+    v_ref,
+    after_ref,
+    g_ref,
+    cols_ref,
+    out_ref,
+    lhs_ref,
+    *acc_refs,
+):
     step = pl.program_id(0)
-    pairs, taps, chans, mid = out_ref.shape
-    pixels = v_ref.shape[3]
-    cols = before_ref.shape[3]
-    for index, (source, *members) in enumerate(source_order):
+    pixels, chans = v_ref.shape[2:]
+    cols = lanes
+    if jobs:
+
+        @pl.when(step == 0)
+        def _():
+            greet_blocks(blocks)
+            for job in jobs:
+                job[0]()
+
+    masks = cols_ref[...]
+    for index, members in enumerate(lists):
         window = jnp.concatenate(
-            [before_ref[0, source], v_ref[0, source], after_ref[0, source]], axis=1
-        )
-        tap_rows(lhs_ref, index * taps * chans, window, mask_ref, pixels, cols)
-        grads = jnp.concatenate([g_ref[0, pair] for pair in members], axis=1)
-        product = jnp.dot(
-            lhs_ref[index * taps * chans : (index + 1) * taps * chans, :],
-            grads,
-            preferred_element_type=jnp.float32,
+            [before_ref[0, index], v_ref[0, index], after_ref[0, index]], axis=0
+        ).astype(jnp.float32)
+        size = window.shape[0]
+        shifted_by = (pltpu.roll(window, 1, 0), window, pltpu.roll(window, size - 1, 0))
+        for tap, (row_step, col_step) in enumerate(tap_offsets):
+            top = (1 + row_step) * cols
+            part = shifted_by[col_step + 1][top : top + pixels]
+            lhs_ref[:, tap * chans : (tap + 1) * chans] = (
+                part * masks[:, tap : tap + 1]
+            ).astype(jnp.bfloat16)
+        grads = jnp.concatenate([g_ref[0, member] for member in members], axis=1)
+        product = lax.dot_general(
+            lhs_ref[...], grads, (((0,), (0,)), ((), ())), preferred_element_type=jnp.float32
         )
         acc_ref = acc_refs[index]
 
@@ -849,47 +1457,68 @@
         def _(acc_ref=acc_ref, product=product):
             acc_ref[...] += product
 
-    @pl.when(step == pl.num_programs(0) - 1)
+    @pl.when(step == blocks - 1)
     def _():
-        for index, (source, *members) in enumerate(source_order):
-            for place, pair in enumerate(members):
-                for tap in range(taps):
-                    out_ref[pair, tap] = acc_refs[index][
-                        tap * chans : (tap + 1) * chans, place * mid : (place + 1) * mid
-                    ]
-
-
-def messages_weight(values, grads, mask, cols):
-    count, sources, chans, pixels = values.shape
-    _, pairs, _, mid = grads.shape
-    last = count - 1
-    tail = pixels // cols - 1
-    return pl.pallas_call(
-        messages_weight_kernel,
-        grid=(count,),
+        store(out_ref, acc_refs)
+        for job in jobs:
+            job[1]()
+        for job in jobs:
+            job[2]()
+
+
+def weight_gradient(key, blocks, jobs, lists, store, out_shape, values, grads, mask_cols):
+    _, count, pixels, chans = values.shape
+    _, members, _, mid = grads.shape
+    f32, low = jnp.float32, jnp.bfloat16
+    tail = pixels // lanes - 1
+    return job_call(
+        functools.partial(weight_kernel, blocks, lists, store),
+        jobs,
+        blocks,
+        grid=(blocks,),
         in_specs=[
-            pl.BlockSpec((1, sources, chans, cols), lambda i: (jnp.maximum(i - 1, 0), 0, 0, tail)),
-            pl.BlockSpec((1, sources, chans, pixels), lambda i: (i, 0, 0, 0)),
-            pl.BlockSpec((1, sources, chans, cols), lambda i: (jnp.minimum(i + 1, last), 0, 0, 0)),
-            pl.BlockSpec((1, pairs, pixels, mid), lambda i: (i, 0, 0, 0)),
-            pl.BlockSpec((1, 9, pixels), lambda i: (i, 0, 0)),
+            pl.BlockSpec((1, count, lanes, chans), lambda i: (jnp.maximum(i - 1, 0), 0, tail, 0)),
+            pl.BlockSpec((1, count, pixels, chans), lambda i: (i, 0, 0, 0)),
+            pl.BlockSpec(
+                (1, count, lanes, chans), lambda i: (jnp.minimum(i + 1, blocks - 1), 0, 0, 0)
+            ),
+            pl.BlockSpec((1, members, pixels, mid), lambda i: (i, 0, 0, 0)),
+            pl.BlockSpec((pixels, lanes), lambda i: (i, 0)),
         ],
-        out_specs=whole((pairs, 9, chans, mid)),
-        out_shape=jax.ShapeDtypeStruct((pairs, 9, chans, mid), jnp.float32),
-        scratch_shapes=[pltpu.VMEM((sources * 9 * chans, pixels), jnp.bfloat16)]
-        + [
-            pltpu.VMEM((9 * chans, (len(entry) - 1) * mid), jnp.float32) for entry in source_order
-        ],
-        compiler_params=kernel_params(),
+        out_specs=[whole(out_shape)],
+        out_shape=[jax.ShapeDtypeStruct(out_shape, f32)],
+        scratch_shapes=[pltpu.VMEM((pixels, 9 * chans), low)]
+        + [pltpu.VMEM((9 * chans, len(entry) * mid), f32) for entry in lists],
+        compiler_params=comm_params(key)
+        if jobs
+        else pltpu.CompilerParams(vmem_limit_bytes=60 * 2**20),
         cost_estimate=pl.CostEstimate(
-            flops=18 * chans * count * pixels * pairs * mid,
-            bytes_accessed=4 * 9 * chans * pairs * mid,
+            flops=18 * chans * pixels * blocks * mid * sum(len(entry) for entry in lists),
+            bytes_accessed=10**7,
             transcendentals=0,
         ),
-    )(values, values, values, grads, mask)
-
-
-MESH = pl.DeviceIdType.MESH
+    )(values, values, values, grads, mask_cols)
+
+
+def heads_store(out_ref, acc_refs):
+    head_count, taps, chans, mid = out_ref.shape
+    for head in range(head_count):
+        for tap in range(taps):
+            out_ref[head, tap] = acc_refs[0][
+                tap * chans : (tap + 1) * chans, head * mid : (head + 1) * mid
+            ]
+
+
+def messages_store(out_ref, acc_refs):
+    _, taps, size, mid = out_ref.shape
+    for index, members in enumerate(group_pairs):
+        for place, pair in enumerate(members):
+            side = groups[index].index(message_pairs[pair][0])
+            for tap in range(taps):
+                start = (2 * tap + side) * size
+                out_ref[pair, tap] = acc_refs[index][
+                    start : start + size, place * mid : (place + 1) * mid
+                ]
 
 
 def greet(blocks, parts):
@@ -1023,6 +1652,8 @@
 def trunk_forward_kernel(
     blocks,
     parts,
+    fetch,
+    jobs,
     cur_ref,
     wr_ref,
     wd_ref,
@@ -1034,32 +1665,17 @@
     bias2_ref,
     gain3_ref,
     bias3_ref,
-    out_ref,
-    ext_out_ref,
-    full_ref,
-    normed1_ref,
-    inverse1_ref,
-    normed2_ref,
-    inverse2_ref,
-    normed3_ref,
-    inverse3_ref,
-    pre1_ref,
-    pre3_ref,
-    ext_ref,
-    z_ref,
-    gath_ref,
-    stat1_ref,
-    stat2_ref,
-    stat3_ref,
-    term1_ref,
-    term3_ref,
-    stat_send,
-    stat_recv,
-    halo_send,
-    halo_recv,
-    part_send,
-    part_recv,
+    *refs,
 ):
+    if fetch:
+        raw_r, raw_e, *refs = refs
+    out_ref, ext_out_ref, full_ref, normed1_ref, inverse1_ref, normed2_ref, inverse2_ref = refs[:7]
+    normed3_ref, inverse3_ref = refs[7:9]
+    refs = refs[9:]
+    if fetch:
+        full_r, full_e, *refs = refs
+    pre1_ref, pre3_ref, ext_ref, z_ref, gath_ref, stat1_ref, stat2_ref, stat3_ref = refs[:8]
+    term1_ref, term3_ref, stat_send, stat_recv, halo_send, halo_recv, part_send, part_recv = refs[8:16]
     pixels, feat = cur_ref.shape
     mid = normed1_ref.shape[1]
     wide = normed3_ref.shape[1]
@@ -1067,6 +1683,13 @@
     ch = lax.axis_index(CH)
     pixel_count = float(pixels * blocks)
     greet(blocks, parts)
+    for job in jobs:
+        job[0]()
+    if fetch:
+        start, spread, forward, finish = weights_job(
+            raw_r, raw_e, fetch, (full_r, full_e), refs[16:], blocks, parts
+        )
+        start()
 
     def terms(total, square):
         mean_value = total / pixel_count
@@ -1086,6 +1709,8 @@
         pre1_ref[part, :] = value * sigmoid(value)
         return state
 
+    if fetch:
+        spread()
     own_mid = pl.ds(pl.multiple_of(ch * mid, mid), mid)
     normed1_ref[...] = (pre1_ref[:, own_mid] - term1_ref[0:1, own_mid]) * term1_ref[1:2, own_mid]
     inverse1_ref[...] = term1_ref[1:2, own_mid]
@@ -1156,17 +1781,22 @@
 
     row_loop(pixels, 16, last, 0)
     own_wide = pl.ds(pl.multiple_of(ch * wide, wide), wide)
+    if fetch:
+        for array in range(2):
+            forward(array)
+    for job in jobs:
+        job[1]()
     normed3_ref[...] = (pre3_ref[:, own_wide] - term3_ref[0:1, own_wide]) * term3_ref[1:2, own_wide]
     inverse3_ref[...] = term3_ref[1:2, own_wide]
-
-
-def trunk_params(key):
-    return pltpu.CompilerParams(
-        vmem_limit_bytes=60 * 2**20, collective_id=key, has_side_effects=True
-    )
-
-
-def trunk_forward(blocks, parts, cols, current, reduce_w, dilated_w, expand_w, mask, norms):
+    if fetch:
+        finish()
+    for job in jobs:
+        job[2]()
+
+
+def trunk_forward(
+    blocks, parts, cols, layer, jobs, current, reduce_w, dilated_w, expand_w, mask, norms, raw
+):
     pixels, feat = current.shape
     narrow = reduce_w.shape[0]
     mid, wide = narrow // parts, feat // parts
@@ -1174,8 +1804,15 @@
     f32, low = jnp.float32, jnp.bfloat16
     shape = jax.ShapeDtypeStruct
     rows = edge * 2 + pixels
-    return pl.pallas_call(
-        functools.partial(trunk_forward_kernel, blocks, parts),
+    inside = pl.BlockSpec(memory_space=pltpu.VMEM)
+    anywhere = pl.BlockSpec(memory_space=pl.ANY)
+    fetch = layer + 1 if raw else 0
+    return job_call(
+        functools.partial(trunk_forward_kernel, blocks, parts, fetch),
+        jobs,
+        blocks,
+        in_specs=[inside] * 11 + [anywhere] * len(raw),
+        out_specs=[inside] * 9 + [anywhere] * len(raw),
         out_shape=[
             shape((pixels, feat), low),
             shape((rows, narrow), low),
@@ -1186,7 +1823,8 @@
             shape((1, mid), f32),
             shape((pixels, wide), f32),
             shape((1, wide), f32),
-        ],
+        ]
+        + [shape((narrow, feat), low)] * len(raw),
         scratch_shapes=[
             pltpu.VMEM((pixels, narrow), f32),
             pltpu.VMEM((pixels, feat), f32),
@@ -1204,14 +1842,15 @@
             pltpu.SemaphoreType.DMA((2,)),
             pltpu.SemaphoreType.DMA((parts,)),
             pltpu.SemaphoreType.DMA((parts,)),
-        ],
-        compiler_params=trunk_params(1),
+        ]
+        + (weights_sems(blocks, parts) if raw else []),
+        compiler_params=comm_params(50 + layer),
         cost_estimate=pl.CostEstimate(
             flops=2 * pixels * (2 * narrow * feat + 9 * mid * narrow),
-            bytes_accessed=20 * 2**20,
+            bytes_accessed=150 * 2**20,
             transcendentals=0,
         ),
-    )(current, reduce_w, dilated_w, expand_w, mask, *norms)
+    )(current, reduce_w, dilated_w, expand_w, mask, *norms, *raw)
 
 
 def slope_of(values):
@@ -1251,6 +1890,7 @@
     gain1_ref,
     bias1_ref,
     wr_ref,
+    gate_ref,
     out_ref,
     expand_ref,
     dilated_ref,
@@ -1258,6 +1898,7 @@
     wide_ref,
     second_ref,
     first_ref,
+    gate_out,
     third_ref,
     grad_ref,
     im_ref,
@@ -1276,6 +1917,7 @@
     stat3_ref,
     stat2_ref,
     stat1_ref,
+    gates_ref,
     stat_send,
     stat_recv,
     halo_send,
@@ -1297,6 +1939,10 @@
     low = jnp.bfloat16
     greet(blocks, parts)
     own_wide = pl.ds(pl.multiple_of(ch * wide, wide), wide)
+    gates_ref[blk] = gate_ref[...]
+    wait_gates = send_slots(
+        lambda _: gates_ref.at[blk], gates_ref, stat_send.at[3], stat_recv.at[3], BLK, blocks
+    )
 
     def start(part, state):
         normed = normed3_ref[part, :]
@@ -1432,6 +2078,8 @@
     for part in range(parts):
         low_ref[:, part * mid : (part + 1) * mid] = gath_ref[part]
     out_ref[...] += jnp.dot(low_ref[...], wr_ref[:, own_wide], preferred_element_type=jnp.float32)
+    wait_gates()
+    gate_out[...] = sum_slots(gates_ref, blocks)
     wait_expand()
     expand_ref[...] = sum_slots(ex_recv_ref, blocks)
     wait_dilated()
@@ -1459,6 +2107,7 @@
             shape((2, wide), f32),
             shape((2, mid), f32),
             shape((2, mid), f32),
+            shape(operands[-1].shape, f32),
         ],
         scratch_shapes=[
             pltpu.VMEM((pixels, wide), low),
@@ -1479,8 +2128,9 @@
             pltpu.VMEM((blocks, 2, wide), f32),
             pltpu.VMEM((blocks, 2, mid), f32),
             pltpu.VMEM((blocks, 2, mid), f32),
-            pltpu.SemaphoreType.DMA((3, blocks)),
-            pltpu.SemaphoreType.DMA((3, blocks)),
+            pltpu.VMEM((blocks,) + operands[-1].shape, f32),
+            pltpu.SemaphoreType.DMA((4, blocks)),
+            pltpu.SemaphoreType.DMA((4, blocks)),
             pltpu.SemaphoreType.DMA((2,)),
             pltpu.SemaphoreType.DMA((2,)),
             pltpu.SemaphoreType.DMA((3, parts)),
@@ -1488,22 +2138,15 @@
             pltpu.SemaphoreType.DMA((3, blocks)),
             pltpu.SemaphoreType.DMA((3, blocks)),
         ],
-        compiler_params=trunk_params(2),
+        compiler_params=comm_params(2),
         cost_estimate=pl.CostEstimate(
             flops=4 * pixels * (2 * narrow * wide + 9 * mid * narrow),
-            bytes_accessed=20 * 2**20,
+            bytes_accessed=200 * 2**20,
             transcendentals=0,
         ),
     )(*operands)
 
 
-def neighbour_rows(low_part, high_part):
-    count = lax.axis_size(BLK)
-    forward = [(i, i + 1) for i in range(count - 1)]
-    backward = [(target, source) for source, target in forward]
-    return lax.ppermute(low_part, BLK, forward), lax.ppermute(high_part, BLK, backward)
-
-
 def gather_parts(values):
     return lax.all_gather(values, CH, axis=0, tiled=False)
 
@@ -1514,49 +2157,6 @@
 
 def own_slice(values, size, axis):
     return lax.dynamic_slice_in_dim(values, lax.axis_index(CH) * size, size, axis)
-
-
-def gather_weights(weights, axis):
-    blocks = lax.axis_size(BLK)
-    parts = lax.axis_size(CH)
-    other = 3 - axis
-    size = weights.shape[other] // blocks
-    mine = lax.dynamic_slice_in_dim(weights, lax.axis_index(BLK) * size, size, other)
-    everything = lax.all_gather(mine, (BLK, CH), axis=0, tiled=False)
-    everything = everything.reshape((blocks, parts) + mine.shape)
-    layers = weights.shape[0]
-    if axis == 1:
-        return everything.transpose(2, 1, 3, 0, 4).reshape(
-            layers, parts * weights.shape[1], weights.shape[2]
-        )
-    return everything.transpose(2, 0, 3, 1, 4).reshape(
-        layers, weights.shape[1], parts * weights.shape[2]
-    )
-
-
-def canvas_masks(canvas_ids, dilation):
-    rows, cols = canvas_ids.shape
-    padded = jnp.pad(canvas_ids, 2, constant_values=-1)
-    result = []
-    for row_step, col_step in tap_offsets:
-        top = 2 + row_step * dilation
-        left = 2 + col_step * dilation
-        result.append(padded[top : top + rows, left : left + cols] == canvas_ids)
-    return jnp.stack(result).astype(jnp.float32)
-
-
-def spread(mask):
-    taps, rows, cols = mask.shape
-    return jnp.broadcast_to(mask.reshape(taps, rows * cols, 1), (taps, rows * cols, lanes))
-
-
-def mask_set(canvas_ids, row_count, dilation):
-    everything = canvas_masks(canvas_ids, dilation)
-    own = lax.dynamic_slice_in_dim(everything, lax.axis_index(BLK) * row_count, row_count, 1)
-    turned = jnp.stack(
-        [jnp.roll(own[tap], step[1] * dilation, axis=1) for tap, step in enumerate(tap_offsets)]
-    )
-    return everything, own, spread(turned), spread(own[::-1])
 
 
 def shards(
@@ -1580,36 +2180,53 @@
     pixels = rows * cols
     blocks = lax.axis_size(BLK)
     parts = lax.axis_size(CH)
-    pixel_count = float(pixels * blocks)
     layers = w_reduce.shape[0]
     mid = w_reduce.shape[1]
     feat = wide * parts
     narrow = mid * parts
     low = jnp.bfloat16
-    all_masks, _, forward_one, backward_one = mask_set(canvas_ids, rows, 1)
-    _, _, forward_two, backward_two = mask_set(canvas_ids, rows, 2)
-    chunk_masks = all_masks.reshape(9, blocks, pixels).transpose(1, 0, 2)
-
-    reduce_full = gather_weights(w_reduce, 1)
-    expand_full = gather_weights(w_expand, 2)
-    small = jnp.concatenate(
-        [norm_gain[:, 0], norm_bias[:, 0]], axis=0
-    )
-    small_full = gather_parts(small).transpose(1, 0, 2).reshape(2, layers, narrow)
-    wide_full = (
-        gather_parts(jnp.concatenate([wide_gain, wide_bias], axis=0))
-        .transpose(1, 0, 2)
-        .reshape(2, layers, feat)
-    )
-    current = gather_parts(features_in.reshape(pixels, wide)).transpose(1, 0, 2).reshape(pixels, feat)
     dilated_t = w_dilated.transpose(0, 2, 1, 3)
     heads_t = w_heads.transpose(0, 1, 3, 2, 4)
     messages_t = w_messages.transpose(0, 1, 3, 2, 4)
+    current, *rest = prologue(
+        blocks,
+        parts,
+        features_in.reshape(pixels, wide),
+        w_reduce,
+        w_expand,
+        jnp.concatenate([norm_gain[:, 0], norm_bias[:, 0]], axis=0),
+        jnp.concatenate([wide_gain, wide_bias], axis=0),
+        canvas_ids,
+    )
+    reduce_full, expand_full = [rest[0]], [rest[1]]
+    narrow_all, wide_all, forward_one, backward_one, forward_two, backward_two, mask_cols = rest[2:]
+    narrow_all = narrow_all.transpose(1, 0, 2).reshape(2, layers, narrow)
+    wide_all = wide_all.transpose(1, 0, 2).reshape(2, layers, feat)
 
     kept = []
-    task_list = []
     for layer in range(layers):
         keep = types.SimpleNamespace(input=current)
+        results, swapped = trunk_forward(
+            blocks,
+            parts,
+            cols,
+            layer,
+            [(swap_kind, current)] if layer else [],
+            current,
+            reduce_full[layer],
+            dilated_t[layer],
+            expand_full[layer],
+            forward_two,
+            (
+                narrow_all[0, layer][None],
+                narrow_all[1, layer][None],
+                norm_gain[layer, 1][None],
+                norm_bias[layer, 1][None],
+                wide_all[0, layer][None],
+                wide_all[1, layer][None],
+            ),
+            (w_reduce, w_expand) if layer + 1 < layers else (),
+        )
         (
             current,
             keep.first_ext,
@@ -1620,86 +2237,96 @@
             keep.inverse2,
             keep.normed3,
             keep.inverse3,
-        ) = trunk_forward(
-            blocks,
-            parts,
-            cols,
-            current,
-            reduce_full[layer],
-            dilated_t[layer],
-            expand_full[layer],
-            forward_two,
-            (
-                small_full[0, layer][None],
-                small_full[1, layer][None],
-                norm_gain[layer, 1][None],
-                norm_bias[layer, 1][None],
-                wide_full[0, layer][None],
-                wide_full[1, layer][None],
-            ),
-        )
+            *fetched,
+        ) = results
+        if fetched:
+            reduce_full.append(fetched[0])
+            expand_full.append(fetched[1])
+        if layer:
+            kept[-1].values = swapped[0]
+            current, kept[-1].features = lax.optimization_barrier((current, kept[-1].features))
         keep.output = current
+        keep.heads_pre, features = heads_forward(blocks, layer, cols, current, heads_t, forward_one)
+        current, features = lax.optimization_barrier((current, features))
+        keep.features = gather_parts(features)
         kept.append(keep)
     output = own_slice(current, wide, 1).reshape(rows, cols, wide)
 
-    partial_heads = []
-    gate_grads = []
     for layer in range(layers):
         keep = kept[layer]
-        out_full = keep.output
-        before, after = neighbour_rows(out_full[-cols:], out_full[:cols])
-        extended = jnp.concatenate([before, out_full, after], axis=0)
-        heads_pre, features = heads_forward(extended, heads_t[layer], forward_one)
-        keep.heads_pre = heads_pre
-        features_all = gather_parts(features)
-        before, after = neighbour_rows(features_all[:, :, -cols:], features_all[:, :, :cols])
-        messages = messages_forward(before, features_all, after, messages_t[layer], forward_one)
-        values = features.astype(jnp.float32)
-        maps = [values[0], None, None, values[3]]
-        cotangents = [
-            task_cotangents[layer, 0].reshape(pixels, mid).astype(jnp.float32),
-            None,
-            None,
-            task_cotangents[layer, 1].reshape(pixels, mid).astype(jnp.float32),
-        ]
-        head_grads = [cotangents[0], jnp.zeros_like(cotangents[0]), jnp.zeros_like(cotangents[0]), cotangents[3]]
-        message_grads, gain_terms, bias_terms = [], [], []
-        for pair, (source, target) in enumerate(message_pairs):
-            gate = jax.nn.sigmoid(gate_gain[layer, pair] * values[target] + gate_bias[layer, pair])
-            maps[target] = maps[target] + gate * messages[pair]
-            message_grads.append((cotangents[target] * gate).astype(low))
-            slope = cotangents[target] * messages[pair] * gate * (1.0 - gate)
-            gain_terms.append(jnp.sum(slope * values[target], axis=0))
-            bias_terms.append(jnp.sum(slope, axis=0))
-            head_grads[target] = head_grads[target] + slope * gate_gain[layer, pair]
-        task_list.append(jnp.stack([maps[0], maps[3]]).astype(low).reshape(2, rows, cols, mid))
-        gate_grads.append(jnp.stack([jnp.stack(gain_terms), jnp.stack(bias_terms)]))
-        message_low = jnp.stack(message_grads)
-        before, after = neighbour_rows(message_low[:, -cols:], message_low[:, :cols])
-        source_sums = reduce_parts(
-            messages_backward(before, message_low, after, messages_t[layer], backward_one, parts)
-        )
-        chans = narrow // blocks
-        feature_cols = features_all.transpose(1, 0, 3, 2).reshape(4, blocks, chans, pixels)
-        feature_cols = feature_cols.transpose(1, 0, 2, 3)
-        feature_cols = lax.all_to_all(feature_cols, BLK, 0, 0)
-        grads_all = lax.all_gather(message_low, BLK, axis=0, tiled=False)
-        keep.messages_grad = messages_weight(feature_cols, grads_all, chunk_masks, cols)
-        head_total = jnp.stack(head_grads) + source_sums.astype(jnp.float32)
-        heads_low = (head_total * silu_slope(heads_pre)).astype(low)
-        before, after = neighbour_rows(heads_low[:, -cols:], heads_low[:, :cols])
-        partial_heads.append(
-            reduce_parts(
-                heads_backward(before, heads_low, after, heads_t[layer], backward_one, parts)
+        jobs = [(gather_kind, keep_before.message_low) for keep_before in kept[:layer][-1:]]
+        if layer == 0:
+            jobs = [(swap_kind, kept[-1].output)]
+        results, moved = messages_both(
+            blocks,
+            layer,
+            jobs,
+            cols,
+            keep.features,
+            messages_t,
+            task_cotangents[layer].reshape(2, pixels, mid),
+            gate_gain,
+            gate_bias,
+            forward_one,
+            backward_one,
+        )
+        keep.maps, keep.local, keep.gate_sums, keep.message_low, partial, keep.message_values = results
+        if layer == 0:
+            kept[-1].values = moved[0]
+        else:
+            kept[layer - 1].message_all = moved[0]
+        keep.source_sums = reduce_parts(partial)
+
+    def heads_low_of(keep):
+        sums = keep.source_sums.astype(jnp.float32)
+        total = jnp.stack([sums[0] + keep.local[0], sums[1], sums[2], sums[3] + keep.local[1]])
+        return (total * silu_slope(keep.heads_pre)).astype(low)
+
+    def messages_weight(layer, jobs):
+        keep = kept[layer]
+        (keep.messages_grad,), moved = weight_gradient(
+            30 + layer,
+            blocks,
+            jobs,
+            group_pairs,
+            messages_store,
+            (6, 9, narrow // blocks, mid),
+            keep.message_values,
+            keep.message_all,
+            mask_cols,
+        )
+        return moved
+
+    def heads_weight(layer):
+        keep = kept[layer]
+        (keep.heads_grad,), _ = weight_gradient(
+            40 + layer,
+            blocks,
+            [],
+            (tuple(range(4)),),
+            heads_store,
+            (4, 9, feat // blocks, mid),
+            keep.values[:, None],
+            keep.heads_all,
+            mask_cols,
+        )
+
+    for layer in range(layers):
+        keep = kept[layer]
+        keep.heads_low = heads_low_of(keep)
+        jobs = [(gather_kind, kept[-1].message_low)] if layer == 0 else []
+        (partial,), moved = heads_backward(
+            blocks, layer, jobs, cols, keep.heads_low, heads_t, backward_one, parts
+        )
+        if layer == 0:
+            kept[-1].message_all = moved[0]
+        keep.heads_partial = reduce_parts(partial)
+        (keep.heads_all,) = messages_weight(layer, [(gather_kind, keep.heads_low)])
+        if layer + 1 < layers:
+            kept[layer + 1].source_sums, keep.messages_grad = lax.optimization_barrier(
+                (kept[layer + 1].source_sums, keep.messages_grad)
             )
-        )
-        chans = feat // blocks
-        value_cols = out_full.T.reshape(blocks, chans, pixels)
-        value_cols = lax.all_to_all(value_cols, BLK, 0, 0)
-        grads_all = lax.all_gather(heads_low, BLK, axis=0, tiled=False)
-        keep.heads_grad = heads_weight(value_cols, grads_all, chunk_masks, cols)
-
-    gate_sums = lax.psum(jnp.stack(gate_grads), BLK)
+    heads_weight(0)
 
     upstream = output_cotangent.reshape(pixels, wide).astype(jnp.float32)
     for layer in reversed(range(layers)):
@@ -1712,12 +2339,13 @@
             keep.wide_sums,
             keep.second_sums,
             keep.first_sums,
+            keep.gates,
         ) = trunk_backward(
             blocks,
             parts,
             (
                 upstream,
-                partial_heads[layer],
+                keep.heads_partial,
                 keep.input,
                 keep.normed3,
                 keep.inverse3,
@@ -1738,17 +2366,22 @@
                 norm_gain[layer, 0][None],
                 norm_bias[layer, 0][None],
                 reduce_full[layer],
+                keep.gate_sums,
             ),
         )
+
+    for layer in range(1, layers):
+        heads_weight(layer)
 
     def stacked(of):
         return jnp.stack([of(keep) for keep in kept])
 
     narrow_sums = stacked(lambda keep: jnp.stack([keep.first_sums, keep.second_sums]))
     wide_sums = stacked(lambda keep: keep.wide_sums)
+    gate_sums = stacked(lambda keep: keep.gates.reshape(2, 6, mid))
     return (
         output,
-        jnp.stack(task_list),
+        stacked(lambda keep: keep.maps.reshape(2, rows, cols, mid)),
         upstream.reshape(rows, cols, wide),
         stacked(lambda keep: keep.reduce_grad),
         stacked(lambda keep: keep.dilated_grad),
@@ -1766,7 +2399,9 @@
 
 def route(*args):
     mid = args[1].shape[1]
-    if mid % lanes == 0 and args[0].shape[1] % lanes == 0:
+    blocks, parts = lax.axis_size(BLK), lax.axis_size(CH)
+    whole_tiles = args[1].shape[0] == 2 and mid % lanes == 0 and args[0].shape[1] == lanes and parts >= 2
+    if whole_tiles and blocks % 2 == 0 and 2 * mid * parts == lanes * blocks:
         return shards(*args)
     return plain_shards(*args)
 

time: 996 us -> 804 us (0.81)
  Pallas kernels: 422 us -> 720 us
  waiting for transfers between devices: 190 us -> 11.1 us
  local copies, waits for them, and re-layouts: 137 us -> 22.1 us
  starting transfers between devices: 84 us -> 0.42 us
  blocking collectives: 74.6 us -> 0 us
  other arithmetic: 57 us -> 27.5 us
    pallas_call x14 -> x13, Pallas kernels: 281 us -> 593 us  [the longest x10 494 us: call(): pl.pallas_call(wrapped, in_specs=list(in_specs) + [anywhere] * count, out...]
    all_gather x6 -> x0, waiting for transfers between devices: 94 us -> none  [the longest x2 94 us: gather_weights(): everything = lax.all_gather(mine, (BLK, CH), axis=0, tiled=False)]
    ppermute x16 -> x0, starting transfers between devices: 64.1 us -> none  [the longest x8 53 us: neighbour_rows(): lax.ppermute(low_part, BLK, forward)]
    psum x1 -> x0, blocking collectives: 47.6 us -> none  [shards(): gate_sums = lax.psum(jnp.stack(gate_grads), BLK)]
    squeeze x4 -> x0, local copies, waits for them, and re-layouts: 36.9 us -> none  [the longest x1 26.3 us: shards(): heads_pre, features = heads_forward(extended, heads_t[layer], forward_one)]
    reduce_scatter x4, waiting for transfers between devices: 44.8 us -> 10.9 us  [reduce_parts(): return lax.psum_scatter(values, CH, scatter_dimension=0, tiled=False)]
    all_gather x2 -> x0, blocking collectives: 27 us -> none  [gather_parts(): return lax.all_gather(values, CH, axis=0, tiled=False)]
    all_to_all x4 -> x0, waiting for transfers between devices: 22.7 us -> none  [the longest x2 16.4 us: shards(): value_cols = lax.all_to_all(value_cols, BLK, 0, 0)]
  transfers between devices with their start and end apart: 33 -> 6, of which waited for: 12 -> 1; matrix products, arithmetic and copies ran while one was open for 16% -> 3% of each run, Pallas kernels for 28% -> 58%
where the time goes in v2:
time: 804 us; the launch traced here: 796 us
  Pallas kernels  720 us (90%)
  other arithmetic  27.5 us (3%)
  local copies, waits for them, and re-layouts  22.1 us (3%)
  between operations  14.8 us (2%)
  waiting for transfers between devices  11.1 us (1%)
    pallas_call x10, Pallas kernels, call(): pl.pallas_call(wrapped, in_specs=list(in_specs) + [anywhere] * count, out...  494 us
    pallas_call x2, Pallas kernels, trunk_backward(): pl.pallas_call(functools.partial(trunk_backward_kernel, blocks, parts), o...  127 us
    pallas_call x1, Pallas kernels, prologue(): pl.pallas_call(functools.partial(prologue_kernel, blocks, parts), in_spec...  60.1 us
    pallas_call x2, Pallas kernels, heads_forward(): pl.pallas_call(functools.partial(heads_forward_kernel, blocks), grid=(9,)...  38 us
    another operation x10, other arithmetic, stacked(): return jnp.stack([of(keep) for keep in kept])  20.4 us
  transfers between devices with their start and end apart: 6, of which 1 were waited for; matrix products, arithmetic and copies ran while one was open for 3% of the time, Pallas kernels for 58%

profile of v2, /device:TPU:0, one launch (start us, length us, event | category | flops | bytes accessed | tf_op | source)
XLA Modules:
  0.0 795.7 jit_solution(16287408873007725310)
XLA Ops:
  7.2 1.4 slice_bitcast_fusion.17
  8.7 3.2 slice_bitcast_fusion
  13.2 2.4 broadcast_in_dim.12.ids_ref
  15.6 60.1 %shard_map.254 = (bf16[512,2048]{1,0:T(8,128)(2,1)}, bf16[512,2048]{1,0:T(8,128)(2,1)}, bf16[512,2048]{1,0:T(8,128)(2,1)}, f32[4,4,128]{2,1,0:T(4,128)}, f32[4,4...) custom-call(bf16[512,512]{1,0:T(8,128)(2,1)} %bitcast.122, ...), custom_call_target="tpu_custom_call" | custom-call | flops 1000000 | bytes 100000000 | tf_op jit(solution)/shard_map/pallas_call | solution.py:885
  78.5 71.8 %shard_map.255 = (bf16[512,2048]{1,0:T(8,128)(2,1)}, bf16[1024,512]{1,0:T(8,128)(2,1)}, bf16[512,512]{1,0:T(8,128)(2,1)}, f32[512,128]{1,0:T(8,128)}, f32[1,128]...) custom-call(bf16[512,2048]{1,0:T(8,128)(2,1)} %get-tuple-element.93., ...), custom_call_target="tpu_custom_call" | custom-call | flops 2751463424 | bytes 157286400 | tf_op jit(solution)/shard_map/pallas_call | solution.py:607
  150.3 19.0 %shard_map.256 = (f32[4,512,128]{2,1,0:T(8,128)}, bf16[4,512,128]{2,1,0:T(8,128)(2,1)}) custom-call(bf16[512,2048]{1,0:T(8,128)(2,1)} %get-tuple-element.102.main_ref.refs_0_.refs_11_.cur_ref, bf16[2,4,9,128,2048]{4,3,2,1,0:T(8,128)(2,1)} %bitcast.110, f32[9,512,128]{2,1,0:T(8,128)} %get-tuple-element.100.mask_ref.refs_5_), custom_call_target="tpu_custom_call" | custom-call | flops 9663676416 | bytes 18874368 | tf_op jit(solution)/shard_map/pallas_call | solution.py:1059
  169.4 74.7 %shard_map.257 = (bf16[512,2048]{1,0:T(8,128)(2,1)}, bf16[1024,512]{1,0:T(8,128)(2,1)}, bf16[512,512]{1,0:T(8,128)(2,1)}, f32[512,128]{1,0:T(8,128)}, f32[1,128]...) custom-call(bf16[512,2048]{1,0:T(8,128)(2,1)} %get-tuple-element.102, ...), custom_call_target="tpu_custom_call" | custom-call | flops 2751463424 | bytes 157286400 | tf_op jit(solution)/shard_map/pallas_call | solution.py:607
  244.1 19.0 %shard_map.258 = (f32[4,512,128]{2,1,0:T(8,128)}, bf16[4,512,128]{2,1,0:T(8,128)(2,1)}) custom-call(bf16[512,2048]{1,0:T(8,128)(2,1)} %get-tuple-element.109.main_ref.refs_7_, bf16[2,4,9,128,2048]{4,3,2,1,0:T(8,128)(2,1)} %bitcast.111, f32[9,512,128]{2,1,0:T(8,128)} %get-tuple-element.100.mask_ref.refs_5_), custom_call_target="tpu_custom_call" | custom-call | flops 9663676416 | bytes 18874368 | tf_op jit(solution)/shard_map/pallas_call | solution.py:1059
  265.2 70.0 %shard_map.259 = (bf16[2,512,128]{2,1,0:T(8,128)(2,1)}, f32[2,512,128]{2,1,0:T(8,128)}, f32[12,128]{1,0:T(8,128)}, bf16[6,512,128]{2,1,0:T(8,128)(2,1)}, bf16[4,...) custom-call(bf16[4,4,512,128]{3,2,1,0:T(8,128)(2,1)} %bitcast.155, ...), custom_call_target="tpu_custom_call" | custom-call | flops 7247757312 | bytes 7077888 | tf_op jit(solution)/shard_map/pallas_call | solution.py:607
  335.4 86.2 %shard_map.260 = (bf16[2,512,128]{2,1,0:T(8,128)(2,1)}, f32[2,512,128]{2,1,0:T(8,128)}, f32[12,128]{1,0:T(8,128)}, bf16[6,512,128]{2,1,0:T(8,128)(2,1)}, bf16[4,...) custom-call(bf16[4,4,512,128]{3,2,1,0:T(8,128)(2,1)} %bitcast.156, ...), custom_call_target="tpu_custom_call" | custom-call | flops 7247757312 | bytes 7077888 | tf_op jit(solution)/shard_map/pallas_call | solution.py:607
  421.7 1.2 convert_element_type.20
  423.1 1.2 fusion.refs_5_.refs_0_
  424.3 32.7 %shard_map.261 = (f32[6,9,64,128]{3,2,1,0:T(8,128)}, bf16[8,4,512,128]{3,2,1,0:T(8,128)(2,1)}) custom-call(bf16[8,2,512,128]{3,2,1,0:T(8,128)(2,1)} %get-tuple-element.117.refs_0_.refs_1_.refs_2_, bf16[8,2,512,128]{3,2,1,0:T(8,128)(2,1)} %get-tuple-element.117.refs_0_.refs_1_.refs_2_, bf16[8,2,512,128]{3,2,1,0:T(8,128)(2,1)} %get-tuple-element.117.refs_0_.refs_1_.refs_2_, ...), custom_call_target="tpu_custom_call" | custom-call | flops 7247757312 | bytes 10000000 | tf_op jit(solution)/shard_map/pallas_call | solution.py:607
  457.1 10.9 %reduce-scatter.5.cloned.1.call-done = bf16[1,4,512,128]{3,2,1,0:T(8,128)(2,1)} async-done(((bf16[4,4,512,128]{3,2,1,0:T(8,128)(2,1)}), bf16[1,4,512,128]{3,2,1,0:T(8,128)(2,1)}) %reduce-scatter.5.cloned.1.call-update) | async-done | bytes 524304 | tf_op jit(solution)/shard_map/reduce_scatter | solution.py:2155
  468.0 1.1 slice.212
  469.1 1.1 convert_element_type.22
  470.3 1.2 fusion.1.refs_0_.refs_5_
  471.5 19.3 %shard_map.262 = bf16[4,512,512]{2,1,0:T(8,128)(2,1)} custom-call(bf16[4,512,128]{2,1,0:T(8,128)(2,1)} %fusion.1.refs_0_.refs_5_, bf16[2,4,9,128,2048]{4,3,2,1,0:T(8,128)(2,1)} %bitcast.112, f32[9,512,128]{2,1,0:T(8,128)} %get-tuple-element.111.refs_6_.refs_2_), custom_call_target="tpu_custom_call" | custom-call | flops 9663676416 | bytes 18874368 | tf_op jit(solution)/shard_map/pallas_call | solution.py:607
  491.1 52.6 %shard_map.264 = (bf16[4,512,512]{2,1,0:T(8,128)(2,1)}, bf16[8,6,512,128]{3,2,1,0:T(8,128)(2,1)}) custom-call(bf16[4,512,128]{2,1,0:T(8,128)(2,1)} %fusion.refs_5_.refs_0_, bf16[2,4,9,128,2048]{4,3,2,1,0:T(8,128)(2,1)} %bitcast.113, f32[9,512,128]{2,1,0:T(8,128)} %get-tuple-element.111.refs_6_.refs_2_, bf16[6,512,128]{2,1,0:T(8,128)(2,1)} %get-tuple-element.138.refs_3_), custom_call_target="tpu_custom_call" | custom-call | flops 9663676416 | bytes 18874368 | tf_op jit(solution)/shard_map/pallas_call | solution.py:607
  544.9 1.1 slice_bitcast_fusion.3
  545.9 1.1 bitcast_convert_fusion.up_ref
  547.1 1.9 constant_dynamic-slice_fusion
  549.8 27.2 %shard_map.266 = f32[4,9,256,128]{3,2,1,0:T(8,128)} custom-call(bf16[8,1,512,256]{3,2,1,0:T(8,128)(2,1)} %bitcast.152, bf16[8,1,512,256]{3,2,1,0:T(8,128)(2,1)} %bitcast.153, bf16[8,1,512,256]{3,2,1,0:T(8,128)(2,1)} %bitcast.154, bf16[8,4,512,128]{3,2,1,0:T(8,128)(2,1)} %get-tuple-element.157.refs_3_, f32[4096,128]{1,0:T(8,128)} %get-tuple-element.119.refs_4_), custom_call_target="tpu_custom_call" | custom-call | flops 9663676416 | bytes 10000000 | tf_op jit(solution)/shard_map/pallas_call | solution.py:607
  577.0 32.5 %shard_map.267 = (f32[6,9,64,128]{3,2,1,0:T(8,128)}, bf16[8,4,512,128]{3,2,1,0:T(8,128)(2,1)}) custom-call(bf16[8,2,512,128]{3,2,1,0:T(8,128)(2,1)} %get-tuple-element.159.refs_0_.refs_1_.refs_2_, bf16[8,2,512,128]{3,2,1,0:T(8,128)(2,1)} %get-tuple-element.159.refs_0_.refs_1_.refs_2_, bf16[8,2,512,128]{3,2,1,0:T(8,128)(2,1)} %get-tuple-element.159.refs_0_.refs_1_.refs_2_, ...), custom_call_target="tpu_custom_call" | custom-call | flops 7247757312 | bytes 10000000 | tf_op jit(solution)/shard_map/pallas_call | solution.py:607
  609.5 3.7 pad_maximum_fusion.1
  613.2 27.4 %shard_map.268 = f32[4,9,256,128]{3,2,1,0:T(8,128)} custom-call(bf16[8,1,512,256]{3,2,1,0:T(8,128)(2,1)} %bitcast.157, bf16[8,1,512,256]{3,2,1,0:T(8,128)(2,1)} %bitcast.158, bf16[8,1,512,256]{3,2,1,0:T(8,128)(2,1)} %bitcast.159, bf16[8,4,512,128]{3,2,1,0:T(8,128)(2,1)} %get-tuple-element.161.refs_3_, f32[4096,128]{1,0:T(8,128)} %get-tuple-element.119.refs_4_), custom_call_target="tpu_custom_call" | custom-call | flops 9663676416 | bytes 10000000 | tf_op jit(solution)/shard_map/pallas_call | solution.py:607
  640.6 8.7 %pad_maximum_fusion = f32[2,4,9,256,128]{4,3,2,1,0:T(8,128)} fusion(f32[1,4,9,256,128]{4,3,2,1,0:T(8,128)} %bitcast.115, f32[1,4,9,256,128]{4,3,2,1,0:T(8,128)} %bitcast.114), kind=kLoop, calls=%fused_computation | loop fusion | flops 2359296 | bytes 18874368 | tf_op jit(solution)/shard_map/stack | solution.py:2377
  649.3 62.0 %shard_map.263 = (f32[512,512]{1,0:T(8,128)}, f32[64,512]{1,0:T(8,128)}, f32[9,64,128]{2,1,0:T(8,128)}, f32[256,128]{1,0:T(8,128)}, f32[2,512]{1,0:T(2,128)}, /*...) custom-call(f32[512,512]{1,0:T(8,128)} %bitcast_convert_fusion.up_ref, bf16[512,512]{1,0:T(8,128)(2,1)} %bitcast.124, ...), custom_call_target="tpu_custom_call" | custom-call | flops 2281701376 | bytes 209715200 | tf_op jit(solution)/shard_map/pallas_call | solution.py:2100
  712.0 65.4 %shard_map.265 = (f32[512,512]{1,0:T(8,128)}, f32[64,512]{1,0:T(8,128)}, f32[9,64,128]{2,1,0:T(8,128)}, f32[256,128]{1,0:T(8,128)}, f32[2,512]{1,0:T(2,128)}, /*...) custom-call(f32[512,512]{1,0:T(8,128)} %get-tuple-element.137.up_ref, bf16[512,512]{1,0:T(8,128)(2,1)} %bitcast.123, ...), custom_call_target="tpu_custom_call" | custom-call | flops 2281701376 | bytes 209715200 | tf_op jit(solution)/shard_map/pallas_call | solution.py:2100
  781.3 1.6 pad_maximum_fusion.4
  784.2 1.6 pad_maximum_fusion.5
  785.8 1.8 pad_maximum_fusion.2
  (96 shorter events, 15.9 us)
Async XLA Ops:
  7.2 236.9 %all-gather.5.cloned.1.call-start = ((), (), s32[]{:S(2)}) async-start(), calls=%async_computation.8 | async-start | bytes 2621440 | tf_op jit(solution)/shard_map/all_gather | solution.py:2151
  8.6 3.3 slice-start
  8.6 3.3 slice-start.1
  8.6 3.9 copy-start.15
  8.7 3.8 copy-start.16
  8.7 4.4 copy-start.14
  169.3 166.1 %all-gather.7.cloned.1.call-start = ((), (), s32[]{:S(2)}) async-start(), calls=%async_computation.9 | async-start | bytes 2621440 | tf_op jit(solution)/shard_map/all_gather | solution.py:2151
  244.1 19.1 %copy-start.17 = (f32[2,6,128]{2,0,1:T(2,128)S(1)}, f32[2,6,128]{2,0,1:T(2,128)}, u32[]{:S(2)}) copy-start(f32[2,6,128]{2,0,1:T(2,128)} %param.25) | copy-start | bytes 18436
  244.1 19.7 %copy-start.18 = (f32[2,6,128]{2,0,1:T(2,128)S(1)}, f32[2,6,128]{2,0,1:T(2,128)}, u32[]{:S(2)}) copy-start(f32[2,6,128]{2,0,1:T(2,128)} %param.26) | copy-start | bytes 18436
  244.1 20.3 %copy-start.8 = (bf16[2,2,4,128,128]{4,3,2,1,0:T(8,128)(2,1)S(1)}, bf16[2,2,4,128,128]{4,3,2,1,0:T(8,128)(2,1)}, u32[]{:S(2)}) copy-start(bf16[2,2,4,128,128]{4,3,2,1,0:T(8,128)(2,1)} %param.29) | copy-start | bytes 1572868
  263.2 158.5 %reduce-scatter.7.cloned.1.call-start = ((), (), s32[]{:S(2)}) async-start(), calls=%async_computation.5 | async-start | bytes 2621440 | tf_op jit(solution)/shard_map/reduce_scatter | solution.py:2155
  335.3 132.7 %reduce-scatter.5.cloned.1.call-start = ((), (), s32[]{:S(2)}) async-start(), calls=%async_computation.4 | async-start | bytes 2621440 | tf_op jit(solution)/shard_map/reduce_scatter | solution.py:2155
  421.6 1.4 copy-start.6
  421.6 1.5 copy-start.2
  421.6 227.7 %reduce-scatter.9.cloned.1.call-start = ((), (), s32[]{:S(2)}) async-start(), calls=%async_computation.6 | async-start | bytes 2621440 | tf_op jit(solution)/shard_map/reduce_scatter | solution.py:2155
  457.1 13.1 %copy-start.7 = (f32[2,512,128]{2,1,0:T(8,128)S(1)}, f32[2,512,128]{2,1,0:T(8,128)}, u32[]{:S(2)}) copy-start(f32[2,512,128]{2,1,0:T(8,128)} %get-tuple-element.125) | copy-start | bytes 1572868
  468.0 2.3 copy-start.3
  490.8 221.1 %reduce-scatter.11.cloned.1.call-start = ((), (), s32[]{:S(2)}) async-start(), calls=%async_computation.7 | async-start | bytes 2621440 | tf_op jit(solution)/shard_map/reduce_scatter | solution.py:2155
  543.6 1.2 copy-start
  543.6 2.3 copy-start.5
  544.9 4.1 copy-start.10
  544.9 4.1 copy-start.11
  577.0 32.5 %copy-start.1 = (f32[6,9,64,128]{3,2,1,0:T(8,128)S(1)}, f32[6,9,64,128]{3,2,1,0:T(8,128)}, u32[]{:S(2)}) copy-start(f32[6,9,64,128]{3,2,1,0:T(8,128)} %get-tuple-element.162) | copy-start | bytes 5308420
  712.0 65.4 %copy-start.19 = (f32[2,512]{1,0:T(2,128)S(1)}, f32[2,512]{1,0:T(2,128)}, u32[]{:S(2)}) copy-start(f32[2,512]{1,0:T(2,128)} %get-tuple-element.169) | copy-start | bytes 12292
  712.0 69.3 %copy-start.20 = (f32[2,128]{1,0:T(2,128)S(1)}, f32[2,128]{1,0:T(2,128)}, u32[]{:S(2)}) copy-start(f32[2,128]{1,0:T(2,128)} %get-tuple-element.167) | copy-start | bytes 3076
  712.0 69.3 %copy-start.21 = (f32[2,128]{1,0:T(2,128)S(1)}, f32[2,128]{1,0:T(2,128)}, u32[]{:S(2)}) copy-start(f32[2,128]{1,0:T(2,128)} %get-tuple-element.166) | copy-start | bytes 3076
  712.0 69.3 %copy-start.13 = (f32[256,128]{1,0:T(8,128)S(1)}, f32[256,128]{1,0:T(8,128)}, u32[]{:S(2)}) copy-start(f32[256,128]{1,0:T(8,128)} %get-tuple-element.151) | copy-start | bytes 393220
  712.0 72.2 %copy-start.12 = (f32[64,512]{1,0:T(8,128)S(1)}, f32[64,512]{1,0:T(8,128)}, u32[]{:S(2)}) copy-start(f32[64,512]{1,0:T(8,128)} %get-tuple-element.155) | copy-start | bytes 393220
  712.0 73.8 %copy-start.9 = (f32[9,64,128]{2,1,0:T(8,128)S(1)}, f32[9,64,128]{2,1,0:T(8,128)}, u32[]{:S(2)}) copy-start(f32[9,64,128]{2,1,0:T(8,128)} %get-tuple-element.153) | copy-start | bytes 884740
  777.4 10.3 %copy-start.4 = (f32[512,512]{1,0:T(8,128)S(1)}, f32[512,512]{1,0:T(8,128)}, u32[]{:S(2)}) copy-start(f32[512,512]{1,0:T(8,128)} %get-tuple-element.149) | copy-start | bytes 3145732
Sparse Core Ops, SparseCore 0:
  169.4 53.6 all-gather.4
  263.3 56.5 all-gather.6
  335.4 49.8 reduce-scatter.6
  421.7 46.2 reduce-scatter.4
  491.0 46.2 reduce-scatter.8
  543.8 42.6 reduce-scatter.10

commit v3 on v2

--- a/solution.py
+++ b/solution.py
@@ -459,8 +459,18 @@
     return 1.0 / (1.0 + jnp.exp(-values))
 
 
+def masked(values, bits, place):
+    taken = (bits & (1 << place)) != 0
+    width = values.shape[1]
+    parts = [
+        jnp.where(taken, values[:, start : start + lanes], 0.0) for start in range(0, width, lanes)
+    ]
+    return parts[0] if len(parts) == 1 else jnp.concatenate(parts, axis=1)
+
+
 MESH = pl.DeviceIdType.MESH
 groups = ((1, 2), (0, 3))
+targets = (0, 3)
 group_pairs = ((0, 4, 1, 5), (3, 2))
 
 
@@ -567,13 +577,39 @@
     return start, lambda: None, finish
 
 
-job_kinds = (gather_job, swap_job)
-gather_kind, swap_kind = 0, 1
+def slot_job(source, target, sems, blocks):
+    slot_send, slot_recv, _, local_sem = sems
+    me = lax.axis_index(BLK)
+    own = pltpu.make_async_copy(source.at[me], target.at[me], local_sem.at[0])
+
+    def copy(step, peer, slot):
+        return remote(
+            source.at[peer], target.at[slot], slot_send.at[step], slot_recv.at[slot], BLK, peer
+        )
+
+    def start():
+        for step, peer in enumerate(others(BLK, blocks)):
+            copy(step, peer, me).start()
+        own.start()
+
+    def finish():
+        for step, peer in enumerate(others(BLK, blocks)):
+            copy(step, peer, peer).wait_recv()
+            copy(step, peer, me).wait_send()
+        own.wait()
+
+    return start, lambda: None, finish
+
+
+job_kinds = (gather_job, swap_job, slot_job)
+gather_kind, swap_kind, slot_kind = 0, 1, 2
 
 
 def job_target(kind, source, blocks):
     if kind == gather_kind:
         return jax.ShapeDtypeStruct((blocks,) + source.shape, source.dtype)
+    if kind == slot_kind:
+        return jax.ShapeDtypeStruct(source.shape, source.dtype)
     return jax.ShapeDtypeStruct(
         (blocks, source.shape[0], source.shape[1] // blocks), source.dtype
     )
@@ -737,11 +773,8 @@
     full_e,
     narrow_out,
     wide_out,
-    f1_ref,
-    b1_ref,
-    f2_ref,
-    b2_ref,
-    cols_ref,
+    own_ref,
+    all_ref,
     line_send,
     line_recv,
     small_send,
@@ -822,32 +855,37 @@
             small_copy(place, step, peer, ch).start()
     spread()
 
-    rows = f1_ref.shape[1] // lanes
-    for f_ref, b_ref, reach in ((f1_ref, b1_ref, 1), (f2_ref, b2_ref, 2)):
-        for row in range(rows):
-            place = 2 + blk * rows + row
+    rows = own_ref.shape[1] // lanes
+
+    def same(row, row_move, col_move, other_move):
+        here = ids_ref[row, 4 + other_move : 4 + other_move + lanes, :]
+        there = ids_ref[row + row_move, 4 + col_move : 4 + col_move + lanes, :]
+        return here, here == there
+
+    def own_row(row, state):
+        place = 2 + blk * rows + row
+        for word, reach in enumerate((1, 2)):
+            bits = jnp.zeros((lanes, lanes), jnp.int32)
             for tap, (row_step, col_step) in enumerate(tap_offsets):
                 a, b = row_step * reach, col_step * reach
-                here = ids_ref[place, 4 - b : 4 - b + lanes, :]
-                there = ids_ref[place + a, 4 : 4 + lanes, :]
-                f_ref[tap, row * lanes : (row + 1) * lanes] = jnp.where(
-                    (here == there) & (here >= 0), 1.0, 0.0
-                )
-                here = ids_ref[place, 4 : 4 + lanes, :]
-                there = ids_ref[place - a, 4 - b : 4 - b + lanes, :]
-                b_ref[tap, row * lanes : (row + 1) * lanes] = jnp.where(here == there, 1.0, 0.0)
-    lane = lax.broadcasted_iota(jnp.int32, (lanes, lanes), 1)
-
-    def all_rows(row, state):
-        here = ids_ref[2 + row, 4 : 4 + lanes, :]
-        value = jnp.zeros((lanes, lanes), jnp.float32)
+                here, equal = same(place, a, 0, -b)
+                bits = bits | jnp.where(equal & (here >= 0), 1 << tap, 0)
+                _, equal = same(place, -a, -b, 0)
+                bits = bits | jnp.where(equal, 1 << (9 + tap), 0)
+            own_ref[word, pl.ds(pl.multiple_of(row * lanes, lanes), lanes), :] = bits
+        return state
+
+    lax.fori_loop(0, rows, own_row, 0)
+
+    def any_row(row, state):
+        bits = jnp.zeros((lanes, lanes), jnp.int32)
         for tap, (row_step, col_step) in enumerate(tap_offsets):
-            there = ids_ref[2 + row + row_step, 4 + col_step : 4 + col_step + lanes, :]
-            value = jnp.where((lane == tap) & (here == there), 1.0, value)
-        cols_ref[pl.ds(pl.multiple_of(row * lanes, lanes), lanes), :] = value
+            _, equal = same(2 + row, row_step, col_step, 0)
+            bits = bits | jnp.where(equal, 1 << tap, 0)
+        all_ref[pl.ds(pl.multiple_of(row * lanes, lanes), lanes), :] = bits
         return state
 
-    lax.fori_loop(0, ids_ref.shape[0] - 4, all_rows, 0)
+    lax.fori_loop(0, ids_ref.shape[0] - 4, any_row, 0)
     for hop in range(1, parts):
         line_hop(hop)
         if hop <= 2:
@@ -881,22 +919,18 @@
     anywhere = pl.BlockSpec(memory_space=pl.ANY)
     inside = pl.BlockSpec(memory_space=pltpu.VMEM)
     dma = pltpu.SemaphoreType.DMA
-    mask = shape((9, pixels, lanes), f32)
     return pl.pallas_call(
         functools.partial(prologue_kernel, blocks, parts),
         in_specs=[anywhere] * 5 + [inside],
-        out_specs=[anywhere] * 5 + [inside] * 5,
+        out_specs=[anywhere] * 5 + [inside] * 2,
         out_shape=[
             shape((pixels, feat), low),
             shape((narrow, feat), low),
             shape((narrow, feat), low),
             shape((parts,) + narrow_terms.shape, f32),
             shape((parts,) + wide_terms.shape, f32),
-            mask,
-            mask,
-            mask,
-            mask,
-            shape((pixels * blocks, lanes), f32),
+            shape((2, pixels, lanes), jnp.int32),
+            shape((pixels * blocks, lanes), jnp.int32),
         ],
         scratch_shapes=[
             dma((2, parts)),
@@ -977,19 +1011,13 @@
     return start, finish
 
 
-def heads_forward_kernel(
-    blocks,
-    main_ref,
-    w_ref,
-    mask_ref,
-    pre_ref,
-    act_ref,
-    ext_ref,
-    z_ref,
-    local_sem,
-    halo_send,
-    halo_recv,
-):
+def heads_forward_kernel(blocks, parts, fetch, main_ref, w_ref, mask_ref, *refs):
+    if fetch:
+        raw_r, raw_e, *refs = refs
+    pre_ref, act_ref, ends_ref, *refs = refs
+    if fetch:
+        full_r, full_e, *refs = refs
+    ext_ref, z_ref, local_sem, halo_send, halo_recv, *sems = refs
     step = pl.program_id(0)
     head_count, pixels, mid = pre_ref.shape
     cols = (ext_ref.shape[0] - pixels) // 2
@@ -1004,35 +1032,42 @@
         blocks,
     )
     own = pltpu.make_async_copy(main_ref, ext_ref.at[pl.ds(cols, pixels)], local_sem.at[0])
+    if fetch:
+        first, spread, forward, last = weights_job(
+            raw_r, raw_e, fetch, (full_r, full_e), sems, blocks, parts
+        )
 
     @pl.when(step == 0)
     def _():
         own.start()
-        greet_line(blocks)
+        if fetch:
+            greet(blocks, parts)
+        else:
+            greet_line(blocks)
         start()
+        if fetch:
+            first()
         own.wait()
 
     @pl.when(step == 3)
     def _():
         finish()
+        if fetch:
+            spread()
 
     row_step = jnp.where(step < 3, 1, jnp.where(step < 6, 0, 2))
     col_step = lax.rem(step, 3)
     window = ext_ref[pl.ds(pl.multiple_of(row_step * cols, cols), pixels), :]
     product = contract_last(window, w_ref[0].reshape(head_count * mid, feat))
-    mask = mask_ref[0]
+    product = masked(product, mask_ref[0], tap_at(step))
 
     @pl.when(step < 3)
     def _():
-        for head in range(head_count):
-            part = slice(head * mid, (head + 1) * mid)
-            z_ref[col_step, :, part] = mask * product[:, part]
+        z_ref[col_step] = product
 
     @pl.when(step >= 3)
     def _():
-        for head in range(head_count):
-            part = slice(head * mid, (head + 1) * mid)
-            z_ref[col_step, :, part] += mask * product[:, part]
+        z_ref[col_step] += product
 
     @pl.when(step == 8)
     def _():
@@ -1044,55 +1079,73 @@
                 + pltpu.roll(z_ref[2, :, part], pixels - 1, 0)
             )
             pre_ref[head] = total
-            act_ref[head] = (total * sigmoid(total)).astype(jnp.bfloat16)
+            value = (total * sigmoid(total)).astype(jnp.bfloat16)
+            act_ref[head] = value
+            if head in targets:
+                ends_ref[targets.index(head)] = value
+        if fetch:
+            for array in range(2):
+                forward(array)
+            last()
 
 
 def tap_at(step):
     return jnp.where(step < 3, step + 3, jnp.where(step < 6, step - 3, step))
 
 
-def heads_forward(blocks, layer, cols, main, weights, mask):
+def heads_forward(blocks, parts, layer, cols, main, weights, mask, raw):
     _, head_count, _, mid, feat = weights.shape
-    pixels = mask.shape[1]
+    pixels = main.shape[0]
+    f32, low = jnp.float32, jnp.bfloat16
+    shape = jax.ShapeDtypeStruct
     anywhere = pl.BlockSpec(memory_space=pl.ANY)
     dma = pltpu.SemaphoreType.DMA
+    narrow = mid * parts
     return pl.pallas_call(
-        functools.partial(heads_forward_kernel, blocks),
+        functools.partial(heads_forward_kernel, blocks, parts, layer + 1 if raw else 0),
         grid=(9,),
         in_specs=[
             anywhere,
             pl.BlockSpec((1, head_count, 1, mid, feat), lambda t: (layer, 0, tap_at(t), 0, 0)),
-            pl.BlockSpec((1, pixels, lanes), lambda t: (tap_at(t), 0, 0)),
-        ],
-        out_specs=[whole((head_count, pixels, mid))] * 2,
+            pl.BlockSpec((1, pixels, lanes), lambda t: (0, 0, 0)),
+        ]
+        + [anywhere] * len(raw),
+        out_specs=[whole((head_count, pixels, mid))] * 2
+        + [whole((2, pixels, mid))]
+        + [anywhere] * len(raw),
         out_shape=[
-            jax.ShapeDtypeStruct((head_count, pixels, mid), jnp.float32),
-            jax.ShapeDtypeStruct((head_count, pixels, mid), jnp.bfloat16),
-        ],
+            shape((head_count, pixels, mid), f32),
+            shape((head_count, pixels, mid), low),
+            shape((2, pixels, mid), low),
+        ]
+        + [shape((narrow, feat), low)] * len(raw),
         scratch_shapes=[
-            pltpu.VMEM((pixels + 2 * cols, feat), jnp.bfloat16),
-            pltpu.VMEM((3, pixels, head_count * mid), jnp.float32),
+            pltpu.VMEM((pixels + 2 * cols, feat), low),
+            pltpu.VMEM((3, pixels, head_count * mid), f32),
             dma((1,)),
             dma((2,)),
             dma((2,)),
-        ],
+        ]
+        + (weights_sems(blocks, parts) if raw else []),
         compiler_params=comm_params(6 + layer),
         cost_estimate=pl.CostEstimate(
             flops=18 * pixels * head_count * mid * feat,
             bytes_accessed=18 * head_count * mid * feat,
             transcendentals=0,
         ),
-    )(main, weights, mask)
-
-
-def fill_taps(im_ref, slot, grad, mask_ref, pixels, cols, dilation):
+    )(main, weights, mask, *raw)
+
+
+def fill_taps(im_ref, slot, grad, bits, pixels, cols, dilation):
     rows, mid = grad.shape
     wide = grad.astype(jnp.float32)
     shifted_by = (pltpu.roll(wide, rows - dilation, 0), wide, pltpu.roll(wide, dilation, 0))
     for tap, (row_step, col_step) in enumerate(tap_offsets):
         start = (1 - row_step) * dilation * cols
         part = shifted_by[col_step + 1][start : start + pixels]
-        im_ref[slot, :, tap * mid : (tap + 1) * mid] = (part * mask_ref[tap]).astype(jnp.bfloat16)
+        im_ref[slot, :, tap * mid : (tap + 1) * mid] = masked(part, bits, 9 + tap).astype(
+            jnp.bfloat16
+        )
 
 
 def messages_kernel(
@@ -1104,14 +1157,12 @@
     cot_ref,
     gain_ref,
     bias_ref,
-    f_ref,
-    b_ref,
+    mask_ref,
     maps_ref,
     local_ref,
     sums_ref,
-    grad_ref,
     part_ref,
-    cols_out,
+    pack_ref,
     main_ref,
     low_ref,
     high_ref,
@@ -1121,15 +1172,13 @@
     lhs_ref,
     z_ref,
     im_ref,
-    pack_ref,
+    grad_ref,
     w_sem,
     local_sem,
     halo_send,
     halo_recv,
     cot_send,
     cot_recv,
-    slot_send,
-    slot_recv,
 ):
     parts, heads, pixels, mid = feat_ref.shape
     cols = low_ref.shape[2]
@@ -1144,7 +1193,7 @@
     main_copy.start()
     for pair in (0, 4, 1, 5, 3, 2):
         loads[pair].start()
-    announce([(BLK, peer) for peer in others(BLK, blocks)])
+    greet_blocks(blocks)
     start, finish = edge_copies(feat_ref, low_ref, high_ref, cols, halo_send, halo_recv, blocks)
     start()
     cot_start, cot_finish = edge_copies(
@@ -1160,19 +1209,11 @@
                 [main_ref[part, one][:, first : first + size], main_ref[part, two][:, first : first + size]],
                 axis=1,
             )
-    for index, peer in enumerate(others(BLK, blocks)):
-        remote(
-            pack_ref.at[peer], cols_out.at[me], slot_send.at[index], slot_recv.at[me], BLK, peer
-        ).start()
-    keep = pltpu.make_async_copy(pack_ref.at[me], cols_out.at[me], local_sem.at[1])
-    keep.start()
-    for job in jobs:
-        job[0]()
-
     for source in range(heads):
         for part in range(parts):
             lhs_ref[source, cols : cols + pixels, part * mid : (part + 1) * mid] = main_ref[part, source]
     order = (0, 4, 1, 5, 3, 2)
+    bits = mask_ref[0]
 
     def taps(pair, row_step):
         source = message_pairs[pair][0]
@@ -1181,7 +1222,9 @@
             w_ref[pair, 3 * row_step : 3 * row_step + 3].reshape(3 * mid, parts * mid),
         )
         for col_step in range(3):
-            value = f_ref[row_step * 3 + col_step] * product[:, col_step * mid : (col_step + 1) * mid]
+            value = masked(
+                product[:, col_step * mid : (col_step + 1) * mid], bits, row_step * 3 + col_step
+            )
             if row_step == 1:
                 z_ref[pair, col_step] = value
             else:
@@ -1191,6 +1234,9 @@
         loads[pair].wait()
         taps(pair, 1)
     finish()
+    cot_finish()
+    for job in jobs:
+        job[0]()
     for source in range(heads):
         for part in range(parts):
             chan = slice(part * mid, (part + 1) * mid)
@@ -1199,7 +1245,6 @@
     for pair in order:
         taps(pair, 0)
         taps(pair, 2)
-    cot_finish()
     values = {}
     cots = {}
     for place, target in enumerate((0, 3)):
@@ -1241,7 +1286,7 @@
         grad = jnp.concatenate(
             [border(cot_low, low_ref), grad_ref[pair], border(cot_high, high_ref)], axis=0
         )
-        fill_taps(im_ref, slot, grad, b_ref, pixels, cols, 1)
+        fill_taps(im_ref, slot, grad, bits, pixels, cols, 1)
         return jnp.dot(
             im_ref[slot],
             w_ref[pair].reshape(9 * mid, parts * mid),
@@ -1256,18 +1301,11 @@
             part_ref[part, source] = total[:, part * mid : (part + 1) * mid].astype(low)
     for job in jobs:
         job[1]()
-    for index, peer in enumerate(others(BLK, blocks)):
-        copy = remote(
-            pack_ref.at[peer], cols_out.at[peer], slot_send.at[index], slot_recv.at[peer], BLK, peer
-        )
-        copy.wait_recv()
-        copy.wait_send()
-    keep.wait()
     for job in jobs:
         job[2]()
 
 
-def messages_both(blocks, layer, jobs, cols, features, weights, cotangents, gains, biases, forward, backward):
+def messages_both(blocks, layer, jobs, cols, features, weights, cotangents, gains, biases, mask):
     parts, heads, pixels, mid = features.shape
     pairs = weights.shape[1]
     narrow = parts * mid
@@ -1281,13 +1319,12 @@
         functools.partial(messages_kernel, blocks, layer),
         jobs,
         blocks,
-        in_specs=[anywhere, anywhere] + [inside] * 5,
-        out_specs=[inside] * 5 + [anywhere],
+        in_specs=[anywhere, anywhere] + [inside] * 4,
+        out_specs=[inside] * 5,
         out_shape=[
             shape((2, pixels, mid), low),
             shape((2, pixels, mid), f32),
             shape((2 * pairs, mid), f32),
-            shape((pairs, pixels, mid), low),
             shape((parts, heads, pixels, mid), low),
             shape((blocks, 2, pixels, wide), low),
         ],
@@ -1301,15 +1338,13 @@
             pltpu.VMEM((heads, pixels + 2 * cols, narrow), low),
             pltpu.VMEM((pairs, 3, pixels, mid), f32),
             pltpu.VMEM((2, pixels, 9 * mid), low),
-            pltpu.VMEM((blocks, 2, pixels, wide), low),
+            pltpu.VMEM((pairs, pixels, mid), low),
             dma((pairs,)),
+            dma((1,)),
             dma((2,)),
             dma((2,)),
             dma((2,)),
             dma((2,)),
-            dma((2,)),
-            dma((blocks,)),
-            dma((blocks,)),
         ],
         compiler_params=comm_params(10 + layer),
         cost_estimate=pl.CostEstimate(
@@ -1317,7 +1352,7 @@
             bytes_accessed=18 * pairs * mid * narrow,
             transcendentals=0,
         ),
-    )(features, weights, cotangents, gains, biases, forward, backward)
+    )(features, weights, cotangents, gains, biases, mask)
 
 
 def heads_backward_kernel(
@@ -1345,12 +1380,12 @@
         else:
             greet_line(blocks)
         start()
+        finish()
         for job in jobs:
             job[0]()
-        finish()
         for head in range(head_count):
             grad = jnp.concatenate([low_ref[head], main_ref[head], high_ref[head]], axis=0)
-            fill_taps(im_ref, head, grad, mask_ref, pixels, cols, 1)
+            fill_taps(im_ref, head, grad, mask_ref[0], pixels, cols, 1)
 
     total = None
     for head in range(head_count):
@@ -1374,7 +1409,7 @@
 
 def heads_backward(blocks, layer, jobs, cols, main, weights, mask, parts):
     _, head_count, taps, mid, feat = weights.shape
-    pixels = mask.shape[1]
+    pixels = main.shape[1]
     width = feat // parts
     dma = pltpu.SemaphoreType.DMA
     return job_call(
@@ -1385,7 +1420,7 @@
         in_specs=[
             whole(main.shape),
             pl.BlockSpec((1, head_count, taps, mid, width), lambda j: (layer, 0, 0, 0, j)),
-            whole(mask.shape),
+            pl.BlockSpec((1, pixels, lanes), lambda j: (0, 0, 0)),
         ],
         out_specs=[pl.BlockSpec((1, pixels, width), lambda j: (j, 0, 0))],
         out_shape=[jax.ShapeDtypeStruct((parts, pixels, width), jnp.bfloat16)],
@@ -1405,20 +1440,9 @@
     )(main, weights, mask)
 
 
-def weight_kernel(
-    blocks,
-    lists,
-    store,
-    jobs,
-    before_ref,
-    v_ref,
-    after_ref,
-    g_ref,
-    cols_ref,
-    out_ref,
-    lhs_ref,
-    *acc_refs,
-):
+def weight_kernel(blocks, lists, load, store, jobs, before_ref, v_ref, after_ref, bits_ref, *refs):
+    count = len(lists)
+    g_refs, (out_ref, lhs_ref, *acc_refs) = refs[: len(refs) - 2 - count], refs[-2 - count :]
     step = pl.program_id(0)
     pixels, chans = v_ref.shape[2:]
     cols = lanes
@@ -1430,7 +1454,7 @@
             for job in jobs:
                 job[0]()
 
-    masks = cols_ref[...]
+    bits = bits_ref[...]
     for index, members in enumerate(lists):
         window = jnp.concatenate(
             [before_ref[0, index], v_ref[0, index], after_ref[0, index]], axis=0
@@ -1440,10 +1464,10 @@
         for tap, (row_step, col_step) in enumerate(tap_offsets):
             top = (1 + row_step) * cols
             part = shifted_by[col_step + 1][top : top + pixels]
-            lhs_ref[:, tap * chans : (tap + 1) * chans] = (
-                part * masks[:, tap : tap + 1]
-            ).astype(jnp.bfloat16)
-        grads = jnp.concatenate([g_ref[0, member] for member in members], axis=1)
+            lhs_ref[:, tap * chans : (tap + 1) * chans] = masked(part, bits, tap).astype(
+                jnp.bfloat16
+            )
+        grads = jnp.concatenate([load(g_refs, member) for member in members], axis=1)
         product = lax.dot_general(
             lhs_ref[...], grads, (((0,), (0,)), ((), ())), preferred_element_type=jnp.float32
         )
@@ -1466,13 +1490,13 @@
             job[2]()
 
 
-def weight_gradient(key, blocks, jobs, lists, store, out_shape, values, grads, mask_cols):
+def weight_gradient(key, blocks, jobs, lists, load, store, out_shape, values, bits, grads, specs):
     _, count, pixels, chans = values.shape
-    _, members, _, mid = grads.shape
+    mid = out_shape[-1]
     f32, low = jnp.float32, jnp.bfloat16
     tail = pixels // lanes - 1
     return job_call(
-        functools.partial(weight_kernel, blocks, lists, store),
+        functools.partial(weight_kernel, blocks, lists, load, store),
         jobs,
         blocks,
         grid=(blocks,),
@@ -1482,9 +1506,9 @@
             pl.BlockSpec(
                 (1, count, lanes, chans), lambda i: (jnp.minimum(i + 1, blocks - 1), 0, 0, 0)
             ),
-            pl.BlockSpec((1, members, pixels, mid), lambda i: (i, 0, 0, 0)),
             pl.BlockSpec((pixels, lanes), lambda i: (i, 0)),
-        ],
+        ]
+        + specs,
         out_specs=[whole(out_shape)],
         out_shape=[jax.ShapeDtypeStruct(out_shape, f32)],
         scratch_shapes=[pltpu.VMEM((pixels, 9 * chans), low)]
@@ -1497,7 +1521,22 @@
             bytes_accessed=10**7,
             transcendentals=0,
         ),
-    )(values, values, values, grads, mask_cols)
+    )(values, values, values, bits, *grads)
+
+
+def heads_load(refs, head):
+    return refs[0][0, head]
+
+
+def messages_load(layer):
+    def load(refs, pair):
+        cot_ref, feat_ref, gain_ref, bias_ref = refs
+        place = targets.index(message_pairs[pair][1])
+        gain, bias = gain_ref[layer, pair : pair + 1], bias_ref[layer, pair : pair + 1]
+        gate = sigmoid(gain * feat_ref[0, place].astype(jnp.float32) + bias)
+        return (cot_ref[0, 0, place].astype(jnp.float32) * gate).astype(jnp.bfloat16)
+
+    return load
 
 
 def heads_store(out_ref, acc_refs):
@@ -1728,7 +1767,11 @@
             wd_ref[3 * row_step : 3 * row_step + 3].reshape(3 * mid, parts * mid),
         )
         for col_step in range(3):
-            part = mask_ref[row_step * 3 + col_step] * product[:, col_step * mid : (col_step + 1) * mid]
+            part = masked(
+                product[:, col_step * mid : (col_step + 1) * mid],
+                mask_ref[1],
+                row_step * 3 + col_step,
+            )
             if row_step == 1:
                 z_ref[col_step] = part
             else:
@@ -1882,8 +1925,7 @@
     gain2_ref,
     bias2_ref,
     wd_ref,
-    mask_f_ref,
-    mask_b_ref,
+    mask_ref,
     ext_ref,
     normed1_ref,
     inverse1_ref,
@@ -2024,7 +2066,7 @@
     for row_step in range(3):
         side = jnp.concatenate(
             [
-                (mask_f_ref[row_step * 3 + col_step] * turned[col_step]).astype(low)
+                masked(turned[col_step], mask_ref[1], row_step * 3 + col_step).astype(low)
                 for col_step in range(3)
             ],
             axis=1,
@@ -2043,7 +2085,7 @@
                 ].astype(low)
     di_recv_ref[blk] = di_send_ref[blk]
     wait_halo()
-    fill_taps(im_ref, 0, grad_ref[...], mask_b_ref, pixels, half, 2)
+    fill_taps(im_ref, 0, grad_ref[...], mask_ref[1], pixels, half, 2)
     product = jnp.dot(
         im_ref[0], wd_ref[...].reshape(9 * mid, narrow), preferred_element_type=jnp.float32
     )
@@ -2093,7 +2135,7 @@
     feat = wide * parts
     mid = operands[9].shape[1]
     narrow = mid * parts
-    rows = operands[16].shape[0]
+    rows = operands[15].shape[0]
     f32, low = jnp.float32, jnp.bfloat16
     shape = jax.ShapeDtypeStruct
     small, large = narrow // blocks, feat // blocks
@@ -2199,24 +2241,24 @@
         canvas_ids,
     )
     reduce_full, expand_full = [rest[0]], [rest[1]]
-    narrow_all, wide_all, forward_one, backward_one, forward_two, backward_two, mask_cols = rest[2:]
+    narrow_all, wide_all, bits, all_bits = rest[2:]
     narrow_all = narrow_all.transpose(1, 0, 2).reshape(2, layers, narrow)
     wide_all = wide_all.transpose(1, 0, 2).reshape(2, layers, feat)
 
     kept = []
     for layer in range(layers):
         keep = types.SimpleNamespace(input=current)
-        results, swapped = trunk_forward(
+        results, _ = trunk_forward(
             blocks,
             parts,
             cols,
             layer,
-            [(swap_kind, current)] if layer else [],
+            [],
             current,
             reduce_full[layer],
             dilated_t[layer],
             expand_full[layer],
-            forward_two,
+            bits,
             (
                 narrow_all[0, layer][None],
                 narrow_all[1, layer][None],
@@ -2225,7 +2267,7 @@
                 wide_all[0, layer][None],
                 wide_all[1, layer][None],
             ),
-            (w_reduce, w_expand) if layer + 1 < layers else (),
+            (),
         )
         (
             current,
@@ -2237,44 +2279,51 @@
             keep.inverse2,
             keep.normed3,
             keep.inverse3,
-            *fetched,
         ) = results
+        if layer:
+            current, kept[-1].features = lax.optimization_barrier((current, kept[-1].features))
+        keep.output = current
+        keep.heads_pre, features, keep.ends, *fetched = heads_forward(
+            blocks,
+            parts,
+            layer,
+            cols,
+            current,
+            heads_t,
+            bits,
+            (w_reduce, w_expand) if layer + 1 < layers else (),
+        )
         if fetched:
             reduce_full.append(fetched[0])
             expand_full.append(fetched[1])
-        if layer:
-            kept[-1].values = swapped[0]
-            current, kept[-1].features = lax.optimization_barrier((current, kept[-1].features))
-        keep.output = current
-        keep.heads_pre, features = heads_forward(blocks, layer, cols, current, heads_t, forward_one)
         current, features = lax.optimization_barrier((current, features))
         keep.features = gather_parts(features)
         kept.append(keep)
     output = own_slice(current, wide, 1).reshape(rows, cols, wide)
 
+    cotangents = task_cotangents.reshape(layers, 2, pixels, mid)
     for layer in range(layers):
         keep = kept[layer]
-        jobs = [(gather_kind, keep_before.message_low) for keep_before in kept[:layer][-1:]]
         if layer == 0:
-            jobs = [(swap_kind, kept[-1].output)]
-        results, moved = messages_both(
+            jobs = [(gather_kind, cotangents), (gather_kind, keep.ends)]
+        else:
+            jobs = [(gather_kind, keep.ends), (swap_kind, kept[0].output)]
+        (keep.maps, keep.local, keep.gate_sums, partial, keep.message_values), moved = messages_both(
             blocks,
             layer,
             jobs,
             cols,
             keep.features,
             messages_t,
-            task_cotangents[layer].reshape(2, pixels, mid),
+            cotangents[layer],
             gate_gain,
             gate_bias,
-            forward_one,
-            backward_one,
-        )
-        keep.maps, keep.local, keep.gate_sums, keep.message_low, partial, keep.message_values = results
+            bits,
+        )
         if layer == 0:
-            kept[-1].values = moved[0]
+            cotangents_all, keep.ends_all = moved
         else:
-            kept[layer - 1].message_all = moved[0]
+            keep.ends_all, kept[0].values = moved
         keep.source_sums = reduce_parts(partial)
 
     def heads_low_of(keep):
@@ -2289,44 +2338,63 @@
             blocks,
             jobs,
             group_pairs,
+            messages_load(layer),
             messages_store,
             (6, 9, narrow // blocks, mid),
             keep.message_values,
-            keep.message_all,
-            mask_cols,
+            all_bits,
+            (cotangents_all, keep.ends_all, gate_gain, gate_bias),
+            [
+                pl.BlockSpec((1, 1, 2, pixels, mid), lambda i: (i, layer, 0, 0, 0)),
+                pl.BlockSpec((1, 2, pixels, mid), lambda i: (i, 0, 0, 0)),
+                whole(gate_gain.shape),
+                whole(gate_bias.shape),
+            ],
         )
         return moved
 
-    def heads_weight(layer):
+    def heads_weight(layer, jobs):
         keep = kept[layer]
-        (keep.heads_grad,), _ = weight_gradient(
+        (keep.heads_grad,), moved = weight_gradient(
             40 + layer,
             blocks,
-            [],
+            jobs,
             (tuple(range(4)),),
+            heads_load,
             heads_store,
             (4, 9, feat // blocks, mid),
             keep.values[:, None],
-            keep.heads_all,
-            mask_cols,
-        )
+            all_bits,
+            (keep.heads_all,),
+            [pl.BlockSpec((1, 4, pixels, mid), lambda i: (i, 0, 0, 0))],
+        )
+        return moved
 
     for layer in range(layers):
         keep = kept[layer]
         keep.heads_low = heads_low_of(keep)
-        jobs = [(gather_kind, kept[-1].message_low)] if layer == 0 else []
+        jobs = [(slot_kind, each.message_values) for each in kept] if layer == 0 else []
         (partial,), moved = heads_backward(
-            blocks, layer, jobs, cols, keep.heads_low, heads_t, backward_one, parts
+            blocks, layer, jobs, cols, keep.heads_low, heads_t, bits, parts
         )
         if layer == 0:
-            kept[-1].message_all = moved[0]
+            for each, values in zip(kept, moved):
+                each.message_values = values
         keep.heads_partial = reduce_parts(partial)
-        (keep.heads_all,) = messages_weight(layer, [(gather_kind, keep.heads_low)])
         if layer + 1 < layers:
-            kept[layer + 1].source_sums, keep.messages_grad = lax.optimization_barrier(
-                (kept[layer + 1].source_sums, keep.messages_grad)
+            kept[layer + 1].source_sums, partial = lax.optimization_barrier(
+                (kept[layer + 1].source_sums, partial)
             )
-    heads_weight(0)
+    kept[0].message_values, partial = lax.optimization_barrier((kept[0].message_values, partial))
+    (kept[0].heads_all,) = messages_weight(0, [(gather_kind, kept[0].heads_low)])
+    kept[1].message_values, kept[0].heads_all = lax.optimization_barrier(
+        (kept[1].message_values, kept[0].heads_all)
+    )
+    (kept[1].heads_all,) = messages_weight(1, [(gather_kind, kept[1].heads_low)])
+    (kept[1].values,) = heads_weight(0, [(swap_kind, kept[1].output)])
+    kept[1].heads_partial, kept[0].heads_grad = lax.optimization_barrier(
+        (kept[1].heads_partial, kept[0].heads_grad)
+    )
 
     upstream = output_cotangent.reshape(pixels, wide).astype(jnp.float32)
     for layer in reversed(range(layers)):
@@ -2358,8 +2426,7 @@
                 norm_gain[layer, 1][None],
                 norm_bias[layer, 1][None],
                 dilated_t[layer],
-                forward_two,
-                backward_two,
+                bits,
                 keep.first_ext,
                 keep.normed1,
                 keep.inverse1,
@@ -2370,8 +2437,7 @@
             ),
         )
 
-    for layer in range(1, layers):
-        heads_weight(layer)
+    heads_weight(1, [])
 
     def stacked(of):
         return jnp.stack([of(keep) for keep in kept])

time: 804 us -> 736 us (0.915)
  Pallas kernels: 720 us -> 660 us
    pallas_call x10, Pallas kernels: 494 us -> 408 us  [call(): pl.pallas_call(wrapped, in_specs=list(in_specs) + [anywhere] * count, out...]
    pallas_call x2, Pallas kernels: 38 us -> 65.8 us  [heads_forward(): pl.pallas_call(functools.partial(heads_forward_kernel, blocks, parts, lay...]
    reduce_scatter x4, waiting for transfers between devices: 10.9 us -> 0.06 us  [reduce_parts(): return lax.psum_scatter(values, CH, scatter_dimension=0, tiled=False)]
  transfers between devices with their start and end apart: 6 -> 6, of which waited for: 1 -> 1; matrix products, arithmetic and copies ran while one was open for 3% -> 2% of each run, Pallas kernels for 58% -> 56%
where the time goes in v3:
time: 736 us; the launch traced here: 728 us
  Pallas kernels  660 us (90%)
  other arithmetic  24.9 us (3%)
  local copies, waits for them, and re-layouts  21.8 us (3%)
  between operations  14.8 us (2%)
    pallas_call x10, Pallas kernels, call(): pl.pallas_call(wrapped, in_specs=list(in_specs) + [anywhere] * count, out...  408 us
    pallas_call x2, Pallas kernels, trunk_backward(): pl.pallas_call(functools.partial(trunk_backward_kernel, blocks, parts), o...  129 us
    pallas_call x2, Pallas kernels, heads_forward(): pl.pallas_call(functools.partial(heads_forward_kernel, blocks, parts, lay...  65.8 us
    pallas_call x1, Pallas kernels, prologue(): pl.pallas_call(functools.partial(prologue_kernel, blocks, parts), in_spec...  57.4 us
    another operation x10, other arithmetic, stacked(): return jnp.stack([of(keep) for keep in kept])  17.9 us
  transfers between devices with their start and end apart: 6, of which 1 were waited for; matrix products, arithmetic and copies ran while one was open for 2% of the time, Pallas kernels for 56%

profile of v3, /device:TPU:0, one launch (start us, length us, event | category | flops | bytes accessed | tf_op | source)
XLA Modules:
  0.0 727.8 jit_solution(12346021208084363945)
XLA Ops:
  7.2 1.4 slice_bitcast_fusion.17
  8.7 3.3 slice_bitcast_fusion
  13.3 2.4 broadcast_in_dim.12.ids_ref
  15.7 57.4 %shard_map.254 = (bf16[512,2048]{1,0:T(8,128)(2,1)}, bf16[512,2048]{1,0:T(8,128)(2,1)}, bf16[512,2048]{1,0:T(8,128)(2,1)}, f32[4,4,128]{2,1,0:T(4,128)}, f32[4,4...) custom-call(bf16[512,512]{1,0:T(8,128)(2,1)} %bitcast.123, bf16[2,128,2048]{2,1,0:T(8,128)(2,1)} %refs_0_.1, ...), custom_call_target="tpu_custom_call" | custom-call | flops 1000000 | bytes 100000000 | tf_op jit(solution)/shard_map/pallas_call | solution.py:922
  75.8 43.9 %shard_map.255 = (bf16[512,2048]{1,0:T(8,128)(2,1)}, bf16[1024,512]{1,0:T(8,128)(2,1)}, bf16[512,512]{1,0:T(8,128)(2,1)}, f32[512,128]{1,0:T(8,128)}, f32[1,128]...) custom-call(bf16[512,2048]{1,0:T(8,128)(2,1)} %get-tuple-element.98.refs_0_.cur_re, ...), custom_call_target="tpu_custom_call" | custom-call | flops 2751463424 | bytes 157286400 | tf_op jit(solution)/shard_map/pallas_call | solution.py:643
  119.8 47.0 %shard_map.256 = (f32[4,512,128]{2,1,0:T(8,128)}, bf16[4,512,128]{2,1,0:T(8,128)(2,1)}, bf16[2,512,128]{2,1,0:T(8,128)(2,1)}, bf16[512,2048]{1,0:T(8,128)(2,1)}, bf16[512,2048]{1,0:T(8,128)(2,1)}) custom-call(bf16[512,2048]{1,0:T(8,128)(2,1)} %get-tuple-element.106.main_ref.refs_0_.refs_7_.cur_ref, bf16[2,4,9,128,2048]{4,3,2,1,0:T(8,128)(2,1)} %bitcast.111, ...), custom_call_target="tpu_custom_call" | custom-call | flops 9663676416 | bytes 18874368 | tf_op jit(solution)/shard_map/pallas_call | solution.py:1104
  166.9 50.3 %shard_map.257 = (bf16[512,2048]{1,0:T(8,128)(2,1)}, bf16[1024,512]{1,0:T(8,128)(2,1)}, bf16[512,512]{1,0:T(8,128)(2,1)}, f32[512,128]{1,0:T(8,128)}, f32[1,128]...) custom-call(bf16[512,2048]{1,0:T(8,128)(2,1)} %get-tuple-element.106.main_ref.refs, ...), custom_call_target="tpu_custom_call" | custom-call | flops 2751463424 | bytes 157286400 | tf_op jit(solution)/shard_map/pallas_call | solution.py:643
  217.2 4.7 all-gather.5.cloned.1.call-done
  222.0 18.7 %shard_map.258 = (f32[4,512,128]{2,1,0:T(8,128)}, bf16[4,512,128]{2,1,0:T(8,128)(2,1)}, bf16[2,512,128]{2,1,0:T(8,128)(2,1)}) custom-call(bf16[512,2048]{1,0:T(8,128)(2,1)} %get-tuple-element.113.main_ref.refs_5_, bf16[2,4,9,128,2048]{4,3,2,1,0:T(8,128)(2,1)} %bitcast.112, s32[2,512,128]{2,1,0:T(8,128)} %get-tuple-element.101.refs_4_.mask_ref.refs_5_.refs_2_), custom_call_target="tpu_custom_call" | custom-call | flops 9663676416 | bytes 18874368 | tf_op jit(solution)/shard_map/pallas_call | solution.py:1104
  242.8 66.3 %shard_map.259 = (bf16[2,512,128]{2,1,0:T(8,128)(2,1)}, f32[2,512,128]{2,1,0:T(8,128)}, f32[12,128]{1,0:T(8,128)}, bf16[4,4,512,128]{3,2,1,0:T(8,128)(2,1)}, bf1...) custom-call(bf16[4,4,512,128]{3,2,1,0:T(8,128)(2,1)} %bitcast.154, ...), custom_call_target="tpu_custom_call" | custom-call | flops 7247757312 | bytes 7077888 | tf_op jit(solution)/shard_map/pallas_call | solution.py:643
  309.2 51.2 %shard_map.260 = (bf16[2,512,128]{2,1,0:T(8,128)(2,1)}, f32[2,512,128]{2,1,0:T(8,128)}, f32[12,128]{1,0:T(8,128)}, bf16[4,4,512,128]{3,2,1,0:T(8,128)(2,1)}, bf1...) custom-call(bf16[4,4,512,128]{3,2,1,0:T(8,128)(2,1)} %bitcast.155, ...), custom_call_target="tpu_custom_call" | custom-call | flops 7247757312 | bytes 7077888 | tf_op jit(solution)/shard_map/pallas_call | solution.py:643
  361.0 1.1 convert_element_type.20
  362.2 1.2 fusion.refs_0_.refs_8_
  363.5 55.4 %shard_map.261 = (bf16[4,512,512]{2,1,0:T(8,128)(2,1)}, bf16[8,2,512,128]{3,2,1,0:T(8,128)(2,1)}, bf16[8,2,512,128]{3,2,1,0:T(8,128)(2,1)}) custom-call(bf16[4,512,128]{2,1,0:T(8,128)(2,1)} %fusion.refs_0_.refs_8_, bf16[2,4,9,128,2048]{4,3,2,1,0:T(8,128)(2,1)} %bitcast.113, s32[2,512,128]{2,1,0:T(8,128)} %get-tuple-element.101.refs_4_.mask_ref.refs_5_.refs_2_, ...), custom_call_target="tpu_custom_call" | custom-call | flops 9663676416 | bytes 18874368 | tf_op jit(solution)/shard_map/pallas_call | solution.py:643
  419.0 1.1 slice.214
  420.1 1.1 convert_element_type.22
  421.3 1.2 fusion.1.refs_0_.refs_8_
  422.4 22.6 %shard_map.262 = bf16[4,512,512]{2,1,0:T(8,128)(2,1)} custom-call(bf16[4,512,128]{2,1,0:T(8,128)(2,1)} %fusion.1.refs_0_.refs_8_, bf16[2,4,9,128,2048]{4,3,2,1,0:T(8,128)(2,1)} %bitcast.114, s32[2,512,128]{2,1,0:T(8,128)} %get-tuple-element.101.refs_4_.mask_ref.refs_5_.refs_2_), custom_call_target="tpu_custom_call" | custom-call | flops 9663676416 | bytes 18874368 | tf_op jit(solution)/shard_map/pallas_call | solution.py:643
  445.4 1.0 copy-done
  446.3 1.0 slice_bitcast_fusion.3
  448.0 1.1 bitcast_convert_fusion.up_ref
  449.1 1.9 constant_dynamic-slice_fusion
  451.8 36.4 %shard_map.263 = (f32[6,9,64,128]{3,2,1,0:T(8,128)}, bf16[8,4,512,128]{3,2,1,0:T(8,128)(2,1)}) custom-call(bf16[8,2,512,128]{3,2,1,0:T(8,128)(2,1)} %get-tuple-element.134.refs_0_.refs_1_.refs_2_, bf16[8,2,512,128]{3,2,1,0:T(8,128)(2,1)} %get-tuple-element.134.refs_0_.refs_1_.refs_2_, bf16[8,2,512,128]{3,2,1,0:T(8,128)(2,1)} %get-tuple-element.134.refs_0_.refs_1_.refs_2_, ...), custom_call_target="tpu_custom_call" | custom-call | flops 7247757312 | bytes 10000000 | tf_op jit(solution)/shard_map/pallas_call | solution.py:643
  488.2 32.6 %shard_map.267 = (f32[6,9,64,128]{3,2,1,0:T(8,128)}, bf16[8,4,512,128]{3,2,1,0:T(8,128)(2,1)}) custom-call(bf16[8,2,512,128]{3,2,1,0:T(8,128)(2,1)} %get-tuple-element.169.refs_0_.refs_1_.refs_2_, bf16[8,2,512,128]{3,2,1,0:T(8,128)(2,1)} %get-tuple-element.169.refs_0_.refs_1_.refs_2_, bf16[8,2,512,128]{3,2,1,0:T(8,128)(2,1)} %get-tuple-element.169.refs_0_.refs_1_.refs_2_, ...), custom_call_target="tpu_custom_call" | custom-call | flops 7247757312 | bytes 10000000 | tf_op jit(solution)/shard_map/pallas_call | solution.py:643
  520.9 3.8 pad_maximum_fusion.1
  524.6 29.2 %shard_map.264 = (f32[4,9,256,128]{3,2,1,0:T(8,128)}, bf16[8,512,256]{2,1,0:T(8,128)(2,1)}) custom-call(bf16[8,1,512,256]{3,2,1,0:T(8,128)(2,1)} %bitcast.156, bf16[8,1,512,256]{3,2,1,0:T(8,128)(2,1)} %bitcast.157, bf16[8,1,512,256]{3,2,1,0:T(8,128)(2,1)} %bitcast.158, s32[4096,128]{1,0:T(8,128)} %get-tuple-element.131.refs_3_, ...), custom_call_target="tpu_custom_call" | custom-call | flops 9663676416 | bytes 10000000 | tf_op jit(solution)/shard_map/pallas_call | solution.py:643
  553.9 19.8 %shard_map.268 = f32[4,9,256,128]{3,2,1,0:T(8,128)} custom-call(bf16[8,1,512,256]{3,2,1,0:T(8,128)(2,1)} %bitcast.159, bf16[8,1,512,256]{3,2,1,0:T(8,128)(2,1)} %bitcast.160, bf16[8,1,512,256]{3,2,1,0:T(8,128)(2,1)} %bitcast.161, s32[4096,128]{1,0:T(8,128)} %get-tuple-element.131.refs_3_, bf16[8,4,512,128]{3,2,1,0:T(8,128)(2,1)} %get-tuple-element.171.refs_4_), custom_call_target="tpu_custom_call" | custom-call | flops 9663676416 | bytes 10000000 | tf_op jit(solution)/shard_map/pallas_call | solution.py:643
  573.6 66.6 %shard_map.265 = (f32[512,512]{1,0:T(8,128)}, f32[64,512]{1,0:T(8,128)}, f32[9,64,128]{2,1,0:T(8,128)}, f32[256,128]{1,0:T(8,128)}, f32[2,512]{1,0:T(2,128)}, /*...) custom-call(f32[512,512]{1,0:T(8,128)} %bitcast_convert_fusion.up_ref, bf16[512,512]{1,0:T(8,128)(2,1)} %bitcast.125, ...), custom_call_target="tpu_custom_call" | custom-call | flops 2281701376 | bytes 209715200 | tf_op jit(solution)/shard_map/pallas_call | solution.py:2142
  640.3 62.9 %shard_map.266 = (f32[512,512]{1,0:T(8,128)}, f32[64,512]{1,0:T(8,128)}, f32[9,64,128]{2,1,0:T(8,128)}, f32[256,128]{1,0:T(8,128)}, f32[2,512]{1,0:T(2,128)}, /*...) custom-call(f32[512,512]{1,0:T(8,128)} %get-tuple-element.150.up_ref, bf16[512,512]{1,0:T(8,128)(2,1)} %bitcast.124, ...), custom_call_target="tpu_custom_call" | custom-call | flops 2281701376 | bytes 209715200 | tf_op jit(solution)/shard_map/pallas_call | solution.py:2142
  707.1 1.6 pad_maximum_fusion.4
  708.8 8.7 %pad_maximum_fusion = f32[2,4,9,256,128]{4,3,2,1,0:T(8,128)} fusion(f32[1,4,9,256,128]{4,3,2,1,0:T(8,128)} %bitcast.116, f32[1,4,9,256,128]{4,3,2,1,0:T(8,128)} %bitcast.115), kind=kLoop, calls=%fused_computation | loop fusion | flops 2359296 | bytes 18874368 | tf_op jit(solution)/shard_map/stack | solution.py:2443
  719.7 1.0 copy.79
  (106 shorter events, 14.9 us)
Async XLA Ops:
  7.2 214.8 %all-gather.5.cloned.1.call-start = ((), (), s32[]{:S(2)}) async-start(), calls=%async_computation.8 | async-start | bytes 2621440 | tf_op jit(solution)/shard_map/all_gather | solution.py:2193
  8.6 3.4 slice-start
  8.6 3.4 slice-start.1
  8.6 4.0 copy-start.17
  8.7 4.0 copy-start.18
  8.7 4.6 copy-start.16
  166.9 142.4 %all-gather.7.cloned.1.call-start = ((), (), s32[]{:S(2)}) async-start(), calls=%async_computation.9 | async-start | bytes 2621440 | tf_op jit(solution)/shard_map/all_gather | solution.py:2193
  221.9 18.8 %copy-start.20 = (f32[2,6,128]{2,0,1:T(2,128)S(1)}, f32[2,6,128]{2,0,1:T(2,128)}, u32[]{:S(2)}) copy-start(f32[2,6,128]{2,0,1:T(2,128)} %param.25) | copy-start | bytes 18436
  222.0 19.4 %copy-start.21 = (f32[2,6,128]{2,0,1:T(2,128)S(1)}, f32[2,6,128]{2,0,1:T(2,128)}, u32[]{:S(2)}) copy-start(f32[2,6,128]{2,0,1:T(2,128)} %param.26) | copy-start | bytes 18436
  222.0 20.0 %copy-start.8 = (bf16[2,2,4,128,128]{4,3,2,1,0:T(8,128)(2,1)S(1)}, bf16[2,2,4,128,128]{4,3,2,1,0:T(8,128)(2,1)}, u32[]{:S(2)}) copy-start(bf16[2,2,4,128,128]{4,3,2,1,0:T(8,128)(2,1)} %param.29) | copy-start | bytes 1572868
  240.7 120.3 %reduce-scatter.7.cloned.1.call-start = ((), (), s32[]{:S(2)}) async-start(), calls=%async_computation.5 | async-start | bytes 2621440 | tf_op jit(solution)/shard_map/reduce_scatter | solution.py:2197
  309.1 109.8 %reduce-scatter.5.cloned.1.call-start = ((), (), s32[]{:S(2)}) async-start(), calls=%async_computation.4 | async-start | bytes 2621440 | tf_op jit(solution)/shard_map/reduce_scatter | solution.py:2197
  360.5 213.2 %reduce-scatter.9.cloned.1.call-start = ((), (), s32[]{:S(2)}) async-start(), calls=%async_computation.6 | async-start | bytes 2621440 | tf_op jit(solution)/shard_map/reduce_scatter | solution.py:2197
  418.9 2.3 copy-start.7
  418.9 2.3 copy-start.3
  445.1 2.8 copy-start.5
  445.1 195.1 %reduce-scatter.11.cloned.1.call-start = ((), (), s32[]{:S(2)}) async-start(), calls=%async_computation.7 | async-start | bytes 2621440 | tf_op jit(solution)/shard_map/reduce_scatter | solution.py:2197
  447.4 3.6 copy-start.11
  447.4 3.6 copy-start.12
  488.2 32.6 %copy-start.1 = (f32[6,9,64,128]{3,2,1,0:T(8,128)S(1)}, f32[6,9,64,128]{3,2,1,0:T(8,128)}, u32[]{:S(2)}) copy-start(f32[6,9,64,128]{3,2,1,0:T(8,128)} %get-tuple-element.172) | copy-start | bytes 5308420
  640.3 62.9 %copy-start.22 = (f32[2,512]{1,0:T(2,128)S(1)}, f32[2,512]{1,0:T(2,128)}, u32[]{:S(2)}) copy-start(f32[2,512]{1,0:T(2,128)} %get-tuple-element.179) | copy-start | bytes 12292
  640.3 65.6 %copy-start.19 = (f32[12,128]{1,0:T(8,128)S(1)}, f32[12,128]{1,0:T(8,128)}, u32[]{:S(2)}) copy-start(f32[12,128]{1,0:T(8,128)} %get-tuple-element.181) | copy-start | bytes 18436
  640.3 66.8 %copy-start.14 = (f32[256,128]{1,0:T(8,128)S(1)}, f32[256,128]{1,0:T(8,128)}, u32[]{:S(2)}) copy-start(f32[256,128]{1,0:T(8,128)} %get-tuple-element.162) | copy-start | bytes 393220
  708.7 8.8 %copy-start.25 = (f32[2,128]{1,0:T(2,128)S(1)}, f32[2,128]{1,0:T(2,128)}, u32[]{:S(2)}) copy-start(f32[2,128]{1,0:T(2,128)} %get-tuple-element.175) | copy-start | bytes 3076
  708.7 8.8 %copy-start.26 = (f32[2,128]{1,0:T(2,128)S(1)}, f32[2,128]{1,0:T(2,128)}, u32[]{:S(2)}) copy-start(f32[2,128]{1,0:T(2,128)} %get-tuple-element.174) | copy-start | bytes 3076
  708.7 8.8 %copy-start.23 = (f32[2,128]{1,0:T(2,128)S(1)}, f32[2,128]{1,0:T(2,128)}, u32[]{:S(2)}) copy-start(f32[2,128]{1,0:T(2,128)} %get-tuple-element.177) | copy-start | bytes 3076
  708.7 8.8 %copy-start.24 = (f32[2,128]{1,0:T(2,128)S(1)}, f32[2,128]{1,0:T(2,128)}, u32[]{:S(2)}) copy-start(f32[2,128]{1,0:T(2,128)} %get-tuple-element.176) | copy-start | bytes 3076
  708.7 9.4 %copy-start.13 = (f32[64,512]{1,0:T(8,128)S(1)}, f32[64,512]{1,0:T(8,128)}, u32[]{:S(2)}) copy-start(f32[64,512]{1,0:T(8,128)} %get-tuple-element.166) | copy-start | bytes 393220
  708.7 9.4 %copy-start.15 = (f32[64,512]{1,0:T(8,128)S(1)}, f32[64,512]{1,0:T(8,128)}, u32[]{:S(2)}) copy-start(f32[64,512]{1,0:T(8,128)} %get-tuple-element.165) | copy-start | bytes 393220
  708.7 10.1 %copy-start.9 = (f32[9,64,128]{2,1,0:T(8,128)S(1)}, f32[9,64,128]{2,1,0:T(8,128)}, u32[]{:S(2)}) copy-start(f32[9,64,128]{2,1,0:T(8,128)} %get-tuple-element.164) | copy-start | bytes 884740
  708.7 10.1 %copy-start.10 = (f32[9,64,128]{2,1,0:T(8,128)S(1)}, f32[9,64,128]{2,1,0:T(8,128)}, u32[]{:S(2)}) copy-start(f32[9,64,128]{2,1,0:T(8,128)} %get-tuple-element.163) | copy-start | bytes 884740
  717.5 2.2 copy-start.4
  (3 other events, 4.8 us)
Sparse Core Ops, SparseCore 0:
  167.0 54.9 all-gather.4
  240.9 57.5 all-gather.6
  309.3 46.3 reduce-scatter.6
  360.6 49.8 reduce-scatter.4
  445.3 51.2 reduce-scatter.8
  498.8 43.1 reduce-scatter.10

commit v4 on v3

--- a/solution.py
+++ b/solution.py
@@ -653,36 +653,29 @@
     return call
 
 
-def weights_job(wr_ref, we_ref, layer, fulls, sems, blocks, parts):
-    part_send, part_recv, near_send, near_recv, pass_send, local_sem = sems
+def stripe_job(wr_ref, we_ref, layer, mine, sems, blocks, parts):
+    part_send, part_recv, local_sem = sems
     _, mid, feat = wr_ref.shape
     _, narrow, wide = we_ref.shape
-    cw, rw = feat // blocks, narrow // blocks
     blk, ch = lax.axis_index(BLK), lax.axis_index(CH)
-    sibling, peers = near_blocks(blocks)
 
     def cut(index, size):
         return pl.ds(pl.multiple_of(index * size, size), size)
 
     def source(array):
         if array == 0:
-            return wr_ref.at[layer, :, cut(blk, cw)]
-        return we_ref.at[layer, cut(blk, rw), :]
+            return wr_ref.at[layer, :, cut(blk, feat // blocks)]
+        return we_ref.at[layer, cut(blk, narrow // blocks), :]
 
     def share(array, part):
         if array == 0:
-            return fulls[0].at[cut(part, mid), cut(blk, cw)]
-        return fulls[1].at[cut(blk, rw), cut(part, wide)]
-
-    def stripe(array, block):
-        if array == 0:
-            return fulls[0].at[:, cut(block, cw)]
-        return fulls[1].at[cut(block, rw), :]
+            return mine[0].at[cut(part, mid), :]
+        return mine[1].at[:, cut(part, wide)]
 
     def own(array):
         return pltpu.make_async_copy(source(array), share(array, ch), local_sem.at[array])
 
-    def part_copy(array, step, peer, slot):
+    def copy(array, step, peer, slot):
         return remote(
             source(array),
             share(array, slot),
@@ -692,9 +685,53 @@
             peer,
         )
 
+    def start():
+        for array in range(2):
+            own(array).start()
+            for step, peer in enumerate(others(CH, parts)):
+                copy(array, step, peer, ch).start()
+
+    def finish():
+        for array in range(2):
+            for step, peer in enumerate(others(CH, parts)):
+                copy(array, step, peer, peer).wait_recv()
+            own(array).wait()
+            for step, peer in enumerate(others(CH, parts)):
+                copy(array, step, peer, ch).wait_send()
+
+    return start, finish
+
+
+def stripe_sems(parts):
+    dma = pltpu.SemaphoreType.DMA
+    return [dma((2, parts)), dma((2, parts)), dma((2,))]
+
+
+def stripe_shapes(parts, blocks, reduce_w, expand_w):
+    _, mid, feat = reduce_w.shape
+    narrow = mid * parts
+    return [
+        jax.ShapeDtypeStruct((narrow, feat // blocks), reduce_w.dtype),
+        jax.ShapeDtypeStruct((narrow // blocks, feat), expand_w.dtype),
+    ]
+
+
+def spread_job(mine, fulls, sems, blocks):
+    near_send, near_recv, pass_send, local_sem = sems
+    blk = lax.axis_index(BLK)
+    sibling, peers = near_blocks(blocks)
+    sizes = (mine[0].shape[1], mine[1].shape[0])
+
+    def stripe(array, block):
+        part = pl.ds(pl.multiple_of(block * sizes[array], sizes[array]), sizes[array])
+        return fulls[0].at[:, part] if array == 0 else fulls[1].at[part, :]
+
+    def own(array):
+        return pltpu.make_async_copy(mine[array], stripe(array, blk), local_sem.at[array])
+
     def near_copy(array, step, peer):
         return remote(
-            stripe(array, blk),
+            mine[array],
             stripe(array, blk),
             near_send.at[array, step],
             near_recv.at[array, blk],
@@ -715,14 +752,6 @@
     def start():
         for array in range(2):
             own(array).start()
-            for step, peer in enumerate(others(CH, parts)):
-                part_copy(array, step, peer, ch).start()
-
-    def spread():
-        for array in range(2):
-            for step, peer in enumerate(others(CH, parts)):
-                part_copy(array, step, peer, peer).wait_recv()
-            own(array).wait()
             for step, peer in enumerate(peers + [sibling]):
                 near_copy(array, step, peer).start()
 
@@ -736,27 +765,19 @@
         for array in range(2):
             for step in range(blocks // 2):
                 passing(array, 0, lax.rem(sibling + 2 * step, blocks)).wait_recv()
-            for step, peer in enumerate(others(CH, parts)):
-                part_copy(array, step, peer, ch).wait_send()
             for step, peer in enumerate(peers + [sibling]):
                 near_copy(array, step, peer).wait_send()
             for step, peer in enumerate(peers):
                 passing(array, step, peer).wait_send()
-
-    return start, spread, forward, finish
-
-
-def weights_sems(blocks, parts):
+            own(array).wait()
+
+    return start, forward, finish
+
+
+def spread_sems(blocks):
     dma = pltpu.SemaphoreType.DMA
     near = blocks // 2
-    return [
-        dma((2, parts)),
-        dma((2, parts)),
-        dma((2, near)),
-        dma((2, blocks)),
-        dma((2, near)),
-        dma((2,)),
-    ]
+    return [dma((2, near)), dma((2, blocks)), dma((2, near)), dma((2,))]
 
 
 def prologue_kernel(
@@ -769,6 +790,8 @@
     wide_ref,
     ids_ref,
     cur_ref,
+    mine_r,
+    mine_e,
     full_r,
     full_e,
     narrow_out,
@@ -790,9 +813,8 @@
     def lane_part(index):
         return cur_ref.at[:, pl.ds(pl.multiple_of(index * wide, wide), wide)]
 
-    start, spread, forward, finish = weights_job(
-        wr_ref, we_ref, 0, (full_r, full_e), sems, blocks, parts
-    )
+    start, gathered = stripe_job(wr_ref, we_ref, 0, (mine_r, mine_e), sems[:3], blocks, parts)
+    spread, forward, finish = spread_job((mine_r, mine_e), (full_r, full_e), sems[3:], blocks)
     own = pltpu.make_async_copy(feat_ref, lane_part(ch), local_sem.at[0])
     own.start()
     announce(
@@ -853,6 +875,7 @@
         small_own(place).start()
         for step, peer in enumerate(others(CH, parts)):
             small_copy(place, step, peer, ch).start()
+    gathered()
     spread()
 
     rows = own_ref.shape[1] // lanes
@@ -922,9 +945,10 @@
     return pl.pallas_call(
         functools.partial(prologue_kernel, blocks, parts),
         in_specs=[anywhere] * 5 + [inside],
-        out_specs=[anywhere] * 5 + [inside] * 2,
+        out_specs=[anywhere] * 7 + [inside] * 2,
         out_shape=[
             shape((pixels, feat), low),
+            *stripe_shapes(parts, blocks, reduce_w, expand_w),
             shape((narrow, feat), low),
             shape((narrow, feat), low),
             shape((parts,) + narrow_terms.shape, f32),
@@ -939,7 +963,8 @@
             dma((2, parts)),
             dma((3,)),
         ]
-        + weights_sems(blocks, parts),
+        + stripe_sems(parts)
+        + spread_sems(blocks),
         compiler_params=comm_params(5),
         cost_estimate=pl.CostEstimate(flops=10**6, bytes_accessed=10**8, transcendentals=0),
     )(features, reduce_w, expand_w, narrow_terms, wide_terms, ids)
@@ -1011,9 +1036,9 @@
     return start, finish
 
 
-def heads_forward_kernel(blocks, parts, fetch, main_ref, w_ref, mask_ref, *refs):
+def heads_forward_kernel(blocks, fetch, jobs, main_ref, w_ref, mask_ref, *refs):
     if fetch:
-        raw_r, raw_e, *refs = refs
+        mine_r, mine_e, *refs = refs
     pre_ref, act_ref, ends_ref, *refs = refs
     if fetch:
         full_r, full_e, *refs = refs
@@ -1033,27 +1058,25 @@
     )
     own = pltpu.make_async_copy(main_ref, ext_ref.at[pl.ds(cols, pixels)], local_sem.at[0])
     if fetch:
-        first, spread, forward, last = weights_job(
-            raw_r, raw_e, fetch, (full_r, full_e), sems, blocks, parts
-        )
+        spread, forward, last = spread_job((mine_r, mine_e), (full_r, full_e), sems, blocks)
 
     @pl.when(step == 0)
     def _():
         own.start()
-        if fetch:
-            greet(blocks, parts)
+        if fetch or jobs:
+            greet_blocks(blocks)
         else:
             greet_line(blocks)
         start()
         if fetch:
-            first()
+            spread()
+        for job in jobs:
+            job[0]()
         own.wait()
 
     @pl.when(step == 3)
     def _():
         finish()
-        if fetch:
-            spread()
 
     row_step = jnp.where(step < 3, 1, jnp.where(step < 6, 0, 2))
     col_step = lax.rem(step, 3)
@@ -1087,38 +1110,43 @@
             for array in range(2):
                 forward(array)
             last()
+        for job in jobs:
+            job[1]()
+        for job in jobs:
+            job[2]()
 
 
 def tap_at(step):
     return jnp.where(step < 3, step + 3, jnp.where(step < 6, step - 3, step))
 
 
-def heads_forward(blocks, parts, layer, cols, main, weights, mask, raw):
+def heads_forward(blocks, layer, jobs, cols, main, weights, mask, mine):
     _, head_count, _, mid, feat = weights.shape
     pixels = main.shape[0]
     f32, low = jnp.float32, jnp.bfloat16
     shape = jax.ShapeDtypeStruct
     anywhere = pl.BlockSpec(memory_space=pl.ANY)
     dma = pltpu.SemaphoreType.DMA
-    narrow = mid * parts
-    return pl.pallas_call(
-        functools.partial(heads_forward_kernel, blocks, parts, layer + 1 if raw else 0),
+    return job_call(
+        functools.partial(heads_forward_kernel, blocks, bool(mine)),
+        jobs,
+        blocks,
         grid=(9,),
         in_specs=[
             anywhere,
             pl.BlockSpec((1, head_count, 1, mid, feat), lambda t: (layer, 0, tap_at(t), 0, 0)),
             pl.BlockSpec((1, pixels, lanes), lambda t: (0, 0, 0)),
         ]
-        + [anywhere] * len(raw),
+        + [anywhere] * len(mine),
         out_specs=[whole((head_count, pixels, mid))] * 2
         + [whole((2, pixels, mid))]
-        + [anywhere] * len(raw),
+        + [anywhere] * len(mine),
         out_shape=[
             shape((head_count, pixels, mid), f32),
             shape((head_count, pixels, mid), low),
             shape((2, pixels, mid), low),
         ]
-        + [shape((narrow, feat), low)] * len(raw),
+        + [shape((mine[0].shape[0], feat), low) for _ in mine],
         scratch_shapes=[
             pltpu.VMEM((pixels + 2 * cols, feat), low),
             pltpu.VMEM((3, pixels, head_count * mid), f32),
@@ -1126,14 +1154,14 @@
             dma((2,)),
             dma((2,)),
         ]
-        + (weights_sems(blocks, parts) if raw else []),
+        + (spread_sems(blocks) if mine else []),
         compiler_params=comm_params(6 + layer),
         cost_estimate=pl.CostEstimate(
             flops=18 * pixels * head_count * mid * feat,
             bytes_accessed=18 * head_count * mid * feat,
             transcendentals=0,
         ),
-    )(main, weights, mask, *raw)
+    )(main, weights, mask, *mine)
 
 
 def fill_taps(im_ref, slot, grad, bits, pixels, cols, dilation):
@@ -1440,110 +1468,148 @@
     )(main, weights, mask)
 
 
-def weight_kernel(blocks, lists, load, store, jobs, before_ref, v_ref, after_ref, bits_ref, *refs):
-    count = len(lists)
-    g_refs, (out_ref, lhs_ref, *acc_refs) = refs[: len(refs) - 2 - count], refs[-2 - count :]
-    step = pl.program_id(0)
-    pixels, chans = v_ref.shape[2:]
-    cols = lanes
-    if jobs:
-
-        @pl.when(step == 0)
+class WeightChunks:
+    def __init__(self, blocks, layer, sources, gates, buffers, accs, lhs, sems):
+        self.blocks, self.layer = blocks, layer
+        (self.mv, self.cot, self.ends, self.hv, self.hg, self.bits) = sources
+        self.gain, self.bias = gates
+        (self.mv_buf, self.cot_buf, self.ends_buf, self.hv_buf, self.hg_buf, self.bits_buf) = buffers
+        self.accs, self.lhs, self.sems = accs, lhs, sems
+        self.done = 0
+        self.pixels = self.hv.shape[1]
+
+    def copies(self, heads, index):
+        pixels, last = self.pixels, self.blocks - 1
+        before, after = jnp.maximum(index - 1, 0), jnp.minimum(index + 1, last)
+        slot = lax.rem(index, 2)
+        values, buffer = (self.hv, self.hv_buf) if heads else (self.mv, self.mv_buf)
+        lead = () if heads else (slice(None),)
+        pairs = [
+            (
+                values.at[(before,) + lead + (pl.ds(pixels - lanes, lanes),)],
+                buffer.at[(slot,) + lead + (pl.ds(0, lanes),)],
+            ),
+            (values.at[index], buffer.at[(slot,) + lead + (pl.ds(lanes, pixels),)]),
+            (
+                values.at[(after,) + lead + (pl.ds(0, lanes),)],
+                buffer.at[(slot,) + lead + (pl.ds(lanes + pixels, lanes),)],
+            ),
+            (
+                self.bits.at[pl.ds(pl.multiple_of(index * pixels, pixels), pixels)],
+                self.bits_buf.at[slot],
+            ),
+        ]
+        if heads:
+            pairs.append((self.hg.at[index], self.hg_buf.at[slot]))
+        else:
+            pairs.append((self.cot.at[index], self.cot_buf.at[slot]))
+            pairs.append((self.ends.at[index], self.ends_buf.at[slot]))
+        return [
+            pltpu.make_async_copy(source, target, self.sems.at[slot, place])
+            for place, (source, target) in enumerate(pairs)
+        ]
+
+    def fetch(self, heads, index):
+        for copy in self.copies(heads, index):
+            copy.start()
+
+    def begin(self):
+        for acc in self.accs:
+            acc[...] = jnp.zeros(acc.shape, acc.dtype)
+        self.fetch(False, 0)
+
+    def add(self, heads, index):
+        slot = lax.rem(index, 2)
+        pixels = self.pixels
+        for copy in self.copies(heads, index):
+            copy.wait()
+
+        @pl.when(index + 1 < self.blocks)
         def _():
-            greet_blocks(blocks)
-            for job in jobs:
-                job[0]()
-
-    bits = bits_ref[...]
-    for index, members in enumerate(lists):
-        window = jnp.concatenate(
-            [before_ref[0, index], v_ref[0, index], after_ref[0, index]], axis=0
-        ).astype(jnp.float32)
-        size = window.shape[0]
-        shifted_by = (pltpu.roll(window, 1, 0), window, pltpu.roll(window, size - 1, 0))
-        for tap, (row_step, col_step) in enumerate(tap_offsets):
-            top = (1 + row_step) * cols
-            part = shifted_by[col_step + 1][top : top + pixels]
-            lhs_ref[:, tap * chans : (tap + 1) * chans] = masked(part, bits, tap).astype(
-                jnp.bfloat16
+            self.fetch(heads, index + 1)
+
+        if not heads:
+
+            @pl.when(index + 1 == self.blocks)
+            def _():
+                self.fetch(True, 0)
+
+        bits = self.bits_buf[slot]
+        for place, members in enumerate((tuple(range(4)),) if heads else group_pairs):
+            window = (self.hv_buf[slot] if heads else self.mv_buf[slot, place]).astype(jnp.float32)
+            size, chans = window.shape
+            shifted_by = (pltpu.roll(window, 1, 0), window, pltpu.roll(window, size - 1, 0))
+            for tap, (row_step, col_step) in enumerate(tap_offsets):
+                top = (1 + row_step) * lanes
+                part = shifted_by[col_step + 1][top : top + pixels]
+                self.lhs[:, tap * chans : (tap + 1) * chans] = masked(part, bits, tap).astype(
+                    jnp.bfloat16
+                )
+            if heads:
+                grads = [self.hg_buf[slot, member] for member in members]
+            else:
+                grads = [self.message_grad(slot, pair) for pair in members]
+            acc = self.accs[2] if heads else self.accs[place]
+            acc[...] += lax.dot_general(
+                self.lhs[:, : 9 * chans],
+                jnp.concatenate(grads, axis=1),
+                (((0,), (0,)), ((), ())),
+                preferred_element_type=jnp.float32,
             )
-        grads = jnp.concatenate([load(g_refs, member) for member in members], axis=1)
-        product = lax.dot_general(
-            lhs_ref[...], grads, (((0,), (0,)), ((), ())), preferred_element_type=jnp.float32
-        )
-        acc_ref = acc_refs[index]
-
-        @pl.when(step == 0)
-        def _(acc_ref=acc_ref, product=product):
-            acc_ref[...] = product
-
-        @pl.when(step > 0)
-        def _(acc_ref=acc_ref, product=product):
-            acc_ref[...] += product
-
-    @pl.when(step == blocks - 1)
-    def _():
-        store(out_ref, acc_refs)
-        for job in jobs:
-            job[1]()
-        for job in jobs:
-            job[2]()
-
-
-def weight_gradient(key, blocks, jobs, lists, load, store, out_shape, values, bits, grads, specs):
-    _, count, pixels, chans = values.shape
-    mid = out_shape[-1]
-    f32, low = jnp.float32, jnp.bfloat16
-    tail = pixels // lanes - 1
-    return job_call(
-        functools.partial(weight_kernel, blocks, lists, load, store),
+
+    def message_grad(self, slot, pair):
+        place = targets.index(message_pairs[pair][1])
+        gain = self.gain[self.layer, pair : pair + 1]
+        bias = self.bias[self.layer, pair : pair + 1]
+        gate = sigmoid(gain * self.ends_buf[slot, place].astype(jnp.float32) + bias)
+        return (self.cot_buf[slot, place].astype(jnp.float32) * gate).astype(jnp.bfloat16)
+
+    def run(self, count):
+        while count:
+            heads = self.done >= self.blocks
+            start = self.done % self.blocks
+            size = min(count, self.blocks - start)
+
+            def step(index, state):
+                self.add(heads, index)
+                return state
+
+            lax.fori_loop(start, start + size, step, 0)
+            self.done += size
+            count -= size
+
+
+def exchange_kernel(blocks, jobs, done_ref):
+    greet_blocks(blocks)
+    for job in jobs:
+        job[0]()
+    for job in jobs:
+        job[1]()
+    for job in jobs:
+        job[2]()
+    done_ref[...] = jnp.zeros(done_ref.shape, done_ref.dtype)
+
+
+def exchange(blocks, jobs):
+    _, moved = job_call(
+        functools.partial(exchange_kernel, blocks),
         jobs,
         blocks,
-        grid=(blocks,),
-        in_specs=[
-            pl.BlockSpec((1, count, lanes, chans), lambda i: (jnp.maximum(i - 1, 0), 0, tail, 0)),
-            pl.BlockSpec((1, count, pixels, chans), lambda i: (i, 0, 0, 0)),
-            pl.BlockSpec(
-                (1, count, lanes, chans), lambda i: (jnp.minimum(i + 1, blocks - 1), 0, 0, 0)
-            ),
-            pl.BlockSpec((pixels, lanes), lambda i: (i, 0)),
-        ]
-        + specs,
-        out_specs=[whole(out_shape)],
-        out_shape=[jax.ShapeDtypeStruct(out_shape, f32)],
-        scratch_shapes=[pltpu.VMEM((pixels, 9 * chans), low)]
-        + [pltpu.VMEM((9 * chans, len(entry) * mid), f32) for entry in lists],
-        compiler_params=comm_params(key)
-        if jobs
-        else pltpu.CompilerParams(vmem_limit_bytes=60 * 2**20),
-        cost_estimate=pl.CostEstimate(
-            flops=18 * chans * pixels * blocks * mid * sum(len(entry) for entry in lists),
-            bytes_accessed=10**7,
-            transcendentals=0,
-        ),
-    )(values, values, values, bits, *grads)
-
-
-def heads_load(refs, head):
-    return refs[0][0, head]
-
-
-def messages_load(layer):
-    def load(refs, pair):
-        cot_ref, feat_ref, gain_ref, bias_ref = refs
-        place = targets.index(message_pairs[pair][1])
-        gain, bias = gain_ref[layer, pair : pair + 1], bias_ref[layer, pair : pair + 1]
-        gate = sigmoid(gain * feat_ref[0, place].astype(jnp.float32) + bias)
-        return (cot_ref[0, 0, place].astype(jnp.float32) * gate).astype(jnp.bfloat16)
-
-    return load
-
-
-def heads_store(out_ref, acc_refs):
+        in_specs=[],
+        out_specs=[pl.BlockSpec(memory_space=pltpu.VMEM)],
+        out_shape=[jax.ShapeDtypeStruct((8, lanes), jnp.float32)],
+        scratch_shapes=[],
+        compiler_params=comm_params(30),
+        cost_estimate=pl.CostEstimate(flops=10**6, bytes_accessed=10**8, transcendentals=0),
+    )()
+    return moved
+
+
+def heads_store(out_ref, acc_ref):
     head_count, taps, chans, mid = out_ref.shape
     for head in range(head_count):
         for tap in range(taps):
-            out_ref[head, tap] = acc_refs[0][
+            out_ref[head, tap] = acc_ref[
                 tap * chans : (tap + 1) * chans, head * mid : (head + 1) * mid
             ]
 
@@ -1607,11 +1673,14 @@
     return finish
 
 
-def block_totals(first, second, stat_ref, send_sem, recv_sem, blocks):
+def block_totals(first, second, stat_ref, send_sem, recv_sem, blocks, meanwhile=None):
     me = lax.axis_index(BLK)
     stat_ref[me, 0:1] = first
     stat_ref[me, 1:2] = second
-    send_slots(lambda _: stat_ref.at[me], stat_ref, send_sem, recv_sem, BLK, blocks)()
+    finish = send_slots(lambda _: stat_ref.at[me], stat_ref, send_sem, recv_sem, BLK, blocks)
+    if meanwhile is not None:
+        meanwhile()
+    finish()
     total = stat_ref[0]
     for block in range(1, blocks):
         total = total + stat_ref[block]
@@ -1691,6 +1760,7 @@
 def trunk_forward_kernel(
     blocks,
     parts,
+    layer,
     fetch,
     jobs,
     cur_ref,
@@ -1722,13 +1792,10 @@
     ch = lax.axis_index(CH)
     pixel_count = float(pixels * blocks)
     greet(blocks, parts)
-    for job in jobs:
-        job[0]()
     if fetch:
-        start, spread, forward, finish = weights_job(
+        start, finish = stripe_job(
             raw_r, raw_e, fetch, (full_r, full_e), refs[16:], blocks, parts
         )
-        start()
 
     def terms(total, square):
         mean_value = total / pixel_count
@@ -1748,8 +1815,6 @@
         pre1_ref[part, :] = value * sigmoid(value)
         return state
 
-    if fetch:
-        spread()
     own_mid = pl.ds(pl.multiple_of(ch * mid, mid), mid)
     normed1_ref[...] = (pre1_ref[:, own_mid] - term1_ref[0:1, own_mid]) * term1_ref[1:2, own_mid]
     inverse1_ref[...] = term1_ref[1:2, own_mid]
@@ -1764,7 +1829,7 @@
         top = 2 * row_step * half
         product = contract_last(
             ext_ref[top : top + pixels, :],
-            wd_ref[3 * row_step : 3 * row_step + 3].reshape(3 * mid, parts * mid),
+            wd_ref[layer, 3 * row_step : 3 * row_step + 3].reshape(3 * mid, parts * mid),
         )
         for col_step in range(3):
             part = masked(
@@ -1797,8 +1862,12 @@
     wait_parts = send_slots(
         lambda _: gath_ref.at[ch], gath_ref, part_send, part_recv, CH, parts
     )
+    for job in jobs:
+        job[0]()
     ext_out_ref[...] = ext_ref[...]
     wait_parts()
+    if fetch:
+        start()
     for part in range(parts):
         full_ref[:, part * mid : (part + 1) * mid] = gath_ref[part]
     for part in range(parts):
@@ -1824,9 +1893,6 @@
 
     row_loop(pixels, 16, last, 0)
     own_wide = pl.ds(pl.multiple_of(ch * wide, wide), wide)
-    if fetch:
-        for array in range(2):
-            forward(array)
     for job in jobs:
         job[1]()
     normed3_ref[...] = (pre3_ref[:, own_wide] - term3_ref[0:1, own_wide]) * term3_ref[1:2, own_wide]
@@ -1851,7 +1917,7 @@
     anywhere = pl.BlockSpec(memory_space=pl.ANY)
     fetch = layer + 1 if raw else 0
     return job_call(
-        functools.partial(trunk_forward_kernel, blocks, parts, fetch),
+        functools.partial(trunk_forward_kernel, blocks, parts, layer, fetch),
         jobs,
         blocks,
         in_specs=[inside] * 11 + [anywhere] * len(raw),
@@ -1867,7 +1933,7 @@
             shape((pixels, wide), f32),
             shape((1, wide), f32),
         ]
-        + [shape((narrow, feat), low)] * len(raw),
+        + (stripe_shapes(parts, blocks, *raw) if raw else []),
         scratch_shapes=[
             pltpu.VMEM((pixels, narrow), f32),
             pltpu.VMEM((pixels, feat), f32),
@@ -1886,7 +1952,7 @@
             pltpu.SemaphoreType.DMA((parts,)),
             pltpu.SemaphoreType.DMA((parts,)),
         ]
-        + (weights_sems(blocks, parts) if raw else []),
+        + (stripe_sems(parts) if raw else []),
         compiler_params=comm_params(50 + layer),
         cost_estimate=pl.CostEstimate(
             flops=2 * pixels * (2 * narrow * feat + 9 * mid * narrow),
@@ -1908,67 +1974,45 @@
     return total
 
 
+plan = (2, 4, 2, 4, 1, 3)
+
+
 def trunk_backward_kernel(
     blocks,
     parts,
-    up_ref,
-    heads_ref,
-    cur_ref,
-    normed3_ref,
-    inverse3_ref,
-    gain3_ref,
-    bias3_ref,
-    we_ref,
-    full_ref,
-    normed2_ref,
-    inverse2_ref,
-    gain2_ref,
-    bias2_ref,
-    wd_ref,
-    mask_ref,
-    ext_ref,
-    normed1_ref,
-    inverse1_ref,
-    gain1_ref,
-    bias1_ref,
-    wr_ref,
-    gate_ref,
-    out_ref,
-    expand_ref,
-    dilated_ref,
-    reduce_ref,
-    wide_ref,
-    second_ref,
-    first_ref,
-    gate_out,
-    third_ref,
-    grad_ref,
-    im_ref,
-    send2_ref,
-    recv2_ref,
-    send1_ref,
-    recv1_ref,
-    gath_ref,
-    low_ref,
-    ex_send_ref,
-    ex_recv_ref,
-    di_send_ref,
-    di_recv_ref,
-    re_send_ref,
-    re_recv_ref,
-    stat3_ref,
-    stat2_ref,
-    stat1_ref,
-    gates_ref,
-    stat_send,
-    stat_recv,
-    halo_send,
-    halo_recv,
-    part_send,
-    part_recv,
-    sum_send,
-    sum_recv,
+    layer,
+    *refs,
 ):
+    up_ref, heads_ref, cur_ref, normed3_ref, inverse3_ref = refs[:5]
+    refs = refs[5:]
+    gain3_ref, bias3_ref, we_ref, full_ref, normed2_ref = refs[:5]
+    refs = refs[5:]
+    inverse2_ref, gain2_ref, bias2_ref, wd_ref, mask_ref = refs[:5]
+    refs = refs[5:]
+    ext_ref, normed1_ref, inverse1_ref, gain1_ref, bias1_ref = refs[:5]
+    refs = refs[5:]
+    wr_ref, gate_ref = refs[:2]
+    refs = refs[2:]
+    sources, gates, refs = refs[:6], refs[6:8], refs[8:]
+    out_ref, expand_ref, dilated_ref, reduce_ref, wide_ref = refs[:5]
+    refs = refs[5:]
+    second_ref, first_ref, gate_out = refs[:3]
+    refs = refs[3:]
+    messages_out, heads_out, *refs = refs
+    third_ref, grad_ref, im_ref, send2_ref, recv2_ref = refs[:5]
+    refs = refs[5:]
+    send1_ref, recv1_ref, gath_ref, low_ref, ex_send_ref = refs[:5]
+    refs = refs[5:]
+    ex_recv_ref, di_send_ref, di_recv_ref, re_send_ref, re_recv_ref = refs[:5]
+    refs = refs[5:]
+    stat3_ref, stat2_ref, stat1_ref, gates_ref, stat_send = refs[:5]
+    refs = refs[5:]
+    stat_recv, halo_send, halo_recv, part_send, part_recv = refs[:5]
+    refs = refs[5:]
+    sum_send, sum_recv = refs[:2]
+    refs = refs[2:]
+    buffers, accs, (lhs_ref, chunk_sem) = refs[:6], refs[6:9], refs[9:]
+    chunks = WeightChunks(blocks, layer, sources, gates, buffers, accs, lhs_ref, chunk_sem)
     pixels, wide = up_ref.shape
     mid = normed1_ref.shape[1]
     narrow = mid * parts
@@ -1980,6 +2024,7 @@
     pixel_count = float(pixels * blocks)
     low = jnp.bfloat16
     greet(blocks, parts)
+    chunks.begin()
     own_wide = pl.ds(pl.multiple_of(ch * wide, wide), wide)
     gates_ref[blk] = gate_ref[...]
     wait_gates = send_slots(
@@ -2004,6 +2049,7 @@
         stat_send.at[0],
         stat_recv.at[0],
         blocks,
+        lambda: chunks.run(plan[0]),
     )
     wide_ref[0:1] = gain_grad
     wide_ref[1:2] = bias_grad
@@ -2035,6 +2081,7 @@
     wait_expand = send_slots(
         lambda peer: ex_send_ref.at[peer], ex_recv_ref, sum_send.at[0], sum_recv.at[0], BLK, blocks
     )
+    chunks.run(plan[1])
     wait_parts()
 
     def narrow_norm(recv_ref, normed_ref, inverse_ref, gain_ref, bias_ref, stat_ref, phase, sums_ref):
@@ -2047,6 +2094,7 @@
             stat_send.at[phase],
             stat_recv.at[phase],
             blocks,
+            lambda: chunks.run(plan[2 * phase]),
         )
         sums_ref[0:1] = gain_grad
         sums_ref[1:2] = bias_grad
@@ -2087,7 +2135,7 @@
     wait_halo()
     fill_taps(im_ref, 0, grad_ref[...], mask_ref[1], pixels, half, 2)
     product = jnp.dot(
-        im_ref[0], wd_ref[...].reshape(9 * mid, narrow), preferred_element_type=jnp.float32
+        im_ref[0], wd_ref[layer].reshape(9 * mid, narrow), preferred_element_type=jnp.float32
     )
     for part in range(parts):
         send1_ref[part] = product[:, part * mid : (part + 1) * mid].astype(low)
@@ -2098,6 +2146,7 @@
     wait_dilated = send_slots(
         lambda peer: di_send_ref.at[peer], di_recv_ref, sum_send.at[1], sum_recv.at[1], BLK, blocks
     )
+    chunks.run(plan[3])
     wait_parts()
     grad = narrow_norm(
         recv1_ref, normed1_ref, inverse1_ref, gain1_ref, bias1_ref, stat1_ref, 2, first_ref
@@ -2116,10 +2165,14 @@
     wait_reduce = send_slots(
         lambda peer: re_send_ref.at[peer], re_recv_ref, sum_send.at[2], sum_recv.at[2], BLK, blocks
     )
+    chunks.run(plan[5])
     wait_parts()
     for part in range(parts):
         low_ref[:, part * mid : (part + 1) * mid] = gath_ref[part]
     out_ref[...] += jnp.dot(low_ref[...], wr_ref[:, own_wide], preferred_element_type=jnp.float32)
+    chunks.run(2 * blocks - chunks.done)
+    messages_store(messages_out, accs[:2])
+    heads_store(heads_out, accs[2])
     wait_gates()
     gate_out[...] = sum_slots(gates_ref, blocks)
     wait_expand()
@@ -2130,7 +2183,7 @@
     reduce_ref[...] = sum_slots(re_recv_ref, blocks)
 
 
-def trunk_backward(blocks, parts, operands):
+def trunk_backward(blocks, parts, layer, operands, sources, gates):
     pixels, wide = operands[0].shape
     feat = wide * parts
     mid = operands[9].shape[1]
@@ -2139,8 +2192,12 @@
     f32, low = jnp.float32, jnp.bfloat16
     shape = jax.ShapeDtypeStruct
     small, large = narrow // blocks, feat // blocks
+    inside = pl.BlockSpec(memory_space=pltpu.VMEM)
+    anywhere = pl.BlockSpec(memory_space=pl.ANY)
+    rows_two = pixels + 2 * lanes
     return pl.pallas_call(
-        functools.partial(trunk_backward_kernel, blocks, parts),
+        functools.partial(trunk_backward_kernel, blocks, parts, layer),
+        in_specs=[inside] * len(operands) + [anywhere] * len(sources) + [inside] * len(gates),
         out_shape=[
             shape((pixels, wide), f32),
             shape((small, wide), f32),
@@ -2150,6 +2207,8 @@
             shape((2, mid), f32),
             shape((2, mid), f32),
             shape(operands[-1].shape, f32),
+            shape((6, 9, small, mid), f32),
+            shape((4, 9, large, mid), f32),
         ],
         scratch_shapes=[
             pltpu.VMEM((pixels, wide), low),
@@ -2179,14 +2238,25 @@
             pltpu.SemaphoreType.DMA((3, parts)),
             pltpu.SemaphoreType.DMA((3, blocks)),
             pltpu.SemaphoreType.DMA((3, blocks)),
+            pltpu.VMEM((2, 2, rows_two, 2 * small), low),
+            pltpu.VMEM((2, 2, pixels, mid), low),
+            pltpu.VMEM((2, 2, pixels, mid), low),
+            pltpu.VMEM((2, rows_two, large), low),
+            pltpu.VMEM((2, 4, pixels, mid), low),
+            pltpu.VMEM((2, pixels, lanes), jnp.int32),
+            pltpu.VMEM((18 * small, len(group_pairs[0]) * mid), f32),
+            pltpu.VMEM((18 * small, len(group_pairs[1]) * mid), f32),
+            pltpu.VMEM((9 * large, 4 * mid), f32),
+            pltpu.VMEM((pixels, 9 * max(large, 2 * small)), low),
+            pltpu.SemaphoreType.DMA((2, 6)),
         ],
-        compiler_params=comm_params(2),
+        compiler_params=comm_params(60 + layer),
         cost_estimate=pl.CostEstimate(
-            flops=4 * pixels * (2 * narrow * wide + 9 * mid * narrow),
+            flops=4 * pixels * (2 * narrow * wide + 9 * mid * narrow) + 2 * 10**10,
             bytes_accessed=200 * 2**20,
             transcendentals=0,
         ),
-    )(*operands)
+    )(*operands, *sources, *gates)
 
 
 def gather_parts(values):
@@ -2240,23 +2310,24 @@
         jnp.concatenate([wide_gain, wide_bias], axis=0),
         canvas_ids,
     )
-    reduce_full, expand_full = [rest[0]], [rest[1]]
-    narrow_all, wide_all, bits, all_bits = rest[2:]
+    reduce_full, expand_full = [rest[2]], [rest[3]]
+    narrow_all, wide_all, bits, all_bits = rest[4:]
+    cotangents = task_cotangents.reshape(layers, 2, pixels, mid)
     narrow_all = narrow_all.transpose(1, 0, 2).reshape(2, layers, narrow)
     wide_all = wide_all.transpose(1, 0, 2).reshape(2, layers, feat)
 
     kept = []
     for layer in range(layers):
         keep = types.SimpleNamespace(input=current)
-        results, _ = trunk_forward(
+        results, (keep.cotangents,) = trunk_forward(
             blocks,
             parts,
             cols,
             layer,
-            [],
+            [(gather_kind, cotangents[layer])],
             current,
             reduce_full[layer],
-            dilated_t[layer],
+            dilated_t,
             expand_full[layer],
             bits,
             (
@@ -2267,7 +2338,7 @@
                 wide_all[0, layer][None],
                 wide_all[1, layer][None],
             ),
-            (),
+            (w_reduce, w_expand) if layer + 1 < layers else (),
         )
         (
             current,
@@ -2279,20 +2350,23 @@
             keep.inverse2,
             keep.normed3,
             keep.inverse3,
+            *mine,
         ) = results
         if layer:
             current, kept[-1].features = lax.optimization_barrier((current, kept[-1].features))
         keep.output = current
-        keep.heads_pre, features, keep.ends, *fetched = heads_forward(
+        (keep.heads_pre, features, keep.ends, *fetched), moved = heads_forward(
             blocks,
-            parts,
             layer,
+            [(swap_kind, kept[0].output)] if layer else [],
             cols,
             current,
             heads_t,
             bits,
-            (w_reduce, w_expand) if layer + 1 < layers else (),
-        )
+            mine,
+        )
+        if layer:
+            kept[0].values = moved[0]
         if fetched:
             reduce_full.append(fetched[0])
             expand_full.append(fetched[1])
@@ -2301,17 +2375,12 @@
         kept.append(keep)
     output = own_slice(current, wide, 1).reshape(rows, cols, wide)
 
-    cotangents = task_cotangents.reshape(layers, 2, pixels, mid)
     for layer in range(layers):
         keep = kept[layer]
-        if layer == 0:
-            jobs = [(gather_kind, cotangents), (gather_kind, keep.ends)]
-        else:
-            jobs = [(gather_kind, keep.ends), (swap_kind, kept[0].output)]
         (keep.maps, keep.local, keep.gate_sums, partial, keep.message_values), moved = messages_both(
             blocks,
             layer,
-            jobs,
+            [(gather_kind, keep.ends)] + ([] if layer else [(swap_kind, kept[1].output)]),
             cols,
             keep.features,
             messages_t,
@@ -2320,10 +2389,9 @@
             gate_bias,
             bits,
         )
+        keep.ends_all = moved[0]
         if layer == 0:
-            cotangents_all, keep.ends_all = moved
-        else:
-            keep.ends_all, kept[0].values = moved
+            kept[1].values = moved[1]
         keep.source_sums = reduce_parts(partial)
 
     def heads_low_of(keep):
@@ -2331,69 +2399,27 @@
         total = jnp.stack([sums[0] + keep.local[0], sums[1], sums[2], sums[3] + keep.local[1]])
         return (total * silu_slope(keep.heads_pre)).astype(low)
 
-    def messages_weight(layer, jobs):
-        keep = kept[layer]
-        (keep.messages_grad,), moved = weight_gradient(
-            30 + layer,
-            blocks,
-            jobs,
-            group_pairs,
-            messages_load(layer),
-            messages_store,
-            (6, 9, narrow // blocks, mid),
-            keep.message_values,
-            all_bits,
-            (cotangents_all, keep.ends_all, gate_gain, gate_bias),
-            [
-                pl.BlockSpec((1, 1, 2, pixels, mid), lambda i: (i, layer, 0, 0, 0)),
-                pl.BlockSpec((1, 2, pixels, mid), lambda i: (i, 0, 0, 0)),
-                whole(gate_gain.shape),
-                whole(gate_bias.shape),
-            ],
-        )
-        return moved
-
-    def heads_weight(layer, jobs):
-        keep = kept[layer]
-        (keep.heads_grad,), moved = weight_gradient(
-            40 + layer,
-            blocks,
-            jobs,
-            (tuple(range(4)),),
-            heads_load,
-            heads_store,
-            (4, 9, feat // blocks, mid),
-            keep.values[:, None],
-            all_bits,
-            (keep.heads_all,),
-            [pl.BlockSpec((1, 4, pixels, mid), lambda i: (i, 0, 0, 0))],
-        )
-        return moved
-
     for layer in range(layers):
         keep = kept[layer]
         keep.heads_low = heads_low_of(keep)
-        jobs = [(slot_kind, each.message_values) for each in kept] if layer == 0 else []
-        (partial,), moved = heads_backward(
-            blocks, layer, jobs, cols, keep.heads_low, heads_t, bits, parts
-        )
-        if layer == 0:
-            for each, values in zip(kept, moved):
-                each.message_values = values
+        (partial,), (keep.message_values,) = heads_backward(
+            blocks,
+            layer,
+            [(slot_kind, keep.message_values)],
+            cols,
+            keep.heads_low,
+            heads_t,
+            bits,
+            parts,
+        )
         keep.heads_partial = reduce_parts(partial)
         if layer + 1 < layers:
             kept[layer + 1].source_sums, partial = lax.optimization_barrier(
                 (kept[layer + 1].source_sums, partial)
             )
-    kept[0].message_values, partial = lax.optimization_barrier((kept[0].message_values, partial))
-    (kept[0].heads_all,) = messages_weight(0, [(gather_kind, kept[0].heads_low)])
-    kept[1].message_values, kept[0].heads_all = lax.optimization_barrier(
-        (kept[1].message_values, kept[0].heads_all)
-    )
-    (kept[1].heads_all,) = messages_weight(1, [(gather_kind, kept[1].heads_low)])
-    (kept[1].values,) = heads_weight(0, [(swap_kind, kept[1].output)])
-    kept[1].heads_partial, kept[0].heads_grad = lax.optimization_barrier(
-        (kept[1].heads_partial, kept[0].heads_grad)
+    kept[0].heads_low, partial = lax.optimization_barrier((kept[0].heads_low, partial))
+    kept[0].heads_all, kept[1].heads_all = exchange(
+        blocks, [(gather_kind, keep.heads_low) for keep in kept]
     )
 
     upstream = output_cotangent.reshape(pixels, wide).astype(jnp.float32)
@@ -2408,9 +2434,12 @@
             keep.second_sums,
             keep.first_sums,
             keep.gates,
+            keep.messages_grad,
+            keep.heads_grad,
         ) = trunk_backward(
             blocks,
             parts,
+            layer,
             (
                 upstream,
                 keep.heads_partial,
@@ -2425,7 +2454,7 @@
                 keep.inverse2,
                 norm_gain[layer, 1][None],
                 norm_bias[layer, 1][None],
-                dilated_t[layer],
+                dilated_t,
                 bits,
                 keep.first_ext,
                 keep.normed1,
@@ -2435,9 +2464,17 @@
                 reduce_full[layer],
                 keep.gate_sums,
             ),
-        )
-
-    heads_weight(1, [])
+            (
+                keep.message_values,
+                keep.cotangents,
+                keep.ends_all,
+                keep.values,
+                keep.heads_all,
+                all_bits,
+            ),
+            (gate_gain, gate_bias),
+        )
+
 
     def stacked(of):
         return jnp.stack([of(keep) for keep in kept])

time: 736 us -> 701 us (0.952)
  Pallas kernels: 660 us -> 601 us
  waiting for transfers between devices: 4.93 us -> 29.2 us
    pallas_call x4 -> x2, Pallas kernels: 195 us -> 148 us  [trunk_backward(): pl.pallas_call(functools.partial(trunk_backward_kernel, blocks, parts, la...]
    reduce_scatter x4, waiting for transfers between devices: 0.06 us -> 27.3 us  [reduce_parts(): return lax.psum_scatter(values, CH, scatter_dimension=0, tiled=False)]
    pallas_call x10 -> x9, Pallas kernels: 408 us -> 396 us  [call(): pl.pallas_call(wrapped, in_specs=list(in_specs) + [anywhere] * count, out...]
  transfers between devices with their start and end apart: 6 -> 6, of which waited for: 1 -> 3; matrix products, arithmetic and copies ran while one was open for 2% -> 1% of each run, Pallas kernels for 56% -> 46%
where the time goes in v4:
time: 701 us; the launch traced here: 693 us
  Pallas kernels  601 us (86%)
  waiting for transfers between devices  29.2 us (4%)
  other arithmetic  26.6 us (4%)
  local copies, waits for them, and re-layouts  20.6 us (3%)
  between operations  14.9 us (2%)
    pallas_call x9, Pallas kernels, call(): pl.pallas_call(wrapped, in_specs=list(in_specs) + [anywhere] * count, out...  396 us
    pallas_call x2, Pallas kernels, trunk_backward(): pl.pallas_call(functools.partial(trunk_backward_kernel, blocks, parts, la...  148 us
    pallas_call x1, Pallas kernels, prologue(): pl.pallas_call(functools.partial(prologue_kernel, blocks, parts), in_spec...  57.3 us
    reduce_scatter x4, waiting for transfers between devices, reduce_parts(): return lax.psum_scatter(values, CH, scatter_dimension=0, tiled=False)  27.3 us
    another operation x10, other arithmetic, stacked(): return jnp.stack([of(keep) for keep in kept])  18.8 us
  transfers between devices with their start and end apart: 6, of which 3 were waited for; matrix products, arithmetic and copies ran while one was open for 1% of the time, Pallas kernels for 46%

profile of v4, /device:TPU:0, one launch (start us, length us, event | category | flops | bytes accessed | tf_op | source)
XLA Modules:
  0.0 693.0 jit_solution(6077535200693839908)
XLA Ops:
  8.6 1.4 slice_bitcast_fusion.15
  10.0 1.9 fusion.6
  12.5 1.3 pad_maximum_fusion.6.wide_ref
  14.6 2.4 broadcast_in_dim.2.ids_ref
  16.9 57.3 %shard_map.254 = (bf16[512,2048]{1,0:T(8,128)(2,1)}, bf16[512,256]{1,0:T(8,128)(2,1)}, bf16[64,2048]{1,0:T(8,128)(2,1)}, bf16[512,2048]{1,0:T(8,128)(2,1)}, bf16...) custom-call(bf16[512,512]{1,0:T(8,128)(2,1)} %bitcast.121, ...), custom_call_target="tpu_custom_call" | custom-call | flops 1000000 | bytes 100000000 | tf_op jit(solution)/shard_map/pallas_call | solution.py:945
  77.1 49.4 %shard_map.255 = (bf16[512,2048]{1,0:T(8,128)(2,1)}, bf16[1024,512]{1,0:T(8,128)(2,1)}, bf16[512,512]{1,0:T(8,128)(2,1)}, f32[512,128]{1,0:T(8,128)}, f32[1,128]...) custom-call(bf16[512,2048]{1,0:T(8,128)(2,1)} %get-tuple-element.99., ...), custom_call_target="tpu_custom_call" | custom-call | flops 2751463424 | bytes 157286400 | tf_op jit(solution)/shard_map/pallas_call | solution.py:643
  126.5 43.1 %shard_map.256 = (f32[4,512,128]{2,1,0:T(8,128)}, bf16[4,512,128]{2,1,0:T(8,128)(2,1)}, bf16[2,512,128]{2,1,0:T(8,128)(2,1)}, bf16[512,2048]{1,0:T(8,128)(2,1)}, bf16[512,2048]{1,0:T(8,128)(2,1)}) custom-call(bf16[512,2048]{1,0:T(8,128)(2,1)} %get-tuple-element.109.refs_0_.refs_3_.refs_2_, bf16[2,4,9,128,2048]{4,3,2,1,0:T(8,128)(2,1)} %bitcast.104, ...), custom_call_target="tpu_custom_call" | custom-call | flops 9663676416 | bytes 18874368 | tf_op jit(solution)/shard_map/pallas_call | solution.py:643
  169.6 55.6 %shard_map.257 = (bf16[512,2048]{1,0:T(8,128)(2,1)}, bf16[1024,512]{1,0:T(8,128)(2,1)}, bf16[512,512]{1,0:T(8,128)(2,1)}, f32[512,128]{1,0:T(8,128)}, f32[1,128]...) custom-call(bf16[512,2048]{1,0:T(8,128)(2,1)} %get-tuple-element.109, ...), custom_call_target="tpu_custom_call" | custom-call | flops 2751463424 | bytes 157286400 | tf_op jit(solution)/shard_map/pallas_call | solution.py:643
  225.2 1.7 all-gather.5.cloned.1.call-done
  226.9 35.9 %shard_map.258 = (f32[4,512,128]{2,1,0:T(8,128)}, bf16[4,512,128]{2,1,0:T(8,128)(2,1)}, bf16[2,512,128]{2,1,0:T(8,128)(2,1)}, bf16[8,512,256]{2,1,0:T(8,128)(2,1)}) custom-call(bf16[512,2048]{1,0:T(8,128)(2,1)} %get-tuple-element.116.refs_0_.refs_7_, bf16[2,4,9,128,2048]{4,3,2,1,0:T(8,128)(2,1)} %bitcast.105, ...), custom_call_target="tpu_custom_call" | custom-call | flops 9663676416 | bytes 18874368 | tf_op jit(solution)/shard_map/pallas_call | solution.py:643
  264.2 56.9 %shard_map.259 = (bf16[2,512,128]{2,1,0:T(8,128)(2,1)}, f32[2,512,128]{2,1,0:T(8,128)}, f32[12,128]{1,0:T(8,128)}, bf16[4,4,512,128]{3,2,1,0:T(8,128)(2,1)}, bf1...) custom-call(bf16[4,4,512,128]{3,2,1,0:T(8,128)(2,1)} %bitcast.149, ...), custom_call_target="tpu_custom_call" | custom-call | flops 7247757312 | bytes 7077888 | tf_op jit(solution)/shard_map/pallas_call | solution.py:643
  321.2 37.5 %shard_map.260 = (bf16[2,512,128]{2,1,0:T(8,128)(2,1)}, f32[2,512,128]{2,1,0:T(8,128)}, f32[12,128]{1,0:T(8,128)}, bf16[4,4,512,128]{3,2,1,0:T(8,128)(2,1)}, bf1...) custom-call(bf16[4,4,512,128]{3,2,1,0:T(8,128)(2,1)} %bitcast.150, ...), custom_call_target="tpu_custom_call" | custom-call | flops 7247757312 | bytes 7077888 | tf_op jit(solution)/shard_map/pallas_call | solution.py:643
  358.9 14.5 %reduce-scatter.7.cloned.1.call-done = bf16[1,4,512,128]{3,2,1,0:T(8,128)(2,1)} async-done(((bf16[4,4,512,128]{3,2,1,0:T(8,128)(2,1)}), bf16[1,4,512,128]{3,2,1,0:T(8,128)(2,1)}) %reduce-scatter.7.cloned.1.call-update) | async-done | bytes 524304 | tf_op jit(solution)/shard_map/reduce_scatter | solution.py:2267
  373.4 1.1 convert_element_type.20
  374.7 1.2 fusion.refs_0_
  375.9 30.2 %shard_map.261 = (bf16[4,512,512]{2,1,0:T(8,128)(2,1)}, bf16[8,2,512,128]{3,2,1,0:T(8,128)(2,1)}) custom-call(bf16[4,512,128]{2,1,0:T(8,128)(2,1)} %fusion.refs_0_, bf16[2,4,9,128,2048]{4,3,2,1,0:T(8,128)(2,1)} %bitcast.106, s32[2,512,128]{2,1,0:T(8,128)} %get-tuple-element.102.refs_4_.refs_2_.refs_5_.refs_14_, ...), custom_call_target="tpu_custom_call" | custom-call | flops 9663676416 | bytes 18874368 | tf_op jit(solution)/shard_map/pallas_call | solution.py:643
  406.2 12.8 %reduce-scatter.5.cloned.1.call-done = bf16[1,4,512,128]{3,2,1,0:T(8,128)(2,1)} async-done(((bf16[4,4,512,128]{3,2,1,0:T(8,128)(2,1)}), bf16[1,4,512,128]{3,2,1,0:T(8,128)(2,1)}) %reduce-scatter.5.cloned.1.call-update) | async-done | bytes 524304 | tf_op jit(solution)/shard_map/reduce_scatter | solution.py:2267
  418.9 1.1 slice.204
  420.0 1.1 convert_element_type.22
  421.2 1.2 fusion.1.refs_0_.refs_1_
  422.4 29.7 %shard_map.262 = (bf16[4,512,512]{2,1,0:T(8,128)(2,1)}, bf16[8,2,512,128]{3,2,1,0:T(8,128)(2,1)}) custom-call(bf16[4,512,128]{2,1,0:T(8,128)(2,1)} %fusion.1.refs_0_.refs_1_, bf16[2,4,9,128,2048]{4,3,2,1,0:T(8,128)(2,1)} %bitcast.107, s32[2,512,128]{2,1,0:T(8,128)} %get-tuple-element.102.refs_4_.refs_2_.refs_5_.refs_14_, ...), custom_call_target="tpu_custom_call" | custom-call | flops 9663676416 | bytes 18874368 | tf_op jit(solution)/shard_map/pallas_call | solution.py:643
  453.4 1.0 slice_bitcast_fusion.1
  454.4 1.1 bitcast_convert_fusion.refs_0_
  455.6 1.9 constant_dynamic-slice_fusion
  458.3 57.4 %shard_map.263 = (f32[8,128]{1,0:T(8,128)}, bf16[8,4,512,128]{3,2,1,0:T(8,128)(2,1)}, bf16[8,4,512,128]{3,2,1,0:T(8,128)(2,1)}) custom-call(bf16[4,512,128]{2,1,0:T(8,128)(2,1)} %fusion.refs_0_, bf16[4,512,128]{2,1,0:T(8,128)(2,1)} %fusion.1.refs_0_.refs_1_), custom_call_target="tpu_custom_call" | custom-call | flops 1000000 | bytes 100000000 | tf_op jit(solution)/shard_map/pallas_call | solution.py:643
  515.7 79.0 %shard_map.264 = (f32[512,512]{1,0:T(8,128)}, f32[64,512]{1,0:T(8,128)}, f32[9,64,128]{2,1,0:T(8,128)}, f32[256,128]{1,0:T(8,128)}, f32[2,512]{1,0:T(2,128)}, /*...) custom-call(f32[512,512]{1,0:T(8,128)} %bitcast_convert_fusion.refs_, ...), custom_call_target="tpu_custom_call" | custom-call | flops 22281701376 | bytes 209715200 | tf_op jit(solution)/shard_map/pallas_call | solution.py:2198
  594.8 68.9 %shard_map.265 = (f32[512,512]{1,0:T(8,128)}, f32[64,512]{1,0:T(8,128)}, f32[9,64,128]{2,1,0:T(8,128)}, f32[256,128]{1,0:T(8,128)}, f32[2,512]{1,0:T(2,128)}, /*...) custom-call(f32[512,512]{1,0:T(8,128)} %get-tuple-element.150.refs_0, ...), custom_call_target="tpu_custom_call" | custom-call | flops 22281701376 | bytes 209715200 | tf_op jit(solution)/shard_map/pallas_call | solution.py:2198
  667.7 1.6 pad_maximum_fusion.4
  670.6 1.6 pad_maximum_fusion.5
  672.2 1.8 pad_maximum_fusion.2
  674.0 3.8 pad_maximum_fusion.1
  677.8 7.0 %pad_maximum_fusion = f32[2,4,9,256,128]{4,3,2,1,0:T(8,128)} fusion(f32[1,4,9,256,128]{4,3,2,1,0:T(8,128)S(1)} %bitcast.108, f32[1,4,9,256,128]{4,3,2,1,0:T(8,128)} %bitcast.109), kind=kLoop, calls=%fused_computation | loop fusion | flops 2359296 | bytes 18874368 | tf_op jit(solution)/shard_map/stack | solution.py:2480
  (90 shorter events, 15.7 us)
Async XLA Ops:
  7.2 219.7 %all-gather.5.cloned.1.call-start = ((), (), s32[]{:S(2)}) async-start(), calls=%async_computation.8 | async-start | bytes 2621440 | tf_op jit(solution)/shard_map/all_gather | solution.py:2263
  169.6 151.5 %all-gather.7.cloned.1.call-start = ((), (), s32[]{:S(2)}) async-start(), calls=%async_computation.9 | async-start | bytes 2621440 | tf_op jit(solution)/shard_map/all_gather | solution.py:2263
  226.9 36.0 %copy-start.17 = (f32[2,6,128]{2,0,1:T(2,128)S(1)}, f32[2,6,128]{2,0,1:T(2,128)}, u32[]{:S(2)}) copy-start(f32[2,6,128]{2,0,1:T(2,128)} %param.25) | copy-start | bytes 18436
  226.9 36.6 %copy-start.18 = (f32[2,6,128]{2,0,1:T(2,128)S(1)}, f32[2,6,128]{2,0,1:T(2,128)}, u32[]{:S(2)}) copy-start(f32[2,6,128]{2,0,1:T(2,128)} %param.26) | copy-start | bytes 18436
  262.9 110.5 %reduce-scatter.7.cloned.1.call-start = ((), (), s32[]{:S(2)}) async-start(), calls=%async_computation.5 | async-start | bytes 2621440 | tf_op jit(solution)/shard_map/reduce_scatter | solution.py:2267
  321.1 97.8 %reduce-scatter.5.cloned.1.call-start = ((), (), s32[]{:S(2)}) async-start(), calls=%async_computation.4 | async-start | bytes 2621440 | tf_op jit(solution)/shard_map/reduce_scatter | solution.py:2267
  358.6 16.0 %copy-start.7 = (f32[2,512,128]{2,1,0:T(8,128)S(1)}, f32[2,512,128]{2,1,0:T(8,128)}, u32[]{:S(2)}) copy-start(f32[2,512,128]{2,1,0:T(8,128)} %get-tuple-element.125) | copy-start | bytes 1572868
  358.7 16.0 %copy-start.3 = (f32[4,512,128]{2,1,0:T(8,128)S(1)}, f32[4,512,128]{2,1,0:T(8,128)}, u32[]{:S(2)}) copy-start(f32[4,512,128]{2,1,0:T(8,128)} %get-tuple-element.126) | copy-start | bytes 3145732
  358.7 157.0 %reduce-scatter.9.cloned.1.call-start = ((), (), s32[]{:S(2)}) async-start(), calls=%async_computation.6 | async-start | bytes 2621440 | tf_op jit(solution)/shard_map/reduce_scatter | solution.py:2267
  406.1 15.0 %copy-start.8 = (f32[2,512,128]{2,1,0:T(8,128)S(1)}, f32[2,512,128]{2,1,0:T(8,128)}, u32[]{:S(2)}) copy-start(f32[2,512,128]{2,1,0:T(8,128)} %get-tuple-element.130) | copy-start | bytes 1572868
  418.9 2.3 copy-start.4
  452.1 0.7 copy-start.14
  452.1 0.7 copy-start.15
  452.1 1.3 copy-start
  452.2 2.3 copy-start.6
  452.2 142.6 %reduce-scatter.11.cloned.1.call-start = ((), (), s32[]{:S(2)}) async-start(), calls=%async_computation.7 | async-start | bytes 2621440 | tf_op jit(solution)/shard_map/reduce_scatter | solution.py:2267
  453.4 4.1 copy-start.10
  453.4 4.1 copy-start.11
  594.8 68.9 %copy-start.19 = (f32[2,512]{1,0:T(2,128)S(1)}, f32[2,512]{1,0:T(2,128)}, u32[]{:S(2)}) copy-start(f32[2,512]{1,0:T(2,128)} %get-tuple-element.181) | copy-start | bytes 12292
  594.8 71.7 %copy-start.16 = (f32[12,128]{1,0:T(8,128)S(1)}, f32[12,128]{1,0:T(8,128)}, u32[]{:S(2)}) copy-start(f32[12,128]{1,0:T(8,128)} %get-tuple-element.183) | copy-start | bytes 18436
  594.8 72.9 %copy-start.13 = (f32[256,128]{1,0:T(8,128)S(1)}, f32[256,128]{1,0:T(8,128)}, u32[]{:S(2)}) copy-start(f32[256,128]{1,0:T(8,128)} %get-tuple-element.167) | copy-start | bytes 393220
  594.8 75.2 %copy-start.20 = (f32[2,128]{1,0:T(2,128)S(1)}, f32[2,128]{1,0:T(2,128)}, u32[]{:S(2)}) copy-start(f32[2,128]{1,0:T(2,128)} %get-tuple-element.179) | copy-start | bytes 3076
  594.8 75.2 %copy-start.21 = (f32[2,128]{1,0:T(2,128)S(1)}, f32[2,128]{1,0:T(2,128)}, u32[]{:S(2)}) copy-start(f32[2,128]{1,0:T(2,128)} %get-tuple-element.178) | copy-start | bytes 3076
  594.8 75.8 %copy-start.12 = (f32[64,512]{1,0:T(8,128)S(1)}, f32[64,512]{1,0:T(8,128)}, u32[]{:S(2)}) copy-start(f32[64,512]{1,0:T(8,128)} %get-tuple-element.171) | copy-start | bytes 393220
  594.8 77.4 %copy-start.9 = (f32[9,64,128]{2,1,0:T(8,128)S(1)}, f32[9,64,128]{2,1,0:T(8,128)}, u32[]{:S(2)}) copy-start(f32[9,64,128]{2,1,0:T(8,128)} %get-tuple-element.169) | copy-start | bytes 884740
  663.7 10.3 %copy-start.2 = (f32[6,9,64,128]{3,2,1,0:T(8,128)S(1)}, f32[6,9,64,128]{3,2,1,0:T(8,128)}, u32[]{:S(2)}) copy-start(f32[6,9,64,128]{3,2,1,0:T(8,128)} %get-tuple-element.175) | copy-start | bytes 5308420
  674.0 3.8 copy-start.1
  677.8 7.0 %copy-start.5 = (f32[512,512]{1,0:T(8,128)S(1)}, f32[512,512]{1,0:T(8,128)}, u32[]{:S(2)}) copy-start(f32[512,512]{1,0:T(8,128)} %get-tuple-element.165) | copy-start | bytes 3145732
Sparse Core Ops, SparseCore 0:
  169.7 57.1 all-gather.4
  263.0 56.4 all-gather.6
  321.8 51.5 reduce-scatter.6
  375.7 43.1 reduce-scatter.4
  452.3 46.7 reduce-scatter.8
  501.4 51.5 reduce-scatter.10

commit v5 on v4

--- a/solution.py
+++ b/solution.py
@@ -498,10 +498,13 @@
     pl.semaphore_wait(barrier, len(targets))
 
 
-def near_blocks(blocks):
+def near_blocks():
     me = lax.axis_index(BLK)
-    sibling = me + 1 - 2 * lax.rem(me, 2)
-    return sibling, [lax.rem(me + 2 * step, blocks) for step in range(1, blocks // 2)]
+
+    def turned(bit):
+        return me + bit - 2 * bit * lax.rem(me // bit, 2)
+
+    return turned(1), turned(2), turned(4)
 
 
 def others(axis, count):
@@ -509,43 +512,69 @@
     return [lax.rem(me + step, count) for step in range(1, count)]
 
 
-def gather_job(source, target, sems, blocks):
+def round_trip(own_source, target_of, half_of, sems):
     near_send, slot_recv, pass_send, local_sem = sems
     me = lax.axis_index(BLK)
-    sibling, peers = near_blocks(blocks)
-    own = pltpu.make_async_copy(source, target.at[me], local_sem.at[0])
+    sibling, *peers = near_blocks()
+    far = me + peers[0] - me + peers[1] - me
+    own = pltpu.make_async_copy(own_source, target_of(me), local_sem.at[0])
 
     def near(step, peer):
         return remote(
-            source, target.at[me], near_send.at[step], slot_recv.at[me], BLK, peer
-        )
-
-    def passing(step, peer):
-        return remote(
-            target.at[peer], target.at[peer], pass_send.at[step], slot_recv.at[peer], BLK, sibling
-        )
+            own_source, target_of(me), near_send.at[step], slot_recv.at[me], BLK, peer
+        )
+
+    def half(side, block, recv_sem, peer):
+        part = half_of(block, side)
+        return remote(part, part, near_send.at[3 + side], recv_sem, BLK, peer)
+
+    def passing(step, block):
+        part = target_of(block)
+        return remote(part, part, pass_send.at[step], slot_recv.at[block], BLK, sibling)
 
     def start():
         own.start()
         for step, peer in enumerate(peers + [sibling]):
             near(step, peer).start()
 
+    def sent_half(side):
+        recv_sem = slot_recv.at[peers[0]] if side == 0 else local_sem.at[1]
+        return half(side, peers[side], recv_sem, peers[1 - side])
+
+    def middle():
+        for side in range(2):
+            copy = passing(side, peers[side])
+            copy.wait_recv()
+            sent_half(side).start()
+            copy.start()
+
     def forward():
-        for step, peer in enumerate(peers):
-            copy = passing(step, peer)
-            copy.wait_recv()
-            copy.start()
+        half(0, far, slot_recv.at[far], sibling).wait_recv()
+        half(1, far, local_sem.at[1], sibling).wait_recv()
+        passing(2, far).start()
 
     def finish():
-        for step in range(blocks // 2):
-            passing(0, lax.rem(sibling + 2 * step, blocks)).wait_recv()
+        for block in (sibling, sibling + peers[0] - me, sibling + peers[1] - me, sibling + far - me):
+            passing(0, block).wait_recv()
         for step, peer in enumerate(peers + [sibling]):
             near(step, peer).wait_send()
-        for step, peer in enumerate(peers):
-            passing(step, peer).wait_send()
+        for side in range(2):
+            sent_half(side).wait_send()
+            passing(side, peers[side]).wait_send()
+        passing(2, far).wait_send()
         own.wait()
 
-    return start, forward, finish
+    return start, middle, forward, finish
+
+
+def gather_job(source, target, sems, blocks):
+    count = source.shape[0] // 2
+    return round_trip(
+        source,
+        lambda block: target.at[block],
+        lambda block, side: target.at[block, pl.ds(side * count, count)],
+        sems,
+    )
 
 
 def swap_job(source, target, sems, blocks):
@@ -574,7 +603,7 @@
             copy(step, peer, me).wait_send()
         own.wait()
 
-    return start, lambda: None, finish
+    return start, lambda: None, lambda: None, finish
 
 
 def slot_job(source, target, sems, blocks):
@@ -598,26 +627,89 @@
             copy(step, peer, me).wait_send()
         own.wait()
 
-    return start, lambda: None, finish
-
-
-job_kinds = (gather_job, swap_job, slot_job)
-gather_kind, swap_kind, slot_kind = 0, 1, 2
-
-
-def job_target(kind, source, blocks):
+    return start, lambda: None, lambda: None, finish
+
+
+def line_job(source, target, sems, blocks):
+    line_send, line_recv, _, local_sem = sems
+    parts = target.shape[0]
+    ch = lax.axis_index(CH)
+    right, left = lax.rem(ch + 1, parts), lax.rem(ch + parts - 1, parts)
+    own = pltpu.make_async_copy(source, target.at[ch], local_sem.at[0])
+
+    def sides(hop):
+        return (
+            (0, lax.rem(ch + parts - hop, parts), right, ch - hop >= 0, ch < parts - 1),
+            (1, lax.rem(ch + hop, parts), left, ch + hop < parts, ch > 0),
+        )
+
+    def copy(block, side, hop, peer):
+        return remote(
+            source if hop == 0 else target.at[block],
+            target.at[block],
+            line_send.at[side * (parts - 1) + hop],
+            line_recv.at[block],
+            CH,
+            peer,
+        )
+
+    def move(hop):
+        for side, block, peer, valid, goes in sides(hop):
+            if hop > 0:
+
+                @pl.when(valid)
+                def _():
+                    copy(block, side, hop, peer).wait_recv()
+
+            if hop < parts - 1:
+
+                @pl.when(valid & goes)
+                def _():
+                    copy(block, side, hop, peer).start()
+
+    def start():
+        own.start()
+        move(0)
+
+    def middle():
+        move(1)
+
+    def forward():
+        for hop in range(2, parts - 1):
+            move(hop)
+
+    def finish():
+        if parts > 2:
+            move(parts - 1)
+        for hop in range(parts - 1):
+            for side, block, peer, valid, goes in sides(hop):
+
+                @pl.when(valid & goes)
+                def _():
+                    copy(block, side, hop, peer).wait_send()
+
+        own.wait()
+
+    return start, middle, forward, finish
+
+
+job_kinds = (gather_job, swap_job, slot_job, line_job)
+gather_kind, swap_kind, slot_kind, line_kind = 0, 1, 2, 3
+
+
+def job_target(kind, shape, dtype, blocks):
     if kind == gather_kind:
-        return jax.ShapeDtypeStruct((blocks,) + source.shape, source.dtype)
-    if kind == slot_kind:
-        return jax.ShapeDtypeStruct(source.shape, source.dtype)
-    return jax.ShapeDtypeStruct(
-        (blocks, source.shape[0], source.shape[1] // blocks), source.dtype
-    )
+        shape = (blocks,) + shape
+    elif kind == line_kind:
+        shape = (lax.axis_size(CH),) + shape
+    elif kind == swap_kind:
+        shape = (blocks, shape[0], shape[1] // blocks)
+    return jax.ShapeDtypeStruct(shape, dtype)
 
 
 def job_sems(blocks):
     dma = pltpu.SemaphoreType.DMA
-    return [dma((blocks,)), dma((blocks,)), dma((blocks,)), dma((1,))]
+    return [dma((blocks,)), dma((blocks,)), dma((blocks,)), dma((2,))]
 
 
 def job_call(kernel, jobs, blocks, in_specs, out_specs, out_shape, scratch_shapes, **options):
@@ -633,9 +725,12 @@
         scratch, sems = refs[:n_scratch], refs[n_scratch:]
         running = [
             job_kinds[kind](
-                sources[place], targets[place], sems[4 * place : 4 * place + 4], blocks
+                sources[place].at[index[0]] if index else sources[place],
+                targets[place],
+                sems[4 * place : 4 * place + 4],
+                blocks,
             )
-            for place, (kind, _) in enumerate(jobs)
+            for place, (kind, _, *index) in enumerate(jobs)
         ]
         kernel(running, *ins, *outs, *scratch)
 
@@ -644,10 +739,13 @@
             wrapped,
             in_specs=list(in_specs) + [anywhere] * count,
             out_specs=list(out_specs) + [anywhere] * count,
-            out_shape=list(out_shape) + [job_target(kind, source, blocks) for kind, source in jobs],
+            out_shape=list(out_shape) + [
+                job_target(kind, source.shape[len(index) :], source.dtype, blocks)
+                for kind, source, *index in jobs
+            ],
             scratch_shapes=list(scratch_shapes) + job_sems(blocks) * count,
             **options,
-        )(*operands, *[source for _, source in jobs])
+        )(*operands, *[job[1] for job in jobs])
         return result[:n_out], result[n_out:]
 
     return call
@@ -716,68 +814,28 @@
     ]
 
 
-def spread_job(mine, fulls, sems, blocks):
-    near_send, near_recv, pass_send, local_sem = sems
-    blk = lax.axis_index(BLK)
-    sibling, peers = near_blocks(blocks)
-    sizes = (mine[0].shape[1], mine[1].shape[0])
-
-    def stripe(array, block):
-        part = pl.ds(pl.multiple_of(block * sizes[array], sizes[array]), sizes[array])
-        return fulls[0].at[:, part] if array == 0 else fulls[1].at[part, :]
-
-    def own(array):
-        return pltpu.make_async_copy(mine[array], stripe(array, blk), local_sem.at[array])
-
-    def near_copy(array, step, peer):
-        return remote(
-            mine[array],
-            stripe(array, blk),
-            near_send.at[array, step],
-            near_recv.at[array, blk],
-            BLK,
-            peer,
-        )
-
-    def passing(array, step, peer):
-        return remote(
-            stripe(array, peer),
-            stripe(array, peer),
-            pass_send.at[array, step],
-            near_recv.at[array, peer],
-            BLK,
-            sibling,
-        )
-
-    def start():
-        for array in range(2):
-            own(array).start()
-            for step, peer in enumerate(peers + [sibling]):
-                near_copy(array, step, peer).start()
-
-    def forward(array):
-        for step, peer in enumerate(peers):
-            copy = passing(array, step, peer)
-            copy.wait_recv()
-            copy.start()
-
-    def finish():
-        for array in range(2):
-            for step in range(blocks // 2):
-                passing(array, 0, lax.rem(sibling + 2 * step, blocks)).wait_recv()
-            for step, peer in enumerate(peers + [sibling]):
-                near_copy(array, step, peer).wait_send()
-            for step, peer in enumerate(peers):
-                passing(array, step, peer).wait_send()
-            own(array).wait()
-
-    return start, forward, finish
-
-
-def spread_sems(blocks):
-    dma = pltpu.SemaphoreType.DMA
-    near = blocks // 2
-    return [dma((2, near)), dma((2, blocks)), dma((2, near)), dma((2,))]
+def spread_jobs(mine, fulls, sems, blocks):
+    half_rows = mine[0].shape[0] // 2
+    width, height = mine[0].shape[1], mine[1].shape[0]
+    half_cols = mine[1].shape[1] // 2
+
+    def cut(index, size):
+        return pl.ds(pl.multiple_of(index * size, size), size)
+
+    return [
+        round_trip(
+            mine[0],
+            lambda block: fulls[0].at[:, cut(block, width)],
+            lambda block, side: fulls[0].at[pl.ds(side * half_rows, half_rows), cut(block, width)],
+            sems[:4],
+        ),
+        round_trip(
+            mine[1],
+            lambda block: fulls[1].at[cut(block, height), :],
+            lambda block, side: fulls[1].at[cut(block, height), pl.ds(side * half_cols, half_cols)],
+            sems[4:],
+        ),
+    ]
 
 
 def prologue_kernel(
@@ -786,40 +844,24 @@
     feat_ref,
     wr_ref,
     we_ref,
-    narrow_ref,
-    wide_ref,
-    ids_ref,
-    cur_ref,
-    mine_r,
-    mine_e,
-    full_r,
-    full_e,
-    narrow_out,
-    wide_out,
-    own_ref,
-    all_ref,
-    line_send,
-    line_recv,
-    small_send,
-    small_recv,
-    local_sem,
-    *sems,
+    *refs,
 ):
+    small_refs, ids_ref, cur_ref, mine_r, mine_e = refs[:4], *refs[4:8]
+    full_r, full_e, small_outs, own_ref, all_ref = *refs[8:10], refs[10:14], *refs[14:16]
+    line_send, line_recv, small_send, small_recv, local_sem, *sems = refs[16:]
     pixels, wide = feat_ref.shape
     blk, ch = lax.axis_index(BLK), lax.axis_index(CH)
-    sibling, peers = near_blocks(blocks)
-    smalls = ((narrow_ref, narrow_out), (wide_ref, wide_out))
+    smalls = tuple(zip(small_refs, small_outs))
 
     def lane_part(index):
         return cur_ref.at[:, pl.ds(pl.multiple_of(index * wide, wide), wide)]
 
     start, gathered = stripe_job(wr_ref, we_ref, 0, (mine_r, mine_e), sems[:3], blocks, parts)
-    spread, forward, finish = spread_job((mine_r, mine_e), (full_r, full_e), sems[3:], blocks)
+    jobs = spread_jobs((mine_r, mine_e), (full_r, full_e), sems[3:], blocks)
     own = pltpu.make_async_copy(feat_ref, lane_part(ch), local_sem.at[0])
     own.start()
     announce(
-        [(CH, peer) for peer in others(CH, parts)]
-        + [(BLK, peer) for peer in [sibling] + peers]
+        [(CH, peer) for peer in others(CH, parts)] + [(BLK, peer) for peer in near_blocks()]
     )
     start()
 
@@ -871,51 +913,59 @@
         return pltpu.make_async_copy(source, target.at[ch], local_sem.at[1 + place])
 
     line_hop(0)
-    for place in range(2):
+    for place in range(4):
         small_own(place).start()
         for step, peer in enumerate(others(CH, parts)):
             small_copy(place, step, peer, ch).start()
     gathered()
-    spread()
+    for job in jobs:
+        job[0]()
 
     rows = own_ref.shape[1] // lanes
-
-    def same(row, row_move, col_move, other_move):
-        here = ids_ref[row, 4 + other_move : 4 + other_move + lanes, :]
-        there = ids_ref[row + row_move, 4 + col_move : 4 + col_move + lanes, :]
-        return here, here == there
+    lane = lax.broadcasted_iota(jnp.int32, (1, lanes), 1)
+
+    def moved(values, step):
+        turned = values if step == 0 else pltpu.roll(values, (lanes - step) % lanes, 1)
+        return jnp.where((lane + step >= 0) & (lane + step < lanes), turned, -2)
+
+    def spread(target, row, bits):
+        block = jnp.broadcast_to(bits.astype(jnp.float32), (lanes, lanes)).T
+        target[pl.ds(pl.multiple_of(row * lanes, lanes), lanes), :] = block.astype(jnp.int32)
 
     def own_row(row, state):
         place = 2 + blk * rows + row
         for word, reach in enumerate((1, 2)):
-            bits = jnp.zeros((lanes, lanes), jnp.int32)
+            bits = jnp.zeros((1, lanes), jnp.int32)
             for tap, (row_step, col_step) in enumerate(tap_offsets):
                 a, b = row_step * reach, col_step * reach
-                here, equal = same(place, a, 0, -b)
-                bits = bits | jnp.where(equal & (here >= 0), 1 << tap, 0)
-                _, equal = same(place, -a, -b, 0)
-                bits = bits | jnp.where(equal, 1 << (9 + tap), 0)
-            own_ref[word, pl.ds(pl.multiple_of(row * lanes, lanes), lanes), :] = bits
+                taken = moved(ids_ref[place], -b) == ids_ref[place + a]
+                bits = bits | jnp.where(taken, 1 << tap, 0)
+                taken = moved(ids_ref[place - a], -b) == ids_ref[place]
+                bits = bits | jnp.where(taken, 1 << (9 + tap), 0)
+            spread(own_ref.at[word], row, bits)
         return state
 
     lax.fori_loop(0, rows, own_row, 0)
 
     def any_row(row, state):
-        bits = jnp.zeros((lanes, lanes), jnp.int32)
+        bits = jnp.zeros((1, lanes), jnp.int32)
         for tap, (row_step, col_step) in enumerate(tap_offsets):
-            _, equal = same(2 + row, row_step, col_step, 0)
-            bits = bits | jnp.where(equal, 1 << tap, 0)
-        all_ref[pl.ds(pl.multiple_of(row * lanes, lanes), lanes), :] = bits
+            taken = moved(ids_ref[2 + row + row_step], col_step) == ids_ref[2 + row]
+            bits = bits | jnp.where(taken, 1 << tap, 0)
+        spread(all_ref, row, bits)
         return state
 
     lax.fori_loop(0, ids_ref.shape[0] - 4, any_row, 0)
     for hop in range(1, parts):
         line_hop(hop)
         if hop <= 2:
-            forward(hop - 1)
-    for array in range(parts - 1, 2):
-        forward(array)
-    finish()
+            for job in jobs:
+                job[hop]()
+    if parts == 2:
+        for job in jobs:
+            job[2]()
+    for job in jobs:
+        job[3]()
     for hop in range(parts - 1):
         for side, block, peer, valid, goes in sides(hop):
 
@@ -923,7 +973,7 @@
             def _():
                 line_copy(block, side, hop, peer).wait_send()
 
-    for place in range(2):
+    for place in range(4):
         for step, peer in enumerate(others(CH, parts)):
             small_copy(place, step, peer, peer).wait_recv()
             small_copy(place, step, peer, ch).wait_send()
@@ -931,43 +981,41 @@
     own.wait()
 
 
-def prologue(blocks, parts, features, reduce_w, expand_w, narrow_terms, wide_terms, canvas_ids):
+def prologue(blocks, parts, features, reduce_w, expand_w, terms, canvas_ids):
     layers, mid, feat = reduce_w.shape
     pixels, wide = features.shape
     narrow = mid * parts
     f32, low = jnp.float32, jnp.bfloat16
     shape = jax.ShapeDtypeStruct
-    padded = jnp.pad(canvas_ids, ((2, 2), (4, 4)), constant_values=-1)
-    ids = jnp.broadcast_to(padded[:, :, None], padded.shape + (lanes,))
+    ids = jnp.pad(canvas_ids, ((2, 2), (0, 0)), constant_values=-1)[:, None]
     anywhere = pl.BlockSpec(memory_space=pl.ANY)
     inside = pl.BlockSpec(memory_space=pltpu.VMEM)
     dma = pltpu.SemaphoreType.DMA
     return pl.pallas_call(
         functools.partial(prologue_kernel, blocks, parts),
-        in_specs=[anywhere] * 5 + [inside],
-        out_specs=[anywhere] * 7 + [inside] * 2,
+        in_specs=[anywhere] * 7 + [inside],
+        out_specs=[anywhere] * 9 + [inside] * 2,
         out_shape=[
             shape((pixels, feat), low),
             *stripe_shapes(parts, blocks, reduce_w, expand_w),
             shape((narrow, feat), low),
             shape((narrow, feat), low),
-            shape((parts,) + narrow_terms.shape, f32),
-            shape((parts,) + wide_terms.shape, f32),
+            *[shape((parts,) + term.shape, f32) for term in terms],
             shape((2, pixels, lanes), jnp.int32),
             shape((pixels * blocks, lanes), jnp.int32),
         ],
         scratch_shapes=[
             dma((2, parts)),
             dma((parts,)),
-            dma((2, parts)),
-            dma((2, parts)),
-            dma((3,)),
+            dma((4, parts)),
+            dma((4, parts)),
+            dma((5,)),
         ]
         + stripe_sems(parts)
-        + spread_sems(blocks),
+        + job_sems(blocks) * 2,
         compiler_params=comm_params(5),
         cost_estimate=pl.CostEstimate(flops=10**6, bytes_accessed=10**8, transcendentals=0),
-    )(features, reduce_w, expand_w, narrow_terms, wide_terms, ids)
+    )(features, reduce_w, expand_w, *terms, ids)
 
 
 def greet_line(blocks):
@@ -1058,18 +1106,16 @@
     )
     own = pltpu.make_async_copy(main_ref, ext_ref.at[pl.ds(cols, pixels)], local_sem.at[0])
     if fetch:
-        spread, forward, last = spread_job((mine_r, mine_e), (full_r, full_e), sems, blocks)
+        jobs = jobs + spread_jobs((mine_r, mine_e), (full_r, full_e), sems, blocks)
 
     @pl.when(step == 0)
     def _():
         own.start()
-        if fetch or jobs:
+        if jobs:
             greet_blocks(blocks)
         else:
             greet_line(blocks)
         start()
-        if fetch:
-            spread()
         for job in jobs:
             job[0]()
         own.wait()
@@ -1077,6 +1123,13 @@
     @pl.when(step == 3)
     def _():
         finish()
+
+    if jobs:
+
+        @pl.when(step == 7)
+        def _():
+            for job in jobs:
+                job[1]()
 
     row_step = jnp.where(step < 3, 1, jnp.where(step < 6, 0, 2))
     col_step = lax.rem(step, 3)
@@ -1106,14 +1159,10 @@
             act_ref[head] = value
             if head in targets:
                 ends_ref[targets.index(head)] = value
-        if fetch:
-            for array in range(2):
-                forward(array)
-            last()
-        for job in jobs:
-            job[1]()
         for job in jobs:
             job[2]()
+        for job in jobs:
+            job[3]()
 
 
 def tap_at(step):
@@ -1154,7 +1203,7 @@
             dma((2,)),
             dma((2,)),
         ]
-        + (spread_sems(blocks) if mine else []),
+        + (job_sems(blocks) * 2 if mine else []),
         compiler_params=comm_params(6 + layer),
         cost_estimate=pl.CostEstimate(
             flops=18 * pixels * head_count * mid * feat,
@@ -1179,10 +1228,11 @@
 def messages_kernel(
     blocks,
     layer,
+    ahead,
     jobs,
     feat_ref,
     w_hbm,
-    cot_ref,
+    cots_ref,
     gain_ref,
     bias_ref,
     mask_ref,
@@ -1190,6 +1240,7 @@
     local_ref,
     sums_ref,
     part_ref,
+    values_ref,
     pack_ref,
     main_ref,
     low_ref,
@@ -1201,14 +1252,11 @@
     z_ref,
     im_ref,
     grad_ref,
-    w_sem,
-    local_sem,
-    halo_send,
-    halo_recv,
-    cot_send,
-    cot_recv,
+    *sems,
 ):
+    w_sem, local_sem, halo_send, halo_recv, cot_send, cot_recv, *sems = sems
     parts, heads, pixels, mid = feat_ref.shape
+    cot_ref = cots_ref.at[layer]
     cols = low_ref.shape[2]
     pairs = w_ref.shape[0]
     me, ch = lax.axis_index(BLK), lax.axis_index(CH)
@@ -1221,22 +1269,30 @@
     main_copy.start()
     for pair in (0, 4, 1, 5, 3, 2):
         loads[pair].start()
-    greet_blocks(blocks)
+    greet(blocks, parts)
+    early, jobs = jobs[:ahead], jobs[ahead:]
+    for job in early:
+        job[0]()
     start, finish = edge_copies(feat_ref, low_ref, high_ref, cols, halo_send, halo_recv, blocks)
     start()
     cot_start, cot_finish = edge_copies(
         cot_ref, cot_low, cot_high, cols, cot_send, cot_recv, blocks
     )
     cot_start()
+    for job in jobs:
+        job[0]()
     main_copy.wait()
     size = parts * mid // blocks
     for block in range(blocks):
         part, first = block * size // mid, block * size % mid
         for index, (one, two) in enumerate(groups):
-            pack_ref[block, index] = jnp.concatenate(
+            (pack_ref if sems else values_ref)[block, index] = jnp.concatenate(
                 [main_ref[part, one][:, first : first + size], main_ref[part, two][:, first : first + size]],
                 axis=1,
             )
+    if sems:
+        jobs = jobs + [slot_job(pack_ref, values_ref, sems, blocks)]
+        jobs[-1][0]()
     for source in range(heads):
         for part in range(parts):
             lhs_ref[source, cols : cols + pixels, part * mid : (part + 1) * mid] = main_ref[part, source]
@@ -1263,8 +1319,6 @@
         taps(pair, 1)
     finish()
     cot_finish()
-    for job in jobs:
-        job[0]()
     for source in range(heads):
         for part in range(parts):
             chan = slice(part * mid, (part + 1) * mid)
@@ -1273,6 +1327,8 @@
     for pair in order:
         taps(pair, 0)
         taps(pair, 2)
+    for job in early:
+        job[1]()
     values = {}
     cots = {}
     for place, target in enumerate((0, 3)):
@@ -1300,6 +1356,9 @@
         maps_ref[place] = total.astype(low)
         local_ref[place] = slopes
 
+    for job in jobs:
+        job[1]()
+
     def product_of(pair, slot):
         source, target = message_pairs[pair]
         place = 0 if target == 0 else 1
@@ -1321,19 +1380,22 @@
             preferred_element_type=jnp.float32,
         )
 
-    for source, *members in source_order:
+    for count, (source, *members) in enumerate(source_order):
+        if count == 2:
+            for job in early:
+                job[2]()
         total = product_of(members[0], 0)
         for pair in members[1:]:
             total = total + product_of(pair, 1)
         for part in range(parts):
             part_ref[part, source] = total[:, part * mid : (part + 1) * mid].astype(low)
     for job in jobs:
-        job[1]()
-    for job in jobs:
         job[2]()
-
-
-def messages_both(blocks, layer, jobs, cols, features, weights, cotangents, gains, biases, mask):
+    for job in early + jobs:
+        job[3]()
+
+
+def messages_both(blocks, layer, jobs, ahead, send, cols, features, weights, cotangents, gains, biases, mask):
     parts, heads, pixels, mid = features.shape
     pairs = weights.shape[1]
     narrow = parts * mid
@@ -1343,20 +1405,22 @@
     inside = pl.BlockSpec(memory_space=pltpu.VMEM)
     dma = pltpu.SemaphoreType.DMA
     wide = 2 * narrow // blocks
+    values = shape((blocks, 2, pixels, wide), low)
     return job_call(
-        functools.partial(messages_kernel, blocks, layer),
+        functools.partial(messages_kernel, blocks, layer, ahead),
         jobs,
         blocks,
         in_specs=[anywhere, anywhere] + [inside] * 4,
-        out_specs=[inside] * 5,
+        out_specs=[inside] * 4 + [anywhere if send else inside],
         out_shape=[
             shape((2, pixels, mid), low),
             shape((2, pixels, mid), f32),
             shape((2 * pairs, mid), f32),
             shape((parts, heads, pixels, mid), low),
-            shape((blocks, 2, pixels, wide), low),
+            values,
         ],
         scratch_shapes=[
+            pltpu.VMEM(values.shape if send else (8, lanes), low),
             pltpu.VMEM((parts, heads, pixels, mid), low),
             pltpu.VMEM((parts, heads, cols, mid), low),
             pltpu.VMEM((parts, heads, cols, mid), low),
@@ -1373,7 +1437,8 @@
             dma((2,)),
             dma((2,)),
             dma((2,)),
-        ],
+        ]
+        + (job_sems(blocks) if send else []),
         compiler_params=comm_params(10 + layer),
         cost_estimate=pl.CostEstimate(
             flops=36 * pixels * pairs * mid * narrow,
@@ -1408,9 +1473,9 @@
         else:
             greet_line(blocks)
         start()
-        finish()
         for job in jobs:
             job[0]()
+        finish()
         for head in range(head_count):
             grad = jnp.concatenate([low_ref[head], main_ref[head], high_ref[head]], axis=0)
             fill_taps(im_ref, head, grad, mask_ref[0], pixels, cols, 1)
@@ -1429,10 +1494,9 @@
 
         @pl.when(step == pl.num_programs(0) - 1)
         def _():
-            for job in jobs:
-                job[1]()
-            for job in jobs:
-                job[2]()
+            for part in (1, 2, 3):
+                for job in jobs:
+                    job[part]()
 
 
 def heads_backward(blocks, layer, jobs, cols, main, weights, mask, parts):
@@ -1581,12 +1645,9 @@
 
 def exchange_kernel(blocks, jobs, done_ref):
     greet_blocks(blocks)
-    for job in jobs:
-        job[0]()
-    for job in jobs:
-        job[1]()
-    for job in jobs:
-        job[2]()
+    for part in range(4):
+        for job in jobs:
+            job[part]()
     done_ref[...] = jnp.zeros(done_ref.shape, done_ref.dtype)
 
 
@@ -1768,12 +1829,10 @@
     wd_ref,
     we_ref,
     mask_ref,
-    gain1_ref,
-    bias1_ref,
-    gain2_ref,
-    bias2_ref,
-    gain3_ref,
-    bias3_ref,
+    gains_ref,
+    biases_ref,
+    wide_gains_ref,
+    wide_biases_ref,
     *refs,
 ):
     if fetch:
@@ -1792,6 +1851,14 @@
     ch = lax.axis_index(CH)
     pixel_count = float(pixels * blocks)
     greet(blocks, parts)
+
+    def whole_row(row_of):
+        return jnp.concatenate([row_of(part) for part in range(parts)], axis=1)
+
+    gain1 = whole_row(lambda part: gains_ref[part, layer, 0:1])
+    bias1 = whole_row(lambda part: biases_ref[part, layer, 0:1])
+    gain3 = whole_row(lambda part: wide_gains_ref[part, layer : layer + 1])
+    bias3 = whole_row(lambda part: wide_biases_ref[part, layer : layer + 1])
     if fetch:
         start, finish = stripe_job(
             raw_r, raw_e, fetch, (full_r, full_e), refs[16:], blocks, parts
@@ -1811,7 +1878,7 @@
     term1_ref[1:2] = inverse
 
     def first(part, state):
-        value = gain1_ref[...] * ((pre1_ref[part, :] - mean_value) * inverse) + bias1_ref[...]
+        value = gain1 * ((pre1_ref[part, :] - mean_value) * inverse) + bias1
         pre1_ref[part, :] = value * sigmoid(value)
         return state
 
@@ -1857,7 +1924,7 @@
     normed = (second_pre - mean_value) * inverse
     normed2_ref[...] = normed
     inverse2_ref[...] = inverse
-    value = gain2_ref[...] * normed + bias2_ref[...]
+    value = gains_ref[ch, layer, 1:2] * normed + biases_ref[ch, layer, 1:2]
     gath_ref[ch] = (value * sigmoid(value)).astype(jnp.bfloat16)
     wait_parts = send_slots(
         lambda _: gath_ref.at[ch], gath_ref, part_send, part_recv, CH, parts
@@ -1875,6 +1942,8 @@
         pre3_ref[:, lane] = jnp.dot(
             full_ref[...], we_ref[:, lane], preferred_element_type=jnp.float32
         )
+    for job in jobs:
+        job[1]()
     total, square = moments(pre3_ref, 16)
     mean_value, inverse = terms(
         *block_totals(total, square, stat3_ref, stat_send.at[2], stat_recv.at[2], blocks)
@@ -1884,8 +1953,8 @@
 
     def last(part, state):
         value = (
-            gain3_ref[...] * ((pre3_ref[part, :] - mean_value) * inverse)
-            + bias3_ref[...]
+            gain3 * ((pre3_ref[part, :] - mean_value) * inverse)
+            + bias3
             + cur_ref[part, :].astype(jnp.float32)
         )
         out_ref[part, :] = (value * sigmoid(value)).astype(jnp.bfloat16)
@@ -1894,13 +1963,13 @@
     row_loop(pixels, 16, last, 0)
     own_wide = pl.ds(pl.multiple_of(ch * wide, wide), wide)
     for job in jobs:
-        job[1]()
+        job[2]()
     normed3_ref[...] = (pre3_ref[:, own_wide] - term3_ref[0:1, own_wide]) * term3_ref[1:2, own_wide]
     inverse3_ref[...] = term3_ref[1:2, own_wide]
     if fetch:
         finish()
     for job in jobs:
-        job[2]()
+        job[3]()
 
 
 def trunk_forward(
@@ -1920,7 +1989,7 @@
         functools.partial(trunk_forward_kernel, blocks, parts, layer, fetch),
         jobs,
         blocks,
-        in_specs=[inside] * 11 + [anywhere] * len(raw),
+        in_specs=[inside] * 9 + [anywhere] * len(raw),
         out_specs=[inside] * 9 + [anywhere] * len(raw),
         out_shape=[
             shape((pixels, feat), low),
@@ -1981,18 +2050,17 @@
     blocks,
     parts,
     layer,
+    jobs,
     *refs,
 ):
     up_ref, heads_ref, cur_ref, normed3_ref, inverse3_ref = refs[:5]
     refs = refs[5:]
-    gain3_ref, bias3_ref, we_ref, full_ref, normed2_ref = refs[:5]
+    we_ref, full_ref, normed2_ref, inverse2_ref, wd_ref = refs[:5]
     refs = refs[5:]
-    inverse2_ref, gain2_ref, bias2_ref, wd_ref, mask_ref = refs[:5]
+    mask_ref, ext_ref, normed1_ref, inverse1_ref, wr_ref = refs[:5]
     refs = refs[5:]
-    ext_ref, normed1_ref, inverse1_ref, gain1_ref, bias1_ref = refs[:5]
+    gate_ref, gains_ref, biases_ref, wide_gains_ref, wide_biases_ref = refs[:5]
     refs = refs[5:]
-    wr_ref, gate_ref = refs[:2]
-    refs = refs[2:]
     sources, gates, refs = refs[:6], refs[6:8], refs[8:]
     out_ref, expand_ref, dilated_ref, reduce_ref, wide_ref = refs[:5]
     refs = refs[5:]
@@ -2023,6 +2091,8 @@
     ch = lax.axis_index(CH)
     pixel_count = float(pixels * blocks)
     low = jnp.bfloat16
+    gain3 = wide_gains_ref[layer : layer + 1]
+    bias3 = wide_biases_ref[layer : layer + 1]
     greet(blocks, parts)
     chunks.begin()
     own_wide = pl.ds(pl.multiple_of(ch * wide, wide), wide)
@@ -2034,7 +2104,7 @@
     def start(part, state):
         normed = normed3_ref[part, :]
         summed = (
-            gain3_ref[...] * normed + bias3_ref[...] + cur_ref[part, own_wide].astype(jnp.float32)
+            gain3 * normed + bias3 + cur_ref[part, own_wide].astype(jnp.float32)
         )
         value = (up_ref[part, :] + heads_ref[part, :].astype(jnp.float32)) * slope_of(summed)
         out_ref[part, :] = value
@@ -2053,7 +2123,7 @@
     )
     wide_ref[0:1] = gain_grad
     wide_ref[1:2] = bias_grad
-    scale = gain3_ref[...] * inverse3_ref[...]
+    scale = gain3 * inverse3_ref[...]
     bias_part = bias_grad / pixel_count
     gain_part = gain_grad / pixel_count
 
@@ -2064,7 +2134,7 @@
         return state
 
     row_loop(pixels, 32, third, 0)
-    product = contract_last(third_ref[...], we_ref[...])
+    product = contract_last(third_ref[...], we_ref[layer])
     for part in range(parts):
         send2_ref[part] = product[:, part * mid : (part + 1) * mid].astype(low)
     recv2_ref[ch] = send2_ref[ch]
@@ -2084,9 +2154,11 @@
     chunks.run(plan[1])
     wait_parts()
 
-    def narrow_norm(recv_ref, normed_ref, inverse_ref, gain_ref, bias_ref, stat_ref, phase, sums_ref):
+    def narrow_norm(recv_ref, normed_ref, inverse_ref, norm, stat_ref, phase, sums_ref):
+        gain = gains_ref[layer, norm : norm + 1]
+        bias = biases_ref[layer, norm : norm + 1]
         normed = normed_ref[...]
-        value = sum_slots(recv_ref, parts) * slope_of(gain_ref[...] * normed + bias_ref[...])
+        value = sum_slots(recv_ref, parts) * slope_of(gain * normed + bias)
         bias_grad, gain_grad = block_totals(
             jnp.sum(value, axis=0, keepdims=True),
             jnp.sum(value * normed, axis=0, keepdims=True),
@@ -2099,13 +2171,13 @@
         sums_ref[0:1] = gain_grad
         sums_ref[1:2] = bias_grad
         return (
-            gain_ref[...]
+            gain
             * inverse_ref[...]
             * (value - bias_grad / pixel_count - normed * (gain_grad / pixel_count))
         )
 
     grad = narrow_norm(
-        recv2_ref, normed2_ref, inverse2_ref, gain2_ref, bias2_ref, stat2_ref, 1, second_ref
+        recv2_ref, normed2_ref, inverse2_ref, 1, stat2_ref, 1, second_ref
     )
     grad_ref[edge : edge + pixels, :] = grad.astype(low)
     wait_halo = halo_copies(grad_ref, edge, pixels, halo_send, halo_recv, blocks)
@@ -2146,10 +2218,12 @@
     wait_dilated = send_slots(
         lambda peer: di_send_ref.at[peer], di_recv_ref, sum_send.at[1], sum_recv.at[1], BLK, blocks
     )
+    for job in jobs:
+        job[0]()
     chunks.run(plan[3])
     wait_parts()
     grad = narrow_norm(
-        recv1_ref, normed1_ref, inverse1_ref, gain1_ref, bias1_ref, stat1_ref, 2, first_ref
+        recv1_ref, normed1_ref, inverse1_ref, 0, stat1_ref, 2, first_ref
     )
     gath_ref[ch] = grad.astype(low)
     wait_parts = send_slots(
@@ -2173,6 +2247,9 @@
     chunks.run(2 * blocks - chunks.done)
     messages_store(messages_out, accs[:2])
     heads_store(heads_out, accs[2])
+    for part in (1, 2, 3):
+        for job in jobs:
+            job[part]()
     wait_gates()
     gate_out[...] = sum_slots(gates_ref, blocks)
     wait_expand()
@@ -2183,21 +2260,24 @@
     reduce_ref[...] = sum_slots(re_recv_ref, blocks)
 
 
-def trunk_backward(blocks, parts, layer, operands, sources, gates):
+def trunk_backward(blocks, parts, layer, jobs, operands, norms, sources, gates):
     pixels, wide = operands[0].shape
     feat = wide * parts
-    mid = operands[9].shape[1]
+    mid = operands[7].shape[1]
     narrow = mid * parts
-    rows = operands[15].shape[0]
+    rows = operands[11].shape[0]
     f32, low = jnp.float32, jnp.bfloat16
     shape = jax.ShapeDtypeStruct
     small, large = narrow // blocks, feat // blocks
     inside = pl.BlockSpec(memory_space=pltpu.VMEM)
     anywhere = pl.BlockSpec(memory_space=pl.ANY)
     rows_two = pixels + 2 * lanes
-    return pl.pallas_call(
+    return job_call(
         functools.partial(trunk_backward_kernel, blocks, parts, layer),
-        in_specs=[inside] * len(operands) + [anywhere] * len(sources) + [inside] * len(gates),
+        jobs,
+        blocks,
+        in_specs=[inside] * (len(operands) + len(norms)) + [anywhere] * len(sources) + [inside] * len(gates),
+        out_specs=[inside] * 10,
         out_shape=[
             shape((pixels, wide), f32),
             shape((small, wide), f32),
@@ -2256,7 +2336,7 @@
             bytes_accessed=200 * 2**20,
             transcendentals=0,
         ),
-    )(*operands, *sources, *gates)
+    )(*operands, *norms, *sources, *gates)
 
 
 def gather_parts(values):
@@ -2306,16 +2386,12 @@
         features_in.reshape(pixels, wide),
         w_reduce,
         w_expand,
-        jnp.concatenate([norm_gain[:, 0], norm_bias[:, 0]], axis=0),
-        jnp.concatenate([wide_gain, wide_bias], axis=0),
+        (norm_gain, norm_bias, wide_gain, wide_bias),
         canvas_ids,
     )
     reduce_full, expand_full = [rest[2]], [rest[3]]
-    narrow_all, wide_all, bits, all_bits = rest[4:]
+    norms_all, bits, all_bits = rest[4:8], rest[8], rest[9]
     cotangents = task_cotangents.reshape(layers, 2, pixels, mid)
-    narrow_all = narrow_all.transpose(1, 0, 2).reshape(2, layers, narrow)
-    wide_all = wide_all.transpose(1, 0, 2).reshape(2, layers, feat)
-
     kept = []
     for layer in range(layers):
         keep = types.SimpleNamespace(input=current)
@@ -2324,20 +2400,13 @@
             parts,
             cols,
             layer,
-            [(gather_kind, cotangents[layer])],
+            [(gather_kind, cotangents, layer)],
             current,
             reduce_full[layer],
             dilated_t,
             expand_full[layer],
             bits,
-            (
-                narrow_all[0, layer][None],
-                narrow_all[1, layer][None],
-                norm_gain[layer, 1][None],
-                norm_bias[layer, 1][None],
-                wide_all[0, layer][None],
-                wide_all[1, layer][None],
-            ),
+            norms_all,
             (w_reduce, w_expand) if layer + 1 < layers else (),
         )
         (
@@ -2355,18 +2424,16 @@
         if layer:
             current, kept[-1].features = lax.optimization_barrier((current, kept[-1].features))
         keep.output = current
-        (keep.heads_pre, features, keep.ends, *fetched), moved = heads_forward(
+        (keep.heads_pre, features, keep.ends, *fetched), _ = heads_forward(
             blocks,
             layer,
-            [(swap_kind, kept[0].output)] if layer else [],
+            [],
             cols,
             current,
             heads_t,
             bits,
             mine,
         )
-        if layer:
-            kept[0].values = moved[0]
         if fetched:
             reduce_full.append(fetched[0])
             expand_full.append(fetched[1])
@@ -2381,10 +2448,12 @@
             blocks,
             layer,
             [(gather_kind, keep.ends)] + ([] if layer else [(swap_kind, kept[1].output)]),
+            0,
+            bool(layer),
             cols,
             keep.features,
             messages_t,
-            cotangents[layer],
+            cotangents,
             gate_gain,
             gate_bias,
             bits,
@@ -2402,22 +2471,26 @@
     for layer in range(layers):
         keep = kept[layer]
         keep.heads_low = heads_low_of(keep)
-        (partial,), (keep.message_values,) = heads_backward(
+        (partial,), moved = heads_backward(
             blocks,
             layer,
-            [(slot_kind, keep.message_values)],
+            [] if layer else [(slot_kind, keep.message_values), (swap_kind, keep.output)],
             cols,
             keep.heads_low,
             heads_t,
             bits,
             parts,
         )
+        if layer == 0:
+            keep.message_values, keep.values = moved
         keep.heads_partial = reduce_parts(partial)
         if layer + 1 < layers:
             kept[layer + 1].source_sums, partial = lax.optimization_barrier(
                 (kept[layer + 1].source_sums, partial)
             )
-    kept[0].heads_low, partial = lax.optimization_barrier((kept[0].heads_low, partial))
+    kept[0].heads_low, kept[0].heads_partial, partial = lax.optimization_barrier(
+        (kept[0].heads_low, kept[0].heads_partial, partial)
+    )
     kept[0].heads_all, kept[1].heads_all = exchange(
         blocks, [(gather_kind, keep.heads_low) for keep in kept]
     )
@@ -2436,34 +2509,30 @@
             keep.gates,
             keep.messages_grad,
             keep.heads_grad,
-        ) = trunk_backward(
+        ), _ = trunk_backward(
             blocks,
             parts,
             layer,
+            [],
             (
                 upstream,
                 keep.heads_partial,
                 keep.input,
                 keep.normed3,
                 keep.inverse3,
-                wide_gain[layer][None],
-                wide_bias[layer][None],
-                w_expand[layer],
+                w_expand,
                 keep.second_full,
                 keep.normed2,
                 keep.inverse2,
-                norm_gain[layer, 1][None],
-                norm_bias[layer, 1][None],
                 dilated_t,
                 bits,
                 keep.first_ext,
                 keep.normed1,
                 keep.inverse1,
-                norm_gain[layer, 0][None],
-                norm_bias[layer, 0][None],
                 reduce_full[layer],
                 keep.gate_sums,
             ),
+            (norm_gain, norm_bias, wide_gain, wide_bias),
             (
                 keep.message_values,
                 keep.cotangents,
@@ -2474,8 +2543,6 @@
             ),
             (gate_gain, gate_bias),
         )
-
-
     def stacked(of):
         return jnp.stack([of(keep) for keep in kept])
 
@@ -2504,7 +2571,7 @@
     mid = args[1].shape[1]
     blocks, parts = lax.axis_size(BLK), lax.axis_size(CH)
     whole_tiles = args[1].shape[0] == 2 and mid % lanes == 0 and args[0].shape[1] == lanes and parts >= 2
-    if whole_tiles and blocks % 2 == 0 and 2 * mid * parts == lanes * blocks:
+    if whole_tiles and blocks == 8 and 2 * mid * parts == lanes * blocks:
         return shards(*args)
     return plain_shards(*args)
 

time: 701 us -> 674 us (0.961)
  local copies, waits for them, and re-layouts: 20.6 us -> 10.3 us
    pallas_call x2 -> x0, Pallas kernels: 148 us -> none  [trunk_backward(): pl.pallas_call(functools.partial(trunk_backward_kernel, blocks, parts, la...]
    pallas_call x9 -> x11, Pallas kernels: 396 us -> 534 us  [call(): pl.pallas_call(wrapped, in_specs=list(in_specs) + [anywhere] * count, out...]
    another operation x10 -> x9, other arithmetic: 18.8 us -> 18.7 us  [stacked(): return jnp.stack([of(keep) for keep in kept])]
  transfers between devices with their start and end apart: 6 -> 6, of which waited for: 3 -> 3; matrix products, arithmetic and copies ran while one was open for 1% -> 2% of each run, Pallas kernels for 46% -> 44%
where the time goes in v5:
time: 674 us; the launch traced here: 666 us
  Pallas kernels  594 us (88%)
  other arithmetic  24.7 us (4%)
  waiting for transfers between devices  22.2 us (3%)
  between operations  14.8 us (2%)
  local copies, waits for them, and re-layouts  10.3 us (2%)
    pallas_call x11, Pallas kernels, call(): pl.pallas_call(wrapped, in_specs=list(in_specs) + [anywhere] * count, out...  534 us
    pallas_call x1, Pallas kernels, prologue(): pl.pallas_call(functools.partial(prologue_kernel, blocks, parts), in_spec...  59.5 us
    reduce_scatter x4, waiting for transfers between devices, reduce_parts(): return lax.psum_scatter(values, CH, scatter_dimension=0, tiled=False)  21 us
    another operation x9, other arithmetic, stacked(): return jnp.stack([of(keep) for keep in kept])  18.7 us
  transfers between devices with their start and end apart: 6, of which 3 were waited for; matrix products, arithmetic and copies ran while one was open for 2% of the time, Pallas kernels for 44%

profile of v5, /device:TPU:0, one launch (start us, length us, event | category | flops | bytes accessed | tf_op | source)
XLA Modules:
  0.0 666.2 jit_solution(9286616546292328249)
XLA Ops:
  8.6 59.5 %shard_map.254 = (bf16[512,2048]{1,0:T(8,128)(2,1)}, bf16[512,256]{1,0:T(8,128)(2,1)}, bf16[64,2048]{1,0:T(8,128)(2,1)}, bf16[512,2048]{1,0:T(8,128)(2,1)}, bf16...) custom-call(bf16[512,512]{1,0:T(8,128)(2,1)} %bitcast.77, ...), custom_call_target="tpu_custom_call" | custom-call | flops 1000000 | bytes 100000000 | tf_op jit(solution)/shard_map/pallas_call | solution.py:994
  68.1 49.7 %shard_map.255 = (bf16[512,2048]{1,0:T(8,128)(2,1)}, bf16[1024,512]{1,0:T(8,128)(2,1)}, bf16[512,512]{1,0:T(8,128)(2,1)}, f32[512,128]{1,0:T(8,128)}, f32[1,128]...) custom-call(bf16[512,2048]{1,0:T(8,128)(2,1)} %get-tuple-element.100, ...), custom_call_target="tpu_custom_call" | custom-call | flops 2751463424 | bytes 157286400 | tf_op jit(solution)/shard_map/pallas_call | solution.py:738
  117.8 36.9 %shard_map.256 = (f32[4,512,128]{2,1,0:T(8,128)}, bf16[4,512,128]{2,1,0:T(8,128)(2,1)}, bf16[2,512,128]{2,1,0:T(8,128)(2,1)}, bf16[512,2048]{1,0:T(8,128)(2,1)}, bf16[512,2048]{1,0:T(8,128)(2,1)}) custom-call(bf16[512,2048]{1,0:T(8,128)(2,1)} %get-tuple-element.112.refs_0_.refs_4_.refs_2_, bf16[2,4,9,128,2048]{4,3,2,1,0:T(8,128)(2,1)} %bitcast.57, ...), custom_call_target="tpu_custom_call" | custom-call | flops 9663676416 | bytes 18874368 | tf_op jit(solution)/shard_map/pallas_call | solution.py:738
  154.8 56.0 %shard_map.257 = (bf16[512,2048]{1,0:T(8,128)(2,1)}, bf16[1024,512]{1,0:T(8,128)(2,1)}, bf16[512,512]{1,0:T(8,128)(2,1)}, f32[512,128]{1,0:T(8,128)}, f32[1,128]...) custom-call(bf16[512,2048]{1,0:T(8,128)(2,1)} %get-tuple-element.112, ...), custom_call_target="tpu_custom_call" | custom-call | flops 2751463424 | bytes 157286400 | tf_op jit(solution)/shard_map/pallas_call | solution.py:738
  210.9 1.1 all-gather.5.cloned.1.call-done
  212.0 18.6 %shard_map.258 = (f32[4,512,128]{2,1,0:T(8,128)}, bf16[4,512,128]{2,1,0:T(8,128)(2,1)}, bf16[2,512,128]{2,1,0:T(8,128)(2,1)}) custom-call(bf16[512,2048]{1,0:T(8,128)(2,1)} %get-tuple-element.119.refs_0_.refs_7_, bf16[2,4,9,128,2048]{4,3,2,1,0:T(8,128)(2,1)} %bitcast.58, s32[2,512,128]{2,1,0:T(8,128)} %get-tuple-element.103.refs_4_.refs_2_.refs_5_.refs_10_), custom_call_target="tpu_custom_call" | custom-call | flops 9663676416 | bytes 18874368 | tf_op jit(solution)/shard_map/pallas_call | solution.py:738
  231.9 69.6 %shard_map.259 = (bf16[2,512,128]{2,1,0:T(8,128)(2,1)}, f32[2,512,128]{2,1,0:T(8,128)}, f32[12,128]{1,0:T(8,128)}, bf16[4,4,512,128]{3,2,1,0:T(8,128)(2,1)}, bf1...) custom-call(bf16[4,4,512,128]{3,2,1,0:T(8,128)(2,1)} %bitcast.96, ...), custom_call_target="tpu_custom_call" | custom-call | flops 7247757312 | bytes 7077888 | tf_op jit(solution)/shard_map/pallas_call | solution.py:738
  301.6 52.0 %shard_map.260 = (bf16[2,512,128]{2,1,0:T(8,128)(2,1)}, f32[2,512,128]{2,1,0:T(8,128)}, f32[12,128]{1,0:T(8,128)}, bf16[4,4,512,128]{3,2,1,0:T(8,128)(2,1)}, bf1...) custom-call(bf16[4,4,512,128]{3,2,1,0:T(8,128)(2,1)} %bitcast.97, bf16[2,6,9,128,512]{4,3,2,1,0:T(8,128)(2,1)} %bitcast.95, ...), custom_call_target="tpu_custom_call" | custom-call | flops 7247757312 | bytes 7077888 | tf_op jit(solution)/shard_map/pallas_call | solution.py:738
  353.7 1.2 convert_element_type.20
  355.2 1.2 fusion.refs_0_
  356.4 52.5 %shard_map.261 = (bf16[4,512,512]{2,1,0:T(8,128)(2,1)}, bf16[8,2,512,128]{3,2,1,0:T(8,128)(2,1)}, bf16[8,512,256]{2,1,0:T(8,128)(2,1)}) custom-call(bf16[4,512,128]{2,1,0:T(8,128)(2,1)} %fusion.refs_0_, bf16[2,4,9,128,2048]{4,3,2,1,0:T(8,128)(2,1)} %bitcast.59, s32[2,512,128]{2,1,0:T(8,128)} %get-tuple-element.103.refs_4_.refs_2_.refs_5_.refs_10_, ...), custom_call_target="tpu_custom_call" | custom-call | flops 9663676416 | bytes 18874368 | tf_op jit(solution)/shard_map/pallas_call | solution.py:738
  409.0 1.1 slice.84
  410.1 1.1 convert_element_type.22
  411.3 1.2 fusion.1.refs_0_.refs_1_
  412.5 20.7 %shard_map.262 = bf16[4,512,512]{2,1,0:T(8,128)(2,1)} custom-call(bf16[4,512,128]{2,1,0:T(8,128)(2,1)} %fusion.1.refs_0_.refs_1_, bf16[2,4,9,128,2048]{4,3,2,1,0:T(8,128)(2,1)} %bitcast.60, s32[2,512,128]{2,1,0:T(8,128)} %get-tuple-element.103.refs_4_.refs_2_.refs_5_.refs_10_), custom_call_target="tpu_custom_call" | custom-call | flops 9663676416 | bytes 18874368 | tf_op jit(solution)/shard_map/pallas_call | solution.py:738
  433.3 1.0 copy-done.5
  434.3 1.1 bitcast_convert_fusion.refs_0_
  435.4 1.9 constant_dynamic-slice_fusion
  437.3 0.8 pad_maximum_fusion.3
  438.1 16.4 %reduce-scatter.11.cloned.1.call-done = bf16[1,512,512]{2,1,0:T(8,128)(2,1)} async-done(((bf16[4,512,512]{2,1,0:T(8,128)(2,1)}), bf16[1,512,512]{2,1,0:T(8,128)(2,1)}) %reduce-scatter.11.cloned.1.call-update) | async-done | bytes 524304 | tf_op jit(solution)/shard_map/reduce_scatter | solution.py:2347
  454.5 40.9 %shard_map.263 = (f32[8,128]{1,0:T(8,128)}, bf16[8,4,512,128]{3,2,1,0:T(8,128)(2,1)}, bf16[8,4,512,128]{3,2,1,0:T(8,128)(2,1)}) custom-call(bf16[4,512,128]{2,1,0:T(8,128)(2,1)} %fusion.refs_0_, bf16[4,512,128]{2,1,0:T(8,128)(2,1)} %fusion.1.refs_0_.refs_1_), custom_call_target="tpu_custom_call" | custom-call | flops 1000000 | bytes 100000000 | tf_op jit(solution)/shard_map/pallas_call | solution.py:738
  495.4 4.5 reduce-scatter.9.cloned.1.call-done
  500.0 67.2 %shard_map.264 = (f32[512,512]{1,0:T(8,128)}, f32[64,512]{1,0:T(8,128)}, f32[9,64,128]{2,1,0:T(8,128)}, f32[256,128]{1,0:T(8,128)}, f32[2,512]{1,0:T(2,128)}, /*...) custom-call(f32[512,512]{1,0:T(8,128)} %bitcast_convert_fusion.refs_, ...), custom_call_target="tpu_custom_call" | custom-call | flops 22281701376 | bytes 209715200 | tf_op jit(solution)/shard_map/pallas_call | solution.py:738
  567.3 70.1 %shard_map.265 = (f32[512,512]{1,0:T(8,128)}, f32[64,512]{1,0:T(8,128)}, f32[9,64,128]{2,1,0:T(8,128)}, f32[256,128]{1,0:T(8,128)}, f32[2,512]{1,0:T(2,128)}, /*...) custom-call(f32[512,512]{1,0:T(8,128)} %get-tuple-element.151.refs_0, ...), custom_call_target="tpu_custom_call" | custom-call | flops 22281701376 | bytes 209715200 | tf_op jit(solution)/shard_map/pallas_call | solution.py:738
  637.4 0.8 stack_reshape.14
  639.5 1.6 pad_maximum_fusion.4
  642.3 0.8 pad_maximum_fusion.6
  643.7 1.6 pad_maximum_fusion.5
  645.3 1.8 pad_maximum_fusion.2
  647.2 3.8 pad_maximum_fusion.1
  651.0 7.0 %pad_maximum_fusion = f32[2,4,9,256,128]{4,3,2,1,0:T(8,128)} fusion(f32[1,4,9,256,128]{4,3,2,1,0:T(8,128)S(1)} %bitcast.61, f32[1,4,9,256,128]{4,3,2,1,0:T(8,128)} %bitcast.62), kind=kLoop, calls=%fused_computation | loop fusion | flops 2359296 | bytes 18874368 | tf_op jit(solution)/shard_map/stack | solution.py:2547
  658.0 1.0 copy.65
  (68 shorter events, 6.4 us)
Async XLA Ops:
  7.2 204.8 %all-gather.5.cloned.1.call-start = ((), (), s32[]{:S(2)}) async-start(), calls=%async_computation.8 | async-start | bytes 2621440 | tf_op jit(solution)/shard_map/all_gather | solution.py:2343
  154.8 146.8 %all-gather.7.cloned.1.call-start = ((), (), s32[]{:S(2)}) async-start(), calls=%async_computation.9 | async-start | bytes 2621440 | tf_op jit(solution)/shard_map/all_gather | solution.py:2343
  212.0 18.7 %copy-start.14 = (f32[2,6,128]{2,0,1:T(2,128)S(1)}, f32[2,6,128]{2,0,1:T(2,128)}, u32[]{:S(2)}) copy-start(f32[2,6,128]{2,0,1:T(2,128)} %param.25) | copy-start | bytes 18436
  212.0 19.3 %copy-start.15 = (f32[2,6,128]{2,0,1:T(2,128)S(1)}, f32[2,6,128]{2,0,1:T(2,128)}, u32[]{:S(2)}) copy-start(f32[2,6,128]{2,0,1:T(2,128)} %param.26) | copy-start | bytes 18436
  230.6 123.1 %reduce-scatter.7.cloned.1.call-start = ((), (), s32[]{:S(2)}) async-start(), calls=%async_computation.5 | async-start | bytes 2621440 | tf_op jit(solution)/shard_map/reduce_scatter | solution.py:2347
  301.5 107.4 %reduce-scatter.5.cloned.1.call-start = ((), (), s32[]{:S(2)}) async-start(), calls=%async_computation.4 | async-start | bytes 2621440 | tf_op jit(solution)/shard_map/reduce_scatter | solution.py:2347
  353.6 1.4 copy-start.7
  353.7 1.5 copy-start.2
  353.7 100.8 %reduce-scatter.11.cloned.1.call-start = ((), (), s32[]{:S(2)}) async-start(), calls=%async_computation.7 | async-start | bytes 2621440 | tf_op jit(solution)/shard_map/reduce_scatter | solution.py:2347
  408.9 2.3 copy-start.6
  408.9 91.1 %reduce-scatter.9.cloned.1.call-start = ((), (), s32[]{:S(2)}) async-start(), calls=%async_computation.6 | async-start | bytes 2621440 | tf_op jit(solution)/shard_map/reduce_scatter | solution.py:2347
  409.0 2.3 copy-start.3
  433.2 1.0 copy-start.5
  433.2 4.0 copy-start.9
  433.2 4.0 copy-start.10
  567.2 71.0 %copy-start.13 = (f32[12,128]{1,0:T(8,128)S(1)}, f32[12,128]{1,0:T(8,128)}, u32[]{:S(2)}) copy-start(f32[12,128]{1,0:T(8,128)} %get-tuple-element.185) | copy-start | bytes 18436
  567.2 72.2 %copy-start.12 = (f32[256,128]{1,0:T(8,128)S(1)}, f32[256,128]{1,0:T(8,128)}, u32[]{:S(2)}) copy-start(f32[256,128]{1,0:T(8,128)} %get-tuple-element.169) | copy-start | bytes 393220
  567.2 73.8 %copy-start.17 = (f32[2,128]{1,0:T(2,128)S(1)}, f32[2,128]{1,0:T(2,128)}, u32[]{:S(2)}) copy-start(f32[2,128]{1,0:T(2,128)} %get-tuple-element.181) | copy-start | bytes 3076
  567.3 73.8 %copy-start.18 = (f32[2,128]{1,0:T(2,128)S(1)}, f32[2,128]{1,0:T(2,128)}, u32[]{:S(2)}) copy-start(f32[2,128]{1,0:T(2,128)} %get-tuple-element.180) | copy-start | bytes 3076
  567.3 75.1 %copy-start.16 = (f32[2,512]{1,0:T(2,128)S(1)}, f32[2,512]{1,0:T(2,128)}, u32[]{:S(2)}) copy-start(f32[2,512]{1,0:T(2,128)} %get-tuple-element.183) | copy-start | bytes 12292
  567.3 76.4 %copy-start.11 = (f32[64,512]{1,0:T(8,128)S(1)}, f32[64,512]{1,0:T(8,128)}, u32[]{:S(2)}) copy-start(f32[64,512]{1,0:T(8,128)} %get-tuple-element.173) | copy-start | bytes 393220
  567.3 78.1 %copy-start.8 = (f32[9,64,128]{2,1,0:T(8,128)S(1)}, f32[9,64,128]{2,1,0:T(8,128)}, u32[]{:S(2)}) copy-start(f32[9,64,128]{2,1,0:T(8,128)} %get-tuple-element.171) | copy-start | bytes 884740
  637.4 9.8 %copy-start.1 = (f32[6,9,64,128]{3,2,1,0:T(8,128)S(1)}, f32[6,9,64,128]{3,2,1,0:T(8,128)}, u32[]{:S(2)}) copy-start(f32[6,9,64,128]{3,2,1,0:T(8,128)} %get-tuple-element.177) | copy-start | bytes 5308420
  647.2 3.8 copy-start
  650.9 7.0 %copy-start.4 = (f32[512,512]{1,0:T(8,128)S(1)}, f32[512,512]{1,0:T(8,128)}, u32[]{:S(2)}) copy-start(f32[512,512]{1,0:T(8,128)} %get-tuple-element.167) | copy-start | bytes 3145732
Sparse Core Ops, SparseCore 0:
  154.9 57.0 all-gather.4
  230.8 61.7 all-gather.6
  301.7 42.6 reduce-scatter.6
  353.8 43.4 reduce-scatter.4
  409.0 45.4 reduce-scatter.10
  456.8 43.1 reduce-scatter.8

commit v6 on v5

--- a/solution.py
+++ b/solution.py
@@ -606,6 +606,14 @@
     return start, lambda: None, lambda: None, finish
 
 
+def half_swap_job(half):
+    def job(source, target, sems, blocks):
+        count = source.shape[0] // 2
+        return swap_job(source.at[pl.ds(half * count, count)], target, sems, blocks)
+
+    return job
+
+
 def slot_job(source, target, sems, blocks):
     slot_send, slot_recv, _, local_sem = sems
     me = lax.axis_index(BLK)
@@ -693,8 +701,8 @@
     return start, middle, forward, finish
 
 
-job_kinds = (gather_job, swap_job, slot_job, line_job)
-gather_kind, swap_kind, slot_kind, line_kind = 0, 1, 2, 3
+job_kinds = (gather_job, half_swap_job(0), slot_job, line_job, half_swap_job(1))
+gather_kind, upper_kind, slot_kind, line_kind, lower_kind = 0, 1, 2, 3, 4
 
 
 def job_target(kind, shape, dtype, blocks):
@@ -702,8 +710,8 @@
         shape = (blocks,) + shape
     elif kind == line_kind:
         shape = (lax.axis_size(CH),) + shape
-    elif kind == swap_kind:
-        shape = (blocks, shape[0], shape[1] // blocks)
+    elif kind in (upper_kind, lower_kind):
+        shape = (blocks, shape[0] // 2, shape[1] // blocks)
     return jax.ShapeDtypeStruct(shape, dtype)
 
 
@@ -1535,34 +1543,51 @@
 class WeightChunks:
     def __init__(self, blocks, layer, sources, gates, buffers, accs, lhs, sems):
         self.blocks, self.layer = blocks, layer
-        (self.mv, self.cot, self.ends, self.hv, self.hg, self.bits) = sources
+        (self.mv, self.cot, self.ends, self.hv_up, self.hv_low, self.hg, self.bits) = sources
         self.gain, self.bias = gates
         (self.mv_buf, self.cot_buf, self.ends_buf, self.hv_buf, self.hg_buf, self.bits_buf) = buffers
         self.accs, self.lhs, self.sems = accs, lhs, sems
         self.done = 0
-        self.pixels = self.hv.shape[1]
+        self.pixels = 2 * self.hv_up.shape[1]
 
     def copies(self, heads, index):
         pixels, last = self.pixels, self.blocks - 1
         before, after = jnp.maximum(index - 1, 0), jnp.minimum(index + 1, last)
         slot = lax.rem(index, 2)
-        values, buffer = (self.hv, self.hv_buf) if heads else (self.mv, self.mv_buf)
-        lead = () if heads else (slice(None),)
-        pairs = [
-            (
-                values.at[(before,) + lead + (pl.ds(pixels - lanes, lanes),)],
-                buffer.at[(slot,) + lead + (pl.ds(0, lanes),)],
-            ),
-            (values.at[index], buffer.at[(slot,) + lead + (pl.ds(lanes, pixels),)]),
-            (
-                values.at[(after,) + lead + (pl.ds(0, lanes),)],
-                buffer.at[(slot,) + lead + (pl.ds(lanes + pixels, lanes),)],
-            ),
+        buffer = self.hv_buf if heads else self.mv_buf
+        if heads:
+            half = pixels // 2
+            pairs = [
+                (
+                    self.hv_low.at[before, pl.ds(half - lanes, lanes)],
+                    buffer.at[slot, pl.ds(0, lanes)],
+                ),
+                (self.hv_up.at[index], buffer.at[slot, pl.ds(lanes, half)]),
+                (self.hv_low.at[index], buffer.at[slot, pl.ds(lanes + half, half)]),
+                (
+                    self.hv_up.at[after, pl.ds(0, lanes)],
+                    buffer.at[slot, pl.ds(lanes + pixels, lanes)],
+                ),
+            ]
+        else:
+            every = slice(None)
+            pairs = [
+                (
+                    self.mv.at[before, every, pl.ds(pixels - lanes, lanes)],
+                    buffer.at[slot, every, pl.ds(0, lanes)],
+                ),
+                (self.mv.at[index], buffer.at[slot, every, pl.ds(lanes, pixels)]),
+                (
+                    self.mv.at[after, every, pl.ds(0, lanes)],
+                    buffer.at[slot, every, pl.ds(lanes + pixels, lanes)],
+                ),
+            ]
+        pairs.append(
             (
                 self.bits.at[pl.ds(pl.multiple_of(index * pixels, pixels), pixels)],
                 self.bits_buf.at[slot],
-            ),
-        ]
+            )
+        )
         if heads:
             pairs.append((self.hg.at[index], self.hg_buf.at[slot]))
         else:
@@ -2061,7 +2086,7 @@
     refs = refs[5:]
     gate_ref, gains_ref, biases_ref, wide_gains_ref, wide_biases_ref = refs[:5]
     refs = refs[5:]
-    sources, gates, refs = refs[:6], refs[6:8], refs[8:]
+    sources, gates, refs = refs[:7], refs[7:9], refs[9:]
     out_ref, expand_ref, dilated_ref, reduce_ref, wide_ref = refs[:5]
     refs = refs[5:]
     second_ref, first_ref, gate_out = refs[:3]
@@ -2447,7 +2472,7 @@
         (keep.maps, keep.local, keep.gate_sums, partial, keep.message_values), moved = messages_both(
             blocks,
             layer,
-            [(gather_kind, keep.ends)] + ([] if layer else [(swap_kind, kept[1].output)]),
+            [(gather_kind, keep.ends)] + ([] if layer else [(upper_kind, keep.output)]),
             0,
             bool(layer),
             cols,
@@ -2460,7 +2485,7 @@
         )
         keep.ends_all = moved[0]
         if layer == 0:
-            kept[1].values = moved[1]
+            keep.upper = moved[1]
         keep.source_sums = reduce_parts(partial)
 
     def heads_low_of(keep):
@@ -2474,7 +2499,7 @@
         (partial,), moved = heads_backward(
             blocks,
             layer,
-            [] if layer else [(slot_kind, keep.message_values), (swap_kind, keep.output)],
+            [] if layer else [(slot_kind, keep.message_values), (lower_kind, keep.output)],
             cols,
             keep.heads_low,
             heads_t,
@@ -2482,17 +2507,20 @@
             parts,
         )
         if layer == 0:
-            keep.message_values, keep.values = moved
+            keep.message_values, keep.lower = moved
         keep.heads_partial = reduce_parts(partial)
         if layer + 1 < layers:
             kept[layer + 1].source_sums, partial = lax.optimization_barrier(
                 (kept[layer + 1].source_sums, partial)
             )
-    kept[0].heads_low, kept[0].heads_partial, partial = lax.optimization_barrier(
-        (kept[0].heads_low, kept[0].heads_partial, partial)
-    )
-    kept[0].heads_all, kept[1].heads_all = exchange(
-        blocks, [(gather_kind, keep.heads_low) for keep in kept]
+    kept[0].heads_low, partial = lax.optimization_barrier((kept[0].heads_low, partial))
+    kept[0].heads_all, kept[1].heads_all, kept[1].upper, kept[1].lower = exchange(
+        blocks,
+        [(gather_kind, keep.heads_low) for keep in kept]
+        + [(upper_kind, kept[1].output), (lower_kind, kept[1].output)],
+    )
+    kept[1].heads_all, kept[0].heads_partial = lax.optimization_barrier(
+        (kept[1].heads_all, kept[0].heads_partial)
     )
 
     upstream = output_cotangent.reshape(pixels, wide).astype(jnp.float32)
@@ -2537,7 +2565,8 @@
                 keep.message_values,
                 keep.cotangents,
                 keep.ends_all,
-                keep.values,
+                keep.upper,
+                keep.lower,
                 keep.heads_all,
                 all_bits,
             ),

time: 674 us -> 659 us (0.978)
  waiting for transfers between devices: 22.2 us -> 3.15 us
    reduce_scatter x4, waiting for transfers between devices: 21 us -> 0.08 us  [reduce_parts(): return lax.psum_scatter(values, CH, scatter_dimension=0, tiled=False)]
  transfers between devices with their start and end apart: 6 -> 6, of which waited for: 3 -> 2; matrix products, arithmetic and copies ran while one was open for 2% -> 2% of each run, Pallas kernels for 44% -> 46%
where the time goes in v6:
time: 659 us; the launch traced here: 652 us
  Pallas kernels  599 us (91%)
  other arithmetic  24.7 us (4%)
  between operations  14.8 us (2%)
  local copies, waits for them, and re-layouts  10.3 us (2%)
    pallas_call x11, Pallas kernels, call(): pl.pallas_call(wrapped, in_specs=list(in_specs) + [anywhere] * count, out...  539 us
    pallas_call x1, Pallas kernels, prologue(): pl.pallas_call(functools.partial(prologue_kernel, blocks, parts), in_spec...  59.5 us
    another operation x9, other arithmetic, stacked(): return jnp.stack([of(keep) for keep in kept])  18.7 us
  transfers between devices with their start and end apart: 6, of which 2 were waited for; matrix products, arithmetic and copies ran while one was open for 2% of the time, Pallas kernels for 46%

profile of v6, /device:TPU:0, one launch (start us, length us, event | category | flops | bytes accessed | tf_op | source)
XLA Modules:
  0.0 651.8 jit_solution(12344411279693654623)
XLA Ops:
  7.2 0.7 pad.4
  8.6 59.5 %shard_map.254 = (bf16[512,2048]{1,0:T(8,128)(2,1)}, bf16[512,256]{1,0:T(8,128)(2,1)}, bf16[64,2048]{1,0:T(8,128)(2,1)}, bf16[512,2048]{1,0:T(8,128)(2,1)}, bf16...) custom-call(bf16[512,512]{1,0:T(8,128)(2,1)} %bitcast.77, ...), custom_call_target="tpu_custom_call" | custom-call | flops 1000000 | bytes 100000000 | tf_op jit(solution)/shard_map/pallas_call | solution.py:1002
  68.1 49.7 %shard_map.255 = (bf16[512,2048]{1,0:T(8,128)(2,1)}, bf16[1024,512]{1,0:T(8,128)(2,1)}, bf16[512,512]{1,0:T(8,128)(2,1)}, f32[512,128]{1,0:T(8,128)}, f32[1,128]...) custom-call(bf16[512,2048]{1,0:T(8,128)(2,1)} %get-tuple-element.103, ...), custom_call_target="tpu_custom_call" | custom-call | flops 2751463424 | bytes 157286400 | tf_op jit(solution)/shard_map/pallas_call | solution.py:746
  117.8 36.8 %shard_map.256 = (f32[4,512,128]{2,1,0:T(8,128)}, bf16[4,512,128]{2,1,0:T(8,128)(2,1)}, bf16[2,512,128]{2,1,0:T(8,128)(2,1)}, bf16[512,2048]{1,0:T(8,128)(2,1)}, bf16[512,2048]{1,0:T(8,128)(2,1)}) custom-call(bf16[512,2048]{1,0:T(8,128)(2,1)} %get-tuple-element.115.refs_0_.refs_7_.refs_4_.refs_2_, bf16[2,4,9,128,2048]{4,3,2,1,0:T(8,128)(2,1)} %bitcast.57, ...), custom_call_target="tpu_custom_call" | custom-call | flops 9663676416 | bytes 18874368 | tf_op jit(solution)/shard_map/pallas_call | solution.py:746
  154.8 56.0 %shard_map.257 = (bf16[512,2048]{1,0:T(8,128)(2,1)}, bf16[1024,512]{1,0:T(8,128)(2,1)}, bf16[512,512]{1,0:T(8,128)(2,1)}, f32[512,128]{1,0:T(8,128)}, f32[1,128]...) custom-call(bf16[512,2048]{1,0:T(8,128)(2,1)} %get-tuple-element.115, ...), custom_call_target="tpu_custom_call" | custom-call | flops 2751463424 | bytes 157286400 | tf_op jit(solution)/shard_map/pallas_call | solution.py:746
  210.8 1.1 all-gather.5.cloned.1.call-done
  211.9 18.6 %shard_map.258 = (f32[4,512,128]{2,1,0:T(8,128)}, bf16[4,512,128]{2,1,0:T(8,128)(2,1)}, bf16[2,512,128]{2,1,0:T(8,128)(2,1)}) custom-call(bf16[512,2048]{1,0:T(8,128)(2,1)} %get-tuple-element.122.refs_0_.refs_2_.refs_3_, bf16[2,4,9,128,2048]{4,3,2,1,0:T(8,128)(2,1)} %bitcast.58, s32[2,512,128]{2,1,0:T(8,128)} %get-tuple-element.106.refs_4_.refs_2_.refs_5_.refs_10_), custom_call_target="tpu_custom_call" | custom-call | flops 9663676416 | bytes 18874368 | tf_op jit(solution)/shard_map/pallas_call | solution.py:746
  231.8 58.7 %shard_map.259 = (bf16[2,512,128]{2,1,0:T(8,128)(2,1)}, f32[2,512,128]{2,1,0:T(8,128)}, f32[12,128]{1,0:T(8,128)}, bf16[4,4,512,128]{3,2,1,0:T(8,128)(2,1)}, bf1...) custom-call(bf16[4,4,512,128]{3,2,1,0:T(8,128)(2,1)} %bitcast.96, ...), custom_call_target="tpu_custom_call" | custom-call | flops 7247757312 | bytes 7077888 | tf_op jit(solution)/shard_map/pallas_call | solution.py:746
  290.6 1.9 all-gather.7.cloned.1.call-done
  292.5 52.8 %shard_map.260 = (bf16[2,512,128]{2,1,0:T(8,128)(2,1)}, f32[2,512,128]{2,1,0:T(8,128)}, f32[12,128]{1,0:T(8,128)}, bf16[4,4,512,128]{3,2,1,0:T(8,128)(2,1)}, bf1...) custom-call(bf16[4,4,512,128]{3,2,1,0:T(8,128)(2,1)} %bitcast.97, bf16[2,6,9,128,512]{4,3,2,1,0:T(8,128)(2,1)} %bitcast.95, ...), custom_call_target="tpu_custom_call" | custom-call | flops 7247757312 | bytes 7077888 | tf_op jit(solution)/shard_map/pallas_call | solution.py:746
  345.4 1.2 convert_element_type.20
  346.8 1.2 fusion.refs_0_
  348.0 41.6 %shard_map.261 = (bf16[4,512,512]{2,1,0:T(8,128)(2,1)}, bf16[8,2,512,128]{3,2,1,0:T(8,128)(2,1)}, bf16[8,256,256]{2,1,0:T(8,128)(2,1)}) custom-call(bf16[4,512,128]{2,1,0:T(8,128)(2,1)} %fusion.refs_0_, bf16[2,4,9,128,2048]{4,3,2,1,0:T(8,128)(2,1)} %bitcast.59, s32[2,512,128]{2,1,0:T(8,128)} %get-tuple-element.106.refs_4_.refs_2_.refs_5_.refs_10_, ...), custom_call_target="tpu_custom_call" | custom-call | flops 9663676416 | bytes 18874368 | tf_op jit(solution)/shard_map/pallas_call | solution.py:746
  389.8 1.1 slice.84
  390.9 1.1 convert_element_type.22
  392.1 1.2 fusion.1.refs_0_.refs_1_
  393.3 20.5 %shard_map.262 = bf16[4,512,512]{2,1,0:T(8,128)(2,1)} custom-call(bf16[4,512,128]{2,1,0:T(8,128)(2,1)} %fusion.1.refs_0_.refs_1_, bf16[2,4,9,128,2048]{4,3,2,1,0:T(8,128)(2,1)} %bitcast.60, s32[2,512,128]{2,1,0:T(8,128)} %get-tuple-element.106.refs_4_.refs_2_.refs_5_.refs_10_), custom_call_target="tpu_custom_call" | custom-call | flops 9663676416 | bytes 18874368 | tf_op jit(solution)/shard_map/pallas_call | solution.py:746
  413.9 1.0 copy-done.5
  414.9 1.1 bitcast_convert_fusion.refs_0_
  416.0 1.9 constant_dynamic-slice_fusion
  417.9 0.8 pad_maximum_fusion.3
  418.7 68.0 %shard_map.263 = (f32[8,128]{1,0:T(8,128)}, bf16[8,4,512,128]{3,2,1,0:T(8,128)(2,1)}, bf16[8,4,512,128]{3,2,1,0:T(8,128)(2,1)}, bf16[8,256,256]{2,1,0:T(8,128)(2,1)}, bf16[8,256,256]{2,1,0:T(8,128)(2,1)}) custom-call(bf16[4,512,128]{2,1,0:T(8,128)(2,1)} %fusion.refs_0_, bf16[4,512,128]{2,1,0:T(8,128)(2,1)} %fusion.1.refs_0_.refs_1_, ...), custom_call_target="tpu_custom_call" | custom-call | flops 1000000 | bytes 100000000 | tf_op jit(solution)/shard_map/pallas_call | solution.py:746
  486.8 65.7 %shard_map.264 = (f32[512,512]{1,0:T(8,128)}, f32[64,512]{1,0:T(8,128)}, f32[9,64,128]{2,1,0:T(8,128)}, f32[256,128]{1,0:T(8,128)}, f32[2,512]{1,0:T(2,128)}, /*...) custom-call(f32[512,512]{1,0:T(8,128)} %bitcast_convert_fusion.refs_, ...), custom_call_target="tpu_custom_call" | custom-call | flops 22281701376 | bytes 209715200 | tf_op jit(solution)/shard_map/pallas_call | solution.py:746
  552.6 70.4 %shard_map.265 = (f32[512,512]{1,0:T(8,128)}, f32[64,512]{1,0:T(8,128)}, f32[9,64,128]{2,1,0:T(8,128)}, f32[256,128]{1,0:T(8,128)}, f32[2,512]{1,0:T(2,128)}, /*...) custom-call(f32[512,512]{1,0:T(8,128)} %get-tuple-element.156.refs_0, ...), custom_call_target="tpu_custom_call" | custom-call | flops 22281701376 | bytes 209715200 | tf_op jit(solution)/shard_map/pallas_call | solution.py:746
  623.0 0.8 stack_reshape.14
  625.1 1.6 pad_maximum_fusion.4
  628.0 0.8 pad_maximum_fusion.6
  629.3 1.6 pad_maximum_fusion.5
  631.0 1.8 pad_maximum_fusion.2
  632.8 3.8 pad_maximum_fusion.1
  636.6 7.0 %pad_maximum_fusion = f32[2,4,9,256,128]{4,3,2,1,0:T(8,128)} fusion(f32[1,4,9,256,128]{4,3,2,1,0:T(8,128)S(1)} %bitcast.61, f32[1,4,9,256,128]{4,3,2,1,0:T(8,128)} %bitcast.62), kind=kLoop, calls=%fused_computation | loop fusion | flops 2359296 | bytes 18874368 | tf_op jit(solution)/shard_map/stack | solution.py:2576
  643.6 1.0 copy.65
  (68 shorter events, 5.7 us)
Async XLA Ops:
  7.2 204.7 %all-gather.5.cloned.1.call-start = ((), (), s32[]{:S(2)}) async-start(), calls=%async_computation.8 | async-start | bytes 2621440 | tf_op jit(solution)/shard_map/all_gather | solution.py:2368
  154.7 137.8 %all-gather.7.cloned.1.call-start = ((), (), s32[]{:S(2)}) async-start(), calls=%async_computation.9 | async-start | bytes 2621440 | tf_op jit(solution)/shard_map/all_gather | solution.py:2368
  211.9 18.7 %copy-start.14 = (f32[2,6,128]{2,0,1:T(2,128)S(1)}, f32[2,6,128]{2,0,1:T(2,128)}, u32[]{:S(2)}) copy-start(f32[2,6,128]{2,0,1:T(2,128)} %param.25) | copy-start | bytes 18436
  211.9 19.3 %copy-start.15 = (f32[2,6,128]{2,0,1:T(2,128)S(1)}, f32[2,6,128]{2,0,1:T(2,128)}, u32[]{:S(2)}) copy-start(f32[2,6,128]{2,0,1:T(2,128)} %param.26) | copy-start | bytes 18436
  230.6 114.8 %reduce-scatter.7.cloned.1.call-start = ((), (), s32[]{:S(2)}) async-start(), calls=%async_computation.5 | async-start | bytes 2621440 | tf_op jit(solution)/shard_map/reduce_scatter | solution.py:2372
  290.5 99.2 %reduce-scatter.5.cloned.1.call-start = ((), (), s32[]{:S(2)}) async-start(), calls=%async_computation.4 | async-start | bytes 2621440 | tf_op jit(solution)/shard_map/reduce_scatter | solution.py:2372
  345.3 1.4 copy-start.7
  345.3 1.5 copy-start.2
  345.3 141.4 %reduce-scatter.11.cloned.1.call-start = ((), (), s32[]{:S(2)}) async-start(), calls=%async_computation.7 | async-start | bytes 2621440 | tf_op jit(solution)/shard_map/reduce_scatter | solution.py:2372
  389.7 2.3 copy-start.6
  389.7 97.0 %reduce-scatter.9.cloned.1.call-start = ((), (), s32[]{:S(2)}) async-start(), calls=%async_computation.6 | async-start | bytes 2621440 | tf_op jit(solution)/shard_map/reduce_scatter | solution.py:2372
  389.8 2.3 copy-start.3
  413.8 1.1 copy-start.5
  413.8 4.1 copy-start.9
  413.8 4.1 copy-start.10
  552.5 71.3 %copy-start.13 = (f32[12,128]{1,0:T(8,128)S(1)}, f32[12,128]{1,0:T(8,128)}, u32[]{:S(2)}) copy-start(f32[12,128]{1,0:T(8,128)} %get-tuple-element.191) | copy-start | bytes 18436
  552.5 72.6 %copy-start.12 = (f32[256,128]{1,0:T(8,128)S(1)}, f32[256,128]{1,0:T(8,128)}, u32[]{:S(2)}) copy-start(f32[256,128]{1,0:T(8,128)} %get-tuple-element.175) | copy-start | bytes 393220
  552.5 74.2 %copy-start.17 = (f32[2,128]{1,0:T(2,128)S(1)}, f32[2,128]{1,0:T(2,128)}, u32[]{:S(2)}) copy-start(f32[2,128]{1,0:T(2,128)} %get-tuple-element.187) | copy-start | bytes 3076
  552.5 74.2 %copy-start.18 = (f32[2,128]{1,0:T(2,128)S(1)}, f32[2,128]{1,0:T(2,128)}, u32[]{:S(2)}) copy-start(f32[2,128]{1,0:T(2,128)} %get-tuple-element.186) | copy-start | bytes 3076
  552.5 75.4 %copy-start.16 = (f32[2,512]{1,0:T(2,128)S(1)}, f32[2,512]{1,0:T(2,128)}, u32[]{:S(2)}) copy-start(f32[2,512]{1,0:T(2,128)} %get-tuple-element.189) | copy-start | bytes 12292
  552.5 76.8 %copy-start.11 = (f32[64,512]{1,0:T(8,128)S(1)}, f32[64,512]{1,0:T(8,128)}, u32[]{:S(2)}) copy-start(f32[64,512]{1,0:T(8,128)} %get-tuple-element.179) | copy-start | bytes 393220
  552.5 78.4 %copy-start.8 = (f32[9,64,128]{2,1,0:T(8,128)S(1)}, f32[9,64,128]{2,1,0:T(8,128)}, u32[]{:S(2)}) copy-start(f32[9,64,128]{2,1,0:T(8,128)} %get-tuple-element.177) | copy-start | bytes 884740
  623.0 9.8 %copy-start.1 = (f32[6,9,64,128]{3,2,1,0:T(8,128)S(1)}, f32[6,9,64,128]{3,2,1,0:T(8,128)}, u32[]{:S(2)}) copy-start(f32[6,9,64,128]{3,2,1,0:T(8,128)} %get-tuple-element.183) | copy-start | bytes 5308420
  632.8 3.8 copy-start
  636.6 7.0 %copy-start.4 = (f32[512,512]{1,0:T(8,128)S(1)}, f32[512,512]{1,0:T(8,128)}, u32[]{:S(2)}) copy-start(f32[512,512]{1,0:T(8,128)} %get-tuple-element.173) | copy-start | bytes 3145732
Sparse Core Ops, SparseCore 0:
  154.8 57.0 all-gather.4
  230.7 61.7 all-gather.6
  294.8 42.6 reduce-scatter.6
  345.4 42.2 reduce-scatter.4
  389.9 43.7 reduce-scatter.10
  436.0 43.1 reduce-scatter.8

commit v7 on v6

--- a/solution.py
+++ b/solution.py
@@ -2499,7 +2499,9 @@
         (partial,), moved = heads_backward(
             blocks,
             layer,
-            [] if layer else [(slot_kind, keep.message_values), (lower_kind, keep.output)],
+            [(upper_kind, keep.output), (lower_kind, keep.output)]
+            if layer
+            else [(slot_kind, keep.message_values), (lower_kind, keep.output)],
             cols,
             keep.heads_low,
             heads_t,
@@ -2508,16 +2510,16 @@
         )
         if layer == 0:
             keep.message_values, keep.lower = moved
+        else:
+            keep.upper, keep.lower = moved
         keep.heads_partial = reduce_parts(partial)
         if layer + 1 < layers:
             kept[layer + 1].source_sums, partial = lax.optimization_barrier(
                 (kept[layer + 1].source_sums, partial)
             )
     kept[0].heads_low, partial = lax.optimization_barrier((kept[0].heads_low, partial))
-    kept[0].heads_all, kept[1].heads_all, kept[1].upper, kept[1].lower = exchange(
-        blocks,
-        [(gather_kind, keep.heads_low) for keep in kept]
-        + [(upper_kind, kept[1].output), (lower_kind, kept[1].output)],
+    kept[0].heads_all, kept[1].heads_all = exchange(
+        blocks, [(gather_kind, keep.heads_low) for keep in kept]
     )
     kept[1].heads_all, kept[0].heads_partial = lax.optimization_barrier(
         (kept[1].heads_all, kept[0].heads_partial)

time: 659 us -> 653 us (level)
  Pallas kernels: 599 us -> 587 us
    pallas_call x11, Pallas kernels: 539 us -> 528 us  [call(): pl.pallas_call(wrapped, in_specs=list(in_specs) + [anywhere] * count, out...]
  transfers between devices with their start and end apart: 6 -> 6, of which waited for: 2 -> 3; matrix products, arithmetic and copies ran while one was open for 2% -> 2% of each run, Pallas kernels for 46% -> 44%
where the time goes in v7:
time: 653 us; the launch traced here: 646 us
  Pallas kernels  587 us (90%)
  other arithmetic  24.7 us (4%)
  between operations  14.8 us (2%)
  local copies, waits for them, and re-layouts  10.3 us (2%)
  waiting for transfers between devices  8.2 us (1%)
    pallas_call x11, Pallas kernels, call(): pl.pallas_call(wrapped, in_specs=list(in_specs) + [anywhere] * count, out...  528 us
    pallas_call x1, Pallas kernels, prologue(): pl.pallas_call(functools.partial(prologue_kernel, blocks, parts), in_spec...  59.5 us
    another operation x9, other arithmetic, stacked(): return jnp.stack([of(keep) for keep in kept])  18.7 us
  transfers between devices with their start and end apart: 6, of which 3 were waited for; matrix products, arithmetic and copies ran while one was open for 2% of the time, Pallas kernels for 44%

profile of v7, /device:TPU:0, one launch (start us, length us, event | category | flops | bytes accessed | tf_op | source)
XLA Modules:
  0.0 645.7 jit_solution(7523372074309019807)
XLA Ops:
  8.6 59.5 %shard_map.254 = (bf16[512,2048]{1,0:T(8,128)(2,1)}, bf16[512,256]{1,0:T(8,128)(2,1)}, bf16[64,2048]{1,0:T(8,128)(2,1)}, bf16[512,2048]{1,0:T(8,128)(2,1)}, bf16...) custom-call(bf16[512,512]{1,0:T(8,128)(2,1)} %bitcast.77, ...), custom_call_target="tpu_custom_call" | custom-call | flops 1000000 | bytes 100000000 | tf_op jit(solution)/shard_map/pallas_call | solution.py:1002
  68.1 49.8 %shard_map.255 = (bf16[512,2048]{1,0:T(8,128)(2,1)}, bf16[1024,512]{1,0:T(8,128)(2,1)}, bf16[512,512]{1,0:T(8,128)(2,1)}, f32[512,128]{1,0:T(8,128)}, f32[1,128]...) custom-call(bf16[512,2048]{1,0:T(8,128)(2,1)} %get-tuple-element.104, ...), custom_call_target="tpu_custom_call" | custom-call | flops 2751463424 | bytes 157286400 | tf_op jit(solution)/shard_map/pallas_call | solution.py:746
  117.9 36.9 %shard_map.256 = (f32[4,512,128]{2,1,0:T(8,128)}, bf16[4,512,128]{2,1,0:T(8,128)(2,1)}, bf16[2,512,128]{2,1,0:T(8,128)(2,1)}, bf16[512,2048]{1,0:T(8,128)(2,1)}, bf16[512,2048]{1,0:T(8,128)(2,1)}) custom-call(bf16[512,2048]{1,0:T(8,128)(2,1)} %get-tuple-element.116.refs_0_.refs_7_.refs_4_.refs_2_, bf16[2,4,9,128,2048]{4,3,2,1,0:T(8,128)(2,1)} %bitcast.57, ...), custom_call_target="tpu_custom_call" | custom-call | flops 9663676416 | bytes 18874368 | tf_op jit(solution)/shard_map/pallas_call | solution.py:746
  154.8 56.0 %shard_map.257 = (bf16[512,2048]{1,0:T(8,128)(2,1)}, bf16[1024,512]{1,0:T(8,128)(2,1)}, bf16[512,512]{1,0:T(8,128)(2,1)}, f32[512,128]{1,0:T(8,128)}, f32[1,128]...) custom-call(bf16[512,2048]{1,0:T(8,128)(2,1)} %get-tuple-element.116, ...), custom_call_target="tpu_custom_call" | custom-call | flops 2751463424 | bytes 157286400 | tf_op jit(solution)/shard_map/pallas_call | solution.py:746
  210.8 1.1 all-gather.5.cloned.1.call-done
  212.0 18.6 %shard_map.258 = (f32[4,512,128]{2,1,0:T(8,128)}, bf16[4,512,128]{2,1,0:T(8,128)(2,1)}, bf16[2,512,128]{2,1,0:T(8,128)(2,1)}) custom-call(bf16[512,2048]{1,0:T(8,128)(2,1)} %get-tuple-element.123.refs_0_.refs_3_.refs_4_, bf16[2,4,9,128,2048]{4,3,2,1,0:T(8,128)(2,1)} %bitcast.58, s32[2,512,128]{2,1,0:T(8,128)} %get-tuple-element.107.refs_4_.refs_2_.refs_5_.refs_10_), custom_call_target="tpu_custom_call" | custom-call | flops 9663676416 | bytes 18874368 | tf_op jit(solution)/shard_map/pallas_call | solution.py:746
  231.9 58.7 %shard_map.259 = (bf16[2,512,128]{2,1,0:T(8,128)(2,1)}, f32[2,512,128]{2,1,0:T(8,128)}, f32[12,128]{1,0:T(8,128)}, bf16[4,4,512,128]{3,2,1,0:T(8,128)(2,1)}, bf1...) custom-call(bf16[4,4,512,128]{3,2,1,0:T(8,128)(2,1)} %bitcast.96, ...), custom_call_target="tpu_custom_call" | custom-call | flops 7247757312 | bytes 7077888 | tf_op jit(solution)/shard_map/pallas_call | solution.py:746
  290.6 1.9 all-gather.7.cloned.1.call-done
  292.5 52.8 %shard_map.260 = (bf16[2,512,128]{2,1,0:T(8,128)(2,1)}, f32[2,512,128]{2,1,0:T(8,128)}, f32[12,128]{1,0:T(8,128)}, bf16[4,4,512,128]{3,2,1,0:T(8,128)(2,1)}, bf1...) custom-call(bf16[4,4,512,128]{3,2,1,0:T(8,128)(2,1)} %bitcast.97, bf16[2,6,9,128,512]{4,3,2,1,0:T(8,128)(2,1)} %bitcast.95, ...), custom_call_target="tpu_custom_call" | custom-call | flops 7247757312 | bytes 7077888 | tf_op jit(solution)/shard_map/pallas_call | solution.py:746
  345.4 1.2 convert_element_type.20
  346.9 1.2 fusion.refs_0_
  348.1 41.6 %shard_map.261 = (bf16[4,512,512]{2,1,0:T(8,128)(2,1)}, bf16[8,2,512,128]{3,2,1,0:T(8,128)(2,1)}, bf16[8,256,256]{2,1,0:T(8,128)(2,1)}) custom-call(bf16[4,512,128]{2,1,0:T(8,128)(2,1)} %fusion.refs_0_, bf16[2,4,9,128,2048]{4,3,2,1,0:T(8,128)(2,1)} %bitcast.59, s32[2,512,128]{2,1,0:T(8,128)} %get-tuple-element.107.refs_4_.refs_2_.refs_5_.refs_10_, ...), custom_call_target="tpu_custom_call" | custom-call | flops 9663676416 | bytes 18874368 | tf_op jit(solution)/shard_map/pallas_call | solution.py:746
  390.2 1.1 slice.84
  391.3 1.1 convert_element_type.22
  392.5 1.2 fusion.1.refs_0_.refs_1_
  393.7 31.9 %shard_map.262 = (bf16[4,512,512]{2,1,0:T(8,128)(2,1)}, bf16[8,256,256]{2,1,0:T(8,128)(2,1)}, bf16[8,256,256]{2,1,0:T(8,128)(2,1)}) custom-call(bf16[4,512,128]{2,1,0:T(8,128)(2,1)} %fusion.1.refs_0_.refs_1_, bf16[2,4,9,128,2048]{4,3,2,1,0:T(8,128)(2,1)} %bitcast.60, s32[2,512,128]{2,1,0:T(8,128)} %get-tuple-element.107.refs_4_.refs_2_.refs_5_.refs_10_, ...), custom_call_target="tpu_custom_call" | custom-call | flops 9663676416 | bytes 18874368 | tf_op jit(solution)/shard_map/pallas_call | solution.py:746
  425.6 1.0 copy-done.5
  426.6 1.1 bitcast_convert_fusion.refs_0_
  427.8 1.9 constant_dynamic-slice_fusion
  429.6 0.8 pad_maximum_fusion.3
  430.5 43.7 %shard_map.263 = (f32[8,128]{1,0:T(8,128)}, bf16[8,4,512,128]{3,2,1,0:T(8,128)(2,1)}, bf16[8,4,512,128]{3,2,1,0:T(8,128)(2,1)}) custom-call(bf16[4,512,128]{2,1,0:T(8,128)(2,1)} %fusion.refs_0_, bf16[4,512,128]{2,1,0:T(8,128)(2,1)} %fusion.1.refs_0_.refs_1_), custom_call_target="tpu_custom_call" | custom-call | flops 1000000 | bytes 100000000 | tf_op jit(solution)/shard_map/pallas_call | solution.py:746
  474.2 5.0 reduce-scatter.9.cloned.1.call-done
  479.3 67.4 %shard_map.264 = (f32[512,512]{1,0:T(8,128)}, f32[64,512]{1,0:T(8,128)}, f32[9,64,128]{2,1,0:T(8,128)}, f32[256,128]{1,0:T(8,128)}, f32[2,512]{1,0:T(2,128)}, /*...) custom-call(f32[512,512]{1,0:T(8,128)} %bitcast_convert_fusion.refs_, ...), custom_call_target="tpu_custom_call" | custom-call | flops 22281701376 | bytes 209715200 | tf_op jit(solution)/shard_map/pallas_call | solution.py:746
  546.8 70.2 %shard_map.265 = (f32[512,512]{1,0:T(8,128)}, f32[64,512]{1,0:T(8,128)}, f32[9,64,128]{2,1,0:T(8,128)}, f32[256,128]{1,0:T(8,128)}, f32[2,512]{1,0:T(2,128)}, /*...) custom-call(f32[512,512]{1,0:T(8,128)} %get-tuple-element.158.refs_0, ...), custom_call_target="tpu_custom_call" | custom-call | flops 22281701376 | bytes 209715200 | tf_op jit(solution)/shard_map/pallas_call | solution.py:746
  617.0 0.8 stack_reshape.14
  619.0 1.6 pad_maximum_fusion.4
  621.9 0.8 pad_maximum_fusion.6
  623.3 1.6 pad_maximum_fusion.5
  624.9 1.8 pad_maximum_fusion.2
  626.7 3.8 pad_maximum_fusion.1
  630.5 7.0 %pad_maximum_fusion = f32[2,4,9,256,128]{4,3,2,1,0:T(8,128)} fusion(f32[1,4,9,256,128]{4,3,2,1,0:T(8,128)S(1)} %bitcast.61, f32[1,4,9,256,128]{4,3,2,1,0:T(8,128)} %bitcast.62), kind=kLoop, calls=%fused_computation | loop fusion | flops 2359296 | bytes 18874368 | tf_op jit(solution)/shard_map/stack | solution.py:2578
  637.5 1.0 copy.65
  (68 shorter events, 6.8 us)
Async XLA Ops:
  7.2 204.8 %all-gather.5.cloned.1.call-start = ((), (), s32[]{:S(2)}) async-start(), calls=%async_computation.8 | async-start | bytes 2621440 | tf_op jit(solution)/shard_map/all_gather | solution.py:2368
  154.8 137.7 %all-gather.7.cloned.1.call-start = ((), (), s32[]{:S(2)}) async-start(), calls=%async_computation.9 | async-start | bytes 2621440 | tf_op jit(solution)/shard_map/all_gather | solution.py:2368
  212.0 18.7 %copy-start.14 = (f32[2,6,128]{2,0,1:T(2,128)S(1)}, f32[2,6,128]{2,0,1:T(2,128)}, u32[]{:S(2)}) copy-start(f32[2,6,128]{2,0,1:T(2,128)} %param.25) | copy-start | bytes 18436
  212.0 19.3 %copy-start.15 = (f32[2,6,128]{2,0,1:T(2,128)S(1)}, f32[2,6,128]{2,0,1:T(2,128)}, u32[]{:S(2)}) copy-start(f32[2,6,128]{2,0,1:T(2,128)} %param.26) | copy-start | bytes 18436
  230.6 114.8 %reduce-scatter.7.cloned.1.call-start = ((), (), s32[]{:S(2)}) async-start(), calls=%async_computation.5 | async-start | bytes 2621440 | tf_op jit(solution)/shard_map/reduce_scatter | solution.py:2372
  290.6 99.7 %reduce-scatter.5.cloned.1.call-start = ((), (), s32[]{:S(2)}) async-start(), calls=%async_computation.4 | async-start | bytes 2621440 | tf_op jit(solution)/shard_map/reduce_scatter | solution.py:2372
  345.3 1.4 copy-start.7
  345.3 1.5 copy-start.2
  345.3 128.9 %reduce-scatter.11.cloned.1.call-start = ((), (), s32[]{:S(2)}) async-start(), calls=%async_computation.7 | async-start | bytes 2621440 | tf_op jit(solution)/shard_map/reduce_scatter | solution.py:2372
  389.7 2.7 copy-start.6
  389.8 89.5 %reduce-scatter.9.cloned.1.call-start = ((), (), s32[]{:S(2)}) async-start(), calls=%async_computation.6 | async-start | bytes 2621440 | tf_op jit(solution)/shard_map/reduce_scatter | solution.py:2372
  390.2 2.3 copy-start.3
  425.6 1.0 copy-start.5
  425.6 4.1 copy-start.9
  425.6 4.0 copy-start.10
  546.7 71.1 %copy-start.13 = (f32[12,128]{1,0:T(8,128)S(1)}, f32[12,128]{1,0:T(8,128)}, u32[]{:S(2)}) copy-start(f32[12,128]{1,0:T(8,128)} %get-tuple-element.193) | copy-start | bytes 18436
  546.7 72.3 %copy-start.12 = (f32[256,128]{1,0:T(8,128)S(1)}, f32[256,128]{1,0:T(8,128)}, u32[]{:S(2)}) copy-start(f32[256,128]{1,0:T(8,128)} %get-tuple-element.177) | copy-start | bytes 393220
  546.7 73.9 %copy-start.17 = (f32[2,128]{1,0:T(2,128)S(1)}, f32[2,128]{1,0:T(2,128)}, u32[]{:S(2)}) copy-start(f32[2,128]{1,0:T(2,128)} %get-tuple-element.189) | copy-start | bytes 3076
  546.7 73.9 %copy-start.18 = (f32[2,128]{1,0:T(2,128)S(1)}, f32[2,128]{1,0:T(2,128)}, u32[]{:S(2)}) copy-start(f32[2,128]{1,0:T(2,128)} %get-tuple-element.188) | copy-start | bytes 3076
  546.7 75.2 %copy-start.16 = (f32[2,512]{1,0:T(2,128)S(1)}, f32[2,512]{1,0:T(2,128)}, u32[]{:S(2)}) copy-start(f32[2,512]{1,0:T(2,128)} %get-tuple-element.191) | copy-start | bytes 12292
  546.7 76.6 %copy-start.11 = (f32[64,512]{1,0:T(8,128)S(1)}, f32[64,512]{1,0:T(8,128)}, u32[]{:S(2)}) copy-start(f32[64,512]{1,0:T(8,128)} %get-tuple-element.181) | copy-start | bytes 393220
  546.7 78.2 %copy-start.8 = (f32[9,64,128]{2,1,0:T(8,128)S(1)}, f32[9,64,128]{2,1,0:T(8,128)}, u32[]{:S(2)}) copy-start(f32[9,64,128]{2,1,0:T(8,128)} %get-tuple-element.179) | copy-start | bytes 884740
  616.9 9.8 %copy-start.1 = (f32[6,9,64,128]{3,2,1,0:T(8,128)S(1)}, f32[6,9,64,128]{3,2,1,0:T(8,128)}, u32[]{:S(2)}) copy-start(f32[6,9,64,128]{3,2,1,0:T(8,128)} %get-tuple-element.185) | copy-start | bytes 5308420
  626.7 3.8 copy-start
  630.5 7.0 %copy-start.4 = (f32[512,512]{1,0:T(8,128)S(1)}, f32[512,512]{1,0:T(8,128)}, u32[]{:S(2)}) copy-start(f32[512,512]{1,0:T(8,128)} %get-tuple-element.175) | copy-start | bytes 3145732
Sparse Core Ops, SparseCore 0:
  154.9 57.0 all-gather.4
  230.7 61.7 all-gather.6
  294.8 42.6 reduce-scatter.6
  345.5 42.2 reduce-scatter.4
  389.9 43.8 reduce-scatter.10
  436.0 43.1 reduce-scatter.8

commit v8 on v7

--- a/solution.py
+++ b/solution.py
@@ -2068,7 +2068,7 @@
     return total
 
 
-plan = (2, 4, 2, 4, 1, 3)
+plan = (1, 5, 1, 5, 1, 3)
 
 
 def trunk_backward_kernel(

time: 653 us -> 649 us (level)
  no operation moved by 1% of the time
where the time goes in v8:
time: 649 us; the launch traced here: 641 us
  Pallas kernels  583 us (90%)
  other arithmetic  24.7 us (4%)
  between operations  14.9 us (2%)
  local copies, waits for them, and re-layouts  10.3 us (2%)
  waiting for transfers between devices  8.31 us (1%)
    pallas_call x11, Pallas kernels, call(): pl.pallas_call(wrapped, in_specs=list(in_specs) + [anywhere] * count, out...  523 us
    pallas_call x1, Pallas kernels, prologue(): pl.pallas_call(functools.partial(prologue_kernel, blocks, parts), in_spec...  59.5 us
    another operation x9, other arithmetic, stacked(): return jnp.stack([of(keep) for keep in kept])  18.7 us
  transfers between devices with their start and end apart: 6, of which 3 were waited for; matrix products, arithmetic and copies ran while one was open for 2% of the time, Pallas kernels for 44%

profile of v8, /device:TPU:0, one launch (start us, length us, event | category | flops | bytes accessed | tf_op | source)
XLA Modules:
  0.0 641.4 jit_solution(13879780350096580859)
XLA Ops:
  8.6 59.5 %shard_map.254 = (bf16[512,2048]{1,0:T(8,128)(2,1)}, bf16[512,256]{1,0:T(8,128)(2,1)}, bf16[64,2048]{1,0:T(8,128)(2,1)}, bf16[512,2048]{1,0:T(8,128)(2,1)}, bf16...) custom-call(bf16[512,512]{1,0:T(8,128)(2,1)} %bitcast.77, ...), custom_call_target="tpu_custom_call" | custom-call | flops 1000000 | bytes 100000000 | tf_op jit(solution)/shard_map/pallas_call | solution.py:1002
  68.1 49.8 %shard_map.255 = (bf16[512,2048]{1,0:T(8,128)(2,1)}, bf16[1024,512]{1,0:T(8,128)(2,1)}, bf16[512,512]{1,0:T(8,128)(2,1)}, f32[512,128]{1,0:T(8,128)}, f32[1,128]...) custom-call(bf16[512,2048]{1,0:T(8,128)(2,1)} %get-tuple-element.104, ...), custom_call_target="tpu_custom_call" | custom-call | flops 2751463424 | bytes 157286400 | tf_op jit(solution)/shard_map/pallas_call | solution.py:746
  117.9 36.9 %shard_map.256 = (f32[4,512,128]{2,1,0:T(8,128)}, bf16[4,512,128]{2,1,0:T(8,128)(2,1)}, bf16[2,512,128]{2,1,0:T(8,128)(2,1)}, bf16[512,2048]{1,0:T(8,128)(2,1)}, bf16[512,2048]{1,0:T(8,128)(2,1)}) custom-call(bf16[512,2048]{1,0:T(8,128)(2,1)} %get-tuple-element.116.refs_0_.refs_7_.refs_4_.refs_2_, bf16[2,4,9,128,2048]{4,3,2,1,0:T(8,128)(2,1)} %bitcast.57, ...), custom_call_target="tpu_custom_call" | custom-call | flops 9663676416 | bytes 18874368 | tf_op jit(solution)/shard_map/pallas_call | solution.py:746
  154.8 56.0 %shard_map.257 = (bf16[512,2048]{1,0:T(8,128)(2,1)}, bf16[1024,512]{1,0:T(8,128)(2,1)}, bf16[512,512]{1,0:T(8,128)(2,1)}, f32[512,128]{1,0:T(8,128)}, f32[1,128]...) custom-call(bf16[512,2048]{1,0:T(8,128)(2,1)} %get-tuple-element.116, ...), custom_call_target="tpu_custom_call" | custom-call | flops 2751463424 | bytes 157286400 | tf_op jit(solution)/shard_map/pallas_call | solution.py:746
  210.8 1.1 all-gather.5.cloned.1.call-done
  212.0 18.6 %shard_map.258 = (f32[4,512,128]{2,1,0:T(8,128)}, bf16[4,512,128]{2,1,0:T(8,128)(2,1)}, bf16[2,512,128]{2,1,0:T(8,128)(2,1)}) custom-call(bf16[512,2048]{1,0:T(8,128)(2,1)} %get-tuple-element.123.refs_0_.refs_3_.refs_4_, bf16[2,4,9,128,2048]{4,3,2,1,0:T(8,128)(2,1)} %bitcast.58, s32[2,512,128]{2,1,0:T(8,128)} %get-tuple-element.107.refs_4_.refs_2_.refs_5_.refs_10_), custom_call_target="tpu_custom_call" | custom-call | flops 9663676416 | bytes 18874368 | tf_op jit(solution)/shard_map/pallas_call | solution.py:746
  231.9 58.7 %shard_map.259 = (bf16[2,512,128]{2,1,0:T(8,128)(2,1)}, f32[2,512,128]{2,1,0:T(8,128)}, f32[12,128]{1,0:T(8,128)}, bf16[4,4,512,128]{3,2,1,0:T(8,128)(2,1)}, bf1...) custom-call(bf16[4,4,512,128]{3,2,1,0:T(8,128)(2,1)} %bitcast.96, ...), custom_call_target="tpu_custom_call" | custom-call | flops 7247757312 | bytes 7077888 | tf_op jit(solution)/shard_map/pallas_call | solution.py:746
  290.6 1.9 all-gather.7.cloned.1.call-done
  292.5 52.8 %shard_map.260 = (bf16[2,512,128]{2,1,0:T(8,128)(2,1)}, f32[2,512,128]{2,1,0:T(8,128)}, f32[12,128]{1,0:T(8,128)}, bf16[4,4,512,128]{3,2,1,0:T(8,128)(2,1)}, bf1...) custom-call(bf16[4,4,512,128]{3,2,1,0:T(8,128)(2,1)} %bitcast.97, bf16[2,6,9,128,512]{4,3,2,1,0:T(8,128)(2,1)} %bitcast.95, ...), custom_call_target="tpu_custom_call" | custom-call | flops 7247757312 | bytes 7077888 | tf_op jit(solution)/shard_map/pallas_call | solution.py:746
  345.4 1.2 convert_element_type.20
  346.9 1.2 fusion.refs_0_
  348.1 41.6 %shard_map.261 = (bf16[4,512,512]{2,1,0:T(8,128)(2,1)}, bf16[8,2,512,128]{3,2,1,0:T(8,128)(2,1)}, bf16[8,256,256]{2,1,0:T(8,128)(2,1)}) custom-call(bf16[4,512,128]{2,1,0:T(8,128)(2,1)} %fusion.refs_0_, bf16[2,4,9,128,2048]{4,3,2,1,0:T(8,128)(2,1)} %bitcast.59, s32[2,512,128]{2,1,0:T(8,128)} %get-tuple-element.107.refs_4_.refs_2_.refs_5_.refs_10_, ...), custom_call_target="tpu_custom_call" | custom-call | flops 9663676416 | bytes 18874368 | tf_op jit(solution)/shard_map/pallas_call | solution.py:746
  390.0 1.1 slice.84
  391.1 1.1 convert_element_type.22
  392.3 1.2 fusion.1.refs_0_.refs_1_
  393.5 31.9 %shard_map.262 = (bf16[4,512,512]{2,1,0:T(8,128)(2,1)}, bf16[8,256,256]{2,1,0:T(8,128)(2,1)}, bf16[8,256,256]{2,1,0:T(8,128)(2,1)}) custom-call(bf16[4,512,128]{2,1,0:T(8,128)(2,1)} %fusion.1.refs_0_.refs_1_, bf16[2,4,9,128,2048]{4,3,2,1,0:T(8,128)(2,1)} %bitcast.60, s32[2,512,128]{2,1,0:T(8,128)} %get-tuple-element.107.refs_4_.refs_2_.refs_5_.refs_10_, ...), custom_call_target="tpu_custom_call" | custom-call | flops 9663676416 | bytes 18874368 | tf_op jit(solution)/shard_map/pallas_call | solution.py:746
  425.5 1.0 copy-done.5
  426.5 1.1 bitcast_convert_fusion.refs_0_
  427.7 1.9 constant_dynamic-slice_fusion
  429.5 0.8 pad_maximum_fusion.3
  430.4 43.7 %shard_map.263 = (f32[8,128]{1,0:T(8,128)}, bf16[8,4,512,128]{3,2,1,0:T(8,128)(2,1)}, bf16[8,4,512,128]{3,2,1,0:T(8,128)(2,1)}) custom-call(bf16[4,512,128]{2,1,0:T(8,128)(2,1)} %fusion.refs_0_, bf16[4,512,128]{2,1,0:T(8,128)(2,1)} %fusion.1.refs_0_.refs_1_), custom_call_target="tpu_custom_call" | custom-call | flops 1000000 | bytes 100000000 | tf_op jit(solution)/shard_map/pallas_call | solution.py:746
  474.1 5.2 reduce-scatter.9.cloned.1.call-done
  479.3 65.1 %shard_map.264 = (f32[512,512]{1,0:T(8,128)}, f32[64,512]{1,0:T(8,128)}, f32[9,64,128]{2,1,0:T(8,128)}, f32[256,128]{1,0:T(8,128)}, f32[2,512]{1,0:T(2,128)}, /*...) custom-call(f32[512,512]{1,0:T(8,128)} %bitcast_convert_fusion.refs_, ...), custom_call_target="tpu_custom_call" | custom-call | flops 22281701376 | bytes 209715200 | tf_op jit(solution)/shard_map/pallas_call | solution.py:746
  544.5 68.1 %shard_map.265 = (f32[512,512]{1,0:T(8,128)}, f32[64,512]{1,0:T(8,128)}, f32[9,64,128]{2,1,0:T(8,128)}, f32[256,128]{1,0:T(8,128)}, f32[2,512]{1,0:T(2,128)}, /*...) custom-call(f32[512,512]{1,0:T(8,128)} %get-tuple-element.158.refs_0, ...), custom_call_target="tpu_custom_call" | custom-call | flops 22281701376 | bytes 209715200 | tf_op jit(solution)/shard_map/pallas_call | solution.py:746
  612.5 0.8 stack_reshape.14
  614.6 1.6 pad_maximum_fusion.4
  617.5 0.8 pad_maximum_fusion.6
  618.9 1.6 pad_maximum_fusion.5
  620.5 1.8 pad_maximum_fusion.2
  622.3 3.8 pad_maximum_fusion.1
  626.1 7.0 %pad_maximum_fusion = f32[2,4,9,256,128]{4,3,2,1,0:T(8,128)} fusion(f32[1,4,9,256,128]{4,3,2,1,0:T(8,128)S(1)} %bitcast.61, f32[1,4,9,256,128]{4,3,2,1,0:T(8,128)} %bitcast.62), kind=kLoop, calls=%fused_computation | loop fusion | flops 2359296 | bytes 18874368 | tf_op jit(solution)/shard_map/stack | solution.py:2578
  633.1 1.0 copy.65
  (68 shorter events, 6.6 us)
Async XLA Ops:
  7.2 204.8 %all-gather.5.cloned.1.call-start = ((), (), s32[]{:S(2)}) async-start(), calls=%async_computation.8 | async-start | bytes 2621440 | tf_op jit(solution)/shard_map/all_gather | solution.py:2368
  154.8 137.7 %all-gather.7.cloned.1.call-start = ((), (), s32[]{:S(2)}) async-start(), calls=%async_computation.9 | async-start | bytes 2621440 | tf_op jit(solution)/shard_map/all_gather | solution.py:2368
  212.0 18.7 %copy-start.14 = (f32[2,6,128]{2,0,1:T(2,128)S(1)}, f32[2,6,128]{2,0,1:T(2,128)}, u32[]{:S(2)}) copy-start(f32[2,6,128]{2,0,1:T(2,128)} %param.25) | copy-start | bytes 18436
  212.0 19.3 %copy-start.15 = (f32[2,6,128]{2,0,1:T(2,128)S(1)}, f32[2,6,128]{2,0,1:T(2,128)}, u32[]{:S(2)}) copy-start(f32[2,6,128]{2,0,1:T(2,128)} %param.26) | copy-start | bytes 18436
  230.6 114.8 %reduce-scatter.7.cloned.1.call-start = ((), (), s32[]{:S(2)}) async-start(), calls=%async_computation.5 | async-start | bytes 2621440 | tf_op jit(solution)/shard_map/reduce_scatter | solution.py:2372
  290.6 99.5 %reduce-scatter.5.cloned.1.call-start = ((), (), s32[]{:S(2)}) async-start(), calls=%async_computation.4 | async-start | bytes 2621440 | tf_op jit(solution)/shard_map/reduce_scatter | solution.py:2372
  345.3 1.4 copy-start.7
  345.3 1.5 copy-start.2
  345.3 128.7 %reduce-scatter.11.cloned.1.call-start = ((), (), s32[]{:S(2)}) async-start(), calls=%async_computation.7 | async-start | bytes 2621440 | tf_op jit(solution)/shard_map/reduce_scatter | solution.py:2372
  389.7 2.5 copy-start.6
  389.8 89.5 %reduce-scatter.9.cloned.1.call-start = ((), (), s32[]{:S(2)}) async-start(), calls=%async_computation.6 | async-start | bytes 2621440 | tf_op jit(solution)/shard_map/reduce_scatter | solution.py:2372
  390.0 2.3 copy-start.3
  425.5 1.0 copy-start.5
  425.5 4.1 copy-start.9
  425.5 4.0 copy-start.10
  544.4 69.0 %copy-start.13 = (f32[12,128]{1,0:T(8,128)S(1)}, f32[12,128]{1,0:T(8,128)}, u32[]{:S(2)}) copy-start(f32[12,128]{1,0:T(8,128)} %get-tuple-element.193) | copy-start | bytes 18436
  544.4 70.2 %copy-start.12 = (f32[256,128]{1,0:T(8,128)S(1)}, f32[256,128]{1,0:T(8,128)}, u32[]{:S(2)}) copy-start(f32[256,128]{1,0:T(8,128)} %get-tuple-element.177) | copy-start | bytes 393220
  544.4 71.8 %copy-start.17 = (f32[2,128]{1,0:T(2,128)S(1)}, f32[2,128]{1,0:T(2,128)}, u32[]{:S(2)}) copy-start(f32[2,128]{1,0:T(2,128)} %get-tuple-element.189) | copy-start | bytes 3076
  544.4 71.8 %copy-start.18 = (f32[2,128]{1,0:T(2,128)S(1)}, f32[2,128]{1,0:T(2,128)}, u32[]{:S(2)}) copy-start(f32[2,128]{1,0:T(2,128)} %get-tuple-element.188) | copy-start | bytes 3076
  544.4 73.1 %copy-start.16 = (f32[2,512]{1,0:T(2,128)S(1)}, f32[2,512]{1,0:T(2,128)}, u32[]{:S(2)}) copy-start(f32[2,512]{1,0:T(2,128)} %get-tuple-element.191) | copy-start | bytes 12292
  544.4 74.4 %copy-start.11 = (f32[64,512]{1,0:T(8,128)S(1)}, f32[64,512]{1,0:T(8,128)}, u32[]{:S(2)}) copy-start(f32[64,512]{1,0:T(8,128)} %get-tuple-element.181) | copy-start | bytes 393220
  544.4 76.1 %copy-start.8 = (f32[9,64,128]{2,1,0:T(8,128)S(1)}, f32[9,64,128]{2,1,0:T(8,128)}, u32[]{:S(2)}) copy-start(f32[9,64,128]{2,1,0:T(8,128)} %get-tuple-element.179) | copy-start | bytes 884740
  612.5 9.8 %copy-start.1 = (f32[6,9,64,128]{3,2,1,0:T(8,128)S(1)}, f32[6,9,64,128]{3,2,1,0:T(8,128)}, u32[]{:S(2)}) copy-start(f32[6,9,64,128]{3,2,1,0:T(8,128)} %get-tuple-element.185) | copy-start | bytes 5308420
  622.3 3.8 copy-start
  626.1 7.0 %copy-start.4 = (f32[512,512]{1,0:T(8,128)S(1)}, f32[512,512]{1,0:T(8,128)}, u32[]{:S(2)}) copy-start(f32[512,512]{1,0:T(8,128)} %get-tuple-element.175) | copy-start | bytes 3145732
Sparse Core Ops, SparseCore 0:
  154.9 57.0 all-gather.4
  230.7 61.7 all-gather.6
  294.8 42.6 reduce-scatter.6
  345.5 42.2 reduce-scatter.4
  389.9 43.8 reduce-scatter.10
  436.0 43.1 reduce-scatter.8
